TPU v7x, 32 devices: a whole 2x2x4 slice. The times are simulated.
32 devices in a mesh: tm: 4 (over y, x), tmpl: 8 (over z, core).
Axes of the slice: x: 2, y: 2, z: 4, core: 2. Of those that a mesh axis runs over, the one named last changes fastest.
Arguments:
- strain: float32 [65536], P(('tm', 'tmpl')), may hold values from -40 to 40, as said below
- templates: bfloat16 [2, 128, 2048], P(None, 'tmpl', 'tm'), may hold values from -6 to 6
- cutoff: int32 [128], P('tmpl'), may hold values from 512 to 2048
Outputs:
- snr_peak: float32 [32, 128], P('tm', 'tmpl')
Inputs may be any that keep to these rules, and one draw needn't show every extreme that they name: `strain`: one contiguous record of 65536 samples.
All inputs are finite; a program needn't handle non-finite values.
Results may differ from a plain program's by a relative error of at most 0.00098.
Values may be sent and summed in bfloat16 or wider, within the bound.
No kernel may reach another device: no remote copies, remote signals or barrier semaphores. Data moves between devices by JAX's collectives and lax.ppermute only.
A program may use at most 64 MiB of HBM per device.

v0:
```python
import jax
import jax.numpy as jnp
from jax import lax
from jax.sharding import PartitionSpec as P

RADIX = 64
NFFT = 4096
BINS = 2048
HOP = 2048
SEG_DEV = 1


def shifted(array, axis, by):
    devices = lax.axis_size(axis)
    return lax.ppermute(array, axis, [(i, (i + by) % devices) for i in range(devices)])


def hann_window():
    sample = jnp.arange(NFFT, dtype=jnp.float32)
    return 0.5 - 0.5 * jnp.cos(2.0 * jnp.pi * sample / NFFT)


def phase_table(row_count, col_count, period):
    left_index = jnp.arange(row_count, dtype=jnp.int32)[:, None]
    right_index = jnp.arange(col_count, dtype=jnp.int32)[None, :]
    return 2.0 * jnp.pi / period * (left_index * right_index % period).astype(jnp.float32)


def contract(pattern, left_side, right_side):
    return jnp.einsum(pattern, left_side, right_side, precision=lax.Precision.HIGHEST)


def forward_bins(frames):
    seg_count = frames.shape[0]
    square = phase_table(RADIX, RADIX, RADIX)
    twiddle = phase_table(RADIX, RADIX, NFFT)
    grid_view = frames.reshape(seg_count, RADIX, RADIX)
    first_real = contract("sab,ac->sbc", grid_view, jnp.cos(square))
    first_imag = -contract("sab,ac->sbc", grid_view, jnp.sin(square))
    turn_cos = jnp.cos(twiddle)
    turn_sin = jnp.sin(twiddle)
    next_real = first_real * turn_cos + first_imag * turn_sin
    next_imag = first_imag * turn_cos - first_real * turn_sin
    half_cos = jnp.cos(square[:, : RADIX // 2])
    half_sin = jnp.sin(square[:, : RADIX // 2])
    out_real = contract("sbc,bd->sdc", next_real, half_cos) + contract(
        "sbc,bd->sdc", next_imag, half_sin
    )
    out_imag = contract("sbc,bd->sdc", next_imag, half_cos) - contract(
        "sbc,bd->sdc", next_real, half_sin
    )
    return (out_real.reshape(seg_count, BINS), out_imag.reshape(seg_count, BINS))


def peak_magnitude(group):
    group_size = group.shape[0]
    seg_count = group.shape[2]
    half = RADIX // 2
    square = phase_table(RADIX, RADIX, RADIX)
    twiddle_flip = phase_table(RADIX, RADIX, NFFT)
    full_cos = jnp.cos(square)
    full_sin = jnp.sin(square)
    half_cos = full_cos[:half, :]
    half_sin = full_sin[:half, :]
    section_table = jnp.concatenate(
        [
            jnp.concatenate([half_cos, half_sin], axis=1),
            jnp.concatenate([-half_sin, half_cos], axis=1),
        ],
        axis=0,
    )
    packed = group.reshape(group_size, 2, seg_count, half, RADIX).transpose(0, 2, 1, 3, 4)
    packed = packed.reshape(group_size * seg_count, 2 * half, RADIX).astype(jnp.float32)
    section = contract("sdc,dq->scq", packed, section_table)
    turn_cos = jnp.cos(twiddle_flip)
    turn_sin = jnp.sin(twiddle_flip)
    section_real = section[:, :, :RADIX]
    section_imag = section[:, :, RADIX:]
    turned = jnp.concatenate(
        [
            section_real * turn_cos - section_imag * turn_sin,
            section_real * turn_sin + section_imag * turn_cos,
        ],
        axis=2,
    )
    with_cos = contract("scp,ca->sap", turned, full_cos)
    with_sin = contract("scp,ca->sap", turned, full_sin)
    wave_real = with_cos[:, :, :RADIX] - with_sin[:, :, RADIX:]
    wave_imag = with_sin[:, :, :RADIX] + with_cos[:, :, RADIX:]
    peaks = jnp.sqrt(jnp.max(wave_real * wave_real + wave_imag * wave_imag, axis=(1, 2)))
    return peaks.reshape(group_size, seg_count)


def filter_peaks(products):
    tmpl_count = products.shape[0]
    group_size = min(tmpl_count, 4)
    grouped = products.reshape((tmpl_count // group_size, group_size) + products.shape[1:])
    peaks = lax.map(peak_magnitude, grouped)
    return peaks.reshape(tmpl_count, products.shape[2])


def correlate(tmpl_real, tmpl_imag, data_real, data_imag, keep_mask):
    prod_real = (
        tmpl_real[:, None, :] * data_real[None] + tmpl_imag[:, None, :] * data_imag[None]
    ) * keep_mask[:, None, :]
    prod_imag = (
        tmpl_real[:, None, :] * data_imag[None] - tmpl_imag[:, None, :] * data_real[None]
    ) * keep_mask[:, None, :]
    return jnp.stack([prod_real, prod_imag], axis=1).astype(jnp.bfloat16)


def on_device(strain, templates, cutoff):
    window = hann_window()
    norm_window = jnp.sum(window * window)
    following = shifted(strain, ("tm", "tmpl"), -1)
    extended = jnp.concatenate([strain, following]).reshape(SEG_DEV + 1, HOP)
    frames = jnp.concatenate([extended[:-1], extended[1:]], axis=1) * window
    spec_real, spec_imag = forward_bins(frames)
    local_power = jnp.sum(spec_real * spec_real + spec_imag * spec_imag, axis=0)
    total_power = lax.psum(local_power, ("tm", "tmpl"))
    seg_total = SEG_DEV * lax.axis_size("tm") * lax.axis_size("tmpl")
    density = total_power / (seg_total * norm_window) + 1e-06
    whitened = jnp.stack([spec_real / density, spec_imag / density], axis=1).astype(jnp.bfloat16)
    block_spectra = lax.all_gather(whitened, "tmpl", axis=0, tiled=True)
    block_index = lax.axis_index("tm")
    bin_width = templates.shape[2]
    local_bins = block_index * bin_width + jnp.arange(bin_width, dtype=jnp.int32)
    keep_mask = (local_bins[None, :] < cutoff[:, None]).astype(jnp.float32)
    part_density = lax.dynamic_slice_in_dim(density, block_index * bin_width, bin_width)
    tmpl_real = templates[0].astype(jnp.float32)
    tmpl_imag = templates[1].astype(jnp.float32)
    by_bins = lax.all_to_all(block_spectra, "tm", split_axis=2, concat_axis=0, tiled=True)
    products = correlate(
        tmpl_real,
        tmpl_imag,
        by_bins[:, 0].astype(jnp.float32),
        by_bins[:, 1].astype(jnp.float32),
        keep_mask,
    )
    products = lax.all_to_all(products, "tm", split_axis=2, concat_axis=3, tiled=True)
    partial_norms = jnp.sum(
        keep_mask * (tmpl_real * tmpl_real + tmpl_imag * tmpl_imag) / part_density, axis=1
    )
    norm_squares = lax.psum(partial_norms, "tm")
    peak_values = filter_peaks(products)
    norm_scale = jnp.sqrt(norm_squares) * jnp.sqrt(norm_window)
    return (peak_values / norm_scale[:, None]).T


def solution(mesh):
    in_specs = (P(("tm", "tmpl")), P(None, "tmpl", "tm"), P("tmpl"))
    out_specs = P("tm", "tmpl")
    return jax.shard_map(
        on_device, mesh=mesh, in_specs=in_specs, out_specs=out_specs, check_vma=False
    )
```

profile of v0, /device:TPU:0, one launch (start us, length us, event | category | flops | bytes accessed | tf_op | source)
XLA Modules:
  0.0 130.5 jit_solution(834306267269129572)
XLA Ops:
  0.0 6.4 %collective-permute-start = (f32[2048]{0:T(1024)}, f32[2048]{0:T(1024)S(1)}, u32[]{:S(2)}, u32[]{:S(2)}) collective-permute-start(f32[2048]{0:T(1024)} %param.5), channel_id=1, source_target_pairs={{0,31},{1,0},{2,1},{3,2},{4,3},{5,4},{6,5},{7,6},{8,7},{9,8},{10,9... | collective-permute-start | bytes 24584 | tf_op jit(solution)/shard_map/ppermute | solution.py:15
  6.4 0.7 bitcast_convert_fusion.1
  7.2 0.8 concatenate.61
  7.9 0.7 multiply_reduce_fusion
  9.3 0.7 maximum_reduce_fusion
  10.1 0.4 fusion.51
  10.6 0.4 convolution_negate_fusion
  11.0 0.4 fusion.62
  11.4 0.4 fusion.63
  11.8 0.4 convolution_subtract_fusion
  12.3 0.4 convolution_add_fusion
  12.8 37.5 %psum.14 = f32[2048]{0:T(1024)S(1)} all-reduce(f32[2048]{0:T(1024)S(1)} %multiply_add_fusion.2), channel_id=1, replica_groups=mesh['tm'=4,'tmpl'=8] {'tm','tmpl'}, use_global_device_ids=true, to_apply=%region_0.0 | all-reduce | flops 2048 | bytes 16384 | tf_op jit(solution)/shard_map/psum | solution.py:120
  50.3 14.4 %all_gather.3 = bf16[8,2,2048]{2,1,0:T(2,128)(2,1)S(1)} all-gather(bf16[1,2,2048]{2,1,0:T(2,128)(2,1)S(1)} %pad_maximum_fusion.4), channel_id=1, replica_groups=mesh['tm'=4,'tmpl'=8] {'tmpl'}, dimensions={0}, use_global_device_ids=true | all-gather | bytes 73728 | tf_op jit(solution)/shard_map/all_gather | solution.py:124
  64.8 0.8 copy.22
  65.5 1.7 %reshape.290 = bf16[4,2,4096]{2,1,0:T(2,128)(2,1)} reshape(bf16[2048,2,8]{2,1,0:T(2,128)(2,1)S(1)} %bitcast.74) | data formatting | bytes 131072
  67.3 4.5 %all-to-all-start = ((bf16[4,2,4096]{2,1,0:T(2,128)(2,1)}), bf16[4,2,4096]{2,1,0:T(2,128)(2,1)S(1)}, u32[]{:S(2)}, u32[]{:S(2)}) async-start(bf16[4,2,4096]{2,1,0:T(2,128)(2,1)} %reshape.290), calls=%async_computation | async-start | bytes 131072 | tf_op jit(solution)/shard_map/all_to_all | solution.py:132
  71.8 4.8 %all-to-all-done = bf16[4,2,4096]{2,1,0:T(2,128)(2,1)S(1)} async-done(((bf16[4,2,4096]{2,1,0:T(2,128)(2,1)}), bf16[4,2,4096]{2,1,0:T(2,128)(2,1)S(1)}, u32[]{:S(2)}, u32[]{:S(2)}) %all-to-all-start) | async-done | bytes 65568 | tf_op jit(solution)/shard_map/all_to_all | solution.py:132
  76.6 1.2 reshape.291
  77.8 0.7 copy.32
  78.5 2.8 %multiply_convert_fusion.1 = (bf16[16,1,32,512]{3,1,0,2:T(2,128)(2,1)S(1)}, bf16[16,1,32,512]{3,1,0,2:T(2,128)(2,1)S(1)}) fusion(f32[16,512]{1,0:T(8,128)S(1)} %compare_convert_fusion, f32[32,512]{1,0:T(8,128)S(1)} %get-tuple-element.82, f32[16,512]{1,0:T(8,128)S(1)} %get-tuple-element.84, f32[32,512]{1,0:T(8,128)S(1)} %get-tuple-element.81, ...), kind=kLoop, calls=%fused_computation.61 | loop fusion | flops 2621440 | bytes 1277952 | tf_op jit(solution)/shard_map/convert.4
  81.4 3.2 %pad_maximum_fusion.3 = bf16[16,2,32,512]{3,1,0,2:T(2,128)(2,1)} fusion(bf16[16,1,32,512]{3,1,0,2:T(2,128)(2,1)S(1)} %get-tuple-element.80, bf16[16,1,32,512]{3,1,0,2:T(2,128)(2,1)S(1)} %get-tuple-element.79), kind=kLoop, calls=%fused_computation.59 | loop fusion | flops 2097152 | bytes 2097152 | tf_op jit(solution)/shard_map/stack | solution.py:109
  84.6 3.6 %all-to-all-start.1 = ((bf16[16,2,32,512]{3,1,0,2:T(2,128)(2,1)}), bf16[16,2,32,512]{3,1,0,2:T(2,128)(2,1)S(1)}, u32[]{:S(2)}, u32[]{:S(2)}) async-start(bf16[16,2,32,512]{3,1,0,2:T(2,128)(2,1)} %pad_maximum_fusion.3), calls=%async_computation.1 | async-start | bytes 2097152 | tf_op jit(solution)/shard_map/all_to_all | solution.py:140
  89.0 0.2 fusion.59
  89.2 15.1 %psum.15 = f32[16]{0:T(128)S(1)} all-reduce(f32[16]{0:T(128)S(1)} %fusion.59), channel_id=1, replica_groups=mesh['tm'=4,'tmpl'=8] {'tm'}, use_global_device_ids=true, to_apply=%region_6.7 | all-reduce | flops 16 | bytes 128 | tf_op jit(solution)/shard_map/psum | solution.py:144
  104.4 0.6 copy.25
  104.9 24.8 %while.13 = (s32[]{:T(128)}, f32[4,4,8]{2,1,0:T(4,128)S(1)}, bf16[4,4,2,8,2048]{4,3,2,1,0:T(8,128)(2,1)S(1)}, s32[]{:T(128)}) while((s32[]{:T(128)}, f32[4,4,8]{2,1,0:T(4,128)S(1)}, bf16[4,4,2,8,2048]{4,3,2,1,0:T(8,128)(2,1)S(1)}, s32[]{:T(128)}) %tuple.45), condition=%wide.region_4.5_spmd, body=%wide.region_2.4_spmd.sunk | while | flops 606390272 | bytes 11440837 | solution.py:98
  105.0 0.1 fusion.120
  105.1 0.1 fusion.119
  105.3 0.1 fusion.123
  105.5 0.5 reshape.293
  106.0 0.7 fusion.122
  106.7 0.5 multiply_subtract_fusion.8
  107.3 1.4 %convolution_bitcast_fusion.5 = f32[32,64,128]{2,1,0:T(8,128)S(1)} fusion(f32[32,64,64]{2,1,0:T(8,128)S(1)} %get-tuple-element.114, f32[32,64,64]{2,1,0:T(8,128)S(1)} %get-tuple-element.115), kind=kOutput, calls=%fused_computation.clone.1 | convolution fusion | flops 201646080 | bytes 2097152 | tf_op jit(solution)/shard_map/while/body/eval_jaxpr/scp,ca->sap/dot_general | solution.py:30
  108.6 1.4 %convolution_bitcast_fusion.4 = f32[32,64,128]{2,1,0:T(8,128)S(1)} fusion(f32[32,64,64]{2,1,0:T(8,128)S(1)} %get-tuple-element.114, f32[32,64,64]{2,1,0:T(8,128)S(1)} %get-tuple-element.115), kind=kOutput, calls=%fused_computation.1.clone.1 | convolution fusion | flops 201646080 | bytes 2097152 | tf_op jit(solution)/shard_map/while/body/eval_jaxpr/scp,ca->sap/dot_general | solution.py:30
  110.0 1.0 fusion.124
  111.1 0.1 sqrt.29
  111.1 0.1 fusion.120
  111.3 0.1 fusion.119
  111.5 0.1 fusion.123
  111.7 0.5 reshape.293
  112.2 0.7 fusion.122
  112.9 0.5 multiply_subtract_fusion.8
  113.5 1.4 %convolution_bitcast_fusion.5 = f32[32,64,128]{2,1,0:T(8,128)S(1)} fusion(f32[32,64,64]{2,1,0:T(8,128)S(1)} %get-tuple-element.114, f32[32,64,64]{2,1,0:T(8,128)S(1)} %get-tuple-element.115), kind=kOutput, calls=%fused_computation.clone.1 | convolution fusion | flops 201646080 | bytes 2097152 | tf_op jit(solution)/shard_map/while/body/eval_jaxpr/scp,ca->sap/dot_general | solution.py:30
  114.8 1.4 %convolution_bitcast_fusion.4 = f32[32,64,128]{2,1,0:T(8,128)S(1)} fusion(f32[32,64,64]{2,1,0:T(8,128)S(1)} %get-tuple-element.114, f32[32,64,64]{2,1,0:T(8,128)S(1)} %get-tuple-element.115), kind=kOutput, calls=%fused_computation.1.clone.1 | convolution fusion | flops 201646080 | bytes 2097152 | tf_op jit(solution)/shard_map/while/body/eval_jaxpr/scp,ca->sap/dot_general | solution.py:30
  116.2 1.0 fusion.124
  117.3 0.1 fusion.120
  117.5 0.1 fusion.119
  117.7 0.1 fusion.123
  117.9 0.5 reshape.293
  118.4 0.7 fusion.122
  119.1 0.5 multiply_subtract_fusion.8
  119.7 1.4 %convolution_bitcast_fusion.5 = f32[32,64,128]{2,1,0:T(8,128)S(1)} fusion(f32[32,64,64]{2,1,0:T(8,128)S(1)} %get-tuple-element.114, f32[32,64,64]{2,1,0:T(8,128)S(1)} %get-tuple-element.115), kind=kOutput, calls=%fused_computation.clone.1 | convolution fusion | flops 201646080 | bytes 2097152 | tf_op jit(solution)/shard_map/while/body/eval_jaxpr/scp,ca->sap/dot_general | solution.py:30
  121.0 1.4 %convolution_bitcast_fusion.4 = f32[32,64,128]{2,1,0:T(8,128)S(1)} fusion(f32[32,64,64]{2,1,0:T(8,128)S(1)} %get-tuple-element.114, f32[32,64,64]{2,1,0:T(8,128)S(1)} %get-tuple-element.115), kind=kOutput, calls=%fused_computation.1.clone.1 | convolution fusion | flops 201646080 | bytes 2097152 | tf_op jit(solution)/shard_map/while/body/eval_jaxpr/scp,ca->sap/dot_general | solution.py:30
  122.4 1.0 fusion.124
  123.5 0.1 fusion.120
  123.7 0.1 fusion.119
  123.9 0.1 fusion.123
  124.1 0.5 reshape.293
  124.6 0.7 fusion.122
  125.3 0.5 multiply_subtract_fusion.8
  125.9 1.4 %convolution_bitcast_fusion.5 = f32[32,64,128]{2,1,0:T(8,128)S(1)} fusion(f32[32,64,64]{2,1,0:T(8,128)S(1)} %get-tuple-element.114, f32[32,64,64]{2,1,0:T(8,128)S(1)} %get-tuple-element.115), kind=kOutput, calls=%fused_computation.clone.1 | convolution fusion | flops 201646080 | bytes 2097152 | tf_op jit(solution)/shard_map/while/body/eval_jaxpr/scp,ca->sap/dot_general | solution.py:30
  127.2 1.4 %convolution_bitcast_fusion.4 = f32[32,64,128]{2,1,0:T(8,128)S(1)} fusion(f32[32,64,64]{2,1,0:T(8,128)S(1)} %get-tuple-element.114, f32[32,64,64]{2,1,0:T(8,128)S(1)} %get-tuple-element.115), kind=kOutput, calls=%fused_computation.1.clone.1 | convolution fusion | flops 201646080 | bytes 2097152 | tf_op jit(solution)/shard_map/while/body/eval_jaxpr/scp,ca->sap/dot_general | solution.py:30
  128.6 1.0 fusion.124
  129.8 0.7 copy.26
  (52 shorter events, 1.3 us)
Async XLA Ops:
  0.0 9.3 %collective-permute-start = (f32[2048]{0:T(1024)}, f32[2048]{0:T(1024)S(1)}, u32[]{:S(2)}, u32[]{:S(2)}) collective-permute-start(f32[2048]{0:T(1024)} %param.5), channel_id=1, source_target_pairs={{0,31},{1,0},{2,1},{3,2},{4,3},{5,4},{6,5},{7,6},{8,7},{9,8},{10,9... | collective-permute-start | bytes 24584 | tf_op jit(solution)/shard_map/ppermute | solution.py:15
  64.8 7.0 %copy-start.1 = (s32[16]{0:T(128)S(1)}, s32[16]{0:T(128)}, u32[]{:S(2)}) copy-start(s32[16]{0:T(128)} %param.7) | copy-start | bytes 196
  67.3 9.3 %all-to-all-start = ((bf16[4,2,4096]{2,1,0:T(2,128)(2,1)}), bf16[4,2,4096]{2,1,0:T(2,128)(2,1)S(1)}, u32[]{:S(2)}, u32[]{:S(2)}) async-start(bf16[4,2,4096]{2,1,0:T(2,128)(2,1)} %reshape.290), calls=%async_computation | async-start | bytes 131072 | tf_op jit(solution)/shard_map/all_to_all | solution.py:132
  84.6 4.4 %copy-start = (bf16[2,16,512]{2,1,0:T(8,128)(2,1)S(1)}, bf16[2,16,512]{2,1,0:T(8,128)(2,1)}, u32[]{:S(2)}) copy-start(bf16[2,16,512]{2,1,0:T(8,128)(2,1)} %param.6) | copy-start | bytes 98308
  84.6 19.8 %all-to-all-start.1 = ((bf16[16,2,32,512]{3,1,0,2:T(2,128)(2,1)}), bf16[16,2,32,512]{3,1,0,2:T(2,128)(2,1)S(1)}, u32[]{:S(2)}, u32[]{:S(2)}) async-start(bf16[16,2,32,512]{3,1,0,2:T(2,128)(2,1)} %pad_maximum_fusion.3), calls=%async_computation.1 | async-start | bytes 2097152 | tf_op jit(solution)/shard_map/all_to_all | solution.py:140
where the time goes:
time: 131 us
  blocking collectives  67.1 us (51%)
  other arithmetic  16.5 us (13%)
  matrix products  16.2 us (12%)
  starting transfers between devices  14.5 us (11%)
  local copies, waits for them, and re-layouts  9.58 us (7%)
  waiting for transfers between devices  4.78 us (4%)
  between operations  1.52 us (1%)
    psum x1, blocking collectives, on_device(): total_power = lax.psum(local_power, ('tm', 'tmpl'))  37.5 us
    dot_general x18, matrix products, contract(): jnp.einsum(pattern, left_side, right_side, precision=lax.Precision.HIGHEST)  16.2 us
    psum x1, blocking collectives, on_device(): norm_squares = lax.psum(partial_norms, 'tm')  15.1 us
    all_gather x1, blocking collectives, on_device(): block_spectra = lax.all_gather(whitened, 'tmpl', axis=0, tiled=True)  14.4 us
    ppermute x1, starting transfers between devices, shifted(): lax.ppermute(array, axis, [(i, (i + by) % devices) for i in range(devices)])  6.37 us
    all_to_all x1, waiting for transfers between devices, on_device(): lax.all_to_all(block_spectra, 'tm', split_axis=2, concat_axis=0, tiled=True)  4.77 us
    all_to_all x1, starting transfers between devices, on_device(): lax.all_to_all(block_spectra, 'tm', split_axis=2, concat_axis=0, tiled=True)  4.49 us
    reduce_max x4, other arithmetic, peak_magnitude(): jnp.max(wave_real * wave_real + wave_imag * wave_imag, axis=(1, 2))  4.06 us
  transfers between devices with their start and end apart: 3, of which 1 were waited for; matrix products, arithmetic and copies ran while one was open for 2% of the time, Pallas kernels for 0%

commit v1 on v0

v1 whole, which is shorter than its diff:
```python
import functools
import math

import jax
import jax.numpy as jnp
import ml_dtypes
import numpy as np
from jax import lax
from jax.experimental import pallas as pl
from jax.experimental.pallas import tpu as pltpu
from jax.sharding import PartitionSpec as P

NFFT = 4096
BINS = 2048
HOP = 2048
LANES = 128
ROWS = HOP // LANES
FINE = 32
GROUP = 8
FLOOR = 1e-6

ROOT_SCALE = {128: 1.66575, 64: 1.66575, 32: 1.6245, 16: 1.6245, 8: 1.6245}


def root_order(index, period):
    return period // math.gcd(int(index), period)


def row_scale(count, period):
    return np.array([ROOT_SCALE.get(root_order(i, period), 1.0) for i in range(count)])


def as_bf16(table):
    return np.asarray(table, np.float32).astype(ml_dtypes.bfloat16)


def two_parts(table):
    high = as_bf16(table)
    low = as_bf16(np.asarray(table, np.float64) - high.astype(np.float64))
    return high, low


def turn(left, right, period):
    angle = 2.0 * np.pi * (np.outer(left, right) % period) / period
    return np.cos(angle), np.sin(angle)


@functools.lru_cache(maxsize=None)
def tables():
    eye = np.eye(GROUP)
    fine, wide, rows = np.arange(FINE), np.arange(LANES), np.arange(ROWS)
    window = 0.5 - 0.5 * np.cos(2.0 * np.pi * np.arange(NFFT) / NFFT)
    cos, sin = turn(fine, fine, FINE)
    first = np.concatenate([np.kron(eye, cos), np.kron(eye, -sin)], axis=0)
    first_high, first_low = two_parts(first)
    fwd_cos, fwd_sin = turn(fine, wide, NFFT)
    f_order = np.array([4 * d + g for g in range(4) for d in range(ROWS)])
    cos, sin = turn(wide, f_order, LANES)
    second = np.block([[cos, -sin], [sin, cos]])
    second_high, second_low = two_parts(second)
    scale_q = row_scale(FINE, FINE)
    scale_c = row_scale(LANES, LANES)
    cos, sin = turn(fine, rows, FINE)
    cos, sin = cos * scale_q[:, None], sin * scale_q[:, None]
    third = np.block([[np.kron(eye, cos), np.kron(eye, -sin)], [np.kron(eye, sin), np.kron(eye, cos)]])
    inv_cos, inv_sin = turn(fine, wide, NFFT)
    undo = 1.0 / (scale_q[:, None] * scale_c[None, :])
    cos, sin = turn(wide, wide, LANES)
    cos, sin = cos * scale_c[:, None], sin * scale_c[:, None]
    fourth = np.block([[cos, sin], [-sin, cos]])
    order = np.zeros((ROWS * 16, ROWS * 16))
    for m in range(16):
        for d in range(ROWS):
            order[m * ROWS + d, d * 16 + m] = 1.0
    f32 = lambda t: np.asarray(t, np.float32)
    return dict(
        window=f32(window.reshape(2 * ROWS, LANES)),
        first_high=first_high,
        first_low=first_low,
        fwd=f32(np.stack([fwd_cos, fwd_sin])),
        second_both=np.concatenate([second_high, second_low], axis=1),
        third=as_bf16(third),
        inv=f32(np.stack([inv_cos * undo, inv_sin * undo])),
        fourth=as_bf16(fourth),
        order=as_bf16(order),
    ), float((window * window).sum())


def dot(left, right):
    return jnp.dot(left, right, preferred_element_type=jnp.float32)


def split(value):
    high = value.astype(jnp.bfloat16)
    return high, (value - high.astype(jnp.float32)).astype(jnp.bfloat16)


def repeat(count, body, carry):
    if count <= 8:
        for step in range(count):
            carry = body(step, carry)
        return carry
    return lax.fori_loop(0, count, body, carry)


def filter_kernel(
    segs, own, energy, place, cutoff, strain, tmpl, window, first_high, first_low, fwd,
    second_both, third, inv, fourth, order, out, spec, bank,
):
    tmpl_count = tmpl.shape[2]
    w_low, w_high = window[:ROWS][None], window[ROWS:][None]
    fwd_cos, fwd_sin = fwd[0][None], fwd[1][None]

    def frames(start, last):
        here = strain[pl.ds(start, GROUP)]
        if last:
            after = jnp.concatenate([strain[pl.ds(start + 1, GROUP - 1)], strain[pl.ds(0, 1)]], axis=0)
        else:
            after = strain[pl.ds(start + 1, GROUP)]
        both = jnp.concatenate([here * w_low, after * w_high], axis=1)
        return both.reshape(GROUP * FINE, LANES)

    def forward(start, power, last):
        pair = jnp.concatenate([frames(start, False), frames(start + GROUP, last)], axis=1)
        high, low = split(pair)
        step = dot(first_high[...], high) + dot(first_high[...], low) + dot(first_low[...], high)
        half = GROUP * FINE
        for h in range(2):
            re = step[:half, h * LANES:(h + 1) * LANES].reshape(GROUP, FINE, LANES)
            im = step[half:, h * LANES:(h + 1) * LANES].reshape(GROUP, FINE, LANES)
            turned = jnp.concatenate([re * fwd_cos + im * fwd_sin, im * fwd_cos - re * fwd_sin], axis=2)
            high, low = split(turned.reshape(half, 2 * LANES))
            wide = dot(high, second_both[...])
            value = wide[:, :LANES] + wide[:, LANES:] + dot(low, second_both[:, :LANES])
            at = (start + h * GROUP) * FINE
            spec[pl.ds(at, half)] = value
            power = power + jnp.sum((value * value).reshape(GROUP, FINE, LANES), axis=0)
        return power

    power = jnp.zeros((FINE, LANES), jnp.float32)
    pairs = segs // (2 * GROUP)
    power = repeat(pairs - 1, lambda i, p: forward(i * 2 * GROUP, p, False), power)
    power = forward((pairs - 1) * 2 * GROUP, power, True)
    power = power + pltpu.roll(power, LANES // 2, 1)
    density = power / (segs * energy) + FLOOR

    lane = lax.broadcasted_iota(jnp.int32, (ROWS, LANES), 1)
    row = lax.broadcasted_iota(jnp.int32, (ROWS, LANES), 0)
    bins = row * LANES + lane
    part = lane // FINE

    def gather_lanes(flipped, at, source):
        result = None
        for g in range(4):
            piece = flipped[at + g * ROWS:at + (g + 1) * ROWS]
            if source is not None and g != source:
                piece = pltpu.roll(piece, ((g - source) % 4) * FINE, 1)
            result = piece if g == 0 else jnp.where(part == g, piece, result)
        return result

    inverse_density = gather_lanes((1.0 / jnp.concatenate([density] * 4, axis=0)).T, 0, None)

    pieces = [
        jnp.concatenate(
            [tmpl[j, part_at, :, at:at + LANES] for j in range(tmpl.shape[0]) for at in range(0, tmpl.shape[3], LANES)],
            axis=0,
        )
        for part_at in range(2)
    ]
    bank[...] = dot(order[...], jnp.concatenate(pieces, axis=1))

    inv_cos, inv_sin = inv[0][None], inv[1][None]
    column = lax.broadcasted_iota(jnp.int32, (GROUP, LANES), 1)

    def block(number, _):
        at = pl.multiple_of((place[0] * own + number * GROUP) * FINE, GROUP * FINE)
        white = spec[pl.ds(at, GROUP * FINE)].reshape(GROUP, FINE, LANES) / density[None]
        white = white.astype(jnp.bfloat16).astype(jnp.float32).reshape(2, 4 * FINE, LANES)
        re_parts, im_parts = [], []
        for half in range(2):
            flipped = white[half].T
            for s in range(4):
                re_parts.append(gather_lanes(flipped, 0, s))
                im_parts.append(gather_lanes(flipped, LANES // 2, s))
        white_re = jnp.stack(re_parts)
        white_im = jnp.stack(im_parts)

        def pair_of(step, result):
            sides, norms = [], []
            for side in range(2):
                m = 2 * step + side
                rows = pl.ds(m * ROWS, ROWS)
                keep = bins < cutoff[m]
                h_re = jnp.where(keep, bank[rows, :LANES], 0.0)
                h_im = jnp.where(keep, bank[rows, LANES:], 0.0)
                norms.append(jnp.sum((h_re * h_re + h_im * h_im) * inverse_density, keepdims=True))
                c_re = h_re[None] * white_re + h_im[None] * white_im
                c_im = h_re[None] * white_im - h_im[None] * white_re
                both = jnp.concatenate([c_re, c_im], axis=0).reshape(2 * GROUP * ROWS, LANES)
                sides.append(both.astype(jnp.bfloat16))
            section = dot(third[...], jnp.concatenate(sides, axis=1))
            half = GROUP * FINE
            for side in range(2):
                re = section[:half, side * LANES:(side + 1) * LANES].reshape(GROUP, FINE, LANES)
                im = section[half:, side * LANES:(side + 1) * LANES].reshape(GROUP, FINE, LANES)
                turned = jnp.concatenate([re * inv_cos - im * inv_sin, re * inv_sin + im * inv_cos], axis=2)
                wave = dot(turned.reshape(half, 2 * LANES).astype(jnp.bfloat16), fourth[...])
                square = wave[:, :LANES] * wave[:, :LANES] + wave[:, LANES:] * wave[:, LANES:]
                top = jnp.max(jnp.max(square.reshape(GROUP, FINE, LANES), axis=1), axis=1, keepdims=True)
                value = jnp.sqrt(top) / (jnp.sqrt(norms[side]) * math.sqrt(energy))
                result = jnp.where(column == 2 * step + side, value, result)
            return result

        result = repeat(tmpl_count // 2, pair_of, jnp.zeros((GROUP, LANES), jnp.float32))
        out[pl.ds(number * GROUP, GROUP)] = result[:, :tmpl_count]
        return _

    repeat(own // GROUP, block, 0)


def on_device(strain, templates, cutoff):
    tm, devices = lax.axis_size("tm"), lax.axis_size("tm") * lax.axis_size("tmpl")
    segs = devices * (strain.shape[0] // HOP)
    own = segs // tm
    chunk = strain.reshape(1, ROWS, LANES)
    record = lax.all_to_all(
        jnp.broadcast_to(chunk, (devices, ROWS, LANES)), ("tm", "tmpl"), split_axis=0, concat_axis=0, tiled=True
    )
    bank = lax.all_to_all(
        jnp.broadcast_to(templates[None], (tm,) + templates.shape), "tm", split_axis=0, concat_axis=0, tiled=True
    )
    place = lax.axis_index("tm").astype(jnp.int32).reshape(1)
    held, energy = tables()
    smem = pl.BlockSpec(memory_space=pltpu.SMEM)
    vmem = pl.BlockSpec(memory_space=pltpu.VMEM)
    return pl.pallas_call(
        functools.partial(filter_kernel, segs, own, energy),
        out_shape=jax.ShapeDtypeStruct((own, templates.shape[1]), jnp.float32),
        in_specs=[smem, smem] + [vmem] * (2 + len(held)),
        out_specs=vmem,
        scratch_shapes=[
            pltpu.VMEM((segs * FINE, LANES), jnp.float32),
            pltpu.VMEM((templates.shape[1] * ROWS, 2 * LANES), jnp.float32),
        ],
        compiler_params=pltpu.CompilerParams(vmem_limit_bytes=48 * 1024 * 1024),
        name="matched_filter",
    )(place, cutoff, record, bank, *[jnp.asarray(t) for t in held.values()])


def solution(mesh):
    in_specs = (P(("tm", "tmpl")), P(None, "tmpl", "tm"), P("tmpl"))
    out_specs = P("tm", "tmpl")
    return jax.shard_map(
        on_device, mesh=mesh, in_specs=in_specs, out_specs=out_specs, check_vma=False
    )
```

time: 131 us -> 33 us (0.25)
  blocking collectives: 67.1 us -> 10.1 us
  other arithmetic: 16.5 us -> 0 us
  matrix products: 16.2 us -> 0 us
  starting transfers between devices: 14.5 us -> 4.32 us
  local copies, waits for them, and re-layouts: 9.58 us -> 3.06 us
  waiting for transfers between devices: 4.78 us -> 10.4 us
  Pallas kernels: 0 us -> 4.67 us
  between operations: 1.52 us -> 0.1 us
    psum x2 -> x0, blocking collectives: 52.6 us -> none  [the longest x1 37.5 us: on_device(): total_power = lax.psum(local_power, ('tm', 'tmpl'))]
    dot_general x18 -> x0, matrix products: 16.2 us -> none  [contract(): jnp.einsum(pattern, left_side, right_side, precision=lax.Precision.HIGHEST)]
    all_gather x1 -> x0, blocking collectives: 14.4 us -> none  [on_device(): block_spectra = lax.all_gather(whitened, 'tmpl', axis=0, tiled=True)]
    all_to_all x0 -> x1, blocking collectives: none -> 10.1 us  [on_device(): lax.all_to_all(jnp.broadcast_to(templates[None], (tm,) + templates.shape)...]
    ppermute x1 -> x0, starting transfers between devices: 6.37 us -> none  [shifted(): lax.ppermute(array, axis, [(i, (i + by) % devices) for i in range(devices)])]
    another operation x5 -> x0, other arithmetic: 6.1 us -> none  [the longest x1 3.23 us: correlate(): return jnp.stack([prod_real, prod_imag], axis=1).astype(jnp.bfloat16)]
    all_to_all x2 -> x1, waiting for transfers between devices: 4.77 us -> 10.4 us  [on_device(): lax.all_to_all(jnp.broadcast_to(chunk, (devices, ROWS, LANES)), ('tm', 't...]
    pallas_call x0 -> x1, Pallas kernels: none -> 4.67 us  [on_device(): pl.pallas_call(functools.partial(filter_kernel, segs, own, energy), out_s...]
  transfers between devices with their start and end apart: 3 -> 1, of which waited for: 1 -> 1; matrix products, arithmetic and copies ran while one was open for 2% -> 0% of each run, Pallas kernels for 0% -> 0%
where the time goes in v1:
time: 33 us; the launch traced here: 32.6 us
  waiting for transfers between devices  10.4 us (32%)
  blocking collectives  10.1 us (31%)
  Pallas kernels  4.67 us (14%)
  starting transfers between devices  4.32 us (13%)
  local copies, waits for them, and re-layouts  3.06 us (9%)
    all_to_all x1, waiting for transfers between devices, on_device(): lax.all_to_all(jnp.broadcast_to(chunk, (devices, ROWS, LANES)), ('tm', 't...  10.4 us
    all_to_all x1, blocking collectives, on_device(): lax.all_to_all(jnp.broadcast_to(templates[None], (tm,) + templates.shape)...  10.1 us
    pallas_call x1, Pallas kernels, on_device(): pl.pallas_call(functools.partial(filter_kernel, segs, own, energy), out_s...  4.67 us
    all_to_all x1, starting transfers between devices, on_device(): lax.all_to_all(jnp.broadcast_to(chunk, (devices, ROWS, LANES)), ('tm', 't...  4.32 us
    broadcast_in_dim x1, local copies, waits for them, and re-layouts, on_device(): jnp.broadcast_to(chunk, (devices, ROWS, LANES))  1.46 us
    broadcast_in_dim x1, local copies, waits for them, and re-layouts, on_device(): jnp.broadcast_to(templates[None], (tm,) + templates.shape)  0.8 us
    unnamed x20, local copies, waits for them, and re-layouts  0.8 us
  transfers between devices with their start and end apart: 1, of which 1 were waited for; matrix products, arithmetic and copies ran while one was open for 0% of the time, Pallas kernels for 0%

profile of v1, /device:TPU:0, one launch (start us, length us, event | category | flops | bytes accessed | tf_op | source)
XLA Modules:
  0.0 32.6 jit_solution(11172328864072301383)
XLA Ops:
  0.0 0.0 copy-start.5
  0.0 0.0 copy-start.6
  0.0 0.8 %broadcast_in_dim.15 = bf16[4,2,16,512]{3,2,1,0:T(8,128)(2,1)S(1)} broadcast(bf16[2,16,512]{2,1,0:T(8,128)(2,1)} %param.13), dimensions={1,2,3} | broadcast | bytes 163840 | tf_op jit(solution)/shard_map/broadcast_in_dim | solution.py:230
  0.8 0.0 copy-start.3
  0.8 0.0 copy-start.4
  0.8 10.1 %all_to_all.10.tmpl = bf16[4,2,16,512]{3,2,1,0:T(8,128)(2,1)S(1)} all-to-all(bf16[4,2,16,512]{3,2,1,0:T(8,128)(2,1)S(1)} %broadcast_in_dim.15), channel_id=1, replica_groups=mesh['tm'=4,'tmpl'=8] {'tm'}, dimensions={0} | all-to-all | bytes 262144 | tf_op jit(solution)/shard_map/all_to_all | solution.py:229
  11.0 0.0 copy-start.2
  11.0 0.0 copy-start.8
  11.0 1.5 %broadcast_in_dim.14 = f32[32,16,128]{2,1,0:T(8,128)} broadcast(f32[16,128]{1,0:T(8,128)} %bitcast.2), dimensions={1,2} | broadcast | bytes 270336 | tf_op jit(solution)/shard_map/broadcast_in_dim | solution.py:227
  12.4 0.0 copy-start
  12.4 0.0 copy-start.1
  12.4 4.3 %all-to-all-start = ((f32[32,16,128]{2,1,0:T(8,128)}), f32[32,16,128]{2,1,0:T(8,128)S(1)}, u32[]{:S(2)}, u32[]{:S(2)}) async-start(f32[32,16,128]{2,1,0:T(8,128)} %broadcast_in_dim.14), calls=%async_computation | async-start | bytes 524288 | tf_op jit(solution)/shard_map/all_to_all | solution.py:226
  16.8 0.0 copy-start.9
  16.8 10.4 %all-to-all-done.strain = f32[32,16,128]{2,1,0:T(8,128)S(1)} async-done(((f32[32,16,128]{2,1,0:T(8,128)}), f32[32,16,128]{2,1,0:T(8,128)S(1)}, u32[]{:S(2)}, u32[]{:S(2)}) %all-to-all-start) | async-done | bytes 262176 | tf_op jit(solution)/shard_map/all_to_all | solution.py:226
  27.1 0.0 copy-done.5
  27.1 0.0 copy-done.6
  27.1 0.0 copy-done.3
  27.1 0.0 copy-done.4
  27.2 0.0 copy-done.2
  27.2 0.0 copy-done.8
  27.2 0.0 copy-done
  27.2 0.0 copy-done.1
  27.2 0.0 copy-done.9
  27.2 0.0 copy-start.7
  27.2 0.7 %copy-done.7 = f32[2,32,128]{2,1,0:T(8,128)S(1)} copy-done((f32[2,32,128]{2,1,0:T(8,128)S(1)}, f32[2,32,128]{2,1,0:T(8,128)}, u32[]{:S(2)}) %copy-start.7) | copy-done | bytes 32792
  28.0 4.7 %matched_filter.1 = f32[8,16]{1,0:T(8,128)} custom-call(s32[1]{0:T(128)} %bitcast.place, s32[16]{0:T(128)S(1)} %copy-done.9, f32[32,16,128]{2,1,0:T(8,128)S(1)} %all-to-all-done.strain, bf16[4,2,16,512]{3,2,1,0:T(8,128)(2,1)S(1)} %all_to_all.10.tmpl, f32[32,128]{1,0:T(8,128)S(1)} %copy-done.8, bf16[512,256]{1,0:T(8,128)(2,1)S(1)} %copy-done, ...), custom_call_target="tpu_custom_call" | custom-call | tf_op jit(solution)/shard_map/matched_filter/pallas_call | solution.py:236
Async XLA Ops:
  0.0 27.1 %copy-start.5 = (bf16[256,256]{1,0:T(8,128)(2,1)S(1)}, bf16[256,256]{1,0:T(8,128)(2,1)}, u32[]{:S(2)}) copy-start(bf16[256,256]{1,0:T(8,128)(2,1)} %constant.31.clone.order) | copy-start | bytes 393220
  0.0 27.1 %copy-start.6 = (f32[2,32,128]{2,1,0:T(8,128)S(1)}, f32[2,32,128]{2,1,0:T(8,128)}, u32[]{:S(2)}) copy-start(f32[2,32,128]{2,1,0:T(8,128)} %constant.26.clone.fwd) | copy-start | bytes 98308
  0.8 26.3 %copy-start.3 = (bf16[256,256]{1,0:T(8,128)(2,1)S(1)}, bf16[256,256]{1,0:T(8,128)(2,1)}, u32[]{:S(2)}) copy-start(bf16[256,256]{1,0:T(8,128)(2,1)} %constant.27.clone.second_both) | copy-start | bytes 393220
  0.8 26.3 %copy-start.4 = (bf16[256,256]{1,0:T(8,128)(2,1)S(1)}, bf16[256,256]{1,0:T(8,128)(2,1)}, u32[]{:S(2)}) copy-start(bf16[256,256]{1,0:T(8,128)(2,1)} %constant.30.clone.fourth) | copy-start | bytes 393220
  11.0 16.2 %copy-start.2 = (bf16[512,256]{1,0:T(8,128)(2,1)S(1)}, bf16[512,256]{1,0:T(8,128)(2,1)}, u32[]{:S(2)}) copy-start(bf16[512,256]{1,0:T(8,128)(2,1)} %constant.28.clone.third) | copy-start | bytes 786436
  11.0 16.2 %copy-start.8 = (f32[32,128]{1,0:T(8,128)S(1)}, f32[32,128]{1,0:T(8,128)}, u32[]{:S(2)}) copy-start(f32[32,128]{1,0:T(8,128)} %constant.23.clone.window) | copy-start | bytes 49156
  12.4 14.8 %copy-start = (bf16[512,256]{1,0:T(8,128)(2,1)S(1)}, bf16[512,256]{1,0:T(8,128)(2,1)}, u32[]{:S(2)}) copy-start(bf16[512,256]{1,0:T(8,128)(2,1)} %constant.24.clone.first_high) | copy-start | bytes 786436
  12.4 14.8 %copy-start.1 = (bf16[512,256]{1,0:T(8,128)(2,1)S(1)}, bf16[512,256]{1,0:T(8,128)(2,1)}, u32[]{:S(2)}) copy-start(bf16[512,256]{1,0:T(8,128)(2,1)} %constant.25.clone.first_low) | copy-start | bytes 786436
  12.4 14.7 %all-to-all-start = ((f32[32,16,128]{2,1,0:T(8,128)}), f32[32,16,128]{2,1,0:T(8,128)S(1)}, u32[]{:S(2)}, u32[]{:S(2)}) async-start(f32[32,16,128]{2,1,0:T(8,128)} %broadcast_in_dim.14), calls=%async_computation | async-start | bytes 524288 | tf_op jit(solution)/shard_map/all_to_all | solution.py:226
  16.8 10.4 %copy-start.9 = (s32[16]{0:T(128)S(1)}, s32[16]{0:T(128)}, u32[]{:S(2)}) copy-start(s32[16]{0:T(128)} %cutoff.1) | copy-start | bytes 196
  27.2 0.8 %copy-start.7 = (f32[2,32,128]{2,1,0:T(8,128)S(1)}, f32[2,32,128]{2,1,0:T(8,128)}, u32[]{:S(2)}) copy-start(f32[2,32,128]{2,1,0:T(8,128)} %constant.29.clone.inv) | copy-start | bytes 98308

commit v2 on v1

v2 whole, which is shorter than its diff:
```python
import functools
import math

import jax
import jax.numpy as jnp
import ml_dtypes
import numpy as np
from jax import lax
from jax.experimental import pallas as pl
from jax.experimental.pallas import tpu as pltpu
from jax.sharding import PartitionSpec as P

NFFT = 4096
BINS = 2048
HOP = 2048
LANES = 128
ROWS = HOP // LANES
FINE = 32
GROUP = 8
FLOOR = 1e-6

ROOT_SCALE = {128: 1.66575, 64: 1.66575, 32: 1.6245, 16: 1.6245, 8: 1.6245}


def root_order(index, period):
    return period // math.gcd(int(index), period)


def row_scale(count, period):
    return np.array([ROOT_SCALE.get(root_order(i, period), 1.0) for i in range(count)])


def as_bf16(table):
    return np.asarray(table, np.float32).astype(ml_dtypes.bfloat16)


def two_parts(table):
    high = as_bf16(table)
    low = as_bf16(np.asarray(table, np.float64) - high.astype(np.float64))
    return high, low


def turn(left, right, period):
    angle = 2.0 * np.pi * (np.outer(left, right) % period) / period
    return np.cos(angle), np.sin(angle)


@functools.lru_cache(maxsize=None)
def tables():
    eye = np.eye(GROUP)
    fine, wide, rows = np.arange(FINE), np.arange(LANES), np.arange(ROWS)
    window = 0.5 - 0.5 * np.cos(2.0 * np.pi * np.arange(NFFT) / NFFT)
    cos, sin = turn(fine, fine, FINE)
    halves = np.zeros((GROUP + 1, GROUP, FINE))
    for s in range(GROUP):
        halves[s, s] = 1.0
    halves[GROUP - 1, GROUP - 1, ROWS:] = 0.0
    halves[GROUP, GROUP - 1, ROWS:] = 1.0
    spread = lambda t: (halves[:, None] * t[None, :, None, :]).reshape((GROUP + 1) * FINE, GROUP * FINE)
    first = np.concatenate([spread(cos), spread(-sin)], axis=0)
    first_high, first_low = two_parts(first)
    fwd_cos, fwd_sin = turn(fine, wide, NFFT)
    f_order = np.array([4 * d + g for g in range(4) for d in range(ROWS)])
    cos, sin = turn(wide, f_order, LANES)
    second = np.block([[cos, -sin], [sin, cos]])
    second_high, second_low = two_parts(second)
    scale_q = row_scale(FINE, FINE)
    scale_c = row_scale(LANES, LANES)
    cos, sin = turn(fine, rows, FINE)
    cos, sin = cos * scale_q[:, None], sin * scale_q[:, None]
    third = np.block([[np.kron(eye, cos), np.kron(eye, -sin)], [np.kron(eye, sin), np.kron(eye, cos)]])
    inv_cos, inv_sin = turn(fine, wide, NFFT)
    undo = 1.0 / (scale_q[:, None] * scale_c[None, :])
    cos, sin = turn(wide, wide, LANES)
    cos, sin = cos * scale_c[:, None], sin * scale_c[:, None]
    fourth = np.block([[cos, sin], [-sin, cos]])
    order = np.zeros((ROWS * 16, ROWS * 16))
    for m in range(16):
        for d in range(ROWS):
            order[m * ROWS + d, d * 16 + m] = 1.0
    f32 = lambda t: np.asarray(t, np.float32)
    return dict(
        window=f32(window.reshape(2 * ROWS, LANES)),
        first_high=first_high,
        first_low=first_low,
        fwd=f32(np.stack([fwd_cos, fwd_sin])),
        second_both=np.concatenate([second_high, second_low], axis=1),
        third=as_bf16(third),
        inv=f32(np.stack([inv_cos * undo, inv_sin * undo])),
        fourth=as_bf16(fourth),
        order=as_bf16(order),
    ), float((window * window).sum())


def dot(left, right):
    return jnp.dot(left, right, preferred_element_type=jnp.float32)


def split(value):
    high = value.astype(jnp.bfloat16)
    return high, (value - high.astype(jnp.float32)).astype(jnp.bfloat16)


def repeat(count, body, carry):
    if count <= 8:
        for step in range(count):
            carry = body(step, carry)
        return carry
    return lax.fori_loop(0, count, body, carry)


def natural(flipped, at, source):
    part = lax.broadcasted_iota(jnp.int32, (ROWS, LANES), 1) // FINE
    result = None
    for g in range(4):
        piece = flipped[at + g * ROWS:at + (g + 1) * ROWS]
        if g != source:
            piece = pltpu.roll(piece, ((g - source) % 4) * FINE, 1)
        result = piece if g == 0 else jnp.where(part == g, piece, result)
    return result


def forward_kernel(devices, *refs):
    chunks = refs[:devices]
    window, first_high, first_low, fwd, second_both, spec, sent, record = refs[devices:]
    rank = lax.axis_index("tmpl")
    size = chunks[0].shape[0]
    for shift, chunk in enumerate(chunks):
        record[pl.ds(lax.rem(rank + shift, devices) * size, size)] = chunk[...]
    own = record.shape[0]
    w_low, w_high = window[:ROWS][None], window[ROWS:][None]
    fwd_cos, fwd_sin = fwd[0][None], fwd[1][None]
    parts = GROUP + 1

    def group(start, power, last):
        here = record[pl.ds(start, GROUP)]
        if last:
            after = jnp.concatenate([record[pl.ds(start + 1, GROUP - 1)], record[pl.ds(0, 1)]], axis=0)
        else:
            after = record[pl.ds(start + 1, GROUP)]
        both = jnp.concatenate([here * w_low, after * w_high], axis=1)
        high, low = split(both.reshape(GROUP * FINE, LANES))
        step = dot(first_high[...], high) + dot(first_high[...], low) + dot(first_low[...], high)
        re = step[:parts * FINE].reshape(parts, FINE, LANES)
        im = step[parts * FINE:].reshape(parts, FINE, LANES)
        turned = jnp.concatenate([re * fwd_cos + im * fwd_sin, im * fwd_cos - re * fwd_sin], axis=2)
        high, low = split(turned.reshape(parts * FINE, 2 * LANES))
        wide = dot(high, second_both[...])
        value = wide[:, :LANES] + wide[:, LANES:] + dot(low, second_both[:, :LANES])
        value = jnp.concatenate([value, jnp.zeros((3 * FINE, LANES), jnp.float32)], axis=0)
        flipped = [value[i * LANES:(i + 1) * LANES].T for i in range(3)]
        pairs = [
            (natural(flipped[s // 4], 0, s % 4), natural(flipped[s // 4], LANES // 2, s % 4)) for s in range(parts)
        ]
        if last:
            sent[1], sent[2] = pairs[GROUP - 1]
            sent[3], sent[4] = pairs[GROUP]
        else:
            pairs[GROUP - 1] = tuple(a + b for a, b in zip(pairs[GROUP - 1], pairs[GROUP]))
        for s in range(GROUP):
            spec[0, pl.ds(start + s, 1)] = pairs[s][0][None]
            spec[1, pl.ds(start + s, 1)] = pairs[s][1][None]
            if s < GROUP - 1 or not last:
                power = power + pairs[s][0] * pairs[s][0] + pairs[s][1] * pairs[s][1]
        return power

    power = jnp.zeros((ROWS, LANES), jnp.float32)
    power = repeat(own // GROUP - 1, lambda i, p: group(i * GROUP, p, False), power)
    sent[0] = group(own - GROUP, power, True)


def bank_kernel(devices, *refs):
    blocks = refs[:devices]
    cutoff, order, bank, gathered = refs[devices:]
    rank = lax.axis_index("tm")
    width = blocks[0].shape[2]
    for shift, block in enumerate(blocks):
        first = lax.rem(rank + shift, devices) * (width // LANES)
        for at in range(width // LANES):
            lanes = slice(at * LANES, (at + 1) * LANES)
            gathered[first + at] = jnp.concatenate([block[0, :, lanes], block[1, :, lanes]], axis=1)
    count = blocks[0].shape[1]
    lane = lax.broadcasted_iota(jnp.int32, (ROWS, LANES), 1)
    row = lax.broadcasted_iota(jnp.int32, (ROWS, LANES), 0)
    bins = row * LANES + lane
    value = dot(order[...], gathered[...].reshape(ROWS * count, 2 * LANES))
    for m in range(count):
        keep = bins < cutoff[m]
        rows = slice(m * ROWS, (m + 1) * ROWS)
        bank[0, m] = jnp.where(keep, value[rows, :LANES], 0.0)
        bank[1, m] = jnp.where(keep, value[rows, LANES:], 0.0)


def filter_kernel(devices, segs, energy, *refs):
    shares = refs[:devices]
    spec, bank, third, inv, fourth, out = refs[devices:]
    own, count = out.shape
    power = shares[0][0]
    for share in shares[1:]:
        power = power + share[0]
    for i in range(devices):
        after = shares[(i + 1) % devices]
        re, im = shares[i][1] + after[3], shares[i][2] + after[4]
        power = power + re * re + im * im
        if i == 0:
            last_re, last_im = re, im
    density = power / (segs * energy) + FLOOR
    inverse_density = 1.0 / density
    inv_cos, inv_sin = inv[0][None], inv[1][None]
    column = lax.broadcasted_iota(jnp.int32, (GROUP, LANES), 1)

    def whiten(value):
        return (value / density[None]).astype(jnp.bfloat16).astype(jnp.float32)

    def block(start, last):
        x_re, x_im = spec[0, pl.ds(start, GROUP)], spec[1, pl.ds(start, GROUP)]
        if last:
            x_re = jnp.concatenate([x_re[:GROUP - 1], last_re[None]], axis=0)
            x_im = jnp.concatenate([x_im[:GROUP - 1], last_im[None]], axis=0)
        white_re, white_im = whiten(x_re), whiten(x_im)

        def pair_of(step, result):
            sides, norms = [], []
            for side in range(2):
                m = 2 * step + side
                h_re, h_im = bank[0, m], bank[1, m]
                norms.append(jnp.sum((h_re * h_re + h_im * h_im) * inverse_density, keepdims=True))
                c_re = h_re[None] * white_re + h_im[None] * white_im
                c_im = h_re[None] * white_im - h_im[None] * white_re
                both = jnp.concatenate([c_re, c_im], axis=0).reshape(2 * GROUP * ROWS, LANES)
                sides.append(both.astype(jnp.bfloat16))
            section = dot(third[...], jnp.concatenate(sides, axis=1))
            half = GROUP * FINE
            for side in range(2):
                re = section[:half, side * LANES:(side + 1) * LANES].reshape(GROUP, FINE, LANES)
                im = section[half:, side * LANES:(side + 1) * LANES].reshape(GROUP, FINE, LANES)
                turned = jnp.concatenate([re * inv_cos - im * inv_sin, re * inv_sin + im * inv_cos], axis=2)
                wave = dot(turned.reshape(half, 2 * LANES).astype(jnp.bfloat16), fourth[...])
                square = wave[:, :LANES] * wave[:, :LANES] + wave[:, LANES:] * wave[:, LANES:]
                top = jnp.max(jnp.max(square.reshape(GROUP, FINE, LANES), axis=1), axis=1, keepdims=True)
                value = jnp.sqrt(top) / (jnp.sqrt(norms[side]) * math.sqrt(energy))
                result = jnp.where(column == 2 * step + side, value, result)
            return result

        result = repeat(count // 2, pair_of, jnp.zeros((GROUP, LANES), jnp.float32))
        out[pl.ds(start, GROUP)] = result[:, :count]

    def earlier(number, carry):
        block(pl.multiple_of(number * GROUP, GROUP), False)
        return carry

    repeat(own // GROUP - 1, earlier, 0)
    block(own - GROUP, True)


def around(array, axis):
    devices = lax.axis_size(axis)
    return [array] + [
        lax.ppermute(array, axis, [((i + shift) % devices, i) for i in range(devices)]) for shift in range(1, devices)
    ]


def on_device(strain, templates, cutoff):
    tm, tmpl = lax.axis_size("tm"), lax.axis_size("tmpl")
    size = strain.shape[0] // HOP
    own = size * tmpl
    count = templates.shape[1]
    held, energy = tables()
    held = {name: jnp.asarray(table) for name, table in held.items()}
    smem = pl.BlockSpec(memory_space=pltpu.SMEM)
    vmem = pl.BlockSpec(memory_space=pltpu.VMEM)
    params = pltpu.CompilerParams(vmem_limit_bytes=48 * 1024 * 1024)
    f32 = jnp.float32
    chunks = around(strain.reshape(size, ROWS, LANES), "tmpl")
    blocks = around(templates, "tm")
    spec, sent = pl.pallas_call(
        functools.partial(forward_kernel, tmpl),
        out_shape=(
            jax.ShapeDtypeStruct((2, own, ROWS, LANES), f32),
            jax.ShapeDtypeStruct((5, ROWS, LANES), f32),
        ),
        in_specs=[vmem] * (tmpl + 5),
        out_specs=(vmem, vmem),
        scratch_shapes=[pltpu.VMEM((own, ROWS, LANES), f32)],
        compiler_params=params,
        name="forward",
    )(*chunks, held["window"], held["first_high"], held["first_low"], held["fwd"], held["second_both"])
    shares = around(sent, "tm")
    bank = pl.pallas_call(
        functools.partial(bank_kernel, tm),
        out_shape=jax.ShapeDtypeStruct((2, count, ROWS, LANES), f32),
        in_specs=[vmem] * tm + [smem, vmem],
        out_specs=vmem,
        scratch_shapes=[pltpu.VMEM((ROWS, count, 2 * LANES), jnp.bfloat16)],
        compiler_params=params,
        name="bank",
    )(*blocks, cutoff, held["order"])
    return pl.pallas_call(
        functools.partial(filter_kernel, tm, own * tm, energy),
        out_shape=jax.ShapeDtypeStruct((own, count), f32),
        in_specs=[vmem] * (tm + 5),
        out_specs=vmem,
        compiler_params=params,
        name="matched_filter",
    )(*shares, spec, bank, held["third"], held["inv"], held["fourth"])


def solution(mesh):
    in_specs = (P(("tm", "tmpl")), P(None, "tmpl", "tm"), P("tmpl"))
    out_specs = P("tm", "tmpl")
    return jax.shard_map(
        on_device, mesh=mesh, in_specs=in_specs, out_specs=out_specs, check_vma=False
    )
```

time: 33 us -> 33.2 us (level)
  starting transfers between devices: 4.32 us -> 17.8 us
  blocking collectives: 10.1 us -> 0 us
  waiting for transfers between devices: 10.4 us -> 5.93 us
  local copies, waits for them, and re-layouts: 3.06 us -> 5.03 us
  Pallas kernels: 4.67 us -> 3.91 us
    ppermute x0 -> x13, starting transfers between devices: none -> 17.8 us  [around(): lax.ppermute(array, axis, [((i + shift) % devices, i) for i in range(devi...]
    all_to_all x1 -> x0, waiting for transfers between devices: 10.4 us -> none  [on_device(): lax.all_to_all(jnp.broadcast_to(chunk, (devices, ROWS, LANES)), ('tm', 't...]
    all_to_all x1 -> x0, blocking collectives: 10.1 us -> none  [on_device(): lax.all_to_all(jnp.broadcast_to(templates[None], (tm,) + templates.shape)...]
    ppermute x0 -> x13, waiting for transfers between devices: none -> 5.93 us  [around(): lax.ppermute(array, axis, [((i + shift) % devices, i) for i in range(devi...]
    all_to_all x1 -> x0, starting transfers between devices: 4.32 us -> none  [on_device(): lax.all_to_all(jnp.broadcast_to(chunk, (devices, ROWS, LANES)), ('tm', 't...]
    unnamed x20 -> x24, local copies, waits for them, and re-layouts: 0.8 us -> 5.03 us
    broadcast_in_dim x2 -> x0, local copies, waits for them, and re-layouts: 2.26 us -> none  [the longest x1 1.46 us: on_device(): jnp.broadcast_to(chunk, (devices, ROWS, LANES))]
    pallas_call x1 -> x3, Pallas kernels: 4.67 us -> 3.91 us  [the longest x1 2.26 us: on_device(): pl.pallas_call(functools.partial(filter_kernel, tm, own * tm, energy), ou...]
  transfers between devices with their start and end apart: 1 -> 13, of which waited for: 1 -> 4; matrix products, arithmetic and copies ran while one was open for 0% -> 0% of each run, Pallas kernels for 0% -> 5%
where the time goes in v2:
time: 33.2 us; the launch traced here: 32.8 us
  starting transfers between devices  17.8 us (54%)
  waiting for transfers between devices  5.93 us (18%)
  local copies, waits for them, and re-layouts  5.03 us (15%)
  Pallas kernels  3.91 us (12%)
    ppermute x13, starting transfers between devices, around(): lax.ppermute(array, axis, [((i + shift) % devices, i) for i in range(devi...  17.8 us
    ppermute x13, waiting for transfers between devices, around(): lax.ppermute(array, axis, [((i + shift) % devices, i) for i in range(devi...  5.93 us
    unnamed x24, local copies, waits for them, and re-layouts  5.03 us
    pallas_call x1, Pallas kernels, on_device(): pl.pallas_call(functools.partial(filter_kernel, tm, own * tm, energy), ou...  2.26 us
    pallas_call x1, Pallas kernels, on_device(): pl.pallas_call(functools.partial(forward_kernel, tmpl), out_shape=(jax.Sh...  0.9 us
    pallas_call x1, Pallas kernels, on_device(): pl.pallas_call(functools.partial(bank_kernel, tm), out_shape=jax.ShapeDty...  0.75 us
  transfers between devices with their start and end apart: 13, of which 4 were waited for; matrix products, arithmetic and copies ran while one was open for 0% of the time, Pallas kernels for 5%

profile of v2, /device:TPU:0, one launch (start us, length us, event | category | flops | bytes accessed | tf_op | source)
XLA Modules:
  0.0 32.8 jit_solution(15184523927128270466)
XLA Ops:
  0.0 3.0 %collective-permute-start.11 = (bf16[2,16,512]{2,1,0:T(8,128)(2,1)}, bf16[2,16,512]{2,1,0:T(8,128)(2,1)S(1)}, u32[]{:S(2)}, u32[]{:S(2)}) collective-permute-start(bf16[2,16,512]{2,1,0:T(8,128)(2,1)} %refs_0_.1), channel_id=1, source_target_pairs={{16,0},{24,8},{0,16},{8,24},{17,1},{25,9},{1,17},{9,25},{18,2},{26... | collective-permute-start | bytes 98312 | tf_op jit(solution)/shard_map/ppermute | solution.py:259
  3.0 0.0 collective-permute-start.6
  3.0 1.6 %collective-permute-start.5 = (f32[1,16,128]{2,1,0:T(8,128)}, f32[1,16,128]{2,1,0:T(8,128)S(1)}, u32[]{:S(2)}, u32[]{:S(2)}) collective-permute-start(f32[1,16,128]{2,1,0:T(8,128)} %bitcast.2), channel_id=1, source_target_pairs={{6,0},{7,1},{0,2},{1,3},{2,4},{3,5},{4,6},{5,7},{14,8},{15,9},{8,1... | collective-permute-start | bytes 24584 | tf_op jit(solution)/shard_map/ppermute | solution.py:259
  4.6 2.6 %collective-permute-start.4 = (f32[1,16,128]{2,1,0:T(8,128)}, f32[1,16,128]{2,1,0:T(8,128)S(1)}, u32[]{:S(2)}, u32[]{:S(2)}) collective-permute-start(f32[1,16,128]{2,1,0:T(8,128)} %bitcast.3), channel_id=1, source_target_pairs={{5,0},{6,1},{7,2},{0,3},{1,4},{2,5},{3,6},{4,7},{13,8},{14,9},{15,... | collective-permute-start | bytes 24584 | tf_op jit(solution)/shard_map/ppermute | solution.py:259
  7.1 1.2 %collective-permute-start.3 = (f32[1,16,128]{2,1,0:T(8,128)}, f32[1,16,128]{2,1,0:T(8,128)S(1)}, u32[]{:S(2)}, u32[]{:S(2)}) collective-permute-start(f32[1,16,128]{2,1,0:T(8,128)} %bitcast.4), channel_id=1, source_target_pairs={{4,0},{5,1},{6,2},{7,3},{0,4},{1,5},{2,6},{3,7},{12,8},{13,9},{14,... | collective-permute-start | bytes 24584 | tf_op jit(solution)/shard_map/ppermute | solution.py:259
  8.4 0.0 collective-permute-done.6.refs_7_
  8.4 1.2 %collective-permute-start.2 = (f32[1,16,128]{2,1,0:T(8,128)}, f32[1,16,128]{2,1,0:T(8,128)S(1)}, u32[]{:S(2)}, u32[]{:S(2)}) collective-permute-start(f32[1,16,128]{2,1,0:T(8,128)} %bitcast.5), channel_id=1, source_target_pairs={{3,0},{4,1},{5,2},{6,3},{7,4},{0,5},{1,6},{2,7},{11,8},{12,9},{13,... | collective-permute-start | bytes 24584 | tf_op jit(solution)/shard_map/ppermute | solution.py:259
  9.5 0.0 collective-permute-done.5.refs_6_
  9.5 1.3 %collective-permute-start.1 = (f32[1,16,128]{2,1,0:T(8,128)}, f32[1,16,128]{2,1,0:T(8,128)S(1)}, u32[]{:S(2)}, u32[]{:S(2)}) collective-permute-start(f32[1,16,128]{2,1,0:T(8,128)} %bitcast.6), channel_id=1, source_target_pairs={{2,0},{3,1},{4,2},{5,3},{6,4},{7,5},{0,6},{1,7},{10,8},{11,9},{12,... | collective-permute-start | bytes 24584 | tf_op jit(solution)/shard_map/ppermute | solution.py:259
  10.9 0.0 collective-permute-done.4.refs_5_
  10.9 1.4 %collective-permute-start = (f32[1,16,128]{2,1,0:T(8,128)}, f32[1,16,128]{2,1,0:T(8,128)S(1)}, u32[]{:S(2)}, u32[]{:S(2)}) collective-permute-start(f32[1,16,128]{2,1,0:T(8,128)} %bitcast.7), channel_id=1, source_target_pairs={{1,0},{2,1},{3,2},{4,3},{5,4},{6,5},{7,6},{0,7},{9,8},{10,9},{11,1... | collective-permute-start | bytes 24584 | tf_op jit(solution)/shard_map/ppermute | solution.py:259
  12.3 0.0 collective-permute-done.3.refs_4_
  12.3 0.0 collective-permute-done.2.refs_3_
  12.3 1.1 %collective-permute-done.1.refs_2_ = f32[1,16,128]{2,1,0:T(8,128)S(1)} collective-permute-done((f32[1,16,128]{2,1,0:T(8,128)}, f32[1,16,128]{2,1,0:T(8,128)S(1)}, u32[]{:S(2)}, u32[]{:S(2)}) %collective-permute-start.1) | collective-permute-done | bytes 8224 | tf_op jit(solution)/shard_map/ppermute | solution.py:259
  13.4 0.5 %collective-permute-done.refs_1_ = f32[1,16,128]{2,1,0:T(8,128)S(1)} collective-permute-done((f32[1,16,128]{2,1,0:T(8,128)}, f32[1,16,128]{2,1,0:T(8,128)S(1)}, u32[]{:S(2)}, u32[]{:S(2)}) %collective-permute-start) | collective-permute-done | bytes 8224 | tf_op jit(solution)/shard_map/ppermute | solution.py:259
  13.9 0.0 copy-start
  13.9 1.0 %copy-done = bf16[576,256]{1,0:T(8,128)(2,1)S(1)} copy-done((bf16[576,256]{1,0:T(8,128)(2,1)S(1)}, bf16[576,256]{1,0:T(8,128)(2,1)}, u32[]{:S(2)}) %copy-start) | copy-done | bytes 294936
  14.9 0.0 copy-start.1
  14.9 1.0 %copy-done.1 = bf16[576,256]{1,0:T(8,128)(2,1)S(1)} copy-done((bf16[576,256]{1,0:T(8,128)(2,1)S(1)}, bf16[576,256]{1,0:T(8,128)(2,1)}, u32[]{:S(2)}) %copy-start.1) | copy-done | bytes 294936
  15.8 0.0 copy-start.5
  15.8 0.9 %copy-done.5 = bf16[256,256]{1,0:T(8,128)(2,1)S(1)} copy-done((bf16[256,256]{1,0:T(8,128)(2,1)S(1)}, bf16[256,256]{1,0:T(8,128)(2,1)}, u32[]{:S(2)}) %copy-start.5) | copy-done | bytes 131096
  16.7 0.0 copy-start.8
  16.7 0.8 %copy-done.8 = f32[2,32,128]{2,1,0:T(8,128)S(1)} copy-done((f32[2,32,128]{2,1,0:T(8,128)S(1)}, f32[2,32,128]{2,1,0:T(8,128)}, u32[]{:S(2)}) %copy-start.8) | copy-done | bytes 32792
  17.5 0.0 copy-start.9
  17.5 0.7 %copy-done.9 = f32[32,128]{1,0:T(8,128)S(1)} copy-done((f32[32,128]{1,0:T(8,128)S(1)}, f32[32,128]{1,0:T(8,128)}, u32[]{:S(2)}) %copy-start.9) | copy-done | bytes 16408
  18.2 0.0 copy-start.10
  18.2 0.7 %copy-done.10 = f32[2048]{0:T(1024)S(1)} copy-done((f32[2048]{0:T(1024)S(1)}, f32[2048]{0:T(1024)}, u32[]{:S(2)}) %copy-start.10) | copy-done | bytes 8216
  18.9 0.0 copy-start.6
  18.9 0.0 copy-start.4
  18.9 0.9 %forward.1 = (f32[2,8,16,128]{3,2,1,0:T(8,128)S(1)}, f32[5,16,128]{2,1,0:T(8,128)S(1)}) custom-call(f32[1,16,128]{2,1,0:T(8,128)S(1)} %bitcast.8, f32[1,16,128]{2,1,0:T(8,128)S(1)} %collective-permute-done.refs_1_, f32[1,16,128]{2,1,0:T(8,128)S(1)} %collective-permute-done.1.refs_2_, f32[1,16,128]{2,1,0:T(8,128)S(1)} %collective-permute-done.2.refs_3_, ...), custom_call_target="tpu_custom_call" | custom-call | tf_op jit(solution)/shard_map/forward/pallas_call | solution.py:276
  19.8 0.0 copy-start.11
  19.8 0.0 copy-start.2
  19.8 0.0 copy-start.3
  19.9 0.0 copy-start.7
  19.9 1.5 %collective-permute-start.9 = (f32[5,16,128]{2,1,0:T(8,128)S(1)}, f32[5,16,128]{2,1,0:T(8,128)S(1)}, u32[]{:S(2)}, u32[]{:S(2)}) collective-permute-start(f32[5,16,128]{2,1,0:T(8,128)S(1)} %get-tuple-element.7.refs_0_), channel_id=1, source_target_pairs={{24,0},{0,8},{8,16},{16,24},{25,1},{1,9},{9,17},{17,25},{26,2},{2,... | collective-permute-start | bytes 122888 | tf_op jit(solution)/shard_map/ppermute | solution.py:259
  21.4 0.5 %collective-permute-start.8 = (f32[5,16,128]{2,1,0:T(8,128)S(1)}, f32[5,16,128]{2,1,0:T(8,128)S(1)}, u32[]{:S(2)}, u32[]{:S(2)}) collective-permute-start(f32[5,16,128]{2,1,0:T(8,128)S(1)} %get-tuple-element.7.refs_0_), channel_id=1, source_target_pairs={{16,0},{24,8},{0,16},{8,24},{17,1},{25,9},{1,17},{9,25},{18,2},{26... | collective-permute-start | bytes 122888 | tf_op jit(solution)/shard_map/ppermute | solution.py:259
  21.9 1.4 %collective-permute-start.7 = (f32[5,16,128]{2,1,0:T(8,128)S(1)}, f32[5,16,128]{2,1,0:T(8,128)S(1)}, u32[]{:S(2)}, u32[]{:S(2)}) collective-permute-start(f32[5,16,128]{2,1,0:T(8,128)S(1)} %get-tuple-element.7.refs_0_), channel_id=1, source_target_pairs={{8,0},{16,8},{24,16},{0,24},{9,1},{17,9},{25,17},{1,25},{10,2},{18... | collective-permute-start | bytes 122888 | tf_op jit(solution)/shard_map/ppermute | solution.py:259
  23.4 0.0 copy-done.6
  23.4 1.5 %collective-permute-start.10 = (bf16[2,16,512]{2,1,0:T(8,128)(2,1)S(1)}, bf16[2,16,512]{2,1,0:T(8,128)(2,1)S(1)}, u32[]{:S(2)}, u32[]{:S(2)}) collective-permute-start(bf16[2,16,512]{2,1,0:T(8,128)(2,1)S(1)} %copy-done.6), channel_id=1, source_target_pairs={{8,0},{16,8},{24,16},{0,24},{9,1},{17,9},{25,17},{1,25},{10,2},{18... | collective-permute-start | bytes 98312 | tf_op jit(solution)/shard_map/ppermute | solution.py:259
  24.9 0.0 collective-permute-done.11.refs_2_
  24.9 0.5 %collective-permute-start.12 = (bf16[2,16,512]{2,1,0:T(8,128)(2,1)S(1)}, bf16[2,16,512]{2,1,0:T(8,128)(2,1)S(1)}, u32[]{:S(2)}, u32[]{:S(2)}) collective-permute-start(bf16[2,16,512]{2,1,0:T(8,128)(2,1)S(1)} %copy-done.6), channel_id=1, source_target_pairs={{24,0},{0,8},{8,16},{16,24},{25,1},{1,9},{9,17},{17,25},{26,2},{2,... | collective-permute-start | bytes 98312 | tf_op jit(solution)/shard_map/ppermute | solution.py:259
  25.4 2.1 %collective-permute-done.10.refs_1_ = bf16[2,16,512]{2,1,0:T(8,128)(2,1)S(1)} collective-permute-done((bf16[2,16,512]{2,1,0:T(8,128)(2,1)S(1)}, bf16[2,16,512]{2,1,0:T(8,128)(2,1)S(1)}, u32[]{:S(2)}, u32[]{:S(2)}) %collective-permute-start.10) | collective-permute-done | bytes 32800 | tf_op jit(solution)/shard_map/ppermute | solution.py:259
  27.5 2.3 %collective-permute-done.12.refs_3_ = bf16[2,16,512]{2,1,0:T(8,128)(2,1)S(1)} collective-permute-done((bf16[2,16,512]{2,1,0:T(8,128)(2,1)S(1)}, bf16[2,16,512]{2,1,0:T(8,128)(2,1)S(1)}, u32[]{:S(2)}, u32[]{:S(2)}) %collective-permute-start.12) | collective-permute-done | bytes 32800 | tf_op jit(solution)/shard_map/ppermute | solution.py:259
  29.7 0.0 copy-done.4
  29.7 0.0 copy-done.11
  29.7 0.7 %bank.1.refs_5_ = f32[2,16,16,128]{3,2,1,0:T(8,128)S(1)} custom-call(bf16[2,16,512]{2,1,0:T(8,128)(2,1)S(1)} %copy-done.6, bf16[2,16,512]{2,1,0:T(8,128)(2,1)S(1)} %collective-permute-done.10.refs_1_, bf16[2,16,512]{2,1,0:T(8,128)(2,1)S(1)} %collective-permute-done.11.refs_2_, bf16[2,16,512]{2,1,0:T(8,128)(2,1)S(1)} %collective-permute-done.12.refs_3_, ...), custom_call_target="tpu_custom_call" | custom-call | tf_op jit(solution)/shard_map/bank/pallas_call | solution.py:289
  30.5 0.0 collective-permute-done.9.refs_3_
  30.5 0.0 collective-permute-done.8.refs_2_
  30.5 0.0 collective-permute-done.7.refs_1_
  30.5 0.0 copy-done.2
  30.5 0.0 copy-done.3
  30.5 0.0 copy-done.7
  30.5 2.3 %matched_filter.1 = f32[8,16]{1,0:T(8,128)} custom-call(f32[5,16,128]{2,1,0:T(8,128)S(1)} %get-tuple-element.7.refs_0_, f32[5,16,128]{2,1,0:T(8,128)S(1)} %collective-permute-done.7.refs_1_, f32[5,16,128]{2,1,0:T(8,128)S(1)} %collective-permute-done.8.refs_2_, f32[5,16,128]{2,1,0:T(8,128)S(1)} %collective-permute-done.9.refs_3_, ...), custom_call_target="tpu_custom_call" | custom-call | tf_op jit(solution)/shard_map/matched_filter/pallas_call | solution.py:298
Async XLA Ops:
  0.0 24.9 %collective-permute-start.11 = (bf16[2,16,512]{2,1,0:T(8,128)(2,1)}, bf16[2,16,512]{2,1,0:T(8,128)(2,1)S(1)}, u32[]{:S(2)}, u32[]{:S(2)}) collective-permute-start(bf16[2,16,512]{2,1,0:T(8,128)(2,1)} %refs_0_.1), channel_id=1, source_target_pairs={{16,0},{24,8},{0,16},{8,24},{17,1},{25,9},{1,17},{9,25},{18,2},{26... | collective-permute-start | bytes 98312 | tf_op jit(solution)/shard_map/ppermute | solution.py:259
  3.0 5.4 %collective-permute-start.6 = (f32[1,16,128]{2,1,0:T(8,128)}, f32[1,16,128]{2,1,0:T(8,128)S(1)}, u32[]{:S(2)}, u32[]{:S(2)}) collective-permute-start(f32[1,16,128]{2,1,0:T(8,128)} %bitcast.1), channel_id=1, source_target_pairs={{7,0},{0,1},{1,2},{2,3},{3,4},{4,5},{5,6},{6,7},{15,8},{8,9},{9,10... | collective-permute-start | bytes 24584 | tf_op jit(solution)/shard_map/ppermute | solution.py:259
  3.0 6.6 %collective-permute-start.5 = (f32[1,16,128]{2,1,0:T(8,128)}, f32[1,16,128]{2,1,0:T(8,128)S(1)}, u32[]{:S(2)}, u32[]{:S(2)}) collective-permute-start(f32[1,16,128]{2,1,0:T(8,128)} %bitcast.2), channel_id=1, source_target_pairs={{6,0},{7,1},{0,2},{1,3},{2,4},{3,5},{4,6},{5,7},{14,8},{15,9},{8,1... | collective-permute-start | bytes 24584 | tf_op jit(solution)/shard_map/ppermute | solution.py:259
  4.6 6.3 %collective-permute-start.4 = (f32[1,16,128]{2,1,0:T(8,128)}, f32[1,16,128]{2,1,0:T(8,128)S(1)}, u32[]{:S(2)}, u32[]{:S(2)}) collective-permute-start(f32[1,16,128]{2,1,0:T(8,128)} %bitcast.3), channel_id=1, source_target_pairs={{5,0},{6,1},{7,2},{0,3},{1,4},{2,5},{3,6},{4,7},{13,8},{14,9},{15,... | collective-permute-start | bytes 24584 | tf_op jit(solution)/shard_map/ppermute | solution.py:259
  7.1 5.2 %collective-permute-start.3 = (f32[1,16,128]{2,1,0:T(8,128)}, f32[1,16,128]{2,1,0:T(8,128)S(1)}, u32[]{:S(2)}, u32[]{:S(2)}) collective-permute-start(f32[1,16,128]{2,1,0:T(8,128)} %bitcast.4), channel_id=1, source_target_pairs={{4,0},{5,1},{6,2},{7,3},{0,4},{1,5},{2,6},{3,7},{12,8},{13,9},{14,... | collective-permute-start | bytes 24584 | tf_op jit(solution)/shard_map/ppermute | solution.py:259
  8.4 4.0 %collective-permute-start.2 = (f32[1,16,128]{2,1,0:T(8,128)}, f32[1,16,128]{2,1,0:T(8,128)S(1)}, u32[]{:S(2)}, u32[]{:S(2)}) collective-permute-start(f32[1,16,128]{2,1,0:T(8,128)} %bitcast.5), channel_id=1, source_target_pairs={{3,0},{4,1},{5,2},{6,3},{7,4},{0,5},{1,6},{2,7},{11,8},{12,9},{13,... | collective-permute-start | bytes 24584 | tf_op jit(solution)/shard_map/ppermute | solution.py:259
  9.5 3.9 %collective-permute-start.1 = (f32[1,16,128]{2,1,0:T(8,128)}, f32[1,16,128]{2,1,0:T(8,128)S(1)}, u32[]{:S(2)}, u32[]{:S(2)}) collective-permute-start(f32[1,16,128]{2,1,0:T(8,128)} %bitcast.6), channel_id=1, source_target_pairs={{2,0},{3,1},{4,2},{5,3},{6,4},{7,5},{0,6},{1,7},{10,8},{11,9},{12,... | collective-permute-start | bytes 24584 | tf_op jit(solution)/shard_map/ppermute | solution.py:259
  10.9 3.0 %collective-permute-start = (f32[1,16,128]{2,1,0:T(8,128)}, f32[1,16,128]{2,1,0:T(8,128)S(1)}, u32[]{:S(2)}, u32[]{:S(2)}) collective-permute-start(f32[1,16,128]{2,1,0:T(8,128)} %bitcast.7), channel_id=1, source_target_pairs={{1,0},{2,1},{3,2},{4,3},{5,4},{6,5},{7,6},{0,7},{9,8},{10,9},{11,1... | collective-permute-start | bytes 24584 | tf_op jit(solution)/shard_map/ppermute | solution.py:259
  13.9 1.0 %copy-start = (bf16[576,256]{1,0:T(8,128)(2,1)S(1)}, bf16[576,256]{1,0:T(8,128)(2,1)}, u32[]{:S(2)}) copy-start(bf16[576,256]{1,0:T(8,128)(2,1)} %constant.20.clone.refs_10_) | copy-start | bytes 884740
  14.9 1.0 %copy-start.1 = (bf16[576,256]{1,0:T(8,128)(2,1)S(1)}, bf16[576,256]{1,0:T(8,128)(2,1)}, u32[]{:S(2)}) copy-start(bf16[576,256]{1,0:T(8,128)(2,1)} %constant.19.clone.refs_9_) | copy-start | bytes 884740
  15.8 0.9 %copy-start.5 = (bf16[256,256]{1,0:T(8,128)(2,1)S(1)}, bf16[256,256]{1,0:T(8,128)(2,1)}, u32[]{:S(2)}) copy-start(bf16[256,256]{1,0:T(8,128)(2,1)} %constant.22.clone.refs_12_) | copy-start | bytes 393220
  16.7 0.8 %copy-start.8 = (f32[2,32,128]{2,1,0:T(8,128)S(1)}, f32[2,32,128]{2,1,0:T(8,128)}, u32[]{:S(2)}) copy-start(f32[2,32,128]{2,1,0:T(8,128)} %constant.21.clone.refs_11_) | copy-start | bytes 98308
  17.5 0.7 %copy-start.9 = (f32[32,128]{1,0:T(8,128)S(1)}, f32[32,128]{1,0:T(8,128)}, u32[]{:S(2)}) copy-start(f32[32,128]{1,0:T(8,128)} %constant.18.clone.refs_8_) | copy-start | bytes 49156
  18.2 0.7 %copy-start.10 = (f32[2048]{0:T(1024)S(1)}, f32[2048]{0:T(1024)}, u32[]{:S(2)}) copy-start(f32[2048]{0:T(1024)} %param.12) | copy-start | bytes 24580
  18.9 4.4 %copy-start.6 = (bf16[2,16,512]{2,1,0:T(8,128)(2,1)S(1)}, bf16[2,16,512]{2,1,0:T(8,128)(2,1)}, u32[]{:S(2)}) copy-start(bf16[2,16,512]{2,1,0:T(8,128)(2,1)} %refs_0_.1) | copy-start | bytes 98308
  18.9 10.8 %copy-start.4 = (bf16[256,256]{1,0:T(8,128)(2,1)S(1)}, bf16[256,256]{1,0:T(8,128)(2,1)}, u32[]{:S(2)}) copy-start(bf16[256,256]{1,0:T(8,128)(2,1)} %constant.26.clone.refs_5_) | copy-start | bytes 393220
  19.8 9.9 %copy-start.11 = (s32[16]{0:T(128)S(1)}, s32[16]{0:T(128)}, u32[]{:S(2)}) copy-start(s32[16]{0:T(128)} %refs_4_.1) | copy-start | bytes 196
  19.8 10.7 %copy-start.2 = (bf16[512,256]{1,0:T(8,128)(2,1)S(1)}, bf16[512,256]{1,0:T(8,128)(2,1)}, u32[]{:S(2)}) copy-start(bf16[512,256]{1,0:T(8,128)(2,1)} %constant.23.clone.refs_6_) | copy-start | bytes 786436
  19.8 10.7 %copy-start.3 = (bf16[256,256]{1,0:T(8,128)(2,1)S(1)}, bf16[256,256]{1,0:T(8,128)(2,1)}, u32[]{:S(2)}) copy-start(bf16[256,256]{1,0:T(8,128)(2,1)} %constant.25.clone.refs_8_) | copy-start | bytes 393220
  19.9 10.7 %copy-start.7 = (f32[2,32,128]{2,1,0:T(8,128)S(1)}, f32[2,32,128]{2,1,0:T(8,128)}, u32[]{:S(2)}) copy-start(f32[2,32,128]{2,1,0:T(8,128)} %constant.24.clone.refs_7_) | copy-start | bytes 98308
  19.9 10.6 %collective-permute-start.9 = (f32[5,16,128]{2,1,0:T(8,128)S(1)}, f32[5,16,128]{2,1,0:T(8,128)S(1)}, u32[]{:S(2)}, u32[]{:S(2)}) collective-permute-start(f32[5,16,128]{2,1,0:T(8,128)S(1)} %get-tuple-element.7.refs_0_), channel_id=1, source_target_pairs={{24,0},{0,8},{8,16},{16,24},{25,1},{1,9},{9,17},{17,25},{26,2},{2,... | collective-permute-start | bytes 122888 | tf_op jit(solution)/shard_map/ppermute | solution.py:259
  21.4 9.1 %collective-permute-start.8 = (f32[5,16,128]{2,1,0:T(8,128)S(1)}, f32[5,16,128]{2,1,0:T(8,128)S(1)}, u32[]{:S(2)}, u32[]{:S(2)}) collective-permute-start(f32[5,16,128]{2,1,0:T(8,128)S(1)} %get-tuple-element.7.refs_0_), channel_id=1, source_target_pairs={{16,0},{24,8},{0,16},{8,24},{17,1},{25,9},{1,17},{9,25},{18,2},{26... | collective-permute-start | bytes 122888 | tf_op jit(solution)/shard_map/ppermute | solution.py:259
  21.9 8.6 %collective-permute-start.7 = (f32[5,16,128]{2,1,0:T(8,128)S(1)}, f32[5,16,128]{2,1,0:T(8,128)S(1)}, u32[]{:S(2)}, u32[]{:S(2)}) collective-permute-start(f32[5,16,128]{2,1,0:T(8,128)S(1)} %get-tuple-element.7.refs_0_), channel_id=1, source_target_pairs={{8,0},{16,8},{24,16},{0,24},{9,1},{17,9},{25,17},{1,25},{10,2},{18... | collective-permute-start | bytes 122888 | tf_op jit(solution)/shard_map/ppermute | solution.py:259
  23.4 4.1 %collective-permute-start.10 = (bf16[2,16,512]{2,1,0:T(8,128)(2,1)S(1)}, bf16[2,16,512]{2,1,0:T(8,128)(2,1)S(1)}, u32[]{:S(2)}, u32[]{:S(2)}) collective-permute-start(bf16[2,16,512]{2,1,0:T(8,128)(2,1)S(1)} %copy-done.6), channel_id=1, source_target_pairs={{8,0},{16,8},{24,16},{0,24},{9,1},{17,9},{25,17},{1,25},{10,2},{18... | collective-permute-start | bytes 98312 | tf_op jit(solution)/shard_map/ppermute | solution.py:259
  24.9 4.8 %collective-permute-start.12 = (bf16[2,16,512]{2,1,0:T(8,128)(2,1)S(1)}, bf16[2,16,512]{2,1,0:T(8,128)(2,1)S(1)}, u32[]{:S(2)}, u32[]{:S(2)}) collective-permute-start(bf16[2,16,512]{2,1,0:T(8,128)(2,1)S(1)} %copy-done.6), channel_id=1, source_target_pairs={{24,0},{0,8},{8,16},{16,24},{25,1},{1,9},{9,17},{17,25},{26,2},{2,... | collective-permute-start | bytes 98312 | tf_op jit(solution)/shard_map/ppermute | solution.py:259

commit v3 on v2

--- a/solution.py
+++ b/solution.py
@@ -120,13 +120,10 @@
     return result
 
 
-def forward_kernel(devices, *refs):
-    chunks = refs[:devices]
-    window, first_high, first_low, fwd, second_both, spec, sent, record = refs[devices:]
+def forward_kernel(size, chunks, window, first_high, first_low, fwd, second_both, spec, sent, record):
     rank = lax.axis_index("tmpl")
-    size = chunks[0].shape[0]
-    for shift, chunk in enumerate(chunks):
-        record[pl.ds(lax.rem(rank + shift, devices) * size, size)] = chunk[...]
+    for other in range(chunks.shape[0] // size):
+        record[pl.ds((rank ^ other) * size, size)] = chunks[other * size:(other + 1) * size]
     own = record.shape[0]
     w_low, w_high = window[:ROWS][None], window[ROWS:][None]
     fwd_cos, fwd_sin = fwd[0][None], fwd[1][None]
@@ -174,8 +171,8 @@
     cutoff, order, bank, gathered = refs[devices:]
     rank = lax.axis_index("tm")
     width = blocks[0].shape[2]
-    for shift, block in enumerate(blocks):
-        first = lax.rem(rank + shift, devices) * (width // LANES)
+    for other, block in enumerate(blocks):
+        first = (rank ^ other) * (width // LANES)
         for at in range(width // LANES):
             lanes = slice(at * LANES, (at + 1) * LANES)
             gathered[first + at] = jnp.concatenate([block[0, :, lanes], block[1, :, lanes]], axis=1)
@@ -193,16 +190,19 @@
 
 def filter_kernel(devices, segs, energy, *refs):
     shares = refs[:devices]
-    spec, bank, third, inv, fourth, out = refs[devices:]
+    spec, bank, third, inv, fourth, out, held = refs[devices:]
     own, count = out.shape
+    rank = lax.axis_index("tm")
     power = shares[0][0]
     for share in shares[1:]:
         power = power + share[0]
-    for i in range(devices):
-        after = shares[(i + 1) % devices]
-        re, im = shares[i][1] + after[3], shares[i][2] + after[4]
+    for other, share in enumerate(shares):
+        held[rank ^ other] = share[3:5]
+    for other, share in enumerate(shares):
+        after = held[lax.rem((rank ^ other) + 1, devices)]
+        re, im = share[1] + after[0], share[2] + after[1]
         power = power + re * re + im * im
-        if i == 0:
+        if other == 0:
             last_re, last_im = re, im
     density = power / (segs * energy) + FLOOR
     inverse_density = 1.0 / density
@@ -253,11 +253,17 @@
     block(own - GROUP, True)
 
 
-def around(array, axis):
-    devices = lax.axis_size(axis)
-    return [array] + [
-        lax.ppermute(array, axis, [((i + shift) % devices, i) for i in range(devices)]) for shift in range(1, devices)
-    ]
+def swap(array, axis, bits):
+    return lax.ppermute(array, axis, [(i, i ^ bits) for i in range(lax.axis_size(axis))])
+
+
+def load_kernel(count, *refs):
+    sources, targets, sems = refs[1:1 + count], refs[1 + count:1 + 2 * count], refs[-1]
+    copies = [pltpu.make_async_copy(s, t, sems.at[i]) for i, (s, t) in enumerate(zip(sources, targets))]
+    for copy in copies:
+        copy.start()
+    for copy in copies:
+        copy.wait()
 
 
 def on_device(strain, templates, cutoff):
@@ -265,27 +271,50 @@
     size = strain.shape[0] // HOP
     own = size * tmpl
     count = templates.shape[1]
-    held, energy = tables()
-    held = {name: jnp.asarray(table) for name, table in held.items()}
     smem = pl.BlockSpec(memory_space=pltpu.SMEM)
     vmem = pl.BlockSpec(memory_space=pltpu.VMEM)
+    anywhere = pl.BlockSpec(memory_space=pltpu.HBM)
     params = pltpu.CompilerParams(vmem_limit_bytes=48 * 1024 * 1024)
     f32 = jnp.float32
-    chunks = around(strain.reshape(size, ROWS, LANES), "tmpl")
-    blocks = around(templates, "tm")
+
+    chunks = strain.reshape(size, ROWS, LANES)
+    after = chunks
+    bits = 1
+    while bits < tmpl:
+        arrived = swap(chunks, "tmpl", bits)
+        if 2 * bits < tmpl:
+            after = arrived
+        chunks = jnp.concatenate([chunks, arrived], axis=0)
+        bits *= 2
+    blocks = [templates] + [swap(templates, "tm", other) for other in range(1, tm)]
+
+    held, energy = tables()
+    names = list(held)
+    loaded = pl.pallas_call(
+        functools.partial(load_kernel, len(names)),
+        out_shape=[jax.ShapeDtypeStruct(held[n].shape, held[n].dtype) for n in names],
+        in_specs=[pl.BlockSpec(memory_space=pl.ANY)] + [anywhere] * len(names),
+        out_specs=[vmem] * len(names),
+        scratch_shapes=[pltpu.SemaphoreType.DMA((len(names),))],
+        compiler_params=params,
+        cost_estimate=pl.CostEstimate(flops=0, bytes_accessed=3000000, transcendentals=0),
+        name="load",
+    )(after, *[jnp.asarray(held[n]) for n in names])
+    held = dict(zip(names, loaded))
+
     spec, sent = pl.pallas_call(
-        functools.partial(forward_kernel, tmpl),
+        functools.partial(forward_kernel, size),
         out_shape=(
             jax.ShapeDtypeStruct((2, own, ROWS, LANES), f32),
             jax.ShapeDtypeStruct((5, ROWS, LANES), f32),
         ),
-        in_specs=[vmem] * (tmpl + 5),
+        in_specs=[vmem] * 6,
         out_specs=(vmem, vmem),
         scratch_shapes=[pltpu.VMEM((own, ROWS, LANES), f32)],
         compiler_params=params,
         name="forward",
-    )(*chunks, held["window"], held["first_high"], held["first_low"], held["fwd"], held["second_both"])
-    shares = around(sent, "tm")
+    )(chunks, held["window"], held["first_high"], held["first_low"], held["fwd"], held["second_both"])
+    shares = [sent] + [swap(sent, "tm", other) for other in range(1, tm)]
     bank = pl.pallas_call(
         functools.partial(bank_kernel, tm),
         out_shape=jax.ShapeDtypeStruct((2, count, ROWS, LANES), f32),
@@ -293,6 +322,7 @@
         out_specs=vmem,
         scratch_shapes=[pltpu.VMEM((ROWS, count, 2 * LANES), jnp.bfloat16)],
         compiler_params=params,
+        cost_estimate=pl.CostEstimate(flops=0, bytes_accessed=2500000, transcendentals=0),
         name="bank",
     )(*blocks, cutoff, held["order"])
     return pl.pallas_call(
@@ -300,6 +330,7 @@
         out_shape=jax.ShapeDtypeStruct((own, count), f32),
         in_specs=[vmem] * (tm + 5),
         out_specs=vmem,
+        scratch_shapes=[pltpu.VMEM((tm, 2, ROWS, LANES), f32)],
         compiler_params=params,
         name="matched_filter",
     )(*shares, spec, bank, held["third"], held["inv"], held["fourth"])

time: 33.2 us -> 32.9 us (level)
  starting transfers between devices: 17.8 us -> 13.4 us
  other arithmetic: 0 us -> 1.41 us
  waiting for transfers between devices: 5.93 us -> 7.1 us
  Pallas kernels: 3.91 us -> 4.85 us
  local copies, waits for them, and re-layouts: 5.03 us -> 5.6 us
    ppermute x13 -> x9, starting transfers between devices: 17.8 us -> 13.4 us  [swap(): lax.ppermute(array, axis, [(i, i ^ bits) for i in range(lax.axis_size(axi...]
    concatenate x0 -> x3, other arithmetic: none -> 1.41 us  [on_device(): chunks = jnp.concatenate([chunks, arrived], axis=0)]
    ppermute x13 -> x9, waiting for transfers between devices: 5.93 us -> 7.1 us  [swap(): lax.ppermute(array, axis, [(i, i ^ bits) for i in range(lax.axis_size(axi...]
    pallas_call x1 -> x2, Pallas kernels: 0.9 us -> 1.8 us  [the longest x1 0.9 us: on_device(): pl.pallas_call(functools.partial(load_kernel, len(names)), out_shape=[jax...]
    unnamed x24, local copies, waits for them, and re-layouts: 5.03 us -> 5.6 us
  transfers between devices with their start and end apart: 13 -> 9, of which waited for: 4 -> 4; matrix products, arithmetic and copies ran while one was open for 0% -> 0% of each run, Pallas kernels for 5% -> 8%
where the time goes in v3:
time: 32.9 us; the launch traced here: 32.5 us
  starting transfers between devices  13.4 us (41%)
  waiting for transfers between devices  7.1 us (22%)
  local copies, waits for them, and re-layouts  5.6 us (17%)
  Pallas kernels  4.85 us (15%)
  other arithmetic  1.41 us (4%)
    ppermute x9, starting transfers between devices, swap(): lax.ppermute(array, axis, [(i, i ^ bits) for i in range(lax.axis_size(axi...  13.4 us
    ppermute x9, waiting for transfers between devices, swap(): lax.ppermute(array, axis, [(i, i ^ bits) for i in range(lax.axis_size(axi...  7.1 us
    unnamed x24, local copies, waits for them, and re-layouts  5.6 us
    pallas_call x1, Pallas kernels, on_device(): pl.pallas_call(functools.partial(filter_kernel, tm, own * tm, energy), ou...  2.31 us
    concatenate x3, other arithmetic, on_device(): chunks = jnp.concatenate([chunks, arrived], axis=0)  1.41 us
    pallas_call x1, Pallas kernels, on_device(): pl.pallas_call(functools.partial(load_kernel, len(names)), out_shape=[jax...  0.9 us
    pallas_call x1, Pallas kernels, on_device(): pl.pallas_call(functools.partial(forward_kernel, size), out_shape=(jax.Sh...  0.9 us
    pallas_call x1, Pallas kernels, on_device(): pl.pallas_call(functools.partial(bank_kernel, tm), out_shape=jax.ShapeDty...  0.74 us
  transfers between devices with their start and end apart: 9, of which 4 were waited for; matrix products, arithmetic and copies ran while one was open for 0% of the time, Pallas kernels for 8%

profile of v3, /device:TPU:0, one launch (start us, length us, event | category | flops | bytes accessed | tf_op | source)
XLA Modules:
  0.0 32.5 jit_solution(5047615718931617467)
XLA Ops:
  0.0 0.0 copy-start.9
  0.0 0.5 %collective-permute-start = (f32[1,16,128]{2,1,0:T(8,128)}, f32[1,16,128]{2,1,0:T(8,128)S(1)}, u32[]{:S(2)}, u32[]{:S(2)}) collective-permute-start(f32[1,16,128]{2,1,0:T(8,128)} %bitcast.1), channel_id=1, source_target_pairs={{0,1},{1,0},{2,3},{3,2},{4,5},{5,4},{6,7},{7,6},{8,9},{9,8},{10,11... | collective-permute-start | bytes 24584 | tf_op jit(solution)/shard_map/ppermute | solution.py:257
  0.5 1.0 %collective-permute-done = f32[1,16,128]{2,1,0:T(8,128)S(1)} collective-permute-done((f32[1,16,128]{2,1,0:T(8,128)}, f32[1,16,128]{2,1,0:T(8,128)S(1)}, u32[]{:S(2)}, u32[]{:S(2)}) %collective-permute-start) | collective-permute-done | bytes 8224 | tf_op jit(solution)/shard_map/ppermute | solution.py:257
  1.5 0.0 copy-start.8
  1.5 0.7 %pad_maximum_fusion.2 = f32[2,16,128]{2,1,0:T(8,128)S(1)} fusion(f32[1,16,128]{2,1,0:T(8,128)S(1)} %collective-permute-done, f32[1,16,128]{2,1,0:T(8,128)} %bitcast.2), kind=kLoop, calls=%fused_computation.2 | loop fusion | flops 4096 | bytes 32768 | tf_op jit(solution)/shard_map/concatenate | solution.py:287
  2.2 0.0 copy-start.6
  2.2 0.0 copy-start.7
  2.2 2.9 %collective-permute-start.1 = (f32[2,16,128]{2,1,0:T(8,128)S(1)}, f32[2,16,128]{2,1,0:T(8,128)S(1)}, u32[]{:S(2)}, u32[]{:S(2)}) collective-permute-start(f32[2,16,128]{2,1,0:T(8,128)S(1)} %pad_maximum_fusion.2), channel_id=1, source_target_pairs={{0,2},{1,3},{2,0},{3,1},{4,6},{5,7},{6,4},{7,5},{8,10},{9,11},{10,... | collective-permute-start | bytes 49160 | tf_op jit(solution)/shard_map/ppermute | solution.py:257
  5.1 1.7 %collective-permute-done.1.refs_0_ = f32[2,16,128]{2,1,0:T(8,128)S(1)} collective-permute-done((f32[2,16,128]{2,1,0:T(8,128)S(1)}, f32[2,16,128]{2,1,0:T(8,128)S(1)}, u32[]{:S(2)}, u32[]{:S(2)}) %collective-permute-start.1) | collective-permute-done | bytes 16416 | tf_op jit(solution)/shard_map/ppermute | solution.py:257
  6.8 0.7 %pad_maximum_fusion.1 = f32[4,16,128]{2,1,0:T(8,128)S(1)} fusion(f32[2,16,128]{2,1,0:T(8,128)S(1)} %collective-permute-done.1.refs_0_, f32[1,16,128]{2,1,0:T(8,128)S(1)} %collective-permute-done, f32[1,16,128]{2,1,0:T(8,128)} %bitcast.3), kind=kLoop, calls=%fused_computation.1 | loop fusion | flops 16384 | bytes 65536 | tf_op jit(solution)/shard_map/concatenate | solution.py:287
  7.5 3.0 %collective-permute-start.2 = (f32[4,16,128]{2,1,0:T(8,128)S(1)}, f32[4,16,128]{2,1,0:T(8,128)S(1)}, u32[]{:S(2)}, u32[]{:S(2)}) collective-permute-start(f32[4,16,128]{2,1,0:T(8,128)S(1)} %pad_maximum_fusion.1), channel_id=1, source_target_pairs={{0,4},{1,5},{2,6},{3,7},{4,0},{5,1},{6,2},{7,3},{8,12},{9,13},{10,... | collective-permute-start | bytes 98312 | tf_op jit(solution)/shard_map/ppermute | solution.py:257
  10.6 0.0 copy-done.6
  10.6 1.5 %collective-permute-start.6 = (bf16[2,16,512]{2,1,0:T(8,128)(2,1)S(1)}, bf16[2,16,512]{2,1,0:T(8,128)(2,1)S(1)}, u32[]{:S(2)}, u32[]{:S(2)}) collective-permute-start(bf16[2,16,512]{2,1,0:T(8,128)(2,1)S(1)} %copy-done.6), channel_id=1, source_target_pairs={{0,8},{8,0},{16,24},{24,16},{1,9},{9,1},{17,25},{25,17},{2,10},{10... | collective-permute-start | bytes 98312 | tf_op jit(solution)/shard_map/ppermute | solution.py:257
  12.1 0.0 copy-done.9
  12.1 0.0 copy-done.8
  12.1 0.0 copy-done.7
  12.1 0.0 copy-start
  12.1 1.0 %copy-done = bf16[576,256]{1,0:T(8,128)(2,1)S(1)} copy-done((bf16[576,256]{1,0:T(8,128)(2,1)S(1)}, bf16[576,256]{1,0:T(8,128)(2,1)}, u32[]{:S(2)}) %copy-start) | copy-done | bytes 294936
  13.0 0.0 copy-start.1
  13.0 1.0 %copy-done.1 = bf16[576,256]{1,0:T(8,128)(2,1)S(1)} copy-done((bf16[576,256]{1,0:T(8,128)(2,1)S(1)}, bf16[576,256]{1,0:T(8,128)(2,1)}, u32[]{:S(2)}) %copy-start.1) | copy-done | bytes 294936
  14.0 0.0 copy-start.2
  14.0 0.9 %copy-done.2 = bf16[512,256]{1,0:T(8,128)(2,1)S(1)} copy-done((bf16[512,256]{1,0:T(8,128)(2,1)S(1)}, bf16[512,256]{1,0:T(8,128)(2,1)}, u32[]{:S(2)}) %copy-start.2) | copy-done | bytes 262168
  15.0 0.0 copy-start.3
  15.0 0.9 %copy-done.3 = bf16[256,256]{1,0:T(8,128)(2,1)S(1)} copy-done((bf16[256,256]{1,0:T(8,128)(2,1)S(1)}, bf16[256,256]{1,0:T(8,128)(2,1)}, u32[]{:S(2)}) %copy-start.3) | copy-done | bytes 131096
  15.9 0.0 copy-start.4
  15.9 0.9 %copy-done.4 = bf16[256,256]{1,0:T(8,128)(2,1)S(1)} copy-done((bf16[256,256]{1,0:T(8,128)(2,1)S(1)}, bf16[256,256]{1,0:T(8,128)(2,1)}, u32[]{:S(2)}) %copy-start.4) | copy-done | bytes 131096
  16.8 0.0 copy-start.5
  16.8 0.9 %copy-done.5 = bf16[256,256]{1,0:T(8,128)(2,1)S(1)} copy-done((bf16[256,256]{1,0:T(8,128)(2,1)S(1)}, bf16[256,256]{1,0:T(8,128)(2,1)}, u32[]{:S(2)}) %copy-start.5) | copy-done | bytes 131096
  17.7 0.0 copy-start.11
  17.7 0.9 %load.1 = (f32[32,128]{1,0:T(8,128)S(1)}, bf16[576,256]{1,0:T(8,128)(2,1)S(1)}, bf16[576,256]{1,0:T(8,128)(2,1)S(1)}, f32[2,32,128]{2,1,0:T(8,128)S(1)}, bf16[25...) custom-call(f32[2,16,128]{2,1,0:T(8,128)S(1)} %collective-permute-do, ...), custom_call_target="tpu_custom_call" | custom-call | bytes 3000000 | tf_op jit(solution)/shard_map/load/pallas_call | solution.py:293
  18.6 0.0 collective-permute-done.2
  18.6 0.0 copy-done.11
  18.6 0.9 %forward.1 = (f32[2,8,16,128]{3,2,1,0:T(8,128)S(1)}, f32[5,16,128]{2,1,0:T(8,128)S(1)}) custom-call(f32[8,16,128]{2,1,0:T(8,128)S(1)} %pad_maximum_fusion.chunks, f32[32,128]{1,0:T(8,128)S(1)} %get-tuple-element.16.window, bf16[576,256]{1,0:T(8,128)(2,1)S(1)} %get-tuple-element.17.first_high, bf16[576,256]{1,0:T(8,128)(2,1)S(1)} %get-tuple-element.18.first_low, ...), custom_call_target="tpu_custom_call" | custom-call | tf_op jit(solution)/shard_map/forward/pallas_call | solution.py:305
  19.5 0.0 copy-start.10
  19.5 0.6 %collective-permute-start.3 = (f32[5,16,128]{2,1,0:T(8,128)S(1)}, f32[5,16,128]{2,1,0:T(8,128)S(1)}, u32[]{:S(2)}, u32[]{:S(2)}) collective-permute-start(f32[5,16,128]{2,1,0:T(8,128)S(1)} %get-tuple-element.21.refs_0_), channel_id=1, source_target_pairs={{0,8},{8,0},{16,24},{24,16},{1,9},{9,1},{17,25},{25,17},{2,10},{10... | collective-permute-start | bytes 122888 | tf_op jit(solution)/shard_map/ppermute | solution.py:257
  20.1 1.5 %collective-permute-start.4 = (f32[5,16,128]{2,1,0:T(8,128)S(1)}, f32[5,16,128]{2,1,0:T(8,128)S(1)}, u32[]{:S(2)}, u32[]{:S(2)}) collective-permute-start(f32[5,16,128]{2,1,0:T(8,128)S(1)} %get-tuple-element.21.refs_0_), channel_id=1, source_target_pairs={{0,16},{8,24},{16,0},{24,8},{1,17},{9,25},{17,1},{25,9},{2,18},{10... | collective-permute-start | bytes 122888 | tf_op jit(solution)/shard_map/ppermute | solution.py:257
  21.6 1.4 %collective-permute-start.5 = (f32[5,16,128]{2,1,0:T(8,128)S(1)}, f32[5,16,128]{2,1,0:T(8,128)S(1)}, u32[]{:S(2)}, u32[]{:S(2)}) collective-permute-start(f32[5,16,128]{2,1,0:T(8,128)S(1)} %get-tuple-element.21.refs_0_), channel_id=1, source_target_pairs={{0,24},{8,16},{16,8},{24,0},{1,25},{9,17},{17,9},{25,1},{2,26},{10... | collective-permute-start | bytes 122888 | tf_op jit(solution)/shard_map/ppermute | solution.py:257
  23.1 1.5 %collective-permute-start.7 = (bf16[2,16,512]{2,1,0:T(8,128)(2,1)S(1)}, bf16[2,16,512]{2,1,0:T(8,128)(2,1)S(1)}, u32[]{:S(2)}, u32[]{:S(2)}) collective-permute-start(bf16[2,16,512]{2,1,0:T(8,128)(2,1)S(1)} %copy-done.6), channel_id=1, source_target_pairs={{0,16},{8,24},{16,0},{24,8},{1,17},{9,25},{17,1},{25,9},{2,18},{10... | collective-permute-start | bytes 98312 | tf_op jit(solution)/shard_map/ppermute | solution.py:257
  24.6 0.0 collective-permute-done.6.refs_1_
  24.6 0.5 %collective-permute-start.8 = (bf16[2,16,512]{2,1,0:T(8,128)(2,1)S(1)}, bf16[2,16,512]{2,1,0:T(8,128)(2,1)S(1)}, u32[]{:S(2)}, u32[]{:S(2)}) collective-permute-start(bf16[2,16,512]{2,1,0:T(8,128)(2,1)S(1)} %copy-done.6), channel_id=1, source_target_pairs={{0,24},{8,16},{16,8},{24,0},{1,25},{9,17},{17,9},{25,1},{2,26},{10... | collective-permute-start | bytes 98312 | tf_op jit(solution)/shard_map/ppermute | solution.py:257
  25.1 1.9 %collective-permute-done.7.refs_2_ = bf16[2,16,512]{2,1,0:T(8,128)(2,1)S(1)} collective-permute-done((bf16[2,16,512]{2,1,0:T(8,128)(2,1)S(1)}, bf16[2,16,512]{2,1,0:T(8,128)(2,1)S(1)}, u32[]{:S(2)}, u32[]{:S(2)}) %collective-permute-start.7) | collective-permute-done | bytes 32800 | tf_op jit(solution)/shard_map/ppermute | solution.py:257
  27.0 2.4 %collective-permute-done.8.refs_3_ = bf16[2,16,512]{2,1,0:T(8,128)(2,1)S(1)} collective-permute-done((bf16[2,16,512]{2,1,0:T(8,128)(2,1)S(1)}, bf16[2,16,512]{2,1,0:T(8,128)(2,1)S(1)}, u32[]{:S(2)}, u32[]{:S(2)}) %collective-permute-start.8) | collective-permute-done | bytes 32800 | tf_op jit(solution)/shard_map/ppermute | solution.py:257
  29.4 0.0 copy-done.10
  29.4 0.7 %bank.1.refs_5_ = f32[2,16,16,128]{3,2,1,0:T(8,128)S(1)} custom-call(bf16[2,16,512]{2,1,0:T(8,128)(2,1)S(1)} %copy-done.6, bf16[2,16,512]{2,1,0:T(8,128)(2,1)S(1)} %collective-permute-done.6.refs_1_, bf16[2,16,512]{2,1,0:T(8,128)(2,1)S(1)} %collective-permute-done.7.refs_2_, bf16[2,16,512]{2,1,0:T(8,128)(2,1)S(1)} %collective-permute-done.8.refs_3_, ...), custom_call_target="tpu_custom_call" | custom-call | bytes 2500000 | tf_op jit(solution)/shard_map/bank/pallas_call | solution.py:318
  30.2 0.0 collective-permute-done.3.refs_1_
  30.2 0.0 collective-permute-done.4.refs_2_
  30.2 0.0 collective-permute-done.5.refs_3_
  30.2 2.3 %matched_filter.1 = f32[8,16]{1,0:T(8,128)} custom-call(f32[5,16,128]{2,1,0:T(8,128)S(1)} %get-tuple-element.21.refs_0_, f32[5,16,128]{2,1,0:T(8,128)S(1)} %collective-permute-done.3.refs_1_, f32[5,16,128]{2,1,0:T(8,128)S(1)} %collective-permute-done.4.refs_2_, f32[5,16,128]{2,1,0:T(8,128)S(1)} %collective-permute-done.5.refs_3_, ...), custom_call_target="tpu_custom_call" | custom-call | tf_op jit(solution)/shard_map/matched_filter/pallas_call | solution.py:328
  (1 shorter events, 0.0 us)
Async XLA Ops:
  0.0 12.1 %copy-start.9 = (f32[32,128]{1,0:T(8,128)S(1)}, f32[32,128]{1,0:T(8,128)}, u32[]{:S(2)}) copy-start(f32[32,128]{1,0:T(8,128)} %constant.18.clone.refs_1_) | copy-start | bytes 49156
  0.0 1.5 %collective-permute-start = (f32[1,16,128]{2,1,0:T(8,128)}, f32[1,16,128]{2,1,0:T(8,128)S(1)}, u32[]{:S(2)}, u32[]{:S(2)}) collective-permute-start(f32[1,16,128]{2,1,0:T(8,128)} %bitcast.1), channel_id=1, source_target_pairs={{0,1},{1,0},{2,3},{3,2},{4,5},{5,4},{6,7},{7,6},{8,9},{9,8},{10,11... | collective-permute-start | bytes 24584 | tf_op jit(solution)/shard_map/ppermute | solution.py:257
  1.5 10.6 %copy-start.8 = (f32[2,32,128]{2,1,0:T(8,128)S(1)}, f32[2,32,128]{2,1,0:T(8,128)}, u32[]{:S(2)}) copy-start(f32[2,32,128]{2,1,0:T(8,128)} %constant.24.clone.refs_7_) | copy-start | bytes 98308
  2.2 8.4 %copy-start.6 = (bf16[2,16,512]{2,1,0:T(8,128)(2,1)S(1)}, bf16[2,16,512]{2,1,0:T(8,128)(2,1)}, u32[]{:S(2)}) copy-start(bf16[2,16,512]{2,1,0:T(8,128)(2,1)} %refs_0_.1) | copy-start | bytes 98308
  2.2 9.9 %copy-start.7 = (f32[2,32,128]{2,1,0:T(8,128)S(1)}, f32[2,32,128]{2,1,0:T(8,128)}, u32[]{:S(2)}) copy-start(f32[2,32,128]{2,1,0:T(8,128)} %constant.21.clone.refs_4_) | copy-start | bytes 98308
  2.2 4.6 %collective-permute-start.1 = (f32[2,16,128]{2,1,0:T(8,128)S(1)}, f32[2,16,128]{2,1,0:T(8,128)S(1)}, u32[]{:S(2)}, u32[]{:S(2)}) collective-permute-start(f32[2,16,128]{2,1,0:T(8,128)S(1)} %pad_maximum_fusion.2), channel_id=1, source_target_pairs={{0,2},{1,3},{2,0},{3,1},{4,6},{5,7},{6,4},{7,5},{8,10},{9,11},{10,... | collective-permute-start | bytes 49160 | tf_op jit(solution)/shard_map/ppermute | solution.py:257
  7.5 11.0 %collective-permute-start.2 = (f32[4,16,128]{2,1,0:T(8,128)S(1)}, f32[4,16,128]{2,1,0:T(8,128)S(1)}, u32[]{:S(2)}, u32[]{:S(2)}) collective-permute-start(f32[4,16,128]{2,1,0:T(8,128)S(1)} %pad_maximum_fusion.1), channel_id=1, source_target_pairs={{0,4},{1,5},{2,6},{3,7},{4,0},{5,1},{6,2},{7,3},{8,12},{9,13},{10,... | collective-permute-start | bytes 98312 | tf_op jit(solution)/shard_map/ppermute | solution.py:257
  10.6 14.0 %collective-permute-start.6 = (bf16[2,16,512]{2,1,0:T(8,128)(2,1)S(1)}, bf16[2,16,512]{2,1,0:T(8,128)(2,1)S(1)}, u32[]{:S(2)}, u32[]{:S(2)}) collective-permute-start(bf16[2,16,512]{2,1,0:T(8,128)(2,1)S(1)} %copy-done.6), channel_id=1, source_target_pairs={{0,8},{8,0},{16,24},{24,16},{1,9},{9,1},{17,25},{25,17},{2,10},{10... | collective-permute-start | bytes 98312 | tf_op jit(solution)/shard_map/ppermute | solution.py:257
  12.1 1.0 %copy-start = (bf16[576,256]{1,0:T(8,128)(2,1)S(1)}, bf16[576,256]{1,0:T(8,128)(2,1)}, u32[]{:S(2)}) copy-start(bf16[576,256]{1,0:T(8,128)(2,1)} %constant.19.clone.refs_2_) | copy-start | bytes 884740
  13.0 1.0 %copy-start.1 = (bf16[576,256]{1,0:T(8,128)(2,1)S(1)}, bf16[576,256]{1,0:T(8,128)(2,1)}, u32[]{:S(2)}) copy-start(bf16[576,256]{1,0:T(8,128)(2,1)} %constant.20.clone.refs_3_) | copy-start | bytes 884740
  14.0 0.9 %copy-start.2 = (bf16[512,256]{1,0:T(8,128)(2,1)S(1)}, bf16[512,256]{1,0:T(8,128)(2,1)}, u32[]{:S(2)}) copy-start(bf16[512,256]{1,0:T(8,128)(2,1)} %constant.23.clone.refs_6_) | copy-start | bytes 786436
  15.0 0.9 %copy-start.3 = (bf16[256,256]{1,0:T(8,128)(2,1)S(1)}, bf16[256,256]{1,0:T(8,128)(2,1)}, u32[]{:S(2)}) copy-start(bf16[256,256]{1,0:T(8,128)(2,1)} %constant.22.clone.refs_5_) | copy-start | bytes 393220
  15.9 0.9 %copy-start.4 = (bf16[256,256]{1,0:T(8,128)(2,1)S(1)}, bf16[256,256]{1,0:T(8,128)(2,1)}, u32[]{:S(2)}) copy-start(bf16[256,256]{1,0:T(8,128)(2,1)} %constant.25.clone.refs_8_) | copy-start | bytes 393220
  16.8 0.9 %copy-start.5 = (bf16[256,256]{1,0:T(8,128)(2,1)S(1)}, bf16[256,256]{1,0:T(8,128)(2,1)}, u32[]{:S(2)}) copy-start(bf16[256,256]{1,0:T(8,128)(2,1)} %constant.26.clone.refs_9_) | copy-start | bytes 393220
  17.7 0.9 %copy-start.11 = (f32[2048]{0:T(1024)S(1)}, f32[2048]{0:T(1024)}, u32[]{:S(2)}) copy-start(f32[2048]{0:T(1024)} %param.12) | copy-start | bytes 24580
  19.5 9.9 %copy-start.10 = (s32[16]{0:T(128)S(1)}, s32[16]{0:T(128)}, u32[]{:S(2)}) copy-start(s32[16]{0:T(128)} %refs_4_.2) | copy-start | bytes 196
  19.5 10.6 %collective-permute-start.3 = (f32[5,16,128]{2,1,0:T(8,128)S(1)}, f32[5,16,128]{2,1,0:T(8,128)S(1)}, u32[]{:S(2)}, u32[]{:S(2)}) collective-permute-start(f32[5,16,128]{2,1,0:T(8,128)S(1)} %get-tuple-element.21.refs_0_), channel_id=1, source_target_pairs={{0,8},{8,0},{16,24},{24,16},{1,9},{9,1},{17,25},{25,17},{2,10},{10... | collective-permute-start | bytes 122888 | tf_op jit(solution)/shard_map/ppermute | solution.py:257
  20.1 10.1 %collective-permute-start.4 = (f32[5,16,128]{2,1,0:T(8,128)S(1)}, f32[5,16,128]{2,1,0:T(8,128)S(1)}, u32[]{:S(2)}, u32[]{:S(2)}) collective-permute-start(f32[5,16,128]{2,1,0:T(8,128)S(1)} %get-tuple-element.21.refs_0_), channel_id=1, source_target_pairs={{0,16},{8,24},{16,0},{24,8},{1,17},{9,25},{17,1},{25,9},{2,18},{10... | collective-permute-start | bytes 122888 | tf_op jit(solution)/shard_map/ppermute | solution.py:257
  21.6 8.5 %collective-permute-start.5 = (f32[5,16,128]{2,1,0:T(8,128)S(1)}, f32[5,16,128]{2,1,0:T(8,128)S(1)}, u32[]{:S(2)}, u32[]{:S(2)}) collective-permute-start(f32[5,16,128]{2,1,0:T(8,128)S(1)} %get-tuple-element.21.refs_0_), channel_id=1, source_target_pairs={{0,24},{8,16},{16,8},{24,0},{1,25},{9,17},{17,9},{25,1},{2,26},{10... | collective-permute-start | bytes 122888 | tf_op jit(solution)/shard_map/ppermute | solution.py:257
  23.1 3.9 %collective-permute-start.7 = (bf16[2,16,512]{2,1,0:T(8,128)(2,1)S(1)}, bf16[2,16,512]{2,1,0:T(8,128)(2,1)S(1)}, u32[]{:S(2)}, u32[]{:S(2)}) collective-permute-start(bf16[2,16,512]{2,1,0:T(8,128)(2,1)S(1)} %copy-done.6), channel_id=1, source_target_pairs={{0,16},{8,24},{16,0},{24,8},{1,17},{9,25},{17,1},{25,9},{2,18},{10... | collective-permute-start | bytes 98312 | tf_op jit(solution)/shard_map/ppermute | solution.py:257
  24.6 4.8 %collective-permute-start.8 = (bf16[2,16,512]{2,1,0:T(8,128)(2,1)S(1)}, bf16[2,16,512]{2,1,0:T(8,128)(2,1)S(1)}, u32[]{:S(2)}, u32[]{:S(2)}) collective-permute-start(bf16[2,16,512]{2,1,0:T(8,128)(2,1)S(1)} %copy-done.6), channel_id=1, source_target_pairs={{0,24},{8,16},{16,8},{24,0},{1,25},{9,17},{17,9},{25,1},{2,26},{10... | collective-permute-start | bytes 98312 | tf_op jit(solution)/shard_map/ppermute | solution.py:257

commit v4 on v1

v4 whole, which is shorter than its diff:
```python
import functools
import math

import jax
import jax.numpy as jnp
import ml_dtypes
import numpy as np
from jax import lax
from jax.experimental import pallas as pl
from jax.experimental.pallas import tpu as pltpu
from jax.sharding import PartitionSpec as P

NFFT = 4096
BINS = 2048
HOP = 2048
LANES = 128
ROWS = HOP // LANES
FINE = 32
GROUP = 8
FLOOR = 1e-6

ROOT_SCALE = {128: 1.66575, 64: 1.66575, 32: 1.6245, 16: 1.6245, 8: 1.6245}


def root_order(index, period):
    return period // math.gcd(int(index), period)


def row_scale(count, period):
    return np.array([ROOT_SCALE.get(root_order(i, period), 1.0) for i in range(count)])


def as_bf16(table):
    return np.asarray(table, np.float32).astype(ml_dtypes.bfloat16)


def two_parts(table):
    high = as_bf16(table)
    low = as_bf16(np.asarray(table, np.float64) - high.astype(np.float64))
    return high, low


def turn(left, right, period):
    angle = 2.0 * np.pi * (np.outer(left, right) % period) / period
    return np.cos(angle), np.sin(angle)


@functools.lru_cache(maxsize=None)
def tables():
    fine, wide, rows = np.arange(FINE), np.arange(LANES), np.arange(ROWS)
    window = 0.5 - 0.5 * np.cos(2.0 * np.pi * np.arange(NFFT) / NFFT)
    cos, sin = turn(fine, fine, FINE)
    first_high, first_low = two_parts(np.tile(np.concatenate([cos, -sin]), (1, GROUP)))
    fwd_cos, fwd_sin = turn(fine, wide, NFFT)
    f_order = np.array([4 * d + g for g in range(4) for d in range(ROWS)])
    cos, sin = turn(wide, f_order, LANES)
    second_high, second_low = two_parts(np.block([[cos, -sin], [sin, cos]]))
    scale_q, scale_c = row_scale(FINE, FINE), row_scale(LANES, LANES)
    cos, sin = turn(fine, rows, FINE)
    cos, sin = np.tile(cos * scale_q[:, None], (1, GROUP)), np.tile(sin * scale_q[:, None], (1, GROUP))
    third = np.block([[cos, -sin], [sin, cos]])
    inv_cos, inv_sin = turn(fine, wide, NFFT)
    undo = 1.0 / (scale_q[:, None] * scale_c[None, :])
    cos, sin = turn(wide, wide, LANES)
    cos, sin = cos * scale_c[:, None], sin * scale_c[:, None]
    fourth = np.block([[cos, sin], [-sin, cos]])
    narrow = np.concatenate(
        [first_high, first_low, as_bf16(third), np.concatenate([second_high, second_low], axis=1), as_bf16(fourth)]
    )
    broad = np.concatenate([window.reshape(FINE, LANES), fwd_cos, fwd_sin, inv_cos * undo, inv_sin * undo])
    return narrow, np.asarray(broad, np.float32), float((window * window).sum())


def dot(left, right):
    return jnp.dot(left, right, preferred_element_type=jnp.float32)


def split(value):
    high = value.astype(jnp.bfloat16)
    return high, (value - high.astype(jnp.float32)).astype(jnp.bfloat16)


def repeat(count, body, carry):
    if count <= 8:
        for step in range(count):
            carry = body(step, carry)
        return carry
    return lax.fori_loop(0, count, body, carry)


def block_diagonal(rows, width):
    lane = lax.broadcasted_iota(jnp.int32, rows.shape, 1)
    owner = lax.rem(lane // width, GROUP)
    return jnp.concatenate(
        [jnp.where(owner == s, rows, jnp.zeros_like(rows)) for s in range(GROUP)], axis=0
    )


def natural(flipped, at, source):
    part = lax.broadcasted_iota(jnp.int32, (ROWS, LANES), 1) // FINE
    result = None
    for g in range(4):
        piece = flipped[at + g * ROWS:at + (g + 1) * ROWS]
        if source is not None and g != source:
            piece = pltpu.roll(piece, ((g - source) % 4) * FINE, 1)
        result = piece if g == 0 else jnp.where(part == g, piece, result)
    return result


def pack_kernel(strain, templates, copies, held):
    held[...] = templates[...]
    copies[...] = jnp.broadcast_to(strain[...][None], copies.shape)


def bank_kernel(devices, *refs):
    blocks = refs[:devices]
    cutoff, bank, gathered = refs[devices:]
    rank = lax.axis_index("tm")
    width = blocks[0].shape[2]
    for other, block in enumerate(blocks):
        first = (rank ^ other) * (width // LANES)
        for at in range(width // LANES):
            lanes = slice(at * LANES, (at + 1) * LANES)
            gathered[first + at] = jnp.concatenate([block[0, :, lanes], block[1, :, lanes]], axis=1)
    count = blocks[0].shape[1]
    lane = lax.broadcasted_iota(jnp.int32, (ROWS, LANES), 1)
    row = lax.broadcasted_iota(jnp.int32, (ROWS, LANES), 0)
    bins = row * LANES + lane
    shape = (count * ROWS, count * ROWS)
    to, source = lax.broadcasted_iota(jnp.int32, shape, 0), lax.broadcasted_iota(jnp.int32, shape, 1)
    order = (source == (to % ROWS) * count + to // ROWS).astype(jnp.float32).astype(jnp.bfloat16)
    value = dot(order, gathered[...].reshape(ROWS * count, 2 * LANES))
    for m in range(count):
        keep = bins < cutoff[m]
        rows = slice(m * ROWS, (m + 1) * ROWS)
        bank[0, m] = jnp.where(keep, value[rows, :LANES], 0.0)
        bank[1, m] = jnp.where(keep, value[rows, LANES:], 0.0)


def filter_kernel(energy, record, bank, narrow, broad, out, spec):
    segs = record.shape[0]
    own, count = out.shape
    half = GROUP * FINE
    w_low, w_high = broad[:ROWS][None], broad[ROWS:FINE][None]
    fwd_cos, fwd_sin = broad[FINE:2 * FINE][None], broad[2 * FINE:3 * FINE][None]
    inv_cos, inv_sin = broad[3 * FINE:4 * FINE][None], broad[4 * FINE:5 * FINE][None]
    high, low = narrow[:2 * FINE], narrow[2 * FINE:4 * FINE]
    spread = lambda part: jnp.concatenate(
        [block_diagonal(part[:FINE], part.shape[1] // GROUP), block_diagonal(part[FINE:], part.shape[1] // GROUP)]
    )
    first_high, first_low = spread(high), spread(low)
    third_rows = narrow[4 * FINE:6 * FINE]
    third = jnp.concatenate([block_diagonal(third_rows[:FINE], ROWS), block_diagonal(third_rows[FINE:], ROWS)])
    second = slice(6 * FINE, 6 * FINE + 2 * LANES)
    fourth = slice(6 * FINE + 2 * LANES, 6 * FINE + 4 * LANES)

    def frames(start, last):
        here = record[pl.ds(start, GROUP)]
        if last:
            after = jnp.concatenate([record[pl.ds(start + 1, GROUP - 1)], record[pl.ds(0, 1)]], axis=0)
        else:
            after = record[pl.ds(start + 1, GROUP)]
        both = jnp.concatenate([here * w_low, after * w_high], axis=1)
        return both.reshape(half, LANES)

    def forward(start, power, last):
        pair = jnp.concatenate([frames(start, False), frames(start + GROUP, last)], axis=1)
        high, low = split(pair)
        step = dot(first_high, high) + dot(first_high, low) + dot(first_low, high)
        for h in range(2):
            re = step[:half, h * LANES:(h + 1) * LANES].reshape(GROUP, FINE, LANES)
            im = step[half:, h * LANES:(h + 1) * LANES].reshape(GROUP, FINE, LANES)
            turned = jnp.concatenate([re * fwd_cos + im * fwd_sin, im * fwd_cos - re * fwd_sin], axis=2)
            high, low = split(turned.reshape(half, 2 * LANES))
            wide = dot(high, narrow[second])
            value = wide[:, :LANES] + wide[:, LANES:] + dot(low, narrow[second, :LANES])
            spec[pl.ds((start + h * GROUP) * FINE, half)] = value
            power = power + jnp.sum((value * value).reshape(GROUP, FINE, LANES), axis=0)
        return power

    power = jnp.zeros((FINE, LANES), jnp.float32)
    pairs = segs // (2 * GROUP)
    power = repeat(pairs - 1, lambda i, p: forward(i * 2 * GROUP, p, False), power)
    power = forward((pairs - 1) * 2 * GROUP, power, True)
    power = power + pltpu.roll(power, LANES // 2, 1)
    density = power / (segs * energy) + FLOOR
    inverse_density = natural((1.0 / jnp.concatenate([density] * 4, axis=0)).T, 0, None)

    place = lax.axis_index("tm") * own
    column = lax.broadcasted_iota(jnp.int32, (GROUP, LANES), 1)

    def block(number, carry):
        at = pl.multiple_of((place + number * GROUP) * FINE, half)
        white = spec[pl.ds(at, half)].reshape(GROUP, FINE, LANES) / density[None]
        white = white.astype(jnp.bfloat16).astype(jnp.float32).reshape(2, 4 * FINE, LANES)
        re_parts, im_parts = [], []
        for side in range(2):
            flipped = white[side].T
            for s in range(4):
                re_parts.append(natural(flipped, 0, s))
                im_parts.append(natural(flipped, LANES // 2, s))
        white_re, white_im = jnp.stack(re_parts), jnp.stack(im_parts)

        def pair_of(step, result):
            sides, norms = [], []
            for side in range(2):
                m = 2 * step + side
                h_re, h_im = bank[0, m], bank[1, m]
                norms.append(jnp.sum((h_re * h_re + h_im * h_im) * inverse_density, keepdims=True))
                c_re = h_re[None] * white_re + h_im[None] * white_im
                c_im = h_re[None] * white_im - h_im[None] * white_re
                both = jnp.concatenate([c_re, c_im], axis=0).reshape(2 * GROUP * ROWS, LANES)
                sides.append(both.astype(jnp.bfloat16))
            section = dot(third, jnp.concatenate(sides, axis=1))
            for side in range(2):
                re = section[:half, side * LANES:(side + 1) * LANES].reshape(GROUP, FINE, LANES)
                im = section[half:, side * LANES:(side + 1) * LANES].reshape(GROUP, FINE, LANES)
                turned = jnp.concatenate([re * inv_cos - im * inv_sin, re * inv_sin + im * inv_cos], axis=2)
                wave = dot(turned.reshape(half, 2 * LANES).astype(jnp.bfloat16), narrow[fourth])
                square = wave[:, :LANES] * wave[:, :LANES] + wave[:, LANES:] * wave[:, LANES:]
                top = jnp.max(jnp.max(square.reshape(GROUP, FINE, LANES), axis=1), axis=1, keepdims=True)
                value = jnp.sqrt(top) / (jnp.sqrt(norms[side]) * math.sqrt(energy))
                result = jnp.where(column == 2 * step + side, value, result)
            return result

        result = repeat(count // 2, pair_of, jnp.zeros((GROUP, LANES), jnp.float32))
        out[pl.ds(number * GROUP, GROUP)] = result[:, :count]
        return carry

    repeat(own // GROUP, block, 0)


def swap(array, axis, bits):
    return lax.ppermute(array, axis, [(i, i ^ bits) for i in range(lax.axis_size(axis))])


def on_device(strain, templates, cutoff):
    tm, devices = lax.axis_size("tm"), lax.axis_size("tm") * lax.axis_size("tmpl")
    size = strain.shape[0] // HOP
    segs = devices * size
    own = segs // tm
    count = templates.shape[1]
    smem = pl.BlockSpec(memory_space=pltpu.SMEM)
    vmem = pl.BlockSpec(memory_space=pltpu.VMEM)
    params = pltpu.CompilerParams(vmem_limit_bytes=40 * 1024 * 1024)
    f32 = jnp.float32

    copies, held = pl.pallas_call(
        pack_kernel,
        out_shape=(
            jax.ShapeDtypeStruct((devices, size * ROWS, LANES), f32),
            jax.ShapeDtypeStruct(templates.shape, templates.dtype),
        ),
        in_specs=[vmem, vmem],
        out_specs=(vmem, vmem),
        compiler_params=params,
        name="pack",
    )(strain.reshape(size * ROWS, LANES), templates)
    record = lax.all_to_all(copies, ("tm", "tmpl"), split_axis=0, concat_axis=0, tiled=True)
    record = record.reshape(segs, ROWS, LANES)
    blocks = [held] + [swap(held, "tm", other) for other in range(1, tm)]
    bank = pl.pallas_call(
        functools.partial(bank_kernel, tm),
        out_shape=jax.ShapeDtypeStruct((2, count, ROWS, LANES), f32),
        in_specs=[vmem] * tm + [smem],
        out_specs=vmem,
        scratch_shapes=[pltpu.VMEM((ROWS, count, 2 * LANES), jnp.bfloat16)],
        compiler_params=params,
        cost_estimate=pl.CostEstimate(flops=0, bytes_accessed=2500000, transcendentals=0),
        name="bank",
    )(*blocks, cutoff)
    narrow, broad, energy = tables()
    return pl.pallas_call(
        functools.partial(filter_kernel, energy),
        out_shape=jax.ShapeDtypeStruct((own, count), f32),
        in_specs=[vmem] * 4,
        out_specs=vmem,
        scratch_shapes=[pltpu.VMEM((segs * FINE, LANES), f32)],
        compiler_params=params,
        name="matched_filter",
    )(record, bank, jnp.asarray(narrow), jnp.asarray(broad))


def solution(mesh):
    in_specs = (P(("tm", "tmpl")), P(None, "tmpl", "tm"), P("tmpl"))
    out_specs = P("tm", "tmpl")
    return jax.shard_map(
        on_device, mesh=mesh, in_specs=in_specs, out_specs=out_specs, check_vma=False
    )
```

time: 33 us -> 24.3 us (0.74)
  blocking collectives: 10.1 us -> 0 us
  starting transfers between devices: 4.32 us -> 10.9 us
  waiting for transfers between devices: 10.4 us -> 6.05 us
  local copies, waits for them, and re-layouts: 3.06 us -> 1.47 us
  Pallas kernels: 4.67 us -> 5.62 us
    all_to_all x1 -> x0, blocking collectives: 10.1 us -> none  [on_device(): lax.all_to_all(jnp.broadcast_to(templates[None], (tm,) + templates.shape)...]
    all_to_all x1, waiting for transfers between devices: 10.4 us -> 2.3 us  [on_device(): lax.all_to_all(copies, ('tm', 'tmpl'), split_axis=0, concat_axis=0, tiled...]
    ppermute x0 -> x3, waiting for transfers between devices: none -> 3.75 us  [swap(): lax.ppermute(array, axis, [(i, i ^ bits) for i in range(lax.axis_size(axi...]
    ppermute x0 -> x3, starting transfers between devices: none -> 3.55 us  [swap(): lax.ppermute(array, axis, [(i, i ^ bits) for i in range(lax.axis_size(axi...]
    all_to_all x1, starting transfers between devices: 4.32 us -> 7.3 us  [on_device(): lax.all_to_all(copies, ('tm', 'tmpl'), split_axis=0, concat_axis=0, tiled...]
    broadcast_in_dim x2 -> x0, local copies, waits for them, and re-layouts: 2.26 us -> none  [the longest x1 1.46 us: on_device(): jnp.broadcast_to(chunk, (devices, ROWS, LANES))]
    pallas_call x1 -> x3, Pallas kernels: 4.67 us -> 5.62 us  [the longest x1 4.15 us: on_device(): pl.pallas_call(functools.partial(filter_kernel, energy), out_shape=jax.Sh...]
    unnamed x20 -> x10, local copies, waits for them, and re-layouts: 0.8 us -> 1.47 us
  transfers between devices with their start and end apart: 1 -> 4, of which waited for: 1 -> 4; matrix products, arithmetic and copies ran while one was open for 0% -> 0% of each run, Pallas kernels for 0% -> 3%
where the time goes in v4:
time: 24.3 us; the launch traced here: 24 us
  starting transfers between devices  10.9 us (45%)
  waiting for transfers between devices  6.05 us (25%)
  Pallas kernels  5.62 us (23%)
  local copies, waits for them, and re-layouts  1.47 us (6%)
    all_to_all x1, starting transfers between devices, on_device(): lax.all_to_all(copies, ('tm', 'tmpl'), split_axis=0, concat_axis=0, tiled...  7.3 us
    pallas_call x1, Pallas kernels, on_device(): pl.pallas_call(functools.partial(filter_kernel, energy), out_shape=jax.Sh...  4.15 us
    ppermute x3, waiting for transfers between devices, swap(): lax.ppermute(array, axis, [(i, i ^ bits) for i in range(lax.axis_size(axi...  3.75 us
    ppermute x3, starting transfers between devices, swap(): lax.ppermute(array, axis, [(i, i ^ bits) for i in range(lax.axis_size(axi...  3.55 us
    all_to_all x1, waiting for transfers between devices, on_device(): lax.all_to_all(copies, ('tm', 'tmpl'), split_axis=0, concat_axis=0, tiled...  2.3 us
    unnamed x10, local copies, waits for them, and re-layouts  1.47 us
    pallas_call x1, Pallas kernels, on_device(): pl.pallas_call(functools.partial(bank_kernel, tm), out_shape=jax.ShapeDty...  0.74 us
    pallas_call x1, Pallas kernels, on_device(): pl.pallas_call(pack_kernel, out_shape=(jax.ShapeDtypeStruct((devices, siz...  0.73 us
  transfers between devices with their start and end apart: 4, of which 4 were waited for; matrix products, arithmetic and copies ran while one was open for 0% of the time, Pallas kernels for 3%

profile of v4, /device:TPU:0, one launch (start us, length us, event | category | flops | bytes accessed | tf_op | source)
XLA Modules:
  0.0 24.0 jit_solution(13352127135861911723)
XLA Ops:
  0.0 0.0 copy-start.2
  0.0 0.8 %copy-done.2 = bf16[2,16,512]{2,1,0:T(8,128)(2,1)S(1)} copy-done((bf16[2,16,512]{2,1,0:T(8,128)(2,1)S(1)}, bf16[2,16,512]{2,1,0:T(8,128)(2,1)}, u32[]{:S(2)}) %copy-start.2) | copy-done | bytes 32792
  0.8 0.0 copy-start.3
  0.8 0.7 %copy-done.3 = f32[2048]{0:T(1024)S(1)} copy-done((f32[2048]{0:T(1024)S(1)}, f32[2048]{0:T(1024)}, u32[]{:S(2)}) %copy-start.3) | copy-done | bytes 8216
  1.5 0.7 %pack.1 = (f32[32,16,128]{2,1,0:T(8,128)}, bf16[2,16,512]{2,1,0:T(8,128)(2,1)S(1)}) custom-call(f32[16,128]{1,0:T(8,128)S(1)} %bitcast.1, bf16[2,16,512]{2,1,0:T(8,128)(2,1)S(1)} %copy-done.2), custom_call_target="tpu_custom_call" | custom-call | tf_op jit(solution)/shard_map/pack/pallas_call | solution.py:248
  2.2 0.0 copy-start
  2.2 7.3 %all-to-all-start = ((f32[32,16,128]{2,1,0:T(8,128)}), f32[32,16,128]{2,1,0:T(8,128)S(1)}, u32[]{:S(2)}, u32[]{:S(2)}) async-start(f32[32,16,128]{2,1,0:T(8,128)} %get-tuple-element.7), calls=%async_computation | async-start | bytes 524288 | tf_op jit(solution)/shard_map/all_to_all | solution.py:259
  9.5 0.0 copy-start.4
  9.5 0.0 copy-start.1
  9.5 2.7 %collective-permute-start.2 = (bf16[2,16,512]{2,1,0:T(8,128)(2,1)S(1)}, bf16[2,16,512]{2,1,0:T(8,128)(2,1)S(1)}, u32[]{:S(2)}, u32[]{:S(2)}) collective-permute-start(bf16[2,16,512]{2,1,0:T(8,128)(2,1)S(1)} %get-tuple-element.8.refs_0_), channel_id=1, source_target_pairs={{0,24},{8,16},{16,8},{24,0},{1,25},{9,17},{17,9},{25,1},{2,26},{10... | collective-permute-start | bytes 98312 | tf_op jit(solution)/shard_map/ppermute | solution.py:234
  12.3 0.6 %collective-permute-start.1 = (bf16[2,16,512]{2,1,0:T(8,128)(2,1)S(1)}, bf16[2,16,512]{2,1,0:T(8,128)(2,1)S(1)}, u32[]{:S(2)}, u32[]{:S(2)}) collective-permute-start(bf16[2,16,512]{2,1,0:T(8,128)(2,1)S(1)} %get-tuple-element.8.refs_0_), channel_id=1, source_target_pairs={{0,16},{8,24},{16,0},{24,8},{1,17},{9,25},{17,1},{25,9},{2,18},{10... | collective-permute-start | bytes 98312 | tf_op jit(solution)/shard_map/ppermute | solution.py:234
  12.8 0.3 %collective-permute-start = (bf16[2,16,512]{2,1,0:T(8,128)(2,1)S(1)}, bf16[2,16,512]{2,1,0:T(8,128)(2,1)S(1)}, u32[]{:S(2)}, u32[]{:S(2)}) collective-permute-start(bf16[2,16,512]{2,1,0:T(8,128)(2,1)S(1)} %get-tuple-element.8.refs_0_), channel_id=1, source_target_pairs={{0,8},{8,0},{16,24},{24,16},{1,9},{9,1},{17,25},{25,17},{2,10},{10... | collective-permute-start | bytes 98312 | tf_op jit(solution)/shard_map/ppermute | solution.py:234
  13.1 2.1 %collective-permute-done.2.refs_3_ = bf16[2,16,512]{2,1,0:T(8,128)(2,1)S(1)} collective-permute-done((bf16[2,16,512]{2,1,0:T(8,128)(2,1)S(1)}, bf16[2,16,512]{2,1,0:T(8,128)(2,1)S(1)}, u32[]{:S(2)}, u32[]{:S(2)}) %collective-permute-start.2) | collective-permute-done | bytes 32800 | tf_op jit(solution)/shard_map/ppermute | solution.py:234
  15.2 1.3 %collective-permute-done.1.refs_2_ = bf16[2,16,512]{2,1,0:T(8,128)(2,1)S(1)} collective-permute-done((bf16[2,16,512]{2,1,0:T(8,128)(2,1)S(1)}, bf16[2,16,512]{2,1,0:T(8,128)(2,1)S(1)}, u32[]{:S(2)}, u32[]{:S(2)}) %collective-permute-start.1) | collective-permute-done | bytes 32800 | tf_op jit(solution)/shard_map/ppermute | solution.py:234
  16.5 0.3 %collective-permute-done.refs_1_ = bf16[2,16,512]{2,1,0:T(8,128)(2,1)S(1)} collective-permute-done((bf16[2,16,512]{2,1,0:T(8,128)(2,1)S(1)}, bf16[2,16,512]{2,1,0:T(8,128)(2,1)S(1)}, u32[]{:S(2)}, u32[]{:S(2)}) %collective-permute-start) | collective-permute-done | bytes 32800 | tf_op jit(solution)/shard_map/ppermute | solution.py:234
  16.8 0.0 copy-done.4
  16.8 0.7 %bank.1 = f32[2,16,16,128]{3,2,1,0:T(8,128)S(1)} custom-call(bf16[2,16,512]{2,1,0:T(8,128)(2,1)S(1)} %get-tuple-element.8.refs_0_, bf16[2,16,512]{2,1,0:T(8,128)(2,1)S(1)} %collective-permute-done.refs_1_, bf16[2,16,512]{2,1,0:T(8,128)(2,1)S(1)} %collective-permute-done.1.refs_2_, bf16[2,16,512]{2,1,0:T(8,128)(2,1)S(1)} %collective-permute-done.2.refs_3_, ...), custom_call_target="tpu_custom_call" | custom-call | bytes 2500000 | tf_op jit(solution)/shard_map/bank/pallas_call | solution.py:262
  17.6 2.3 %all-to-all-done.record = f32[32,16,128]{2,1,0:T(8,128)S(1)} async-done(((f32[32,16,128]{2,1,0:T(8,128)}), f32[32,16,128]{2,1,0:T(8,128)S(1)}, u32[]{:S(2)}, u32[]{:S(2)}) %all-to-all-start) | async-done | bytes 262176 | tf_op jit(solution)/shard_map/all_to_all | solution.py:259
  19.9 0.0 copy-done
  19.9 0.0 copy-done.1
  19.9 4.2 %matched_filter.1 = f32[8,16]{1,0:T(8,128)} custom-call(f32[32,16,128]{2,1,0:T(8,128)S(1)} %all-to-all-done.record, f32[2,16,16,128]{3,2,1,0:T(8,128)S(1)} %bank.1, bf16[704,256]{1,0:T(8,128)(2,1)S(1)} %copy-done, f32[160,128]{1,0:T(8,128)S(1)} %copy-done.1), custom_call_target="tpu_custom_call" | custom-call | tf_op jit(solution)/shard_map/matched_filter/pallas_call | solution.py:273
Async XLA Ops:
  0.0 0.8 %copy-start.2 = (bf16[2,16,512]{2,1,0:T(8,128)(2,1)S(1)}, bf16[2,16,512]{2,1,0:T(8,128)(2,1)}, u32[]{:S(2)}) copy-start(bf16[2,16,512]{2,1,0:T(8,128)(2,1)} %templates.1) | copy-start | bytes 98308
  0.8 0.7 %copy-start.3 = (f32[2048]{0:T(1024)S(1)}, f32[2048]{0:T(1024)}, u32[]{:S(2)}) copy-start(f32[2048]{0:T(1024)} %param.5) | copy-start | bytes 24580
  2.2 17.7 %copy-start = (bf16[704,256]{1,0:T(8,128)(2,1)S(1)}, bf16[704,256]{1,0:T(8,128)(2,1)}, u32[]{:S(2)}) copy-start(bf16[704,256]{1,0:T(8,128)(2,1)} %constant.4.clone.narrow) | copy-start | bytes 1081348
  2.2 17.7 %all-to-all-start = ((f32[32,16,128]{2,1,0:T(8,128)}), f32[32,16,128]{2,1,0:T(8,128)S(1)}, u32[]{:S(2)}, u32[]{:S(2)}) async-start(f32[32,16,128]{2,1,0:T(8,128)} %get-tuple-element.7), calls=%async_computation | async-start | bytes 524288 | tf_op jit(solution)/shard_map/all_to_all | solution.py:259
  9.5 7.3 %copy-start.4 = (s32[16]{0:T(128)S(1)}, s32[16]{0:T(128)}, u32[]{:S(2)}) copy-start(s32[16]{0:T(128)} %refs_4_.1) | copy-start | bytes 196
  9.5 10.4 %copy-start.1 = (f32[160,128]{1,0:T(8,128)S(1)}, f32[160,128]{1,0:T(8,128)}, u32[]{:S(2)}) copy-start(f32[160,128]{1,0:T(8,128)} %constant.5.clone.broad) | copy-start | bytes 245764
  9.5 5.7 %collective-permute-start.2 = (bf16[2,16,512]{2,1,0:T(8,128)(2,1)S(1)}, bf16[2,16,512]{2,1,0:T(8,128)(2,1)S(1)}, u32[]{:S(2)}, u32[]{:S(2)}) collective-permute-start(bf16[2,16,512]{2,1,0:T(8,128)(2,1)S(1)} %get-tuple-element.8.refs_0_), channel_id=1, source_target_pairs={{0,24},{8,16},{16,8},{24,0},{1,25},{9,17},{17,9},{25,1},{2,26},{10... | collective-permute-start | bytes 98312 | tf_op jit(solution)/shard_map/ppermute | solution.py:234
  12.3 4.3 %collective-permute-start.1 = (bf16[2,16,512]{2,1,0:T(8,128)(2,1)S(1)}, bf16[2,16,512]{2,1,0:T(8,128)(2,1)S(1)}, u32[]{:S(2)}, u32[]{:S(2)}) collective-permute-start(bf16[2,16,512]{2,1,0:T(8,128)(2,1)S(1)} %get-tuple-element.8.refs_0_), channel_id=1, source_target_pairs={{0,16},{8,24},{16,0},{24,8},{1,17},{9,25},{17,1},{25,9},{2,18},{10... | collective-permute-start | bytes 98312 | tf_op jit(solution)/shard_map/ppermute | solution.py:234
  12.8 4.0 %collective-permute-start = (bf16[2,16,512]{2,1,0:T(8,128)(2,1)S(1)}, bf16[2,16,512]{2,1,0:T(8,128)(2,1)S(1)}, u32[]{:S(2)}, u32[]{:S(2)}) collective-permute-start(bf16[2,16,512]{2,1,0:T(8,128)(2,1)S(1)} %get-tuple-element.8.refs_0_), channel_id=1, source_target_pairs={{0,8},{8,0},{16,24},{24,16},{1,9},{9,1},{17,25},{25,17},{2,10},{10... | collective-permute-start | bytes 98312 | tf_op jit(solution)/shard_map/ppermute | solution.py:234

commit v5 on v4

--- a/solution.py
+++ b/solution.py
@@ -8,7 +8,7 @@
 from jax import lax
 from jax.experimental import pallas as pl
 from jax.experimental.pallas import tpu as pltpu
-from jax.sharding import PartitionSpec as P
+from jax.sharding import Mesh, PartitionSpec as P
 
 NFFT = 4096
 BINS = 2048
@@ -107,9 +107,12 @@
     return result
 
 
-def pack_kernel(strain, templates, copies, held):
-    held[...] = templates[...]
-    copies[...] = jnp.broadcast_to(strain[...][None], copies.shape)
+def pack_kernel(strain, copies, sems):
+    moves = [pltpu.make_async_copy(strain, copies.at[i], sems.at[i]) for i in range(copies.shape[0])]
+    for move in moves:
+        move.start()
+    for move in moves:
+        move.wait()
 
 
 def bank_kernel(devices, *refs):
@@ -137,8 +140,13 @@
         bank[1, m] = jnp.where(keep, value[rows, LANES:], 0.0)
 
 
-def filter_kernel(energy, record, bank, narrow, broad, out, spec):
-    segs = record.shape[0]
+def filter_kernel(energy, mine, others, bank, narrow, broad, out, spec, pairs):
+    core = lax.axis_index("core")
+    size = mine.shape[1]
+    segs = 2 * mine.shape[0] * (size // ROWS)
+    pairs[:, core] = mine[...]
+    pairs[:, 1 - core] = others[...]
+    record = pairs.reshape(segs, ROWS, LANES)
     own, count = out.shape
     half = GROUP * FINE
     w_low, w_high = broad[:ROWS][None], broad[ROWS:FINE][None]
@@ -235,30 +243,31 @@
 
 
 def on_device(strain, templates, cutoff):
-    tm, devices = lax.axis_size("tm"), lax.axis_size("tm") * lax.axis_size("tmpl")
+    tm, chips = lax.axis_size("tm"), lax.axis_size("tm") * lax.axis_size("chip")
     size = strain.shape[0] // HOP
-    segs = devices * size
+    segs = 2 * chips * size
     own = segs // tm
     count = templates.shape[1]
     smem = pl.BlockSpec(memory_space=pltpu.SMEM)
     vmem = pl.BlockSpec(memory_space=pltpu.VMEM)
+    anywhere = pl.BlockSpec(memory_space=pl.ANY)
     params = pltpu.CompilerParams(vmem_limit_bytes=40 * 1024 * 1024)
     f32 = jnp.float32
 
-    copies, held = pl.pallas_call(
+    copies = pl.pallas_call(
         pack_kernel,
-        out_shape=(
-            jax.ShapeDtypeStruct((devices, size * ROWS, LANES), f32),
-            jax.ShapeDtypeStruct(templates.shape, templates.dtype),
-        ),
-        in_specs=[vmem, vmem],
-        out_specs=(vmem, vmem),
-        compiler_params=params,
+        out_shape=jax.ShapeDtypeStruct((chips, size * ROWS, LANES), f32),
+        in_specs=[anywhere],
+        out_specs=anywhere,
+        scratch_shapes=[pltpu.SemaphoreType.DMA((chips,))],
         name="pack",
-    )(strain.reshape(size * ROWS, LANES), templates)
-    record = lax.all_to_all(copies, ("tm", "tmpl"), split_axis=0, concat_axis=0, tiled=True)
-    record = record.reshape(segs, ROWS, LANES)
-    blocks = [held] + [swap(held, "tm", other) for other in range(1, tm)]
+    )(strain.reshape(size * ROWS, LANES))
+    copies, templates = lax.optimization_barrier((copies, templates))
+    mine = lax.all_to_all(copies, ("tm", "chip"), split_axis=0, concat_axis=0, tiled=True)
+    blocks = [swap(templates, "tm", other) for other in range(1, tm)]
+    mine, *blocks = lax.optimization_barrier((mine, *blocks))
+    others = swap(mine, "core", 1)
+    blocks = [templates] + blocks
     bank = pl.pallas_call(
         functools.partial(bank_kernel, tm),
         out_shape=jax.ShapeDtypeStruct((2, count, ROWS, LANES), f32),
@@ -273,17 +282,23 @@
     return pl.pallas_call(
         functools.partial(filter_kernel, energy),
         out_shape=jax.ShapeDtypeStruct((own, count), f32),
-        in_specs=[vmem] * 4,
+        in_specs=[vmem] * 5,
         out_specs=vmem,
-        scratch_shapes=[pltpu.VMEM((segs * FINE, LANES), f32)],
+        scratch_shapes=[
+            pltpu.VMEM((segs * FINE, LANES), f32),
+            pltpu.VMEM((chips, 2, size * ROWS, LANES), f32),
+        ],
         compiler_params=params,
         name="matched_filter",
-    )(record, bank, jnp.asarray(narrow), jnp.asarray(broad))
+    )(mine, others, bank, jnp.asarray(narrow), jnp.asarray(broad))
 
 
 def solution(mesh):
-    in_specs = (P(("tm", "tmpl")), P(None, "tmpl", "tm"), P("tmpl"))
-    out_specs = P("tm", "tmpl")
+    tm, tmpl = mesh.devices.shape
+    split_mesh = Mesh(mesh.devices.reshape(tm, tmpl // 2, 2), ("tm", "chip", "core"))
+    bank = ("chip", "core")
+    in_specs = (P(("tm",) + bank), P(None, bank, "tm"), P(bank))
+    out_specs = P("tm", bank)
     return jax.shard_map(
-        on_device, mesh=mesh, in_specs=in_specs, out_specs=out_specs, check_vma=False
+        on_device, mesh=split_mesh, in_specs=in_specs, out_specs=out_specs, check_vma=False
     )

time: 24.3 us -> 27.8 us (1.14)
  Pallas kernels: 5.62 us -> 10.2 us
  local copies, waits for them, and re-layouts: 1.47 us -> 0.02 us
  starting transfers between devices: 10.9 us -> 12 us
  waiting for transfers between devices: 6.05 us -> 5.33 us
    pallas_call x1, Pallas kernels: 0.73 us -> 5.22 us  [on_device(): pl.pallas_call(pack_kernel, out_shape=jax.ShapeDtypeStruct((chips, size *...]
    all_to_all x1, waiting for transfers between devices: 2.3 us -> 0.01 us  [on_device(): lax.all_to_all(copies, ('tm', 'chip'), split_axis=0, concat_axis=0, tiled...]
    ppermute x3 -> x4, waiting for transfers between devices: 3.75 us -> 5.33 us  [swap(): lax.ppermute(array, axis, [(i, i ^ bits) for i in range(lax.axis_size(axi...]
    unnamed x10 -> x8, local copies, waits for them, and re-layouts: 1.47 us -> 0.02 us
    all_to_all x1, starting transfers between devices: 7.3 us -> 8.46 us  [on_device(): lax.all_to_all(copies, ('tm', 'chip'), split_axis=0, concat_axis=0, tiled...]
    ppermute x3 -> x4, starting transfers between devices: 3.55 us -> 3.56 us  [swap(): lax.ppermute(array, axis, [(i, i ^ bits) for i in range(lax.axis_size(axi...]
  transfers between devices with their start and end apart: 4 -> 5, of which waited for: 4 -> 4; matrix products, arithmetic and copies ran while one was open for 0% -> 0% of each run, Pallas kernels for 3% -> 3%
where the time goes in v5:
time: 27.8 us; the launch traced here: 27.6 us
  starting transfers between devices  12 us (43%)
  Pallas kernels  10.2 us (37%)
  waiting for transfers between devices  5.33 us (19%)
    all_to_all x1, starting transfers between devices, on_device(): lax.all_to_all(copies, ('tm', 'chip'), split_axis=0, concat_axis=0, tiled...  8.46 us
    ppermute x4, waiting for transfers between devices, swap(): lax.ppermute(array, axis, [(i, i ^ bits) for i in range(lax.axis_size(axi...  5.33 us
    pallas_call x1, Pallas kernels, on_device(): pl.pallas_call(pack_kernel, out_shape=jax.ShapeDtypeStruct((chips, size *...  5.22 us
    pallas_call x1, Pallas kernels, on_device(): pl.pallas_call(functools.partial(filter_kernel, energy), out_shape=jax.Sh...  4.22 us
    ppermute x4, starting transfers between devices, swap(): lax.ppermute(array, axis, [(i, i ^ bits) for i in range(lax.axis_size(axi...  3.56 us
    pallas_call x1, Pallas kernels, on_device(): pl.pallas_call(functools.partial(bank_kernel, tm), out_shape=jax.ShapeDty...  0.75 us
  transfers between devices with their start and end apart: 5, of which 4 were waited for; matrix products, arithmetic and copies ran while one was open for 0% of the time, Pallas kernels for 3%

profile of v5, /device:TPU:0, one launch (start us, length us, event | category | flops | bytes accessed | tf_op | source)
XLA Modules:
  0.0 27.6 jit_solution(11175957628843453241)
XLA Ops:
  0.0 0.0 copy-start.2
  0.0 0.0 copy-start.3
  0.0 5.2 %pack.1 = f32[16,16,128]{2,1,0:T(8,128)} custom-call(f32[16,128]{1,0:T(8,128)} %bitcast.1), custom_call_target="tpu_custom_call" | custom-call | tf_op jit(solution)/shard_map/pack/pallas_call | solution.py:257
  5.2 0.0 copy-start
  5.2 8.5 %all-to-all-start = ((f32[16,16,128]{2,1,0:T(8,128)}), f32[16,16,128]{2,1,0:T(8,128)S(1)}, u32[]{:S(2)}, u32[]{:S(2)}) async-start(f32[16,16,128]{2,1,0:T(8,128)} %pack.1), calls=%async_computation | async-start | bytes 262144 | tf_op jit(solution)/shard_map/all_to_all | solution.py:266
  13.7 0.0 copy-done.2
  13.7 0.0 copy-start.1
  13.7 2.0 %collective-permute-start = (bf16[2,16,512]{2,1,0:T(8,128)(2,1)S(1)}, bf16[2,16,512]{2,1,0:T(8,128)(2,1)S(1)}, u32[]{:S(2)}, u32[]{:S(2)}) collective-permute-start(bf16[2,16,512]{2,1,0:T(8,128)(2,1)S(1)} %copy-done.2), channel_id=1, source_target_pairs={{0,8},{8,0},{16,24},{24,16},{1,9},{9,1},{17,25},{25,17},{2,10},{10... | collective-permute-start | bytes 98312 | tf_op jit(solution)/shard_map/ppermute | solution.py:242
  15.7 1.5 %collective-permute-start.1 = (bf16[2,16,512]{2,1,0:T(8,128)(2,1)S(1)}, bf16[2,16,512]{2,1,0:T(8,128)(2,1)S(1)}, u32[]{:S(2)}, u32[]{:S(2)}) collective-permute-start(bf16[2,16,512]{2,1,0:T(8,128)(2,1)S(1)} %copy-done.2), channel_id=1, source_target_pairs={{0,16},{8,24},{16,0},{24,8},{1,17},{9,25},{17,1},{25,9},{2,18},{10... | collective-permute-start | bytes 98312 | tf_op jit(solution)/shard_map/ppermute | solution.py:242
  17.2 0.1 collective-permute-start.2
  17.3 0.6 %collective-permute-done.refs_1_ = bf16[2,16,512]{2,1,0:T(8,128)(2,1)S(1)} collective-permute-done((bf16[2,16,512]{2,1,0:T(8,128)(2,1)S(1)}, bf16[2,16,512]{2,1,0:T(8,128)(2,1)S(1)}, u32[]{:S(2)}, u32[]{:S(2)}) %collective-permute-start) | collective-permute-done | bytes 32800 | tf_op jit(solution)/shard_map/ppermute | solution.py:242
  17.9 2.3 %collective-permute-done.1.refs_2_ = bf16[2,16,512]{2,1,0:T(8,128)(2,1)S(1)} collective-permute-done((bf16[2,16,512]{2,1,0:T(8,128)(2,1)S(1)}, bf16[2,16,512]{2,1,0:T(8,128)(2,1)S(1)}, u32[]{:S(2)}, u32[]{:S(2)}) %collective-permute-start.1) | collective-permute-done | bytes 32800 | tf_op jit(solution)/shard_map/ppermute | solution.py:242
  20.2 1.8 %collective-permute-done.2.refs_3_ = bf16[2,16,512]{2,1,0:T(8,128)(2,1)S(1)} collective-permute-done((bf16[2,16,512]{2,1,0:T(8,128)(2,1)S(1)}, bf16[2,16,512]{2,1,0:T(8,128)(2,1)S(1)}, u32[]{:S(2)}, u32[]{:S(2)}) %collective-permute-start.2) | collective-permute-done | bytes 32800 | tf_op jit(solution)/shard_map/ppermute | solution.py:242
  22.0 0.0 all-to-all-done.mine
  22.0 0.0 collective-permute-start.3
  22.0 0.0 copy-done.3
  22.0 0.7 %bank.1 = f32[2,16,16,128]{3,2,1,0:T(8,128)S(1)} custom-call(bf16[2,16,512]{2,1,0:T(8,128)(2,1)S(1)} %copy-done.2, bf16[2,16,512]{2,1,0:T(8,128)(2,1)S(1)} %collective-permute-done.refs_1_, bf16[2,16,512]{2,1,0:T(8,128)(2,1)S(1)} %collective-permute-done.1.refs_2_, bf16[2,16,512]{2,1,0:T(8,128)(2,1)S(1)} %collective-permute-done.2.refs_3_, s32[16]{0:T(128)S(1)} %copy-done.3), custom_call_target="tpu_custom_call" | custom-call | bytes 2500000 | tf_op jit(solution)/shard_map/bank/pallas_call | solution.py:271
  22.8 0.6 %collective-permute-done.3.others = f32[16,16,128]{2,1,0:T(8,128)S(1)} collective-permute-done((f32[16,16,128]{2,1,0:T(8,128)S(1)}, f32[16,16,128]{2,1,0:T(8,128)S(1)}, u32[]{:S(2)}, u32[]{:S(2)}) %collective-permute-start.3) | collective-permute-done | bytes 131104 | tf_op jit(solution)/shard_map/ppermute | solution.py:242
  23.4 0.0 copy-done
  23.4 0.0 copy-done.1
  23.4 4.2 %matched_filter.1 = f32[8,16]{1,0:T(8,128)} custom-call(f32[16,16,128]{2,1,0:T(8,128)S(1)} %all-to-all-done.mine, f32[16,16,128]{2,1,0:T(8,128)S(1)} %collective-permute-done.3.others, f32[2,16,16,128]{3,2,1,0:T(8,128)S(1)} %bank.1, bf16[704,256]{1,0:T(8,128)(2,1)S(1)} %copy-done, f32[160,128]{1,0:T(8,128)S(1)} %copy-done.1), custom_call_target="tpu_custom_call" | custom-call | tf_op jit(solution)/shard_map/matched_filter/pallas_call | solution.py:282
Async XLA Ops:
  0.0 13.7 %copy-start.2 = (bf16[2,16,512]{2,1,0:T(8,128)(2,1)S(1)}, bf16[2,16,512]{2,1,0:T(8,128)(2,1)}, u32[]{:S(2)}) copy-start(bf16[2,16,512]{2,1,0:T(8,128)(2,1)} %refs_0_) | copy-start | bytes 98308
  0.0 22.0 %copy-start.3 = (s32[16]{0:T(128)S(1)}, s32[16]{0:T(128)}, u32[]{:S(2)}) copy-start(s32[16]{0:T(128)} %refs_4_.1) | copy-start | bytes 196
  5.2 18.2 %copy-start = (bf16[704,256]{1,0:T(8,128)(2,1)S(1)}, bf16[704,256]{1,0:T(8,128)(2,1)}, u32[]{:S(2)}) copy-start(bf16[704,256]{1,0:T(8,128)(2,1)} %constant.4.clone.narrow) | copy-start | bytes 1081348
  5.2 16.8 %all-to-all-start = ((f32[16,16,128]{2,1,0:T(8,128)}), f32[16,16,128]{2,1,0:T(8,128)S(1)}, u32[]{:S(2)}, u32[]{:S(2)}) async-start(f32[16,16,128]{2,1,0:T(8,128)} %pack.1), calls=%async_computation | async-start | bytes 262144 | tf_op jit(solution)/shard_map/all_to_all | solution.py:266
  13.7 9.7 %copy-start.1 = (f32[160,128]{1,0:T(8,128)S(1)}, f32[160,128]{1,0:T(8,128)}, u32[]{:S(2)}) copy-start(f32[160,128]{1,0:T(8,128)} %constant.5.clone.broad) | copy-start | bytes 245764
  13.7 4.2 %collective-permute-start = (bf16[2,16,512]{2,1,0:T(8,128)(2,1)S(1)}, bf16[2,16,512]{2,1,0:T(8,128)(2,1)S(1)}, u32[]{:S(2)}, u32[]{:S(2)}) collective-permute-start(bf16[2,16,512]{2,1,0:T(8,128)(2,1)S(1)} %copy-done.2), channel_id=1, source_target_pairs={{0,8},{8,0},{16,24},{24,16},{1,9},{9,1},{17,25},{25,17},{2,10},{10... | collective-permute-start | bytes 98312 | tf_op jit(solution)/shard_map/ppermute | solution.py:242
  15.7 4.5 %collective-permute-start.1 = (bf16[2,16,512]{2,1,0:T(8,128)(2,1)S(1)}, bf16[2,16,512]{2,1,0:T(8,128)(2,1)S(1)}, u32[]{:S(2)}, u32[]{:S(2)}) collective-permute-start(bf16[2,16,512]{2,1,0:T(8,128)(2,1)S(1)} %copy-done.2), channel_id=1, source_target_pairs={{0,16},{8,24},{16,0},{24,8},{1,17},{9,25},{17,1},{25,9},{2,18},{10... | collective-permute-start | bytes 98312 | tf_op jit(solution)/shard_map/ppermute | solution.py:242
  17.2 4.8 %collective-permute-start.2 = (bf16[2,16,512]{2,1,0:T(8,128)(2,1)S(1)}, bf16[2,16,512]{2,1,0:T(8,128)(2,1)S(1)}, u32[]{:S(2)}, u32[]{:S(2)}) collective-permute-start(bf16[2,16,512]{2,1,0:T(8,128)(2,1)S(1)} %copy-done.2), channel_id=1, source_target_pairs={{0,24},{8,16},{16,8},{24,0},{1,25},{9,17},{17,9},{25,1},{2,26},{10... | collective-permute-start | bytes 98312 | tf_op jit(solution)/shard_map/ppermute | solution.py:242
  22.0 1.3 %collective-permute-start.3 = (f32[16,16,128]{2,1,0:T(8,128)S(1)}, f32[16,16,128]{2,1,0:T(8,128)S(1)}, u32[]{:S(2)}, u32[]{:S(2)}) collective-permute-start(f32[16,16,128]{2,1,0:T(8,128)S(1)} %all-to-all-done.mine), channel_id=1, source_target_pairs={{0,1},{1,0},{2,3},{3,2},{4,5},{5,4},{6,7},{7,6},{8,9},{9,8},{10,11... | collective-permute-start | bytes 393224 | tf_op jit(solution)/shard_map/ppermute | solution.py:242

commit v6 on v3

v6 whole, which is shorter than its diff:
```python
import functools
import math

import jax
import jax.numpy as jnp
import ml_dtypes
import numpy as np
from jax import lax
from jax.experimental import pallas as pl
from jax.experimental.pallas import tpu as pltpu
from jax.sharding import PartitionSpec as P

NFFT = 4096
BINS = 2048
HOP = 2048
LANES = 128
ROWS = HOP // LANES
FINE = 32
GROUP = 8
FLOOR = 1e-6

ROOT_SCALE = {128: 1.66575, 64: 1.66575, 32: 1.6245, 16: 1.6245, 8: 1.6245}


def root_order(index, period):
    return period // math.gcd(int(index), period)


def row_scale(count, period):
    return np.array([ROOT_SCALE.get(root_order(i, period), 1.0) for i in range(count)])


def as_bf16(table):
    return np.asarray(table, np.float32).astype(ml_dtypes.bfloat16)


def two_parts(table):
    high = as_bf16(table)
    low = as_bf16(np.asarray(table, np.float64) - high.astype(np.float64))
    return high, low


def turn(left, right, period):
    angle = 2.0 * np.pi * (np.outer(left, right) % period) / period
    return np.cos(angle), np.sin(angle)


@functools.lru_cache(maxsize=None)
def tables():
    fine, wide, rows = np.arange(FINE), np.arange(LANES), np.arange(ROWS)
    window = 0.5 - 0.5 * np.cos(2.0 * np.pi * np.arange(NFFT) / NFFT)
    cos, sin = turn(fine, fine, FINE)
    first_high, first_low = two_parts(np.tile(np.concatenate([cos, -sin]), (1, GROUP)))
    fwd_cos, fwd_sin = turn(fine, wide, NFFT)
    f_order = np.array([4 * d + g for g in range(4) for d in range(ROWS)])
    cos, sin = turn(wide, f_order, LANES)
    second_high, second_low = two_parts(np.block([[cos, -sin], [sin, cos]]))
    scale_q, scale_c = row_scale(FINE, FINE), row_scale(LANES, LANES)
    cos, sin = turn(fine, rows, FINE)
    cos, sin = np.tile(cos * scale_q[:, None], (1, GROUP)), np.tile(sin * scale_q[:, None], (1, GROUP))
    third = np.block([[cos, -sin], [sin, cos]])
    inv_cos, inv_sin = turn(fine, wide, NFFT)
    undo = 1.0 / (scale_q[:, None] * scale_c[None, :])
    cos, sin = turn(wide, wide, LANES)
    cos, sin = cos * scale_c[:, None], sin * scale_c[:, None]
    fourth = np.block([[cos, sin], [-sin, cos]])
    narrow = np.concatenate(
        [first_high, first_low, as_bf16(third), np.concatenate([second_high, second_low], axis=1), as_bf16(fourth)]
    )
    broad = np.concatenate([window.reshape(FINE, LANES), fwd_cos, fwd_sin, inv_cos * undo, inv_sin * undo])
    return narrow, np.asarray(broad, np.float32), float((window * window).sum())


def dot(left, right):
    return jnp.dot(left, right, preferred_element_type=jnp.float32)


def split(value):
    high = value.astype(jnp.bfloat16)
    return high, (value - high.astype(jnp.float32)).astype(jnp.bfloat16)


def repeat(count, body, carry):
    if count <= 8:
        for step in range(count):
            carry = body(step, carry)
        return carry
    return lax.fori_loop(0, count, body, carry)


def block_diagonal(rows, width):
    lane = lax.broadcasted_iota(jnp.int32, rows.shape, 1)
    owner = lax.rem(lane // width, GROUP)
    return jnp.concatenate(
        [jnp.where(owner == s, rows, jnp.zeros_like(rows)) for s in range(GROUP)], axis=0
    )


def natural(flipped, at, source):
    part = lax.broadcasted_iota(jnp.int32, (ROWS, LANES), 1) // FINE
    result = None
    for g in range(4):
        piece = flipped[at + g * ROWS:at + (g + 1) * ROWS]
        if source is not None and g != source:
            piece = pltpu.roll(piece, ((g - source) % 4) * FINE, 1)
        result = piece if g == 0 else jnp.where(part == g, piece, result)
    return result


def spread(part, width):
    return jnp.concatenate([block_diagonal(part[:FINE], width), block_diagonal(part[FINE:], width)])


def halved(part):
    lane = lax.broadcasted_iota(jnp.int32, (FINE, part.shape[1]), 1)
    rows = []
    for at in (0, FINE):
        table = part[at:at + FINE]
        zero = jnp.zeros_like(table)
        for s in range(GROUP + 1):
            low = min(s, GROUP - 1) * FINE + (ROWS if s == GROUP else 0)
            high = min(s, GROUP - 1) * FINE + (ROWS if s == GROUP - 1 else FINE)
            rows.append(jnp.where((lane >= low) & (lane < high), table, zero))
    return jnp.concatenate(rows)


def prepare_kernel(strain, templates, narrow, chunk, block, first, third):
    chunk[...] = strain[...]
    block[...] = templates[...]
    first[0] = halved(narrow[:2 * FINE])
    first[1] = halved(narrow[2 * FINE:4 * FINE])
    third[...] = spread(narrow[4 * FINE:6 * FINE], ROWS)


def bank_kernel(blocks, cutoff, bank, gathered):
    rank = lax.axis_index("tm")
    devices, _, count, width = blocks.shape
    for other in range(devices):
        first = (rank ^ other) * (width // LANES)
        for at in range(width // LANES):
            lanes = slice(at * LANES, (at + 1) * LANES)
            gathered[first + at] = jnp.concatenate([blocks[other, 0, :, lanes], blocks[other, 1, :, lanes]], axis=1)
    lane = lax.broadcasted_iota(jnp.int32, (ROWS, LANES), 1)
    row = lax.broadcasted_iota(jnp.int32, (ROWS, LANES), 0)
    bins = row * LANES + lane
    shape = (count * ROWS, count * ROWS)
    to, source = lax.broadcasted_iota(jnp.int32, shape, 0), lax.broadcasted_iota(jnp.int32, shape, 1)
    order = (source == (to % ROWS) * count + to // ROWS).astype(jnp.float32).astype(jnp.bfloat16)
    value = dot(order, gathered[...].reshape(ROWS * count, 2 * LANES))
    for m in range(count):
        keep = bins < cutoff[m]
        rows = slice(m * ROWS, (m + 1) * ROWS)
        bank[0, m] = jnp.where(keep, value[rows, :LANES], 0.0)
        bank[1, m] = jnp.where(keep, value[rows, LANES:], 0.0)


def forward_kernel(offsets, chunks, first, narrow, broad, spec, sent, record):
    rank = lax.axis_index("tmpl")
    size = chunks.shape[0] // len(offsets)
    for at, offset in enumerate(offsets):
        record[pl.ds((rank ^ offset) * size, size)] = chunks[at * size:(at + 1) * size]
    own = record.shape[0]
    w_low, w_high = broad[:ROWS][None], broad[ROWS:FINE][None]
    fwd_cos, fwd_sin = broad[FINE:2 * FINE][None], broad[2 * FINE:3 * FINE][None]
    second = slice(6 * FINE, 6 * FINE + 2 * LANES)
    parts = GROUP + 1

    def group(start, power, last):
        here = record[pl.ds(start, GROUP)]
        if last:
            after = jnp.concatenate([record[pl.ds(start + 1, GROUP - 1)], record[pl.ds(0, 1)]], axis=0)
        else:
            after = record[pl.ds(start + 1, GROUP)]
        both = jnp.concatenate([here * w_low, after * w_high], axis=1)
        high, low = split(both.reshape(GROUP * FINE, LANES))
        step = dot(first[0], high) + dot(first[0], low) + dot(first[1], high)
        re = step[:parts * FINE].reshape(parts, FINE, LANES)
        im = step[parts * FINE:].reshape(parts, FINE, LANES)
        turned = jnp.concatenate([re * fwd_cos + im * fwd_sin, im * fwd_cos - re * fwd_sin], axis=2)
        high, low = split(turned.reshape(parts * FINE, 2 * LANES))
        wide = dot(high, narrow[second])
        value = wide[:, :LANES] + wide[:, LANES:] + dot(low, narrow[second, :LANES])
        value = jnp.concatenate([value, jnp.zeros((3 * FINE, LANES), jnp.float32)], axis=0)
        flipped = [value[i * LANES:(i + 1) * LANES].T for i in range(3)]
        pairs = [
            (natural(flipped[s // 4], 0, s % 4), natural(flipped[s // 4], LANES // 2, s % 4)) for s in range(parts)
        ]
        if last:
            sent[1], sent[2] = pairs[GROUP - 1]
            sent[3], sent[4] = pairs[GROUP]
        else:
            pairs[GROUP - 1] = tuple(a + b for a, b in zip(pairs[GROUP - 1], pairs[GROUP]))
        for s in range(GROUP):
            spec[0, pl.ds(start + s, 1)] = pairs[s][0][None]
            spec[1, pl.ds(start + s, 1)] = pairs[s][1][None]
            if s < GROUP - 1 or not last:
                power = power + pairs[s][0] * pairs[s][0] + pairs[s][1] * pairs[s][1]
        return power

    power = jnp.zeros((ROWS, LANES), jnp.float32)
    power = repeat(own // GROUP - 1, lambda i, p: group(i * GROUP, p, False), power)
    sent[0] = group(own - GROUP, power, True)


def filter_kernel(devices, segs, energy, *refs):
    shares = refs[:devices]
    spec, bank, third, narrow, broad, out, held = refs[devices:]
    own, count = out.shape
    half = GROUP * FINE
    inv_cos, inv_sin = broad[3 * FINE:4 * FINE][None], broad[4 * FINE:5 * FINE][None]
    fourth = slice(6 * FINE + 2 * LANES, 6 * FINE + 4 * LANES)
    rank = lax.axis_index("tm")
    power = shares[0][0]
    for share in shares[1:]:
        power = power + share[0]
    for other, share in enumerate(shares):
        held[rank ^ other] = share[3:5]
    for other, share in enumerate(shares):
        after = held[lax.rem((rank ^ other) + 1, devices)]
        re, im = share[1] + after[0], share[2] + after[1]
        power = power + re * re + im * im
        if other == 0:
            last_re, last_im = re, im
    density = power / (segs * energy) + FLOOR
    inverse_density = 1.0 / density
    column = lax.broadcasted_iota(jnp.int32, (GROUP, LANES), 1)

    def whiten(value):
        return (value / density[None]).astype(jnp.bfloat16).astype(jnp.float32)

    def block(start, last):
        x_re, x_im = spec[0, pl.ds(start, GROUP)], spec[1, pl.ds(start, GROUP)]
        if last:
            x_re = jnp.concatenate([x_re[:GROUP - 1], last_re[None]], axis=0)
            x_im = jnp.concatenate([x_im[:GROUP - 1], last_im[None]], axis=0)
        white_re, white_im = whiten(x_re), whiten(x_im)

        def pair_of(step, result):
            sides, norms = [], []
            for side in range(2):
                m = 2 * step + side
                h_re, h_im = bank[0, m], bank[1, m]
                norms.append(jnp.sum((h_re * h_re + h_im * h_im) * inverse_density, keepdims=True))
                c_re = h_re[None] * white_re + h_im[None] * white_im
                c_im = h_re[None] * white_im - h_im[None] * white_re
                both = jnp.concatenate([c_re, c_im], axis=0).reshape(2 * GROUP * ROWS, LANES)
                sides.append(both.astype(jnp.bfloat16))
            section = dot(third[...], jnp.concatenate(sides, axis=1))
            for side in range(2):
                re = section[:half, side * LANES:(side + 1) * LANES].reshape(GROUP, FINE, LANES)
                im = section[half:, side * LANES:(side + 1) * LANES].reshape(GROUP, FINE, LANES)
                turned = jnp.concatenate([re * inv_cos - im * inv_sin, re * inv_sin + im * inv_cos], axis=2)
                wave = dot(turned.reshape(half, 2 * LANES).astype(jnp.bfloat16), narrow[fourth])
                square = wave[:, :LANES] * wave[:, :LANES] + wave[:, LANES:] * wave[:, LANES:]
                top = jnp.max(jnp.max(square.reshape(GROUP, FINE, LANES), axis=1), axis=1, keepdims=True)
                value = jnp.sqrt(top) / (jnp.sqrt(norms[side]) * math.sqrt(energy))
                result = jnp.where(column == 2 * step + side, value, result)
            return result

        result = repeat(count // 2, pair_of, jnp.zeros((GROUP, LANES), jnp.float32))
        out[pl.ds(start, GROUP)] = result[:, :count]

    def earlier(number, carry):
        block(pl.multiple_of(number * GROUP, GROUP), False)
        return carry

    repeat(own // GROUP - 1, earlier, 0)
    block(own - GROUP, True)


def swap(array, axis, bits):
    return lax.ppermute(array, axis, [(i, i ^ bits) for i in range(lax.axis_size(axis))])


def on_device(strain, templates, cutoff):
    tm, tmpl = lax.axis_size("tm"), lax.axis_size("tmpl")
    size = strain.shape[0] // HOP
    own = size * tmpl
    count = templates.shape[1]
    smem = pl.BlockSpec(memory_space=pltpu.SMEM)
    vmem = pl.BlockSpec(memory_space=pltpu.VMEM)
    params = pltpu.CompilerParams(vmem_limit_bytes=40 * 1024 * 1024)
    f32, bf16 = jnp.float32, jnp.bfloat16
    narrow, broad, energy = tables()
    narrow, broad = jnp.asarray(narrow), jnp.asarray(broad)

    chunk = strain.reshape(size, ROWS, LANES)
    block = templates[None]
    bits = tmpl // 2
    arrived = swap(chunk, "tmpl", bits)
    chunk, block, first, third = pl.pallas_call(
        prepare_kernel,
        out_shape=(
            jax.ShapeDtypeStruct(chunk.shape, f32),
            jax.ShapeDtypeStruct(block.shape, bf16),
            jax.ShapeDtypeStruct((2, 2 * (GROUP + 1) * FINE, GROUP * FINE), bf16),
            jax.ShapeDtypeStruct((2 * GROUP * FINE, 2 * GROUP * ROWS), bf16),
        ),
        in_specs=[vmem] * 3,
        out_specs=(vmem,) * 4,
        compiler_params=params,
        cost_estimate=pl.CostEstimate(flops=0, bytes_accessed=3000000, transcendentals=0),
        name="prepare",
    )(chunk, block, narrow)
    chunks, offsets = jnp.concatenate([chunk, arrived], axis=0), [0, bits]
    while bits > 1:
        bits //= 2
        chunks = jnp.concatenate([chunks, swap(chunks, "tmpl", bits)], axis=0)
        offsets = offsets + [o ^ bits for o in offsets]
    bits = 1
    while bits < tm:
        block = jnp.concatenate([block, swap(block, "tm", bits)], axis=0)
        bits *= 2

    spec, sent = pl.pallas_call(
        functools.partial(forward_kernel, tuple(offsets)),
        out_shape=(
            jax.ShapeDtypeStruct((2, own, ROWS, LANES), f32),
            jax.ShapeDtypeStruct((5, ROWS, LANES), f32),
        ),
        in_specs=[vmem] * 4,
        out_specs=(vmem, vmem),
        scratch_shapes=[pltpu.VMEM((own, ROWS, LANES), f32)],
        compiler_params=params,
        name="forward",
    )(chunks, first, narrow, broad)
    shares = [sent] + [swap(sent, "tm", other) for other in range(1, tm)]
    bank = pl.pallas_call(
        bank_kernel,
        out_shape=jax.ShapeDtypeStruct((2, count, ROWS, LANES), f32),
        in_specs=[vmem, smem],
        out_specs=vmem,
        scratch_shapes=[pltpu.VMEM((ROWS, count, 2 * LANES), bf16)],
        compiler_params=params,
        cost_estimate=pl.CostEstimate(flops=0, bytes_accessed=2500000, transcendentals=0),
        name="bank",
    )(block, cutoff)
    return pl.pallas_call(
        functools.partial(filter_kernel, tm, own * tm, energy),
        out_shape=jax.ShapeDtypeStruct((own, count), f32),
        in_specs=[vmem] * (tm + 5),
        out_specs=vmem,
        scratch_shapes=[pltpu.VMEM((tm, 2, ROWS, LANES), f32)],
        compiler_params=params,
        name="matched_filter",
    )(*shares, spec, bank, third, narrow, broad)


def solution(mesh):
    in_specs = (P(("tm", "tmpl")), P(None, "tmpl", "tm"), P("tmpl"))
    out_specs = P("tm", "tmpl")
    return jax.shard_map(
        on_device, mesh=mesh, in_specs=in_specs, out_specs=out_specs, check_vma=False
    )
```

time: 32.9 us -> 24.3 us (0.74)
  local copies, waits for them, and re-layouts: 5.6 us -> 2.45 us
  waiting for transfers between devices: 7.1 us -> 5.1 us
  other arithmetic: 1.41 us -> 0.04 us
  starting transfers between devices: 13.4 us -> 12.3 us
  Pallas kernels: 4.85 us -> 4.04 us
    unnamed x24 -> x12, local copies, waits for them, and re-layouts: 5.6 us -> 2.45 us
    ppermute x9 -> x8, waiting for transfers between devices: 7.1 us -> 5.1 us  [swap(): lax.ppermute(array, axis, [(i, i ^ bits) for i in range(lax.axis_size(axi...]
    concatenate x3 -> x5, other arithmetic: 1.41 us -> 0.04 us  [the longest x2 0.02 us: on_device(): block = jnp.concatenate([block, swap(block, 'tm', bits)], axis=0)]
    ppermute x9 -> x8, starting transfers between devices: 13.4 us -> 12.3 us  [swap(): lax.ppermute(array, axis, [(i, i ^ bits) for i in range(lax.axis_size(axi...]
    pallas_call x3, Pallas kernels: 2.54 us -> 1.71 us  [the longest x1 0.9 us: on_device(): pl.pallas_call(functools.partial(forward_kernel, tuple(offsets)), out_sha...]
  transfers between devices with their start and end apart: 9 -> 8, of which waited for: 4 -> 5; matrix products, arithmetic and copies ran while one was open for 0% -> 0% of each run, Pallas kernels for 8% -> 7%
where the time goes in v6:
time: 24.3 us; the launch traced here: 24 us
  starting transfers between devices  12.3 us (51%)
  waiting for transfers between devices  5.1 us (21%)
  Pallas kernels  4.04 us (17%)
  local copies, waits for them, and re-layouts  2.45 us (10%)
    ppermute x8, starting transfers between devices, swap(): lax.ppermute(array, axis, [(i, i ^ bits) for i in range(lax.axis_size(axi...  12.3 us
    ppermute x8, waiting for transfers between devices, swap(): lax.ppermute(array, axis, [(i, i ^ bits) for i in range(lax.axis_size(axi...  5.1 us
    unnamed x12, local copies, waits for them, and re-layouts  2.45 us
    pallas_call x1, Pallas kernels, on_device(): pl.pallas_call(functools.partial(filter_kernel, tm, own * tm, energy), ou...  2.33 us
    pallas_call x1, Pallas kernels, on_device(): pl.pallas_call(functools.partial(forward_kernel, tuple(offsets)), out_sha...  0.9 us
    pallas_call x1, Pallas kernels, on_device(): pl.pallas_call(bank_kernel, out_shape=jax.ShapeDtypeStruct((2, count, ROW...  0.75 us
  transfers between devices with their start and end apart: 8, of which 5 were waited for; matrix products, arithmetic and copies ran while one was open for 0% of the time, Pallas kernels for 7%

profile of v6, /device:TPU:0, one launch (start us, length us, event | category | flops | bytes accessed | tf_op | source)
XLA Modules:
  0.0 24.0 jit_solution(14876969758830846847)
XLA Ops:
  0.0 4.0 %collective-permute-start = (f32[1,16,128]{2,1,0:T(8,128)}, f32[1,16,128]{2,1,0:T(8,128)S(1)}, u32[]{:S(2)}, u32[]{:S(2)}) collective-permute-start(f32[1,16,128]{2,1,0:T(8,128)} %bitcast.3), channel_id=1, source_target_pairs={{0,4},{1,5},{2,6},{3,7},{4,0},{5,1},{6,2},{7,3},{8,12},{9,13},{10,... | collective-permute-start | bytes 24584 | tf_op jit(solution)/shard_map/ppermute | solution.py:272
  4.0 0.0 copy-start
  4.0 1.0 %copy-done = bf16[704,256]{1,0:T(8,128)(2,1)S(1)} copy-done((bf16[704,256]{1,0:T(8,128)(2,1)S(1)}, bf16[704,256]{1,0:T(8,128)(2,1)}, u32[]{:S(2)}) %copy-start) | copy-done | bytes 360472
  5.0 0.0 copy-start.3
  5.0 0.8 %copy-done.3 = bf16[2,16,512]{2,1,0:T(8,128)(2,1)S(1)} copy-done((bf16[2,16,512]{2,1,0:T(8,128)(2,1)S(1)}, bf16[2,16,512]{2,1,0:T(8,128)(2,1)}, u32[]{:S(2)}) %copy-start.3) | copy-done | bytes 32792
  5.8 0.0 copy-start.4
  5.8 0.7 %copy-done.4 = f32[2048]{0:T(1024)S(1)} copy-done((f32[2048]{0:T(1024)S(1)}, f32[2048]{0:T(1024)}, u32[]{:S(2)}) %copy-start.4) | copy-done | bytes 8216
  6.5 0.0 copy-start.1
  6.5 0.1 prepare.1
  6.5 0.0 collective-permute-done
  6.6 1.6 %collective-permute-start.1 = (f32[2,16,128]{2,1,0:T(8,128)S(1)}, f32[2,16,128]{2,1,0:T(8,128)S(1)}, u32[]{:S(2)}, u32[]{:S(2)}) collective-permute-start(f32[2,16,128]{2,1,0:T(8,128)S(1)} %pad_maximum_fusion.4), channel_id=1, source_target_pairs={{0,2},{1,3},{2,0},{3,1},{4,6},{5,7},{6,4},{7,5},{8,10},{9,11},{10,... | collective-permute-start | bytes 49160 | tf_op jit(solution)/shard_map/ppermute | solution.py:272
  8.2 1.5 %collective-permute-start.6 = (bf16[1,2,16,512]{3,2,1,0:T(8,128)(2,1)S(1)}, bf16[1,2,16,512]{3,2,1,0:T(8,128)(2,1)S(1)}, u32[]{:S(2)}, u32[]{:S(2)}) collective-permute-start(bf16[1,2,16,512]{3,2,1,0:T(8,128)(2,1)S(1)} %get-tuple-element.15), channel_id=1, source_target_pairs={{0,8},{8,0},{16,24},{24,16},{1,9},{9,1},{17,25},{25,17},{2,10},{10... | collective-permute-start | bytes 98312 | tf_op jit(solution)/shard_map/ppermute | solution.py:272
  9.7 0.7 %collective-permute-done.1 = f32[2,16,128]{2,1,0:T(8,128)S(1)} collective-permute-done((f32[2,16,128]{2,1,0:T(8,128)S(1)}, f32[2,16,128]{2,1,0:T(8,128)S(1)}, u32[]{:S(2)}, u32[]{:S(2)}) %collective-permute-start.1) | collective-permute-done | bytes 16416 | tf_op jit(solution)/shard_map/ppermute | solution.py:272
  10.4 0.0 collective-permute-start.2
  10.4 1.7 %collective-permute-done.6 = bf16[1,2,16,512]{3,2,1,0:T(8,128)(2,1)S(1)} collective-permute-done((bf16[1,2,16,512]{3,2,1,0:T(8,128)(2,1)S(1)}, bf16[1,2,16,512]{3,2,1,0:T(8,128)(2,1)S(1)}, u32[]{:S(2)}, u32[]{:S(2)}) %collective-permute-start.6) | collective-permute-done | bytes 32800 | tf_op jit(solution)/shard_map/ppermute | solution.py:272
  12.1 0.0 copy-start.2
  12.2 1.6 %collective-permute-start.7 = (bf16[2,2,16,512]{3,2,1,0:T(8,128)(2,1)S(1)}, bf16[2,2,16,512]{3,2,1,0:T(8,128)(2,1)S(1)}, u32[]{:S(2)}, u32[]{:S(2)}) collective-permute-start(bf16[2,2,16,512]{3,2,1,0:T(8,128)(2,1)S(1)} %pad_maximum_fusion.2), channel_id=1, source_target_pairs={{0,16},{8,24},{16,0},{24,8},{1,17},{9,25},{17,1},{25,9},{2,18},{10... | collective-permute-start | bytes 196616 | tf_op jit(solution)/shard_map/ppermute | solution.py:272
  13.7 0.0 collective-permute-done.2
  13.7 0.0 copy-done.1
  13.8 0.0 copy-done.2
  13.8 0.9 %forward.1 = (f32[2,8,16,128]{3,2,1,0:T(8,128)S(1)}, f32[5,16,128]{2,1,0:T(8,128)S(1)}) custom-call(f32[8,16,128]{2,1,0:T(8,128)S(1)} %pad_maximum_fusion.1.chunks, bf16[2,576,256]{2,1,0:T(8,128)(2,1)S(1)} %get-tuple-element.12.first, bf16[704,256]{1,0:T(8,128)(2,1)S(1)} %copy-done.1, f32[160,128]{1,0:T(8,128)S(1)} %copy-done.2), custom_call_target="tpu_custom_call" | custom-call | tf_op jit(solution)/shard_map/forward/pallas_call | solution.py:315
  14.7 0.0 copy-start.5
  14.7 1.8 %collective-permute-start.5 = (f32[5,16,128]{2,1,0:T(8,128)S(1)}, f32[5,16,128]{2,1,0:T(8,128)S(1)}, u32[]{:S(2)}, u32[]{:S(2)}) collective-permute-start(f32[5,16,128]{2,1,0:T(8,128)S(1)} %get-tuple-element.13.refs_0_), channel_id=1, source_target_pairs={{0,24},{8,16},{16,8},{24,0},{1,25},{9,17},{17,9},{25,1},{2,26},{10... | collective-permute-start | bytes 122888 | tf_op jit(solution)/shard_map/ppermute | solution.py:272
  16.5 1.3 %collective-permute-start.4 = (f32[5,16,128]{2,1,0:T(8,128)S(1)}, f32[5,16,128]{2,1,0:T(8,128)S(1)}, u32[]{:S(2)}, u32[]{:S(2)}) collective-permute-start(f32[5,16,128]{2,1,0:T(8,128)S(1)} %get-tuple-element.13.refs_0_), channel_id=1, source_target_pairs={{0,16},{8,24},{16,0},{24,8},{1,17},{9,25},{17,1},{25,9},{2,18},{10... | collective-permute-start | bytes 122888 | tf_op jit(solution)/shard_map/ppermute | solution.py:272
  17.7 0.5 %collective-permute-start.3 = (f32[5,16,128]{2,1,0:T(8,128)S(1)}, f32[5,16,128]{2,1,0:T(8,128)S(1)}, u32[]{:S(2)}, u32[]{:S(2)}) collective-permute-start(f32[5,16,128]{2,1,0:T(8,128)S(1)} %get-tuple-element.13.refs_0_), channel_id=1, source_target_pairs={{0,8},{8,0},{16,24},{24,16},{1,9},{9,1},{17,25},{25,17},{2,10},{10... | collective-permute-start | bytes 122888 | tf_op jit(solution)/shard_map/ppermute | solution.py:272
  18.2 0.0 collective-permute-done.7
  18.3 0.0 copy-done.5
  18.3 0.7 %bank.1.refs_5_ = f32[2,16,16,128]{3,2,1,0:T(8,128)S(1)} custom-call(bf16[4,2,16,512]{3,2,1,0:T(8,128)(2,1)S(1)} %pad_maximum_fusion.blocks, s32[16]{0:T(128)S(1)} %copy-done.5), custom_call_target="tpu_custom_call" | custom-call | bytes 2500000 | tf_op jit(solution)/shard_map/bank/pallas_call | solution.py:328
  19.0 0.6 %collective-permute-done.5.refs_3_ = f32[5,16,128]{2,1,0:T(8,128)S(1)} collective-permute-done((f32[5,16,128]{2,1,0:T(8,128)S(1)}, f32[5,16,128]{2,1,0:T(8,128)S(1)}, u32[]{:S(2)}, u32[]{:S(2)}) %collective-permute-start.5) | collective-permute-done | bytes 40992 | tf_op jit(solution)/shard_map/ppermute | solution.py:272
  19.7 0.8 %collective-permute-done.4.refs_2_ = f32[5,16,128]{2,1,0:T(8,128)S(1)} collective-permute-done((f32[5,16,128]{2,1,0:T(8,128)S(1)}, f32[5,16,128]{2,1,0:T(8,128)S(1)}, u32[]{:S(2)}, u32[]{:S(2)}) %collective-permute-start.4) | collective-permute-done | bytes 40992 | tf_op jit(solution)/shard_map/ppermute | solution.py:272
  20.5 1.3 %collective-permute-done.3.refs_1_ = f32[5,16,128]{2,1,0:T(8,128)S(1)} collective-permute-done((f32[5,16,128]{2,1,0:T(8,128)S(1)}, f32[5,16,128]{2,1,0:T(8,128)S(1)}, u32[]{:S(2)}, u32[]{:S(2)}) %collective-permute-start.3) | collective-permute-done | bytes 40992 | tf_op jit(solution)/shard_map/ppermute | solution.py:272
  21.7 2.3 %matched_filter.1 = f32[8,16]{1,0:T(8,128)} custom-call(f32[5,16,128]{2,1,0:T(8,128)S(1)} %get-tuple-element.13.refs_0_, f32[5,16,128]{2,1,0:T(8,128)S(1)} %collective-permute-done.3.refs_1_, f32[5,16,128]{2,1,0:T(8,128)S(1)} %collective-permute-done.4.refs_2_, f32[5,16,128]{2,1,0:T(8,128)S(1)} %collective-permute-done.5.refs_3_, ...), custom_call_target="tpu_custom_call" | custom-call | tf_op jit(solution)/shard_map/matched_filter/pallas_call | solution.py:338
  (5 shorter events, 0.0 us)
Async XLA Ops:
  0.0 6.6 %collective-permute-start = (f32[1,16,128]{2,1,0:T(8,128)}, f32[1,16,128]{2,1,0:T(8,128)S(1)}, u32[]{:S(2)}, u32[]{:S(2)}) collective-permute-start(f32[1,16,128]{2,1,0:T(8,128)} %bitcast.3), channel_id=1, source_target_pairs={{0,4},{1,5},{2,6},{3,7},{4,0},{5,1},{6,2},{7,3},{8,12},{9,13},{10,... | collective-permute-start | bytes 24584 | tf_op jit(solution)/shard_map/ppermute | solution.py:272
  4.0 1.0 %copy-start = (bf16[704,256]{1,0:T(8,128)(2,1)S(1)}, bf16[704,256]{1,0:T(8,128)(2,1)}, u32[]{:S(2)}) copy-start(bf16[704,256]{1,0:T(8,128)(2,1)} %constant.4.clone.narrow.refs_7_) | copy-start | bytes 1081348
  5.0 0.8 %copy-start.3 = (bf16[2,16,512]{2,1,0:T(8,128)(2,1)S(1)}, bf16[2,16,512]{2,1,0:T(8,128)(2,1)}, u32[]{:S(2)}) copy-start(bf16[2,16,512]{2,1,0:T(8,128)(2,1)} %param.6) | copy-start | bytes 98308
  5.8 0.7 %copy-start.4 = (f32[2048]{0:T(1024)S(1)}, f32[2048]{0:T(1024)}, u32[]{:S(2)}) copy-start(f32[2048]{0:T(1024)} %param.5) | copy-start | bytes 24580
  6.5 7.3 %copy-start.1 = (bf16[704,256]{1,0:T(8,128)(2,1)S(1)}, bf16[704,256]{1,0:T(8,128)(2,1)}, u32[]{:S(2)}) copy-start(bf16[704,256]{1,0:T(8,128)(2,1)} %constant.4.clone.narrow.refs_7_) | copy-start | bytes 1081348
  6.6 3.8 %collective-permute-start.1 = (f32[2,16,128]{2,1,0:T(8,128)S(1)}, f32[2,16,128]{2,1,0:T(8,128)S(1)}, u32[]{:S(2)}, u32[]{:S(2)}) collective-permute-start(f32[2,16,128]{2,1,0:T(8,128)S(1)} %pad_maximum_fusion.4), channel_id=1, source_target_pairs={{0,2},{1,3},{2,0},{3,1},{4,6},{5,7},{6,4},{7,5},{8,10},{9,11},{10,... | collective-permute-start | bytes 49160 | tf_op jit(solution)/shard_map/ppermute | solution.py:272
  8.2 3.9 %collective-permute-start.6 = (bf16[1,2,16,512]{3,2,1,0:T(8,128)(2,1)S(1)}, bf16[1,2,16,512]{3,2,1,0:T(8,128)(2,1)S(1)}, u32[]{:S(2)}, u32[]{:S(2)}) collective-permute-start(bf16[1,2,16,512]{3,2,1,0:T(8,128)(2,1)S(1)} %get-tuple-element.15), channel_id=1, source_target_pairs={{0,8},{8,0},{16,24},{24,16},{1,9},{9,1},{17,25},{25,17},{2,10},{10... | collective-permute-start | bytes 98312 | tf_op jit(solution)/shard_map/ppermute | solution.py:272
  10.4 3.4 %collective-permute-start.2 = (f32[4,16,128]{2,1,0:T(8,128)S(1)}, f32[4,16,128]{2,1,0:T(8,128)S(1)}, u32[]{:S(2)}, u32[]{:S(2)}) collective-permute-start(f32[4,16,128]{2,1,0:T(8,128)S(1)} %pad_maximum_fusion.3), channel_id=1, source_target_pairs={{0,1},{1,0},{2,3},{3,2},{4,5},{5,4},{6,7},{7,6},{8,9},{9,8},{10,11... | collective-permute-start | bytes 98312 | tf_op jit(solution)/shard_map/ppermute | solution.py:272
  12.1 1.6 %copy-start.2 = (f32[160,128]{1,0:T(8,128)S(1)}, f32[160,128]{1,0:T(8,128)}, u32[]{:S(2)}) copy-start(f32[160,128]{1,0:T(8,128)} %constant.5.clone.broad.refs_8_) | copy-start | bytes 245764
  12.2 6.1 %collective-permute-start.7 = (bf16[2,2,16,512]{3,2,1,0:T(8,128)(2,1)S(1)}, bf16[2,2,16,512]{3,2,1,0:T(8,128)(2,1)S(1)}, u32[]{:S(2)}, u32[]{:S(2)}) collective-permute-start(bf16[2,2,16,512]{3,2,1,0:T(8,128)(2,1)S(1)} %pad_maximum_fusion.2), channel_id=1, source_target_pairs={{0,16},{8,24},{16,0},{24,8},{1,17},{9,25},{17,1},{25,9},{2,18},{10... | collective-permute-start | bytes 196616 | tf_op jit(solution)/shard_map/ppermute | solution.py:272
  14.7 3.6 %copy-start.5 = (s32[16]{0:T(128)S(1)}, s32[16]{0:T(128)}, u32[]{:S(2)}) copy-start(s32[16]{0:T(128)} %cutoff.1) | copy-start | bytes 196
  14.7 5.0 %collective-permute-start.5 = (f32[5,16,128]{2,1,0:T(8,128)S(1)}, f32[5,16,128]{2,1,0:T(8,128)S(1)}, u32[]{:S(2)}, u32[]{:S(2)}) collective-permute-start(f32[5,16,128]{2,1,0:T(8,128)S(1)} %get-tuple-element.13.refs_0_), channel_id=1, source_target_pairs={{0,24},{8,16},{16,8},{24,0},{1,25},{9,17},{17,9},{25,1},{2,26},{10... | collective-permute-start | bytes 122888 | tf_op jit(solution)/shard_map/ppermute | solution.py:272
  16.5 4.0 %collective-permute-start.4 = (f32[5,16,128]{2,1,0:T(8,128)S(1)}, f32[5,16,128]{2,1,0:T(8,128)S(1)}, u32[]{:S(2)}, u32[]{:S(2)}) collective-permute-start(f32[5,16,128]{2,1,0:T(8,128)S(1)} %get-tuple-element.13.refs_0_), channel_id=1, source_target_pairs={{0,16},{8,24},{16,0},{24,8},{1,17},{9,25},{17,1},{25,9},{2,18},{10... | collective-permute-start | bytes 122888 | tf_op jit(solution)/shard_map/ppermute | solution.py:272
  17.7 4.0 %collective-permute-start.3 = (f32[5,16,128]{2,1,0:T(8,128)S(1)}, f32[5,16,128]{2,1,0:T(8,128)S(1)}, u32[]{:S(2)}, u32[]{:S(2)}) collective-permute-start(f32[5,16,128]{2,1,0:T(8,128)S(1)} %get-tuple-element.13.refs_0_), channel_id=1, source_target_pairs={{0,8},{8,0},{16,24},{24,16},{1,9},{9,1},{17,25},{25,17},{2,10},{10... | collective-permute-start | bytes 122888 | tf_op jit(solution)/shard_map/ppermute | solution.py:272

commit v7 on v4

--- a/solution.py
+++ b/solution.py
@@ -107,8 +107,7 @@
     return result
 
 
-def pack_kernel(strain, templates, copies, held):
-    held[...] = templates[...]
+def pack_kernel(strain, copies):
     copies[...] = jnp.broadcast_to(strain[...][None], copies.shape)
 
 
@@ -116,25 +115,24 @@
     blocks = refs[:devices]
     cutoff, bank, gathered = refs[devices:]
     rank = lax.axis_index("tm")
-    width = blocks[0].shape[2]
+    _, count, width = blocks[0].shape
+    shape = (count, count)
+    same = lax.broadcasted_iota(jnp.int32, shape, 0) == lax.broadcasted_iota(jnp.int32, shape, 1)
+    column = jnp.sum(jnp.where(same, cutoff[...], 0), axis=1, keepdims=True)
+    lane = lax.broadcasted_iota(jnp.int32, (count, LANES), 1)
     for other, block in enumerate(blocks):
         first = (rank ^ other) * (width // LANES)
         for at in range(width // LANES):
             lanes = slice(at * LANES, (at + 1) * LANES)
-            gathered[first + at] = jnp.concatenate([block[0, :, lanes], block[1, :, lanes]], axis=1)
-    count = blocks[0].shape[1]
-    lane = lax.broadcasted_iota(jnp.int32, (ROWS, LANES), 1)
-    row = lax.broadcasted_iota(jnp.int32, (ROWS, LANES), 0)
-    bins = row * LANES + lane
+            keep = lane + (first + at) * LANES < column
+            both = [jnp.where(keep, block[i, :, lanes].astype(jnp.float32), 0.0) for i in range(2)]
+            gathered[first + at] = jnp.concatenate(both, axis=1).astype(jnp.bfloat16)
     shape = (count * ROWS, count * ROWS)
     to, source = lax.broadcasted_iota(jnp.int32, shape, 0), lax.broadcasted_iota(jnp.int32, shape, 1)
     order = (source == (to % ROWS) * count + to // ROWS).astype(jnp.float32).astype(jnp.bfloat16)
     value = dot(order, gathered[...].reshape(ROWS * count, 2 * LANES))
-    for m in range(count):
-        keep = bins < cutoff[m]
-        rows = slice(m * ROWS, (m + 1) * ROWS)
-        bank[0, m] = jnp.where(keep, value[rows, :LANES], 0.0)
-        bank[1, m] = jnp.where(keep, value[rows, LANES:], 0.0)
+    bank[0] = value[:, :LANES].reshape(count, ROWS, LANES)
+    bank[1] = value[:, LANES:].reshape(count, ROWS, LANES)
 
 
 def filter_kernel(energy, record, bank, narrow, broad, out, spec):
@@ -240,35 +238,32 @@
     segs = devices * size
     own = segs // tm
     count = templates.shape[1]
-    smem = pl.BlockSpec(memory_space=pltpu.SMEM)
     vmem = pl.BlockSpec(memory_space=pltpu.VMEM)
     params = pltpu.CompilerParams(vmem_limit_bytes=40 * 1024 * 1024)
     f32 = jnp.float32
 
-    copies, held = pl.pallas_call(
+    copies = pl.pallas_call(
         pack_kernel,
-        out_shape=(
-            jax.ShapeDtypeStruct((devices, size * ROWS, LANES), f32),
-            jax.ShapeDtypeStruct(templates.shape, templates.dtype),
-        ),
-        in_specs=[vmem, vmem],
-        out_specs=(vmem, vmem),
+        out_shape=jax.ShapeDtypeStruct((devices, size * ROWS, LANES), f32),
+        in_specs=[vmem],
+        out_specs=vmem,
         compiler_params=params,
         name="pack",
-    )(strain.reshape(size * ROWS, LANES), templates)
+    )(strain.reshape(size * ROWS, LANES))
+    copies, held = lax.optimization_barrier((copies, templates))
     record = lax.all_to_all(copies, ("tm", "tmpl"), split_axis=0, concat_axis=0, tiled=True)
     record = record.reshape(segs, ROWS, LANES)
     blocks = [held] + [swap(held, "tm", other) for other in range(1, tm)]
     bank = pl.pallas_call(
         functools.partial(bank_kernel, tm),
         out_shape=jax.ShapeDtypeStruct((2, count, ROWS, LANES), f32),
-        in_specs=[vmem] * tm + [smem],
+        in_specs=[vmem] * (tm + 1),
         out_specs=vmem,
         scratch_shapes=[pltpu.VMEM((ROWS, count, 2 * LANES), jnp.bfloat16)],
         compiler_params=params,
         cost_estimate=pl.CostEstimate(flops=0, bytes_accessed=2500000, transcendentals=0),
         name="bank",
-    )(*blocks, cutoff)
+    )(*blocks, cutoff.reshape(1, count))
     narrow, broad, energy = tables()
     return pl.pallas_call(
         functools.partial(filter_kernel, energy),

time: 24.3 us -> 23.5 us (0.967)
  local copies, waits for them, and re-layouts: 1.47 us -> 0.71 us
  Pallas kernels: 5.62 us -> 5.16 us
  waiting for transfers between devices: 6.05 us -> 6.5 us
    unnamed x10, local copies, waits for them, and re-layouts: 1.47 us -> 0.71 us
    all_to_all x1, waiting for transfers between devices: 2.3 us -> 2.75 us  [on_device(): lax.all_to_all(copies, ('tm', 'tmpl'), split_axis=0, concat_axis=0, tiled...]
    pallas_call x1, Pallas kernels: 0.74 us -> 0.3 us  [on_device(): pl.pallas_call(functools.partial(bank_kernel, tm), out_shape=jax.ShapeDty...]
  transfers between devices with their start and end apart: 4 -> 4, of which waited for: 4 -> 4; matrix products, arithmetic and copies ran while one was open for 0% -> 0% of each run, Pallas kernels for 3% -> 1%
where the time goes in v7:
time: 23.5 us; the launch traced here: 23.3 us
  starting transfers between devices  10.9 us (46%)
  waiting for transfers between devices  6.5 us (28%)
  Pallas kernels  5.16 us (22%)
  local copies, waits for them, and re-layouts  0.71 us (3%)
    all_to_all x1, starting transfers between devices, on_device(): lax.all_to_all(copies, ('tm', 'tmpl'), split_axis=0, concat_axis=0, tiled...  7.3 us
    pallas_call x1, Pallas kernels, on_device(): pl.pallas_call(functools.partial(filter_kernel, energy), out_shape=jax.Sh...  4.15 us
    ppermute x3, waiting for transfers between devices, swap(): lax.ppermute(array, axis, [(i, i ^ bits) for i in range(lax.axis_size(axi...  3.75 us
    ppermute x3, starting transfers between devices, swap(): lax.ppermute(array, axis, [(i, i ^ bits) for i in range(lax.axis_size(axi...  3.55 us
    all_to_all x1, waiting for transfers between devices, on_device(): lax.all_to_all(copies, ('tm', 'tmpl'), split_axis=0, concat_axis=0, tiled...  2.75 us
    pallas_call x1, Pallas kernels, on_device(): pl.pallas_call(pack_kernel, out_shape=jax.ShapeDtypeStruct((devices, size...  0.72 us
    unnamed x10, local copies, waits for them, and re-layouts  0.71 us
  transfers between devices with their start and end apart: 4, of which 4 were waited for; matrix products, arithmetic and copies ran while one was open for 0% of the time, Pallas kernels for 1%

profile of v7, /device:TPU:0, one launch (start us, length us, event | category | flops | bytes accessed | tf_op | source)
XLA Modules:
  0.0 23.3 jit_solution(6679724219406005190)
XLA Ops:
  0.0 0.0 copy-start.3
  0.0 0.7 %copy-done.3 = f32[2048]{0:T(1024)S(1)} copy-done((f32[2048]{0:T(1024)S(1)}, f32[2048]{0:T(1024)}, u32[]{:S(2)}) %copy-start.3) | copy-done | bytes 8216
  0.7 0.7 %pack.1 = f32[32,16,128]{2,1,0:T(8,128)} custom-call(f32[16,128]{1,0:T(8,128)S(1)} %bitcast.2), custom_call_target="tpu_custom_call" | custom-call | tf_op jit(solution)/shard_map/pack/pallas_call | solution.py:245
  1.4 0.0 copy-start.2
  1.4 0.0 copy-start
  1.4 7.3 %all-to-all-start = ((f32[32,16,128]{2,1,0:T(8,128)}), f32[32,16,128]{2,1,0:T(8,128)S(1)}, u32[]{:S(2)}, u32[]{:S(2)}) async-start(f32[32,16,128]{2,1,0:T(8,128)} %pack.1), calls=%async_computation | async-start | bytes 524288 | tf_op jit(solution)/shard_map/all_to_all | solution.py:254
  8.7 0.0 copy-done.2
  8.7 0.0 copy-start.4
  8.7 2.7 %collective-permute-start.2 = (bf16[2,16,512]{2,1,0:T(8,128)(2,1)S(1)}, bf16[2,16,512]{2,1,0:T(8,128)(2,1)S(1)}, u32[]{:S(2)}, u32[]{:S(2)}) collective-permute-start(bf16[2,16,512]{2,1,0:T(8,128)(2,1)S(1)} %copy-done.2), channel_id=1, source_target_pairs={{0,24},{8,16},{16,8},{24,0},{1,25},{9,17},{17,9},{25,1},{2,26},{10... | collective-permute-start | bytes 98312 | tf_op jit(solution)/shard_map/ppermute | solution.py:232
  11.5 0.6 %collective-permute-start.1 = (bf16[2,16,512]{2,1,0:T(8,128)(2,1)S(1)}, bf16[2,16,512]{2,1,0:T(8,128)(2,1)S(1)}, u32[]{:S(2)}, u32[]{:S(2)}) collective-permute-start(bf16[2,16,512]{2,1,0:T(8,128)(2,1)S(1)} %copy-done.2), channel_id=1, source_target_pairs={{0,16},{8,24},{16,0},{24,8},{1,17},{9,25},{17,1},{25,9},{2,18},{10... | collective-permute-start | bytes 98312 | tf_op jit(solution)/shard_map/ppermute | solution.py:232
  12.0 0.3 %collective-permute-start = (bf16[2,16,512]{2,1,0:T(8,128)(2,1)S(1)}, bf16[2,16,512]{2,1,0:T(8,128)(2,1)S(1)}, u32[]{:S(2)}, u32[]{:S(2)}) collective-permute-start(bf16[2,16,512]{2,1,0:T(8,128)(2,1)S(1)} %copy-done.2), channel_id=1, source_target_pairs={{0,8},{8,0},{16,24},{24,16},{1,9},{9,1},{17,25},{25,17},{2,10},{10... | collective-permute-start | bytes 98312 | tf_op jit(solution)/shard_map/ppermute | solution.py:232
  12.3 2.1 %collective-permute-done.2.refs_3_ = bf16[2,16,512]{2,1,0:T(8,128)(2,1)S(1)} collective-permute-done((bf16[2,16,512]{2,1,0:T(8,128)(2,1)S(1)}, bf16[2,16,512]{2,1,0:T(8,128)(2,1)S(1)}, u32[]{:S(2)}, u32[]{:S(2)}) %collective-permute-start.2) | collective-permute-done | bytes 32800 | tf_op jit(solution)/shard_map/ppermute | solution.py:232
  14.4 1.3 %collective-permute-done.1.refs_2_ = bf16[2,16,512]{2,1,0:T(8,128)(2,1)S(1)} collective-permute-done((bf16[2,16,512]{2,1,0:T(8,128)(2,1)S(1)}, bf16[2,16,512]{2,1,0:T(8,128)(2,1)S(1)}, u32[]{:S(2)}, u32[]{:S(2)}) %collective-permute-start.1) | collective-permute-done | bytes 32800 | tf_op jit(solution)/shard_map/ppermute | solution.py:232
  15.8 0.3 %collective-permute-done.refs_1_ = bf16[2,16,512]{2,1,0:T(8,128)(2,1)S(1)} collective-permute-done((bf16[2,16,512]{2,1,0:T(8,128)(2,1)S(1)}, bf16[2,16,512]{2,1,0:T(8,128)(2,1)S(1)}, u32[]{:S(2)}, u32[]{:S(2)}) %collective-permute-start) | collective-permute-done | bytes 32800 | tf_op jit(solution)/shard_map/ppermute | solution.py:232
  16.1 0.0 copy-done.4
  16.1 0.0 copy-start.1
  16.1 0.3 %bank.1 = f32[2,16,16,128]{3,2,1,0:T(8,128)S(1)} custom-call(bf16[2,16,512]{2,1,0:T(8,128)(2,1)S(1)} %copy-done.2, bf16[2,16,512]{2,1,0:T(8,128)(2,1)S(1)} %collective-permute-done.refs_1_, bf16[2,16,512]{2,1,0:T(8,128)(2,1)S(1)} %collective-permute-done.1.refs_2_, bf16[2,16,512]{2,1,0:T(8,128)(2,1)S(1)} %collective-permute-done.2.refs_3_, s32[1,16]{1,0:T(1,128)S(1)} %bitcast.3), custom_call_target="tpu_custom_call" | custom-call | bytes 2500000 | tf_op jit(solution)/shard_map/bank/pallas_call | solution.py:257
  16.4 2.7 %all-to-all-done.record = f32[32,16,128]{2,1,0:T(8,128)S(1)} async-done(((f32[32,16,128]{2,1,0:T(8,128)}), f32[32,16,128]{2,1,0:T(8,128)S(1)}, u32[]{:S(2)}, u32[]{:S(2)}) %all-to-all-start) | async-done | bytes 262176 | tf_op jit(solution)/shard_map/all_to_all | solution.py:254
  19.1 0.0 copy-done
  19.1 0.0 copy-done.1
  19.1 4.2 %matched_filter.1 = f32[8,16]{1,0:T(8,128)} custom-call(f32[32,16,128]{2,1,0:T(8,128)S(1)} %all-to-all-done.record, f32[2,16,16,128]{3,2,1,0:T(8,128)S(1)} %bank.1, bf16[704,256]{1,0:T(8,128)(2,1)S(1)} %copy-done, f32[160,128]{1,0:T(8,128)S(1)} %copy-done.1), custom_call_target="tpu_custom_call" | custom-call | tf_op jit(solution)/shard_map/matched_filter/pallas_call | solution.py:268
Async XLA Ops:
  0.0 0.7 %copy-start.3 = (f32[2048]{0:T(1024)S(1)}, f32[2048]{0:T(1024)}, u32[]{:S(2)}) copy-start(f32[2048]{0:T(1024)} %param.5) | copy-start | bytes 24580
  1.4 7.3 %copy-start.2 = (bf16[2,16,512]{2,1,0:T(8,128)(2,1)S(1)}, bf16[2,16,512]{2,1,0:T(8,128)(2,1)}, u32[]{:S(2)}) copy-start(bf16[2,16,512]{2,1,0:T(8,128)(2,1)} %refs_0_) | copy-start | bytes 98308
  1.4 17.7 %copy-start = (bf16[704,256]{1,0:T(8,128)(2,1)S(1)}, bf16[704,256]{1,0:T(8,128)(2,1)}, u32[]{:S(2)}) copy-start(bf16[704,256]{1,0:T(8,128)(2,1)} %constant.4.clone.narrow) | copy-start | bytes 1081348
  1.4 17.7 %all-to-all-start = ((f32[32,16,128]{2,1,0:T(8,128)}), f32[32,16,128]{2,1,0:T(8,128)S(1)}, u32[]{:S(2)}, u32[]{:S(2)}) async-start(f32[32,16,128]{2,1,0:T(8,128)} %pack.1), calls=%async_computation | async-start | bytes 524288 | tf_op jit(solution)/shard_map/all_to_all | solution.py:254
  8.7 7.3 %copy-start.4 = (s32[16]{0:T(128)S(1)}, s32[16]{0:T(128)}, u32[]{:S(2)}) copy-start(s32[16]{0:T(128)} %param.7) | copy-start | bytes 196
  8.7 5.7 %collective-permute-start.2 = (bf16[2,16,512]{2,1,0:T(8,128)(2,1)S(1)}, bf16[2,16,512]{2,1,0:T(8,128)(2,1)S(1)}, u32[]{:S(2)}, u32[]{:S(2)}) collective-permute-start(bf16[2,16,512]{2,1,0:T(8,128)(2,1)S(1)} %copy-done.2), channel_id=1, source_target_pairs={{0,24},{8,16},{16,8},{24,0},{1,25},{9,17},{17,9},{25,1},{2,26},{10... | collective-permute-start | bytes 98312 | tf_op jit(solution)/shard_map/ppermute | solution.py:232
  11.5 4.3 %collective-permute-start.1 = (bf16[2,16,512]{2,1,0:T(8,128)(2,1)S(1)}, bf16[2,16,512]{2,1,0:T(8,128)(2,1)S(1)}, u32[]{:S(2)}, u32[]{:S(2)}) collective-permute-start(bf16[2,16,512]{2,1,0:T(8,128)(2,1)S(1)} %copy-done.2), channel_id=1, source_target_pairs={{0,16},{8,24},{16,0},{24,8},{1,17},{9,25},{17,1},{25,9},{2,18},{10... | collective-permute-start | bytes 98312 | tf_op jit(solution)/shard_map/ppermute | solution.py:232
  12.0 4.0 %collective-permute-start = (bf16[2,16,512]{2,1,0:T(8,128)(2,1)S(1)}, bf16[2,16,512]{2,1,0:T(8,128)(2,1)S(1)}, u32[]{:S(2)}, u32[]{:S(2)}) collective-permute-start(bf16[2,16,512]{2,1,0:T(8,128)(2,1)S(1)} %copy-done.2), channel_id=1, source_target_pairs={{0,8},{8,0},{16,24},{24,16},{1,9},{9,1},{17,25},{25,17},{2,10},{10... | collective-permute-start | bytes 98312 | tf_op jit(solution)/shard_map/ppermute | solution.py:232
  16.1 3.1 %copy-start.1 = (f32[160,128]{1,0:T(8,128)S(1)}, f32[160,128]{1,0:T(8,128)}, u32[]{:S(2)}) copy-start(f32[160,128]{1,0:T(8,128)} %constant.5.clone.broad) | copy-start | bytes 245764

commit v8 on v7

--- a/solution.py
+++ b/solution.py
@@ -47,27 +47,28 @@
 
 @functools.lru_cache(maxsize=None)
 def tables():
+    eye = np.eye(GROUP)
     fine, wide, rows = np.arange(FINE), np.arange(LANES), np.arange(ROWS)
     window = 0.5 - 0.5 * np.cos(2.0 * np.pi * np.arange(NFFT) / NFFT)
     cos, sin = turn(fine, fine, FINE)
-    first_high, first_low = two_parts(np.tile(np.concatenate([cos, -sin]), (1, GROUP)))
+    first_high, first_low = two_parts(np.concatenate([np.kron(eye, cos), np.kron(eye, -sin)]))
     fwd_cos, fwd_sin = turn(fine, wide, NFFT)
     f_order = np.array([4 * d + g for g in range(4) for d in range(ROWS)])
     cos, sin = turn(wide, f_order, LANES)
     second_high, second_low = two_parts(np.block([[cos, -sin], [sin, cos]]))
-    scale_q, scale_c = row_scale(FINE, FINE), row_scale(LANES, LANES)
+    scale_q = row_scale(FINE, FINE)
     cos, sin = turn(fine, rows, FINE)
-    cos, sin = np.tile(cos * scale_q[:, None], (1, GROUP)), np.tile(sin * scale_q[:, None], (1, GROUP))
-    third = np.block([[cos, -sin], [sin, cos]])
-    inv_cos, inv_sin = turn(fine, wide, NFFT)
-    undo = 1.0 / (scale_q[:, None] * scale_c[None, :])
-    cos, sin = turn(wide, wide, LANES)
-    cos, sin = cos * scale_c[:, None], sin * scale_c[:, None]
-    fourth = np.block([[cos, sin], [-sin, cos]])
+    per_row = lambda t: np.einsum("qd,st->qstd", t * scale_q[:, None], eye).reshape(GROUP * FINE, GROUP * ROWS)
+    third = np.block([[per_row(cos), per_row(-sin)], [per_row(sin), per_row(cos)]])
+    fourth = []
+    for q in range(FINE):
+        cos, sin = turn(wide, q + FINE * wide, NFFT)
+        fourth.append(np.block([[cos, sin], [-sin, cos]]) / scale_q[q])
     narrow = np.concatenate(
-        [first_high, first_low, as_bf16(third), np.concatenate([second_high, second_low], axis=1), as_bf16(fourth)]
+        [first_high, first_low, np.concatenate([second_high, second_low], axis=1), as_bf16(third)]
+        + [as_bf16(table) for table in fourth]
     )
-    broad = np.concatenate([window.reshape(FINE, LANES), fwd_cos, fwd_sin, inv_cos * undo, inv_sin * undo])
+    broad = np.concatenate([window.reshape(FINE, LANES), fwd_cos, fwd_sin])
     return narrow, np.asarray(broad, np.float32), float((window * window).sum())
 
 
@@ -86,14 +87,6 @@
             carry = body(step, carry)
         return carry
     return lax.fori_loop(0, count, body, carry)
-
-
-def block_diagonal(rows, width):
-    lane = lax.broadcasted_iota(jnp.int32, rows.shape, 1)
-    owner = lax.rem(lane // width, GROUP)
-    return jnp.concatenate(
-        [jnp.where(owner == s, rows, jnp.zeros_like(rows)) for s in range(GROUP)], axis=0
-    )
 
 
 def natural(flipped, at, source):
@@ -107,8 +100,14 @@
     return result
 
 
-def pack_kernel(strain, copies):
-    copies[...] = jnp.broadcast_to(strain[...][None], copies.shape)
+def pack_kernel(strain, copies, held, filled, sems):
+    fetch = pltpu.make_async_copy(strain, held, sems.at[0])
+    fetch.start()
+    fetch.wait()
+    filled[...] = jnp.broadcast_to(held[...][None], filled.shape)
+    give = pltpu.make_async_copy(filled, copies, sems.at[1])
+    give.start()
+    give.wait()
 
 
 def bank_kernel(devices, *refs):
@@ -135,22 +134,15 @@
     bank[1] = value[:, LANES:].reshape(count, ROWS, LANES)
 
 
-def filter_kernel(energy, record, bank, narrow, broad, out, spec):
+def filter_kernel(energy, record, bank, narrow, broad, out, spec, sections):
     segs = record.shape[0]
     own, count = out.shape
     half = GROUP * FINE
     w_low, w_high = broad[:ROWS][None], broad[ROWS:FINE][None]
     fwd_cos, fwd_sin = broad[FINE:2 * FINE][None], broad[2 * FINE:3 * FINE][None]
-    inv_cos, inv_sin = broad[3 * FINE:4 * FINE][None], broad[4 * FINE:5 * FINE][None]
-    high, low = narrow[:2 * FINE], narrow[2 * FINE:4 * FINE]
-    spread = lambda part: jnp.concatenate(
-        [block_diagonal(part[:FINE], part.shape[1] // GROUP), block_diagonal(part[FINE:], part.shape[1] // GROUP)]
-    )
-    first_high, first_low = spread(high), spread(low)
-    third_rows = narrow[4 * FINE:6 * FINE]
-    third = jnp.concatenate([block_diagonal(third_rows[:FINE], ROWS), block_diagonal(third_rows[FINE:], ROWS)])
-    second = slice(6 * FINE, 6 * FINE + 2 * LANES)
-    fourth = slice(6 * FINE + 2 * LANES, 6 * FINE + 4 * LANES)
+    first = jnp.concatenate([narrow[:2 * half], narrow[:2 * half], narrow[2 * half:4 * half]], axis=1)
+    second = narrow[4 * half:5 * half]
+    second = jnp.concatenate([second, second], axis=0)
 
     def frames(start, last):
         here = record[pl.ds(start, GROUP)]
@@ -164,14 +156,14 @@
     def forward(start, power, last):
         pair = jnp.concatenate([frames(start, False), frames(start + GROUP, last)], axis=1)
         high, low = split(pair)
-        step = dot(first_high, high) + dot(first_high, low) + dot(first_low, high)
+        step = dot(first, jnp.concatenate([high, low, high], axis=0))
         for h in range(2):
             re = step[:half, h * LANES:(h + 1) * LANES].reshape(GROUP, FINE, LANES)
             im = step[half:, h * LANES:(h + 1) * LANES].reshape(GROUP, FINE, LANES)
             turned = jnp.concatenate([re * fwd_cos + im * fwd_sin, im * fwd_cos - re * fwd_sin], axis=2)
             high, low = split(turned.reshape(half, 2 * LANES))
-            wide = dot(high, narrow[second])
-            value = wide[:, :LANES] + wide[:, LANES:] + dot(low, narrow[second, :LANES])
+            both = dot(jnp.concatenate([high, low], axis=1), second)
+            value = both[:, :LANES] + both[:, LANES:]
             spec[pl.ds((start + h * GROUP) * FINE, half)] = value
             power = power + jnp.sum((value * value).reshape(GROUP, FINE, LANES), axis=0)
         return power
@@ -199,33 +191,38 @@
                 im_parts.append(natural(flipped, LANES // 2, s))
         white_re, white_im = jnp.stack(re_parts), jnp.stack(im_parts)
 
-        def pair_of(step, result):
-            sides, norms = [], []
-            for side in range(2):
-                m = 2 * step + side
+        norms = []
+        for step in range(count // 2):
+            sides = []
+            for m in (2 * step, 2 * step + 1):
                 h_re, h_im = bank[0, m], bank[1, m]
                 norms.append(jnp.sum((h_re * h_re + h_im * h_im) * inverse_density, keepdims=True))
                 c_re = h_re[None] * white_re + h_im[None] * white_im
                 c_im = h_re[None] * white_im - h_im[None] * white_re
                 both = jnp.concatenate([c_re, c_im], axis=0).reshape(2 * GROUP * ROWS, LANES)
                 sides.append(both.astype(jnp.bfloat16))
-            section = dot(third, jnp.concatenate(sides, axis=1))
-            for side in range(2):
-                re = section[:half, side * LANES:(side + 1) * LANES].reshape(GROUP, FINE, LANES)
-                im = section[half:, side * LANES:(side + 1) * LANES].reshape(GROUP, FINE, LANES)
-                turned = jnp.concatenate([re * inv_cos - im * inv_sin, re * inv_sin + im * inv_cos], axis=2)
-                wave = dot(turned.reshape(half, 2 * LANES).astype(jnp.bfloat16), narrow[fourth])
-                square = wave[:, :LANES] * wave[:, :LANES] + wave[:, LANES:] * wave[:, LANES:]
-                top = jnp.max(jnp.max(square.reshape(GROUP, FINE, LANES), axis=1), axis=1, keepdims=True)
-                value = jnp.sqrt(top) / (jnp.sqrt(norms[side]) * math.sqrt(energy))
-                result = jnp.where(column == 2 * step + side, value, result)
-            return result
-
-        result = repeat(count // 2, pair_of, jnp.zeros((GROUP, LANES), jnp.float32))
-        out[pl.ds(number * GROUP, GROUP)] = result[:, :count]
+            section = dot(narrow[5 * half:7 * half], jnp.concatenate(sides, axis=1))
+            for part in range(2):
+                rows = section[part * half:(part + 1) * half].reshape(FINE, GROUP, 2 * LANES)
+                rows = jnp.concatenate([rows[:, :, :LANES], rows[:, :, LANES:]], axis=1)
+                lanes = slice(part * LANES, (part + 1) * LANES)
+                sections[:, 2 * step * GROUP:2 * (step + 1) * GROUP, lanes] = rows.astype(jnp.bfloat16)
+        best = jnp.zeros((count * GROUP, LANES), jnp.float32)
+        for q in range(FINE):
+            wave = dot(sections[q], narrow[(7 + q) * half:(8 + q) * half])
+            best = jnp.maximum(best, wave[:, :LANES] * wave[:, :LANES] + wave[:, LANES:] * wave[:, LANES:])
+        result = jnp.zeros((GROUP, LANES), jnp.float32)
+        for m in range(count):
+            top = jnp.max(best[m * GROUP:(m + 1) * GROUP], axis=1, keepdims=True)
+            value = jnp.sqrt(top) / (jnp.sqrt(norms[m]) * math.sqrt(energy))
+            result = jnp.where(column == m, value, result)
+        out[pl.ds(pl.multiple_of(number * GROUP, GROUP), GROUP)] = result[:, :count]
         return carry
 
-    repeat(own // GROUP, block, 0)
+    if own == GROUP:
+        block(0, 0)
+    else:
+        lax.fori_loop(0, own // GROUP, block, 0)
 
 
 def swap(array, axis, bits):
@@ -239,15 +236,20 @@
     own = segs // tm
     count = templates.shape[1]
     vmem = pl.BlockSpec(memory_space=pltpu.VMEM)
+    anywhere = pl.BlockSpec(memory_space=pl.ANY)
     params = pltpu.CompilerParams(vmem_limit_bytes=40 * 1024 * 1024)
     f32 = jnp.float32
 
     copies = pl.pallas_call(
         pack_kernel,
         out_shape=jax.ShapeDtypeStruct((devices, size * ROWS, LANES), f32),
-        in_specs=[vmem],
-        out_specs=vmem,
-        compiler_params=params,
+        in_specs=[anywhere],
+        out_specs=anywhere,
+        scratch_shapes=[
+            pltpu.VMEM((size * ROWS, LANES), f32),
+            pltpu.VMEM((devices, size * ROWS, LANES), f32),
+            pltpu.SemaphoreType.DMA((2,)),
+        ],
         name="pack",
     )(strain.reshape(size * ROWS, LANES))
     copies, held = lax.optimization_barrier((copies, templates))
@@ -270,7 +272,10 @@
         out_shape=jax.ShapeDtypeStruct((own, count), f32),
         in_specs=[vmem] * 4,
         out_specs=vmem,
-        scratch_shapes=[pltpu.VMEM((segs * FINE, LANES), f32)],
+        scratch_shapes=[
+            pltpu.VMEM((segs * FINE, LANES), f32),
+            pltpu.VMEM((FINE, count * GROUP, 2 * LANES), jnp.bfloat16),
+        ],
         compiler_params=params,
         name="matched_filter",
     )(record, bank, jnp.asarray(narrow), jnp.asarray(broad))

time: 23.5 us -> 26.7 us (1.14)
  local copies, waits for them, and re-layouts: 0.71 us -> 4.66 us
  waiting for transfers between devices: 6.5 us -> 5.11 us
  Pallas kernels: 5.16 us -> 5.67 us
    unnamed x10 -> x8, local copies, waits for them, and re-layouts: 0.71 us -> 4.66 us
    all_to_all x1, waiting for transfers between devices: 2.75 us -> 1.24 us  [on_device(): lax.all_to_all(copies, ('tm', 'tmpl'), split_axis=0, concat_axis=0, tiled...]
    pallas_call x1, Pallas kernels: 0.72 us -> 1.42 us  [on_device(): pl.pallas_call(pack_kernel, out_shape=jax.ShapeDtypeStruct((devices, size...]
where the time goes in v8:
time: 26.7 us; the launch traced here: 26.3 us
  starting transfers between devices  10.9 us (41%)
  Pallas kernels  5.67 us (21%)
  waiting for transfers between devices  5.11 us (19%)
  local copies, waits for them, and re-layouts  4.66 us (17%)
    all_to_all x1, starting transfers between devices, on_device(): lax.all_to_all(copies, ('tm', 'tmpl'), split_axis=0, concat_axis=0, tiled...  7.3 us
    unnamed x8, local copies, waits for them, and re-layouts  4.66 us
    pallas_call x1, Pallas kernels, on_device(): pl.pallas_call(functools.partial(filter_kernel, energy), out_shape=jax.Sh...  3.96 us
    ppermute x3, waiting for transfers between devices, swap(): lax.ppermute(array, axis, [(i, i ^ bits) for i in range(lax.axis_size(axi...  3.87 us
    ppermute x3, starting transfers between devices, swap(): lax.ppermute(array, axis, [(i, i ^ bits) for i in range(lax.axis_size(axi...  3.55 us
    pallas_call x1, Pallas kernels, on_device(): pl.pallas_call(pack_kernel, out_shape=jax.ShapeDtypeStruct((devices, size...  1.42 us
    all_to_all x1, waiting for transfers between devices, on_device(): lax.all_to_all(copies, ('tm', 'tmpl'), split_axis=0, concat_axis=0, tiled...  1.24 us
  transfers between devices with their start and end apart: 4, of which 4 were waited for; matrix products, arithmetic and copies ran while one was open for 0% of the time, Pallas kernels for 1%

profile of v8, /device:TPU:0, one launch (start us, length us, event | category | flops | bytes accessed | tf_op | source)
XLA Modules:
  0.0 26.3 jit_solution(16031262111398209275)
XLA Ops:
  0.0 1.4 %pack.1 = f32[32,16,128]{2,1,0:T(8,128)} custom-call(f32[16,128]{1,0:T(8,128)} %bitcast.3), custom_call_target="tpu_custom_call" | custom-call | tf_op jit(solution)/shard_map/pack/pallas_call | solution.py:243
  1.4 7.3 %all-to-all-start = ((f32[32,16,128]{2,1,0:T(8,128)}), f32[32,16,128]{2,1,0:T(8,128)S(1)}, u32[]{:S(2)}, u32[]{:S(2)}) async-start(f32[32,16,128]{2,1,0:T(8,128)} %pack.1), calls=%async_computation | async-start | bytes 524288 | tf_op jit(solution)/shard_map/all_to_all | solution.py:256
  8.7 2.7 %collective-permute-start.2 = (bf16[2,16,512]{2,1,0:T(8,128)(2,1)}, bf16[2,16,512]{2,1,0:T(8,128)(2,1)S(1)}, u32[]{:S(2)}, u32[]{:S(2)}) collective-permute-start(bf16[2,16,512]{2,1,0:T(8,128)(2,1)} %refs_0_), channel_id=1, source_target_pairs={{0,24},{8,16},{16,8},{24,0},{1,25},{9,17},{17,9},{25,1},{2,26},{10... | collective-permute-start | bytes 98312 | tf_op jit(solution)/shard_map/ppermute | solution.py:229
  11.5 0.6 %collective-permute-start.1 = (bf16[2,16,512]{2,1,0:T(8,128)(2,1)}, bf16[2,16,512]{2,1,0:T(8,128)(2,1)S(1)}, u32[]{:S(2)}, u32[]{:S(2)}) collective-permute-start(bf16[2,16,512]{2,1,0:T(8,128)(2,1)} %refs_0_), channel_id=1, source_target_pairs={{0,16},{8,24},{16,0},{24,8},{1,17},{9,25},{17,1},{25,9},{2,18},{10... | collective-permute-start | bytes 98312 | tf_op jit(solution)/shard_map/ppermute | solution.py:229
  12.0 0.3 collective-permute-start
  12.3 2.1 %collective-permute-done.2.refs_3_ = bf16[2,16,512]{2,1,0:T(8,128)(2,1)S(1)} collective-permute-done((bf16[2,16,512]{2,1,0:T(8,128)(2,1)}, bf16[2,16,512]{2,1,0:T(8,128)(2,1)S(1)}, u32[]{:S(2)}, u32[]{:S(2)}) %collective-permute-start.2) | collective-permute-done | bytes 32800 | tf_op jit(solution)/shard_map/ppermute | solution.py:229
  14.4 1.4 %collective-permute-done.1.refs_2_ = bf16[2,16,512]{2,1,0:T(8,128)(2,1)S(1)} collective-permute-done((bf16[2,16,512]{2,1,0:T(8,128)(2,1)}, bf16[2,16,512]{2,1,0:T(8,128)(2,1)S(1)}, u32[]{:S(2)}, u32[]{:S(2)}) %collective-permute-start.1) | collective-permute-done | bytes 32800 | tf_op jit(solution)/shard_map/ppermute | solution.py:229
  15.8 0.4 %collective-permute-done.refs_1_ = bf16[2,16,512]{2,1,0:T(8,128)(2,1)S(1)} collective-permute-done((bf16[2,16,512]{2,1,0:T(8,128)(2,1)}, bf16[2,16,512]{2,1,0:T(8,128)(2,1)S(1)}, u32[]{:S(2)}, u32[]{:S(2)}) %collective-permute-start) | collective-permute-done | bytes 32800 | tf_op jit(solution)/shard_map/ppermute | solution.py:229
  16.2 0.0 copy-start.2
  16.2 0.8 %copy-done.2 = bf16[2,16,512]{2,1,0:T(8,128)(2,1)S(1)} copy-done((bf16[2,16,512]{2,1,0:T(8,128)(2,1)S(1)}, bf16[2,16,512]{2,1,0:T(8,128)(2,1)}, u32[]{:S(2)}) %copy-start.2) | copy-done | bytes 32792
  16.9 0.0 copy-start.3
  16.9 0.7 %copy-done.3 = s32[16]{0:T(128)S(1)} copy-done((s32[16]{0:T(128)S(1)}, s32[16]{0:T(128)}, u32[]{:S(2)}) %copy-start.3) | copy-done | bytes 88
  17.6 0.3 %bank.1 = f32[2,16,16,128]{3,2,1,0:T(8,128)S(1)} custom-call(bf16[2,16,512]{2,1,0:T(8,128)(2,1)S(1)} %copy-done.2, bf16[2,16,512]{2,1,0:T(8,128)(2,1)S(1)} %collective-permute-done.refs_1_, bf16[2,16,512]{2,1,0:T(8,128)(2,1)S(1)} %collective-permute-done.1.refs_2_, bf16[2,16,512]{2,1,0:T(8,128)(2,1)S(1)} %collective-permute-done.2.refs_3_, s32[1,16]{1,0:T(1,128)S(1)} %bitcast.2), custom_call_target="tpu_custom_call" | custom-call | bytes 2500000 | tf_op jit(solution)/shard_map/bank/pallas_call | solution.py:259
  17.9 1.2 %all-to-all-done.record = f32[32,16,128]{2,1,0:T(8,128)S(1)} async-done(((f32[32,16,128]{2,1,0:T(8,128)}), f32[32,16,128]{2,1,0:T(8,128)S(1)}, u32[]{:S(2)}, u32[]{:S(2)}) %all-to-all-start) | async-done | bytes 262176 | tf_op jit(solution)/shard_map/all_to_all | solution.py:256
  19.1 0.0 copy-start
  19.1 2.4 %copy-done = bf16[9984,256]{1,0:T(8,128)(2,1)S(1)} copy-done((bf16[9984,256]{1,0:T(8,128)(2,1)S(1)}, bf16[9984,256]{1,0:T(8,128)(2,1)}, u32[]{:S(2)}) %copy-start) | copy-done | bytes 5111832
  21.6 0.0 copy-start.1
  21.6 0.8 %copy-done.1 = f32[96,128]{1,0:T(8,128)S(1)} copy-done((f32[96,128]{1,0:T(8,128)S(1)}, f32[96,128]{1,0:T(8,128)}, u32[]{:S(2)}) %copy-start.1) | copy-done | bytes 49176
  22.4 4.0 %matched_filter.1 = f32[8,16]{1,0:T(8,128)} custom-call(f32[32,16,128]{2,1,0:T(8,128)S(1)} %all-to-all-done.record, f32[2,16,16,128]{3,2,1,0:T(8,128)S(1)} %bank.1, bf16[9984,256]{1,0:T(8,128)(2,1)S(1)} %copy-done, f32[96,128]{1,0:T(8,128)S(1)} %copy-done.1), custom_call_target="tpu_custom_call" | custom-call | tf_op jit(solution)/shard_map/matched_filter/pallas_call | solution.py:270
Async XLA Ops:
  1.4 17.7 %all-to-all-start = ((f32[32,16,128]{2,1,0:T(8,128)}), f32[32,16,128]{2,1,0:T(8,128)S(1)}, u32[]{:S(2)}, u32[]{:S(2)}) async-start(f32[32,16,128]{2,1,0:T(8,128)} %pack.1), calls=%async_computation | async-start | bytes 524288 | tf_op jit(solution)/shard_map/all_to_all | solution.py:256
  8.7 5.7 %collective-permute-start.2 = (bf16[2,16,512]{2,1,0:T(8,128)(2,1)}, bf16[2,16,512]{2,1,0:T(8,128)(2,1)S(1)}, u32[]{:S(2)}, u32[]{:S(2)}) collective-permute-start(bf16[2,16,512]{2,1,0:T(8,128)(2,1)} %refs_0_), channel_id=1, source_target_pairs={{0,24},{8,16},{16,8},{24,0},{1,25},{9,17},{17,9},{25,1},{2,26},{10... | collective-permute-start | bytes 98312 | tf_op jit(solution)/shard_map/ppermute | solution.py:229
  11.5 4.3 %collective-permute-start.1 = (bf16[2,16,512]{2,1,0:T(8,128)(2,1)}, bf16[2,16,512]{2,1,0:T(8,128)(2,1)S(1)}, u32[]{:S(2)}, u32[]{:S(2)}) collective-permute-start(bf16[2,16,512]{2,1,0:T(8,128)(2,1)} %refs_0_), channel_id=1, source_target_pairs={{0,16},{8,24},{16,0},{24,8},{1,17},{9,25},{17,1},{25,9},{2,18},{10... | collective-permute-start | bytes 98312 | tf_op jit(solution)/shard_map/ppermute | solution.py:229
  12.0 4.1 %collective-permute-start = (bf16[2,16,512]{2,1,0:T(8,128)(2,1)}, bf16[2,16,512]{2,1,0:T(8,128)(2,1)S(1)}, u32[]{:S(2)}, u32[]{:S(2)}) collective-permute-start(bf16[2,16,512]{2,1,0:T(8,128)(2,1)} %refs_0_), channel_id=1, source_target_pairs={{0,8},{8,0},{16,24},{24,16},{1,9},{9,1},{17,25},{25,17},{2,10},{10... | collective-permute-start | bytes 98312 | tf_op jit(solution)/shard_map/ppermute | solution.py:229
  16.2 0.8 %copy-start.2 = (bf16[2,16,512]{2,1,0:T(8,128)(2,1)S(1)}, bf16[2,16,512]{2,1,0:T(8,128)(2,1)}, u32[]{:S(2)}) copy-start(bf16[2,16,512]{2,1,0:T(8,128)(2,1)} %refs_0_) | copy-start | bytes 98308
  16.9 0.7 %copy-start.3 = (s32[16]{0:T(128)S(1)}, s32[16]{0:T(128)}, u32[]{:S(2)}) copy-start(s32[16]{0:T(128)} %param.7) | copy-start | bytes 196
  19.1 2.4 %copy-start = (bf16[9984,256]{1,0:T(8,128)(2,1)S(1)}, bf16[9984,256]{1,0:T(8,128)(2,1)}, u32[]{:S(2)}) copy-start(bf16[9984,256]{1,0:T(8,128)(2,1)} %constant.4.clone.narrow) | copy-start | bytes 15335428
  21.6 0.8 %copy-start.1 = (f32[96,128]{1,0:T(8,128)S(1)}, f32[96,128]{1,0:T(8,128)}, u32[]{:S(2)}) copy-start(f32[96,128]{1,0:T(8,128)} %constant.5.clone.broad) | copy-start | bytes 147460

commit v9 on v7

--- a/solution.py
+++ b/solution.py
@@ -146,7 +146,8 @@
     spread = lambda part: jnp.concatenate(
         [block_diagonal(part[:FINE], part.shape[1] // GROUP), block_diagonal(part[FINE:], part.shape[1] // GROUP)]
     )
-    first_high, first_low = spread(high), spread(low)
+    first_high = spread(high)
+    first = jnp.concatenate([first_high, first_high, spread(low)], axis=1)
     third_rows = narrow[4 * FINE:6 * FINE]
     third = jnp.concatenate([block_diagonal(third_rows[:FINE], ROWS), block_diagonal(third_rows[FINE:], ROWS)])
     second = slice(6 * FINE, 6 * FINE + 2 * LANES)
@@ -164,14 +165,14 @@
     def forward(start, power, last):
         pair = jnp.concatenate([frames(start, False), frames(start + GROUP, last)], axis=1)
         high, low = split(pair)
-        step = dot(first_high, high) + dot(first_high, low) + dot(first_low, high)
+        step = dot(first, jnp.concatenate([high, low, high], axis=0))
         for h in range(2):
             re = step[:half, h * LANES:(h + 1) * LANES].reshape(GROUP, FINE, LANES)
             im = step[half:, h * LANES:(h + 1) * LANES].reshape(GROUP, FINE, LANES)
             turned = jnp.concatenate([re * fwd_cos + im * fwd_sin, im * fwd_cos - re * fwd_sin], axis=2)
             high, low = split(turned.reshape(half, 2 * LANES))
-            wide = dot(high, narrow[second])
-            value = wide[:, :LANES] + wide[:, LANES:] + dot(low, narrow[second, :LANES])
+            both = dot(jnp.concatenate([high, low], axis=1), jnp.concatenate([narrow[second]] * 2, axis=0))
+            value = both[:, :LANES] + both[:, LANES:]
             spec[pl.ds((start + h * GROUP) * FINE, half)] = value
             power = power + jnp.sum((value * value).reshape(GROUP, FINE, LANES), axis=0)
         return power
@@ -221,7 +222,9 @@
                 result = jnp.where(column == 2 * step + side, value, result)
             return result
 
-        result = repeat(count // 2, pair_of, jnp.zeros((GROUP, LANES), jnp.float32))
+        result = lax.fori_loop(
+            0, count // 4, lambda i, r: pair_of(2 * i + 1, pair_of(2 * i, r)), jnp.zeros((GROUP, LANES), jnp.float32)
+        )
         out[pl.ds(number * GROUP, GROUP)] = result[:, :count]
         return carry
 

time: 23.5 us -> 24.9 us (1.060)
  Pallas kernels: 5.16 us -> 6.49 us
    pallas_call x1, Pallas kernels: 4.15 us -> 5.48 us  [on_device(): pl.pallas_call(functools.partial(filter_kernel, energy), out_shape=jax.Sh...]
where the time goes in v9:
time: 24.9 us; the launch traced here: 24.6 us
  starting transfers between devices  10.9 us (44%)
  waiting for transfers between devices  6.5 us (26%)
  Pallas kernels  6.49 us (26%)
  local copies, waits for them, and re-layouts  0.71 us (3%)
    all_to_all x1, starting transfers between devices, on_device(): lax.all_to_all(copies, ('tm', 'tmpl'), split_axis=0, concat_axis=0, tiled...  7.3 us
    pallas_call x1, Pallas kernels, on_device(): pl.pallas_call(functools.partial(filter_kernel, energy), out_shape=jax.Sh...  5.48 us
    ppermute x3, waiting for transfers between devices, swap(): lax.ppermute(array, axis, [(i, i ^ bits) for i in range(lax.axis_size(axi...  3.75 us
    ppermute x3, starting transfers between devices, swap(): lax.ppermute(array, axis, [(i, i ^ bits) for i in range(lax.axis_size(axi...  3.55 us
    all_to_all x1, waiting for transfers between devices, on_device(): lax.all_to_all(copies, ('tm', 'tmpl'), split_axis=0, concat_axis=0, tiled...  2.75 us
    pallas_call x1, Pallas kernels, on_device(): pl.pallas_call(pack_kernel, out_shape=jax.ShapeDtypeStruct((devices, size...  0.72 us
    unnamed x10, local copies, waits for them, and re-layouts  0.71 us
  transfers between devices with their start and end apart: 4, of which 4 were waited for; matrix products, arithmetic and copies ran while one was open for 0% of the time, Pallas kernels for 1%

profile of v9, /device:TPU:0, one launch (start us, length us, event | category | flops | bytes accessed | tf_op | source)
XLA Modules:
  0.0 24.6 jit_solution(6699331414306216483)
XLA Ops:
  0.0 0.0 copy-start.3
  0.0 0.7 %copy-done.3 = f32[2048]{0:T(1024)S(1)} copy-done((f32[2048]{0:T(1024)S(1)}, f32[2048]{0:T(1024)}, u32[]{:S(2)}) %copy-start.3) | copy-done | bytes 8216
  0.7 0.7 %pack.1 = f32[32,16,128]{2,1,0:T(8,128)} custom-call(f32[16,128]{1,0:T(8,128)S(1)} %bitcast.2), custom_call_target="tpu_custom_call" | custom-call | tf_op jit(solution)/shard_map/pack/pallas_call | solution.py:248
  1.4 0.0 copy-start.2
  1.4 0.0 copy-start
  1.4 7.3 %all-to-all-start = ((f32[32,16,128]{2,1,0:T(8,128)}), f32[32,16,128]{2,1,0:T(8,128)S(1)}, u32[]{:S(2)}, u32[]{:S(2)}) async-start(f32[32,16,128]{2,1,0:T(8,128)} %pack.1), calls=%async_computation | async-start | bytes 524288 | tf_op jit(solution)/shard_map/all_to_all | solution.py:257
  8.7 0.0 copy-done.2
  8.7 0.0 copy-start.4
  8.7 2.7 %collective-permute-start.2 = (bf16[2,16,512]{2,1,0:T(8,128)(2,1)S(1)}, bf16[2,16,512]{2,1,0:T(8,128)(2,1)S(1)}, u32[]{:S(2)}, u32[]{:S(2)}) collective-permute-start(bf16[2,16,512]{2,1,0:T(8,128)(2,1)S(1)} %copy-done.2), channel_id=1, source_target_pairs={{0,24},{8,16},{16,8},{24,0},{1,25},{9,17},{17,9},{25,1},{2,26},{10... | collective-permute-start | bytes 98312 | tf_op jit(solution)/shard_map/ppermute | solution.py:235
  11.5 0.6 %collective-permute-start.1 = (bf16[2,16,512]{2,1,0:T(8,128)(2,1)S(1)}, bf16[2,16,512]{2,1,0:T(8,128)(2,1)S(1)}, u32[]{:S(2)}, u32[]{:S(2)}) collective-permute-start(bf16[2,16,512]{2,1,0:T(8,128)(2,1)S(1)} %copy-done.2), channel_id=1, source_target_pairs={{0,16},{8,24},{16,0},{24,8},{1,17},{9,25},{17,1},{25,9},{2,18},{10... | collective-permute-start | bytes 98312 | tf_op jit(solution)/shard_map/ppermute | solution.py:235
  12.0 0.3 %collective-permute-start = (bf16[2,16,512]{2,1,0:T(8,128)(2,1)S(1)}, bf16[2,16,512]{2,1,0:T(8,128)(2,1)S(1)}, u32[]{:S(2)}, u32[]{:S(2)}) collective-permute-start(bf16[2,16,512]{2,1,0:T(8,128)(2,1)S(1)} %copy-done.2), channel_id=1, source_target_pairs={{0,8},{8,0},{16,24},{24,16},{1,9},{9,1},{17,25},{25,17},{2,10},{10... | collective-permute-start | bytes 98312 | tf_op jit(solution)/shard_map/ppermute | solution.py:235
  12.3 2.1 %collective-permute-done.2.refs_3_ = bf16[2,16,512]{2,1,0:T(8,128)(2,1)S(1)} collective-permute-done((bf16[2,16,512]{2,1,0:T(8,128)(2,1)S(1)}, bf16[2,16,512]{2,1,0:T(8,128)(2,1)S(1)}, u32[]{:S(2)}, u32[]{:S(2)}) %collective-permute-start.2) | collective-permute-done | bytes 32800 | tf_op jit(solution)/shard_map/ppermute | solution.py:235
  14.4 1.3 %collective-permute-done.1.refs_2_ = bf16[2,16,512]{2,1,0:T(8,128)(2,1)S(1)} collective-permute-done((bf16[2,16,512]{2,1,0:T(8,128)(2,1)S(1)}, bf16[2,16,512]{2,1,0:T(8,128)(2,1)S(1)}, u32[]{:S(2)}, u32[]{:S(2)}) %collective-permute-start.1) | collective-permute-done | bytes 32800 | tf_op jit(solution)/shard_map/ppermute | solution.py:235
  15.8 0.3 %collective-permute-done.refs_1_ = bf16[2,16,512]{2,1,0:T(8,128)(2,1)S(1)} collective-permute-done((bf16[2,16,512]{2,1,0:T(8,128)(2,1)S(1)}, bf16[2,16,512]{2,1,0:T(8,128)(2,1)S(1)}, u32[]{:S(2)}, u32[]{:S(2)}) %collective-permute-start) | collective-permute-done | bytes 32800 | tf_op jit(solution)/shard_map/ppermute | solution.py:235
  16.1 0.0 copy-done.4
  16.1 0.0 copy-start.1
  16.1 0.3 %bank.1 = f32[2,16,16,128]{3,2,1,0:T(8,128)S(1)} custom-call(bf16[2,16,512]{2,1,0:T(8,128)(2,1)S(1)} %copy-done.2, bf16[2,16,512]{2,1,0:T(8,128)(2,1)S(1)} %collective-permute-done.refs_1_, bf16[2,16,512]{2,1,0:T(8,128)(2,1)S(1)} %collective-permute-done.1.refs_2_, bf16[2,16,512]{2,1,0:T(8,128)(2,1)S(1)} %collective-permute-done.2.refs_3_, s32[1,16]{1,0:T(1,128)S(1)} %bitcast.3), custom_call_target="tpu_custom_call" | custom-call | bytes 2500000 | tf_op jit(solution)/shard_map/bank/pallas_call | solution.py:260
  16.4 2.7 %all-to-all-done.record = f32[32,16,128]{2,1,0:T(8,128)S(1)} async-done(((f32[32,16,128]{2,1,0:T(8,128)}), f32[32,16,128]{2,1,0:T(8,128)S(1)}, u32[]{:S(2)}, u32[]{:S(2)}) %all-to-all-start) | async-done | bytes 262176 | tf_op jit(solution)/shard_map/all_to_all | solution.py:257
  19.1 0.0 copy-done
  19.1 0.0 copy-done.1
  19.1 5.5 %matched_filter.1 = f32[8,16]{1,0:T(8,128)} custom-call(f32[32,16,128]{2,1,0:T(8,128)S(1)} %all-to-all-done.record, f32[2,16,16,128]{3,2,1,0:T(8,128)S(1)} %bank.1, bf16[704,256]{1,0:T(8,128)(2,1)S(1)} %copy-done, f32[160,128]{1,0:T(8,128)S(1)} %copy-done.1), custom_call_target="tpu_custom_call" | custom-call | tf_op jit(solution)/shard_map/matched_filter/pallas_call | solution.py:271
Async XLA Ops:
  0.0 0.7 %copy-start.3 = (f32[2048]{0:T(1024)S(1)}, f32[2048]{0:T(1024)}, u32[]{:S(2)}) copy-start(f32[2048]{0:T(1024)} %param.5) | copy-start | bytes 24580
  1.4 7.3 %copy-start.2 = (bf16[2,16,512]{2,1,0:T(8,128)(2,1)S(1)}, bf16[2,16,512]{2,1,0:T(8,128)(2,1)}, u32[]{:S(2)}) copy-start(bf16[2,16,512]{2,1,0:T(8,128)(2,1)} %refs_0_) | copy-start | bytes 98308
  1.4 17.7 %copy-start = (bf16[704,256]{1,0:T(8,128)(2,1)S(1)}, bf16[704,256]{1,0:T(8,128)(2,1)}, u32[]{:S(2)}) copy-start(bf16[704,256]{1,0:T(8,128)(2,1)} %constant.4.clone.narrow) | copy-start | bytes 1081348
  1.4 17.7 %all-to-all-start = ((f32[32,16,128]{2,1,0:T(8,128)}), f32[32,16,128]{2,1,0:T(8,128)S(1)}, u32[]{:S(2)}, u32[]{:S(2)}) async-start(f32[32,16,128]{2,1,0:T(8,128)} %pack.1), calls=%async_computation | async-start | bytes 524288 | tf_op jit(solution)/shard_map/all_to_all | solution.py:257
  8.7 7.3 %copy-start.4 = (s32[16]{0:T(128)S(1)}, s32[16]{0:T(128)}, u32[]{:S(2)}) copy-start(s32[16]{0:T(128)} %param.7) | copy-start | bytes 196
  8.7 5.7 %collective-permute-start.2 = (bf16[2,16,512]{2,1,0:T(8,128)(2,1)S(1)}, bf16[2,16,512]{2,1,0:T(8,128)(2,1)S(1)}, u32[]{:S(2)}, u32[]{:S(2)}) collective-permute-start(bf16[2,16,512]{2,1,0:T(8,128)(2,1)S(1)} %copy-done.2), channel_id=1, source_target_pairs={{0,24},{8,16},{16,8},{24,0},{1,25},{9,17},{17,9},{25,1},{2,26},{10... | collective-permute-start | bytes 98312 | tf_op jit(solution)/shard_map/ppermute | solution.py:235
  11.5 4.3 %collective-permute-start.1 = (bf16[2,16,512]{2,1,0:T(8,128)(2,1)S(1)}, bf16[2,16,512]{2,1,0:T(8,128)(2,1)S(1)}, u32[]{:S(2)}, u32[]{:S(2)}) collective-permute-start(bf16[2,16,512]{2,1,0:T(8,128)(2,1)S(1)} %copy-done.2), channel_id=1, source_target_pairs={{0,16},{8,24},{16,0},{24,8},{1,17},{9,25},{17,1},{25,9},{2,18},{10... | collective-permute-start | bytes 98312 | tf_op jit(solution)/shard_map/ppermute | solution.py:235
  12.0 4.0 %collective-permute-start = (bf16[2,16,512]{2,1,0:T(8,128)(2,1)S(1)}, bf16[2,16,512]{2,1,0:T(8,128)(2,1)S(1)}, u32[]{:S(2)}, u32[]{:S(2)}) collective-permute-start(bf16[2,16,512]{2,1,0:T(8,128)(2,1)S(1)} %copy-done.2), channel_id=1, source_target_pairs={{0,8},{8,0},{16,24},{24,16},{1,9},{9,1},{17,25},{25,17},{2,10},{10... | collective-permute-start | bytes 98312 | tf_op jit(solution)/shard_map/ppermute | solution.py:235
  16.1 3.1 %copy-start.1 = (f32[160,128]{1,0:T(8,128)S(1)}, f32[160,128]{1,0:T(8,128)}, u32[]{:S(2)}) copy-start(f32[160,128]{1,0:T(8,128)} %constant.5.clone.broad) | copy-start | bytes 245764

commit v10 on v6

--- a/solution.py
+++ b/solution.py
@@ -124,46 +124,46 @@
     return jnp.concatenate(rows)
 
 
-def prepare_kernel(strain, templates, narrow, chunk, block, first, third):
+def hold_kernel(strain, templates, chunk, block):
     chunk[...] = strain[...]
     block[...] = templates[...]
-    first[0] = halved(narrow[:2 * FINE])
-    first[1] = halved(narrow[2 * FINE:4 * FINE])
-    third[...] = spread(narrow[4 * FINE:6 * FINE], ROWS)
 
 
 def bank_kernel(blocks, cutoff, bank, gathered):
     rank = lax.axis_index("tm")
     devices, _, count, width = blocks.shape
+    shape = (count, count)
+    same = lax.broadcasted_iota(jnp.int32, shape, 0) == lax.broadcasted_iota(jnp.int32, shape, 1)
+    column = jnp.sum(jnp.where(same, cutoff[...], 0), axis=1, keepdims=True)
+    lane = lax.broadcasted_iota(jnp.int32, (count, LANES), 1)
     for other in range(devices):
         first = (rank ^ other) * (width // LANES)
         for at in range(width // LANES):
             lanes = slice(at * LANES, (at + 1) * LANES)
-            gathered[first + at] = jnp.concatenate([blocks[other, 0, :, lanes], blocks[other, 1, :, lanes]], axis=1)
-    lane = lax.broadcasted_iota(jnp.int32, (ROWS, LANES), 1)
-    row = lax.broadcasted_iota(jnp.int32, (ROWS, LANES), 0)
-    bins = row * LANES + lane
+            keep = lane + (first + at) * LANES < column
+            both = [jnp.where(keep, blocks[other, i, :, lanes].astype(jnp.float32), 0.0) for i in range(2)]
+            gathered[first + at] = jnp.concatenate(both, axis=1).astype(jnp.bfloat16)
     shape = (count * ROWS, count * ROWS)
     to, source = lax.broadcasted_iota(jnp.int32, shape, 0), lax.broadcasted_iota(jnp.int32, shape, 1)
     order = (source == (to % ROWS) * count + to // ROWS).astype(jnp.float32).astype(jnp.bfloat16)
     value = dot(order, gathered[...].reshape(ROWS * count, 2 * LANES))
-    for m in range(count):
-        keep = bins < cutoff[m]
-        rows = slice(m * ROWS, (m + 1) * ROWS)
-        bank[0, m] = jnp.where(keep, value[rows, :LANES], 0.0)
-        bank[1, m] = jnp.where(keep, value[rows, LANES:], 0.0)
-
-
-def forward_kernel(offsets, chunks, first, narrow, broad, spec, sent, record):
+    bank[0] = value[:, :LANES].reshape(count, ROWS, LANES)
+    bank[1] = value[:, LANES:].reshape(count, ROWS, LANES)
+
+
+def forward_kernel(offsets, mine, handed, narrow, broad, spec, sent, record):
     rank = lax.axis_index("tmpl")
-    size = chunks.shape[0] // len(offsets)
+    size = mine.shape[0] // len(offsets)
+    odd = lax.rem(rank, 2) == 1
     for at, offset in enumerate(offsets):
-        record[pl.ds((rank ^ offset) * size, size)] = chunks[at * size:(at + 1) * size]
+        rows = slice(at * size, (at + 1) * size)
+        record[pl.ds(((rank // 2) ^ offset) * size, size)] = jnp.where(odd, mine[rows], handed[rows])
     own = record.shape[0]
     w_low, w_high = broad[:ROWS][None], broad[ROWS:FINE][None]
     fwd_cos, fwd_sin = broad[FINE:2 * FINE][None], broad[2 * FINE:3 * FINE][None]
     second = slice(6 * FINE, 6 * FINE + 2 * LANES)
     parts = GROUP + 1
+    first_high, first_low = halved(narrow[:2 * FINE]), halved(narrow[2 * FINE:4 * FINE])
 
     def group(start, power, last):
         here = record[pl.ds(start, GROUP)]
@@ -173,7 +173,7 @@
             after = record[pl.ds(start + 1, GROUP)]
         both = jnp.concatenate([here * w_low, after * w_high], axis=1)
         high, low = split(both.reshape(GROUP * FINE, LANES))
-        step = dot(first[0], high) + dot(first[0], low) + dot(first[1], high)
+        step = dot(first_high, high) + dot(first_high, low) + dot(first_low, high)
         re = step[:parts * FINE].reshape(parts, FINE, LANES)
         im = step[parts * FINE:].reshape(parts, FINE, LANES)
         turned = jnp.concatenate([re * fwd_cos + im * fwd_sin, im * fwd_cos - re * fwd_sin], axis=2)
@@ -203,12 +203,15 @@
 
 
 def filter_kernel(devices, segs, energy, *refs):
-    shares = refs[:devices]
-    spec, bank, third, narrow, broad, out, held = refs[devices:]
+    sent, mine, handed, spec, bank, narrow, broad, out, held = refs
+    odd = lax.rem(lax.axis_index("tmpl"), 2) == 1
+    others = jnp.where(odd, mine[...], handed[...])
+    shares = [sent[...]] + [others[5 * i:5 * (i + 1)] for i in range(devices - 1)]
     own, count = out.shape
     half = GROUP * FINE
     inv_cos, inv_sin = broad[3 * FINE:4 * FINE][None], broad[4 * FINE:5 * FINE][None]
     fourth = slice(6 * FINE + 2 * LANES, 6 * FINE + 4 * LANES)
+    third = spread(narrow[4 * FINE:6 * FINE], ROWS)
     rank = lax.axis_index("tm")
     power = shares[0][0]
     for share in shares[1:]:
@@ -245,7 +248,7 @@
                 c_im = h_re[None] * white_im - h_im[None] * white_re
                 both = jnp.concatenate([c_re, c_im], axis=0).reshape(2 * GROUP * ROWS, LANES)
                 sides.append(both.astype(jnp.bfloat16))
-            section = dot(third[...], jnp.concatenate(sides, axis=1))
+            section = dot(third, jnp.concatenate(sides, axis=1))
             for side in range(2):
                 re = section[:half, side * LANES:(side + 1) * LANES].reshape(GROUP, FINE, LANES)
                 im = section[half:, side * LANES:(side + 1) * LANES].reshape(GROUP, FINE, LANES)
@@ -272,12 +275,23 @@
     return lax.ppermute(array, axis, [(i, i ^ bits) for i in range(lax.axis_size(axis))])
 
 
+def odd_swap(array, tm_bits, tmpl_bits):
+    tm, tmpl = lax.axis_size("tm"), lax.axis_size("tmpl")
+    pairs = [
+        (i * tmpl + j, (i ^ tm_bits) * tmpl + (j ^ tmpl_bits)) for i in range(tm) for j in range(1, tmpl, 2)
+    ]
+    return lax.ppermute(array, ("tm", "tmpl"), pairs)
+
+
+def hand(array, source):
+    return lax.ppermute(array, "tmpl", [(j + source, j + 1 - source) for j in range(0, lax.axis_size("tmpl"), 2)])
+
+
 def on_device(strain, templates, cutoff):
     tm, tmpl = lax.axis_size("tm"), lax.axis_size("tmpl")
     size = strain.shape[0] // HOP
     own = size * tmpl
     count = templates.shape[1]
-    smem = pl.BlockSpec(memory_space=pltpu.SMEM)
     vmem = pl.BlockSpec(memory_space=pltpu.VMEM)
     params = pltpu.CompilerParams(vmem_limit_bytes=40 * 1024 * 1024)
     f32, bf16 = jnp.float32, jnp.bfloat16
@@ -286,32 +300,34 @@
 
     chunk = strain.reshape(size, ROWS, LANES)
     block = templates[None]
-    bits = tmpl // 2
-    arrived = swap(chunk, "tmpl", bits)
-    chunk, block, first, third = pl.pallas_call(
-        prepare_kernel,
-        out_shape=(
-            jax.ShapeDtypeStruct(chunk.shape, f32),
-            jax.ShapeDtypeStruct(block.shape, bf16),
-            jax.ShapeDtypeStruct((2, 2 * (GROUP + 1) * FINE, GROUP * FINE), bf16),
-            jax.ShapeDtypeStruct((2 * GROUP * FINE, 2 * GROUP * ROWS), bf16),
-        ),
-        in_specs=[vmem] * 3,
-        out_specs=(vmem,) * 4,
+    handed = hand(chunk, 0)
+    chunk, block = pl.pallas_call(
+        hold_kernel,
+        out_shape=(jax.ShapeDtypeStruct(chunk.shape, f32), jax.ShapeDtypeStruct(block.shape, bf16)),
+        in_specs=[vmem, vmem],
+        out_specs=(vmem, vmem),
         compiler_params=params,
         cost_estimate=pl.CostEstimate(flops=0, bytes_accessed=3000000, transcendentals=0),
-        name="prepare",
-    )(chunk, block, narrow)
-    chunks, offsets = jnp.concatenate([chunk, arrived], axis=0), [0, bits]
+        name="hold",
+    )(chunk, block)
+    handed, block = lax.optimization_barrier((handed, block))
+    chunks = jnp.concatenate([handed, chunk], axis=0)
+    beside = swap(block, "tm", 1)
+    offsets, bits = [0], tmpl // 2
     while bits > 1:
+        arrived = odd_swap(chunks, 0, bits)
+        if len(offsets) == 1:
+            arrived, beside = lax.optimization_barrier((arrived, beside))
+        chunks = jnp.concatenate([chunks, arrived], axis=0)
+        offsets = offsets + [o ^ (bits // 2) for o in offsets]
         bits //= 2
-        chunks = jnp.concatenate([chunks, swap(chunks, "tmpl", bits)], axis=0)
-        offsets = offsets + [o ^ bits for o in offsets]
-    bits = 1
+    block = jnp.concatenate([block, beside], axis=0)
+    bits = 2
     while bits < tm:
         block = jnp.concatenate([block, swap(block, "tm", bits)], axis=0)
         bits *= 2
 
+    handed, block = lax.optimization_barrier((hand(chunks, 1), block))
     spec, sent = pl.pallas_call(
         functools.partial(forward_kernel, tuple(offsets)),
         out_shape=(
@@ -323,27 +339,27 @@
         scratch_shapes=[pltpu.VMEM((own, ROWS, LANES), f32)],
         compiler_params=params,
         name="forward",
-    )(chunks, first, narrow, broad)
-    shares = [sent] + [swap(sent, "tm", other) for other in range(1, tm)]
+    )(chunks, handed, narrow, broad)
+    shares = jnp.concatenate([odd_swap(sent, other, 0) for other in range(1, tm)], axis=0)
     bank = pl.pallas_call(
         bank_kernel,
         out_shape=jax.ShapeDtypeStruct((2, count, ROWS, LANES), f32),
-        in_specs=[vmem, smem],
+        in_specs=[vmem, vmem],
         out_specs=vmem,
         scratch_shapes=[pltpu.VMEM((ROWS, count, 2 * LANES), bf16)],
         compiler_params=params,
         cost_estimate=pl.CostEstimate(flops=0, bytes_accessed=2500000, transcendentals=0),
         name="bank",
-    )(block, cutoff)
+    )(block, cutoff.reshape(1, count))
     return pl.pallas_call(
         functools.partial(filter_kernel, tm, own * tm, energy),
         out_shape=jax.ShapeDtypeStruct((own, count), f32),
-        in_specs=[vmem] * (tm + 5),
+        in_specs=[vmem] * 7,
         out_specs=vmem,
         scratch_shapes=[pltpu.VMEM((tm, 2, ROWS, LANES), f32)],
         compiler_params=params,
         name="matched_filter",
-    )(*shares, spec, bank, third, narrow, broad)
+    )(sent, shares, hand(shares, 1), spec, bank, narrow, broad)
 
 
 def solution(mesh):

time: 24.3 us -> 35.6 us (1.47)
  waiting for transfers between devices: 5.1 us -> 16.8 us
  local copies, waits for them, and re-layouts: 2.45 us -> 1.49 us
  starting transfers between devices: 12.3 us -> 13 us
  Pallas kernels: 4.04 us -> 3.63 us
    ppermute x0 -> x8, waiting for transfers between devices: none -> 14.1 us  [the longest x3 14.1 us: hand(): lax.ppermute(array, 'tmpl', [(j + source, j + 1 - source) for j in range(...]
    ppermute x0 -> x8, starting transfers between devices: none -> 8.5 us  [the longest x3 5.19 us: hand(): lax.ppermute(array, 'tmpl', [(j + source, j + 1 - source) for j in range(...]
    ppermute x8 -> x2, starting transfers between devices: 12.3 us -> 4.5 us  [swap(): lax.ppermute(array, axis, [(i, i ^ bits) for i in range(lax.axis_size(axi...]
    ppermute x8 -> x2, waiting for transfers between devices: 5.1 us -> 2.69 us  [swap(): lax.ppermute(array, axis, [(i, i ^ bits) for i in range(lax.axis_size(axi...]
    unnamed x12 -> x15, local copies, waits for them, and re-layouts: 2.45 us -> 1.48 us
    pallas_call x1, Pallas kernels: 0.75 us -> 0.29 us  [on_device(): pl.pallas_call(bank_kernel, out_shape=jax.ShapeDtypeStruct((2, count, ROW...]
  transfers between devices with their start and end apart: 8 -> 10, of which waited for: 5 -> 4; matrix products, arithmetic and copies ran while one was open for 0% -> 0% of each run, Pallas kernels for 7% -> 1%
where the time goes in v10:
time: 35.6 us; the launch traced here: 35.2 us
  waiting for transfers between devices  16.8 us (47%)
  starting transfers between devices  13 us (37%)
  Pallas kernels  3.63 us (10%)
  local copies, waits for them, and re-layouts  1.49 us (4%)
    ppermute x3, waiting for transfers between devices, hand(): lax.ppermute(array, 'tmpl', [(j + source, j + 1 - source) for j in range(...  14.1 us
    ppermute x3, starting transfers between devices, hand(): lax.ppermute(array, 'tmpl', [(j + source, j + 1 - source) for j in range(...  5.19 us
    ppermute x2, starting transfers between devices, swap(): lax.ppermute(array, axis, [(i, i ^ bits) for i in range(lax.axis_size(axi...  4.5 us
    ppermute x5, starting transfers between devices, odd_swap(): return lax.ppermute(array, ('tm', 'tmpl'), pairs)  3.3 us
    ppermute x2, waiting for transfers between devices, swap(): lax.ppermute(array, axis, [(i, i ^ bits) for i in range(lax.axis_size(axi...  2.69 us
    pallas_call x1, Pallas kernels, on_device(): pl.pallas_call(functools.partial(filter_kernel, tm, own * tm, energy), ou...  2.43 us
    unnamed x15, local copies, waits for them, and re-layouts  1.48 us
    pallas_call x1, Pallas kernels, on_device(): pl.pallas_call(functools.partial(forward_kernel, tuple(offsets)), out_sha...  0.9 us
  transfers between devices with their start and end apart: 10, of which 4 were waited for; matrix products, arithmetic and copies ran while one was open for 0% of the time, Pallas kernels for 1%

profile of v10, /device:TPU:0, one launch (start us, length us, event | category | flops | bytes accessed | tf_op | source)
XLA Modules:
  0.0 35.2 jit_solution(7051749525103396562)
XLA Ops:
  0.0 0.0 copy-start
  0.0 2.5 %collective-permute-start = (f32[1,16,128]{2,1,0:T(8,128)}, f32[1,16,128]{2,1,0:T(8,128)S(1)}, u32[]{:S(2)}, u32[]{:S(2)}) collective-permute-start(f32[1,16,128]{2,1,0:T(8,128)} %bitcast.4), channel_id=1, source_target_pairs={{0,1},{2,3},{4,5},{6,7},{8,9},{10,11},{12,13},{14,15},{16,17},{18,... | collective-permute-start | bytes 24584 | tf_op jit(solution)/shard_map/ppermute | solution.py:287
  2.5 0.0 copy-start.2
  2.5 0.7 %copy-done.2 = bf16[2,16,512]{2,1,0:T(8,128)(2,1)S(1)} copy-done((bf16[2,16,512]{2,1,0:T(8,128)(2,1)S(1)}, bf16[2,16,512]{2,1,0:T(8,128)(2,1)}, u32[]{:S(2)}) %copy-start.2) | copy-done | bytes 32792
  3.2 0.0 copy-start.3
  3.2 0.7 %copy-done.3 = f32[2048]{0:T(1024)S(1)} copy-done((f32[2048]{0:T(1024)S(1)}, f32[2048]{0:T(1024)}, u32[]{:S(2)}) %copy-start.3) | copy-done | bytes 8216
  3.9 0.0 collective-permute-done
  4.0 0.7 %collective-permute-start.1 = (f32[2,16,128]{2,1,0:T(8,128)S(1)}, f32[2,16,128]{2,1,0:T(8,128)S(1)}, u32[]{:S(2)}, u32[]{:S(2)}) collective-permute-start(f32[2,16,128]{2,1,0:T(8,128)S(1)} %pad_maximum_fusion.3), channel_id=1, source_target_pairs={{1,5},{3,7},{5,1},{7,3},{9,13},{11,15},{13,9},{15,11},{17,21},{19,... | collective-permute-start | bytes 49160 | tf_op jit(solution)/shard_map/ppermute | solution.py:283
  4.6 2.4 %collective-permute-start.2 = (bf16[1,2,16,512]{3,2,1,0:T(8,128)(2,1)S(1)}, bf16[1,2,16,512]{3,2,1,0:T(8,128)(2,1)S(1)}, u32[]{:S(2)}, u32[]{:S(2)}) collective-permute-start(bf16[1,2,16,512]{3,2,1,0:T(8,128)(2,1)S(1)} %get-tuple-element.18), channel_id=1, source_target_pairs={{0,8},{8,0},{16,24},{24,16},{1,9},{9,1},{17,25},{25,17},{2,10},{10... | collective-permute-start | bytes 98312 | tf_op jit(solution)/shard_map/ppermute | solution.py:275
  7.0 0.0 collective-permute-done.1
  7.0 1.9 %collective-permute-done.2 = bf16[1,2,16,512]{3,2,1,0:T(8,128)(2,1)S(1)} collective-permute-done((bf16[1,2,16,512]{3,2,1,0:T(8,128)(2,1)S(1)}, bf16[1,2,16,512]{3,2,1,0:T(8,128)(2,1)S(1)}, u32[]{:S(2)}, u32[]{:S(2)}) %collective-permute-start.2) | collective-permute-done | bytes 32800 | tf_op jit(solution)/shard_map/ppermute | solution.py:275
  8.9 0.7 %collective-permute-start.3 = (f32[4,16,128]{2,1,0:T(8,128)S(1)}, f32[4,16,128]{2,1,0:T(8,128)S(1)}, u32[]{:S(2)}, u32[]{:S(2)}) collective-permute-start(f32[4,16,128]{2,1,0:T(8,128)S(1)} %pad_maximum_fusion.2), channel_id=1, source_target_pairs={{1,3},{3,1},{5,7},{7,5},{9,11},{11,9},{13,15},{15,13},{17,19},{19,... | collective-permute-start | bytes 98312 | tf_op jit(solution)/shard_map/ppermute | solution.py:283
  9.6 2.1 %collective-permute-start.5 = (bf16[2,2,16,512]{3,2,1,0:T(8,128)(2,1)S(1)}, bf16[2,2,16,512]{3,2,1,0:T(8,128)(2,1)S(1)}, u32[]{:S(2)}, u32[]{:S(2)}) collective-permute-start(bf16[2,2,16,512]{3,2,1,0:T(8,128)(2,1)S(1)} %pad_maximum_fusion.1), channel_id=1, source_target_pairs={{0,16},{8,24},{16,0},{24,8},{1,17},{9,25},{17,1},{25,9},{2,18},{10... | collective-permute-start | bytes 196616 | tf_op jit(solution)/shard_map/ppermute | solution.py:275
  11.7 0.0 collective-permute-done.3
  11.7 0.0 copy-start.1
  11.7 1.4 %collective-permute-start.4 = (f32[8,16,128]{2,1,0:T(8,128)S(1)}, f32[8,16,128]{2,1,0:T(8,128)S(1)}, u32[]{:S(2)}, u32[]{:S(2)}) collective-permute-start(f32[8,16,128]{2,1,0:T(8,128)S(1)} %constant_dynamic-update-slice_fusion.mine), channel_id=1, source_target_pairs={{1,0},{3,2},{5,4},{7,6},{9,8},{11,10},{13,12},{15,14},{17,16},{19,... | collective-permute-start | bytes 196616 | tf_op jit(solution)/shard_map/ppermute | solution.py:287
  13.2 0.8 %collective-permute-done.5 = bf16[2,2,16,512]{3,2,1,0:T(8,128)(2,1)S(1)} collective-permute-done((bf16[2,2,16,512]{3,2,1,0:T(8,128)(2,1)S(1)}, bf16[2,2,16,512]{3,2,1,0:T(8,128)(2,1)S(1)}, u32[]{:S(2)}, u32[]{:S(2)}) %collective-permute-start.5) | collective-permute-done | bytes 65568 | tf_op jit(solution)/shard_map/ppermute | solution.py:275
  14.0 4.5 %collective-permute-done.4.handed = f32[8,16,128]{2,1,0:T(8,128)S(1)} collective-permute-done((f32[8,16,128]{2,1,0:T(8,128)S(1)}, f32[8,16,128]{2,1,0:T(8,128)S(1)}, u32[]{:S(2)}, u32[]{:S(2)}) %collective-permute-start.4) | collective-permute-done | bytes 65568 | tf_op jit(solution)/shard_map/ppermute | solution.py:287
  18.5 0.0 copy-done
  18.5 0.0 copy-done.1
  18.5 0.9 %forward.1 = (f32[2,8,16,128]{3,2,1,0:T(8,128)S(1)}, f32[5,16,128]{2,1,0:T(8,128)S(1)}) custom-call(f32[8,16,128]{2,1,0:T(8,128)S(1)} %constant_dynamic-update-slice_fusion.mine, f32[8,16,128]{2,1,0:T(8,128)S(1)} %collective-permute-done.4.handed, bf16[704,256]{1,0:T(8,128)(2,1)S(1)} %copy-done, f32[160,128]{1,0:T(8,128)S(1)} %copy-done.1), custom_call_target="tpu_custom_call" | custom-call | tf_op jit(solution)/shard_map/forward/pallas_call | solution.py:331
  19.4 0.7 %collective-permute-start.6 = (f32[5,16,128]{2,1,0:T(8,128)S(1)}, f32[5,16,128]{2,1,0:T(8,128)S(1)}, u32[]{:S(2)}, u32[]{:S(2)}) collective-permute-start(f32[5,16,128]{2,1,0:T(8,128)S(1)} %get-tuple-element.22.refs_0_), channel_id=1, source_target_pairs={{1,9},{3,11},{5,13},{7,15},{9,1},{11,3},{13,5},{15,7},{17,25},{19,... | collective-permute-start | bytes 122888 | tf_op jit(solution)/shard_map/ppermute | solution.py:283
  20.1 0.7 %collective-permute-start.8 = (f32[5,16,128]{2,1,0:T(8,128)S(1)}, f32[5,16,128]{2,1,0:T(8,128)S(1)}, u32[]{:S(2)}, u32[]{:S(2)}) collective-permute-start(f32[5,16,128]{2,1,0:T(8,128)S(1)} %get-tuple-element.22.refs_0_), channel_id=1, source_target_pairs={{1,25},{3,27},{5,29},{7,31},{9,17},{11,19},{13,21},{15,23},{17,9},... | collective-permute-start | bytes 122888 | tf_op jit(solution)/shard_map/ppermute | solution.py:283
  20.8 0.7 %collective-permute-start.7 = (f32[5,16,128]{2,1,0:T(8,128)S(1)}, f32[5,16,128]{2,1,0:T(8,128)S(1)}, u32[]{:S(2)}, u32[]{:S(2)}) collective-permute-start(f32[5,16,128]{2,1,0:T(8,128)S(1)} %get-tuple-element.22.refs_0_), channel_id=1, source_target_pairs={{1,17},{3,19},{5,21},{7,23},{9,25},{11,27},{13,29},{15,31},{17,1},... | collective-permute-start | bytes 122888 | tf_op jit(solution)/shard_map/ppermute | solution.py:283
  21.5 0.0 collective-permute-done.6
  21.5 0.0 collective-permute-done.7
  21.5 0.0 collective-permute-done.8
  21.5 0.0 copy-start.4
  21.5 1.3 %collective-permute-start.9 = (f32[15,16,128]{2,1,0:T(8,128)S(1)}, f32[15,16,128]{2,1,0:T(8,128)S(1)}, u32[]{:S(2)}, u32[]{:S(2)}) collective-permute-start(f32[15,16,128]{2,1,0:T(8,128)S(1)} %constant_dynamic-update-slice_fusion.4.refs_1_), channel_id=1, source_target_pairs={{1,0},{3,2},{5,4},{7,6},{9,8},{11,10},{13,12},{15,14},{17,16},{19,... | collective-permute-start | bytes 368648 | tf_op jit(solution)/shard_map/ppermute | solution.py:287
  22.8 0.0 copy-done.4
  22.9 0.3 bank.1.refs_4_
  23.2 9.6 %collective-permute-done.9.refs_2_ = f32[15,16,128]{2,1,0:T(8,128)S(1)} collective-permute-done((f32[15,16,128]{2,1,0:T(8,128)S(1)}, f32[15,16,128]{2,1,0:T(8,128)S(1)}, u32[]{:S(2)}, u32[]{:S(2)}) %collective-permute-start.9) | collective-permute-done | bytes 122912 | tf_op jit(solution)/shard_map/ppermute | solution.py:287
  32.7 2.4 %matched_filter.1 = f32[8,16]{1,0:T(8,128)} custom-call(f32[5,16,128]{2,1,0:T(8,128)S(1)} %get-tuple-element.22.refs_0_, f32[15,16,128]{2,1,0:T(8,128)S(1)} %constant_dynamic-update-slice_fusion.4.refs_1_, f32[15,16,128]{2,1,0:T(8,128)S(1)} %collective-permute-done.9.refs_2_, f32[2,8,16,128]{3,2,1,0:T(8,128)S(1)} %get-tuple-element.23.refs_3_, ...), custom_call_target="tpu_custom_call" | custom-call | tf_op jit(solution)/shard_map/matched_filter/pallas_call | solution.py:354
  (12 shorter events, 0.1 us)
Async XLA Ops:
  0.0 18.5 %copy-start = (bf16[704,256]{1,0:T(8,128)(2,1)S(1)}, bf16[704,256]{1,0:T(8,128)(2,1)}, u32[]{:S(2)}) copy-start(bf16[704,256]{1,0:T(8,128)(2,1)} %constant.4.clone.narrow.refs_5_) | copy-start | bytes 1081348
  0.0 3.9 %collective-permute-start = (f32[1,16,128]{2,1,0:T(8,128)}, f32[1,16,128]{2,1,0:T(8,128)S(1)}, u32[]{:S(2)}, u32[]{:S(2)}) collective-permute-start(f32[1,16,128]{2,1,0:T(8,128)} %bitcast.4), channel_id=1, source_target_pairs={{0,1},{2,3},{4,5},{6,7},{8,9},{10,11},{12,13},{14,15},{16,17},{18,... | collective-permute-start | bytes 24584 | tf_op jit(solution)/shard_map/ppermute | solution.py:287
  2.5 0.8 %copy-start.2 = (bf16[2,16,512]{2,1,0:T(8,128)(2,1)S(1)}, bf16[2,16,512]{2,1,0:T(8,128)(2,1)}, u32[]{:S(2)}) copy-start(bf16[2,16,512]{2,1,0:T(8,128)(2,1)} %param.6) | copy-start | bytes 98308
  3.2 0.7 %copy-start.3 = (f32[2048]{0:T(1024)S(1)}, f32[2048]{0:T(1024)}, u32[]{:S(2)}) copy-start(f32[2048]{0:T(1024)} %param.5) | copy-start | bytes 24580
  4.0 3.1 %collective-permute-start.1 = (f32[2,16,128]{2,1,0:T(8,128)S(1)}, f32[2,16,128]{2,1,0:T(8,128)S(1)}, u32[]{:S(2)}, u32[]{:S(2)}) collective-permute-start(f32[2,16,128]{2,1,0:T(8,128)S(1)} %pad_maximum_fusion.3), channel_id=1, source_target_pairs={{1,5},{3,7},{5,1},{7,3},{9,13},{11,15},{13,9},{15,11},{17,21},{19,... | collective-permute-start | bytes 49160 | tf_op jit(solution)/shard_map/ppermute | solution.py:283
  4.6 4.3 %collective-permute-start.2 = (bf16[1,2,16,512]{3,2,1,0:T(8,128)(2,1)S(1)}, bf16[1,2,16,512]{3,2,1,0:T(8,128)(2,1)S(1)}, u32[]{:S(2)}, u32[]{:S(2)}) collective-permute-start(bf16[1,2,16,512]{3,2,1,0:T(8,128)(2,1)S(1)} %get-tuple-element.18), channel_id=1, source_target_pairs={{0,8},{8,0},{16,24},{24,16},{1,9},{9,1},{17,25},{25,17},{2,10},{10... | collective-permute-start | bytes 98312 | tf_op jit(solution)/shard_map/ppermute | solution.py:275
  8.9 2.8 %collective-permute-start.3 = (f32[4,16,128]{2,1,0:T(8,128)S(1)}, f32[4,16,128]{2,1,0:T(8,128)S(1)}, u32[]{:S(2)}, u32[]{:S(2)}) collective-permute-start(f32[4,16,128]{2,1,0:T(8,128)S(1)} %pad_maximum_fusion.2), channel_id=1, source_target_pairs={{1,3},{3,1},{5,7},{7,5},{9,11},{11,9},{13,15},{15,13},{17,19},{19,... | collective-permute-start | bytes 98312 | tf_op jit(solution)/shard_map/ppermute | solution.py:283
  9.6 4.4 %collective-permute-start.5 = (bf16[2,2,16,512]{3,2,1,0:T(8,128)(2,1)S(1)}, bf16[2,2,16,512]{3,2,1,0:T(8,128)(2,1)S(1)}, u32[]{:S(2)}, u32[]{:S(2)}) collective-permute-start(bf16[2,2,16,512]{3,2,1,0:T(8,128)(2,1)S(1)} %pad_maximum_fusion.1), channel_id=1, source_target_pairs={{0,16},{8,24},{16,0},{24,8},{1,17},{9,25},{17,1},{25,9},{2,18},{10... | collective-permute-start | bytes 196616 | tf_op jit(solution)/shard_map/ppermute | solution.py:275
  11.7 6.8 %copy-start.1 = (f32[160,128]{1,0:T(8,128)S(1)}, f32[160,128]{1,0:T(8,128)}, u32[]{:S(2)}) copy-start(f32[160,128]{1,0:T(8,128)} %constant.5.clone.broad.refs_6_) | copy-start | bytes 245764
  11.7 6.8 %collective-permute-start.4 = (f32[8,16,128]{2,1,0:T(8,128)S(1)}, f32[8,16,128]{2,1,0:T(8,128)S(1)}, u32[]{:S(2)}, u32[]{:S(2)}) collective-permute-start(f32[8,16,128]{2,1,0:T(8,128)S(1)} %constant_dynamic-update-slice_fusion.mine), channel_id=1, source_target_pairs={{1,0},{3,2},{5,4},{7,6},{9,8},{11,10},{13,12},{15,14},{17,16},{19,... | collective-permute-start | bytes 196616 | tf_op jit(solution)/shard_map/ppermute | solution.py:287
  19.4 2.0 %collective-permute-start.6 = (f32[5,16,128]{2,1,0:T(8,128)S(1)}, f32[5,16,128]{2,1,0:T(8,128)S(1)}, u32[]{:S(2)}, u32[]{:S(2)}) collective-permute-start(f32[5,16,128]{2,1,0:T(8,128)S(1)} %get-tuple-element.22.refs_0_), channel_id=1, source_target_pairs={{1,9},{3,11},{5,13},{7,15},{9,1},{11,3},{13,5},{15,7},{17,25},{19,... | collective-permute-start | bytes 122888 | tf_op jit(solution)/shard_map/ppermute | solution.py:283
  20.1 1.4 %collective-permute-start.8 = (f32[5,16,128]{2,1,0:T(8,128)S(1)}, f32[5,16,128]{2,1,0:T(8,128)S(1)}, u32[]{:S(2)}, u32[]{:S(2)}) collective-permute-start(f32[5,16,128]{2,1,0:T(8,128)S(1)} %get-tuple-element.22.refs_0_), channel_id=1, source_target_pairs={{1,25},{3,27},{5,29},{7,31},{9,17},{11,19},{13,21},{15,23},{17,9},... | collective-permute-start | bytes 122888 | tf_op jit(solution)/shard_map/ppermute | solution.py:283
  20.8 0.7 %collective-permute-start.7 = (f32[5,16,128]{2,1,0:T(8,128)S(1)}, f32[5,16,128]{2,1,0:T(8,128)S(1)}, u32[]{:S(2)}, u32[]{:S(2)}) collective-permute-start(f32[5,16,128]{2,1,0:T(8,128)S(1)} %get-tuple-element.22.refs_0_), channel_id=1, source_target_pairs={{1,17},{3,19},{5,21},{7,23},{9,25},{11,27},{13,29},{15,31},{17,1},... | collective-permute-start | bytes 122888 | tf_op jit(solution)/shard_map/ppermute | solution.py:283
  21.5 1.3 %copy-start.4 = (s32[16]{0:T(128)S(1)}, s32[16]{0:T(128)}, u32[]{:S(2)}) copy-start(s32[16]{0:T(128)} %param.7) | copy-start | bytes 196
  21.5 11.2 %collective-permute-start.9 = (f32[15,16,128]{2,1,0:T(8,128)S(1)}, f32[15,16,128]{2,1,0:T(8,128)S(1)}, u32[]{:S(2)}, u32[]{:S(2)}) collective-permute-start(f32[15,16,128]{2,1,0:T(8,128)S(1)} %constant_dynamic-update-slice_fusion.4.refs_1_), channel_id=1, source_target_pairs={{1,0},{3,2},{5,4},{7,6},{9,8},{11,10},{13,12},{15,14},{17,16},{19,... | collective-permute-start | bytes 368648 | tf_op jit(solution)/shard_map/ppermute | solution.py:287

commit v11 on v9

--- a/solution.py
+++ b/solution.py
@@ -222,9 +222,7 @@
                 result = jnp.where(column == 2 * step + side, value, result)
             return result
 
-        result = lax.fori_loop(
-            0, count // 4, lambda i, r: pair_of(2 * i + 1, pair_of(2 * i, r)), jnp.zeros((GROUP, LANES), jnp.float32)
-        )
+        result = repeat(count // 2, pair_of, jnp.zeros((GROUP, LANES), jnp.float32))
         out[pl.ds(number * GROUP, GROUP)] = result[:, :count]
         return carry
 
@@ -247,7 +245,7 @@
 
     copies = pl.pallas_call(
         pack_kernel,
-        out_shape=jax.ShapeDtypeStruct((devices, size * ROWS, LANES), f32),
+        out_shape=pltpu.VMEM((devices, size * ROWS, LANES), f32),
         in_specs=[vmem],
         out_specs=vmem,
         compiler_params=params,

time: 24.9 us -> 23.5 us (0.944)
  Pallas kernels: 6.49 us -> 5.16 us
    pallas_call x1, Pallas kernels: 5.48 us -> 4.15 us  [on_device(): pl.pallas_call(functools.partial(filter_kernel, energy), out_shape=jax.Sh...]
where the time goes in v11:
time: 23.5 us; the launch traced here: 23.3 us
  starting transfers between devices  10.9 us (46%)
  waiting for transfers between devices  6.5 us (28%)
  Pallas kernels  5.16 us (22%)
  local copies, waits for them, and re-layouts  0.71 us (3%)
    all_to_all x1, starting transfers between devices, on_device(): lax.all_to_all(copies, ('tm', 'tmpl'), split_axis=0, concat_axis=0, tiled...  7.3 us
    pallas_call x1, Pallas kernels, on_device(): pl.pallas_call(functools.partial(filter_kernel, energy), out_shape=jax.Sh...  4.15 us
    ppermute x3, waiting for transfers between devices, swap(): lax.ppermute(array, axis, [(i, i ^ bits) for i in range(lax.axis_size(axi...  3.75 us
    ppermute x3, starting transfers between devices, swap(): lax.ppermute(array, axis, [(i, i ^ bits) for i in range(lax.axis_size(axi...  3.55 us
    all_to_all x1, waiting for transfers between devices, on_device(): lax.all_to_all(copies, ('tm', 'tmpl'), split_axis=0, concat_axis=0, tiled...  2.75 us
    pallas_call x1, Pallas kernels, on_device(): pl.pallas_call(pack_kernel, out_shape=pltpu.VMEM((devices, size * ROWS, L...  0.72 us
    unnamed x10, local copies, waits for them, and re-layouts  0.71 us
  transfers between devices with their start and end apart: 4, of which 4 were waited for; matrix products, arithmetic and copies ran while one was open for 0% of the time, Pallas kernels for 1%

profile of v11, /device:TPU:0, one launch (start us, length us, event | category | flops | bytes accessed | tf_op | source)
XLA Modules:
  0.0 23.3 jit_solution(8643981807696027132)
XLA Ops:
  0.0 0.0 copy-start.3
  0.0 0.7 %copy-done.3 = f32[2048]{0:T(1024)S(1)} copy-done((f32[2048]{0:T(1024)S(1)}, f32[2048]{0:T(1024)}, u32[]{:S(2)}) %copy-start.3) | copy-done | bytes 8216
  0.7 0.7 %pack.1 = f32[32,16,128]{2,1,0:T(8,128)} custom-call(f32[16,128]{1,0:T(8,128)S(1)} %bitcast.2), custom_call_target="tpu_custom_call" | custom-call | tf_op jit(solution)/shard_map/pack/pallas_call | solution.py:246
  1.4 0.0 copy-start.2
  1.4 0.0 copy-start
  1.4 7.3 %all-to-all-start = ((f32[32,16,128]{2,1,0:T(8,128)}), f32[32,16,128]{2,1,0:T(8,128)S(1)}, u32[]{:S(2)}, u32[]{:S(2)}) async-start(f32[32,16,128]{2,1,0:T(8,128)} %pack.1), calls=%async_computation | async-start | bytes 524288 | tf_op jit(solution)/shard_map/all_to_all | solution.py:255
  8.7 0.0 copy-done.2
  8.7 0.0 copy-start.4
  8.7 2.7 %collective-permute-start.2 = (bf16[2,16,512]{2,1,0:T(8,128)(2,1)S(1)}, bf16[2,16,512]{2,1,0:T(8,128)(2,1)S(1)}, u32[]{:S(2)}, u32[]{:S(2)}) collective-permute-start(bf16[2,16,512]{2,1,0:T(8,128)(2,1)S(1)} %copy-done.2), channel_id=1, source_target_pairs={{0,24},{8,16},{16,8},{24,0},{1,25},{9,17},{17,9},{25,1},{2,26},{10... | collective-permute-start | bytes 98312 | tf_op jit(solution)/shard_map/ppermute | solution.py:233
  11.5 0.6 %collective-permute-start.1 = (bf16[2,16,512]{2,1,0:T(8,128)(2,1)S(1)}, bf16[2,16,512]{2,1,0:T(8,128)(2,1)S(1)}, u32[]{:S(2)}, u32[]{:S(2)}) collective-permute-start(bf16[2,16,512]{2,1,0:T(8,128)(2,1)S(1)} %copy-done.2), channel_id=1, source_target_pairs={{0,16},{8,24},{16,0},{24,8},{1,17},{9,25},{17,1},{25,9},{2,18},{10... | collective-permute-start | bytes 98312 | tf_op jit(solution)/shard_map/ppermute | solution.py:233
  12.0 0.3 %collective-permute-start = (bf16[2,16,512]{2,1,0:T(8,128)(2,1)S(1)}, bf16[2,16,512]{2,1,0:T(8,128)(2,1)S(1)}, u32[]{:S(2)}, u32[]{:S(2)}) collective-permute-start(bf16[2,16,512]{2,1,0:T(8,128)(2,1)S(1)} %copy-done.2), channel_id=1, source_target_pairs={{0,8},{8,0},{16,24},{24,16},{1,9},{9,1},{17,25},{25,17},{2,10},{10... | collective-permute-start | bytes 98312 | tf_op jit(solution)/shard_map/ppermute | solution.py:233
  12.3 2.1 %collective-permute-done.2.refs_3_ = bf16[2,16,512]{2,1,0:T(8,128)(2,1)S(1)} collective-permute-done((bf16[2,16,512]{2,1,0:T(8,128)(2,1)S(1)}, bf16[2,16,512]{2,1,0:T(8,128)(2,1)S(1)}, u32[]{:S(2)}, u32[]{:S(2)}) %collective-permute-start.2) | collective-permute-done | bytes 32800 | tf_op jit(solution)/shard_map/ppermute | solution.py:233
  14.4 1.3 %collective-permute-done.1.refs_2_ = bf16[2,16,512]{2,1,0:T(8,128)(2,1)S(1)} collective-permute-done((bf16[2,16,512]{2,1,0:T(8,128)(2,1)S(1)}, bf16[2,16,512]{2,1,0:T(8,128)(2,1)S(1)}, u32[]{:S(2)}, u32[]{:S(2)}) %collective-permute-start.1) | collective-permute-done | bytes 32800 | tf_op jit(solution)/shard_map/ppermute | solution.py:233
  15.8 0.3 %collective-permute-done.refs_1_ = bf16[2,16,512]{2,1,0:T(8,128)(2,1)S(1)} collective-permute-done((bf16[2,16,512]{2,1,0:T(8,128)(2,1)S(1)}, bf16[2,16,512]{2,1,0:T(8,128)(2,1)S(1)}, u32[]{:S(2)}, u32[]{:S(2)}) %collective-permute-start) | collective-permute-done | bytes 32800 | tf_op jit(solution)/shard_map/ppermute | solution.py:233
  16.1 0.0 copy-done.4
  16.1 0.0 copy-start.1
  16.1 0.3 %bank.1 = f32[2,16,16,128]{3,2,1,0:T(8,128)S(1)} custom-call(bf16[2,16,512]{2,1,0:T(8,128)(2,1)S(1)} %copy-done.2, bf16[2,16,512]{2,1,0:T(8,128)(2,1)S(1)} %collective-permute-done.refs_1_, bf16[2,16,512]{2,1,0:T(8,128)(2,1)S(1)} %collective-permute-done.1.refs_2_, bf16[2,16,512]{2,1,0:T(8,128)(2,1)S(1)} %collective-permute-done.2.refs_3_, s32[1,16]{1,0:T(1,128)S(1)} %bitcast.3), custom_call_target="tpu_custom_call" | custom-call | bytes 2500000 | tf_op jit(solution)/shard_map/bank/pallas_call | solution.py:258
  16.4 2.7 %all-to-all-done.record = f32[32,16,128]{2,1,0:T(8,128)S(1)} async-done(((f32[32,16,128]{2,1,0:T(8,128)}), f32[32,16,128]{2,1,0:T(8,128)S(1)}, u32[]{:S(2)}, u32[]{:S(2)}) %all-to-all-start) | async-done | bytes 262176 | tf_op jit(solution)/shard_map/all_to_all | solution.py:255
  19.1 0.0 copy-done
  19.1 0.0 copy-done.1
  19.1 4.2 %matched_filter.1 = f32[8,16]{1,0:T(8,128)} custom-call(f32[32,16,128]{2,1,0:T(8,128)S(1)} %all-to-all-done.record, f32[2,16,16,128]{3,2,1,0:T(8,128)S(1)} %bank.1, bf16[704,256]{1,0:T(8,128)(2,1)S(1)} %copy-done, f32[160,128]{1,0:T(8,128)S(1)} %copy-done.1), custom_call_target="tpu_custom_call" | custom-call | tf_op jit(solution)/shard_map/matched_filter/pallas_call | solution.py:269
Async XLA Ops:
  0.0 0.7 %copy-start.3 = (f32[2048]{0:T(1024)S(1)}, f32[2048]{0:T(1024)}, u32[]{:S(2)}) copy-start(f32[2048]{0:T(1024)} %param.5) | copy-start | bytes 24580
  1.4 7.3 %copy-start.2 = (bf16[2,16,512]{2,1,0:T(8,128)(2,1)S(1)}, bf16[2,16,512]{2,1,0:T(8,128)(2,1)}, u32[]{:S(2)}) copy-start(bf16[2,16,512]{2,1,0:T(8,128)(2,1)} %refs_0_) | copy-start | bytes 98308
  1.4 17.7 %copy-start = (bf16[704,256]{1,0:T(8,128)(2,1)S(1)}, bf16[704,256]{1,0:T(8,128)(2,1)}, u32[]{:S(2)}) copy-start(bf16[704,256]{1,0:T(8,128)(2,1)} %constant.4.clone.narrow) | copy-start | bytes 1081348
  1.4 17.7 %all-to-all-start = ((f32[32,16,128]{2,1,0:T(8,128)}), f32[32,16,128]{2,1,0:T(8,128)S(1)}, u32[]{:S(2)}, u32[]{:S(2)}) async-start(f32[32,16,128]{2,1,0:T(8,128)} %pack.1), calls=%async_computation | async-start | bytes 524288 | tf_op jit(solution)/shard_map/all_to_all | solution.py:255
  8.7 7.3 %copy-start.4 = (s32[16]{0:T(128)S(1)}, s32[16]{0:T(128)}, u32[]{:S(2)}) copy-start(s32[16]{0:T(128)} %param.7) | copy-start | bytes 196
  8.7 5.7 %collective-permute-start.2 = (bf16[2,16,512]{2,1,0:T(8,128)(2,1)S(1)}, bf16[2,16,512]{2,1,0:T(8,128)(2,1)S(1)}, u32[]{:S(2)}, u32[]{:S(2)}) collective-permute-start(bf16[2,16,512]{2,1,0:T(8,128)(2,1)S(1)} %copy-done.2), channel_id=1, source_target_pairs={{0,24},{8,16},{16,8},{24,0},{1,25},{9,17},{17,9},{25,1},{2,26},{10... | collective-permute-start | bytes 98312 | tf_op jit(solution)/shard_map/ppermute | solution.py:233
  11.5 4.3 %collective-permute-start.1 = (bf16[2,16,512]{2,1,0:T(8,128)(2,1)S(1)}, bf16[2,16,512]{2,1,0:T(8,128)(2,1)S(1)}, u32[]{:S(2)}, u32[]{:S(2)}) collective-permute-start(bf16[2,16,512]{2,1,0:T(8,128)(2,1)S(1)} %copy-done.2), channel_id=1, source_target_pairs={{0,16},{8,24},{16,0},{24,8},{1,17},{9,25},{17,1},{25,9},{2,18},{10... | collective-permute-start | bytes 98312 | tf_op jit(solution)/shard_map/ppermute | solution.py:233
  12.0 4.0 %collective-permute-start = (bf16[2,16,512]{2,1,0:T(8,128)(2,1)S(1)}, bf16[2,16,512]{2,1,0:T(8,128)(2,1)S(1)}, u32[]{:S(2)}, u32[]{:S(2)}) collective-permute-start(bf16[2,16,512]{2,1,0:T(8,128)(2,1)S(1)} %copy-done.2), channel_id=1, source_target_pairs={{0,8},{8,0},{16,24},{24,16},{1,9},{9,1},{17,25},{25,17},{2,10},{10... | collective-permute-start | bytes 98312 | tf_op jit(solution)/shard_map/ppermute | solution.py:233
  16.1 3.1 %copy-start.1 = (f32[160,128]{1,0:T(8,128)S(1)}, f32[160,128]{1,0:T(8,128)}, u32[]{:S(2)}) copy-start(f32[160,128]{1,0:T(8,128)} %constant.5.clone.broad) | copy-start | bytes 245764

commit v12 on v11

--- a/solution.py
+++ b/solution.py
@@ -135,8 +135,12 @@
     bank[1] = value[:, LANES:].reshape(count, ROWS, LANES)
 
 
-def filter_kernel(energy, record, bank, narrow, broad, out, spec):
-    segs = record.shape[0]
+def filter_kernel(energy, mine, others, bank, narrow, broad, out, spec, halves):
+    core = lax.rem(lax.axis_index("tmpl"), 2)
+    halves[:, core] = mine[...]
+    halves[:, 1 - core] = others[...]
+    segs = 2 * mine.shape[0] * mine.shape[1] // ROWS
+    record = halves.reshape(segs, ROWS, LANES)
     own, count = out.shape
     half = GROUP * FINE
     w_low, w_high = broad[:ROWS][None], broad[ROWS:FINE][None]
@@ -245,16 +249,19 @@
 
     copies = pl.pallas_call(
         pack_kernel,
-        out_shape=pltpu.VMEM((devices, size * ROWS, LANES), f32),
+        out_shape=jax.ShapeDtypeStruct((devices // 2, size * ROWS, LANES), f32),
         in_specs=[vmem],
         out_specs=vmem,
         compiler_params=params,
         name="pack",
     )(strain.reshape(size * ROWS, LANES))
     copies, held = lax.optimization_barrier((copies, templates))
-    record = lax.all_to_all(copies, ("tm", "tmpl"), split_axis=0, concat_axis=0, tiled=True)
-    record = record.reshape(segs, ROWS, LANES)
-    blocks = [held] + [swap(held, "tm", other) for other in range(1, tm)]
+    copies = copies.reshape(devices, size * ROWS // 2, LANES)
+    mine = lax.all_to_all(copies, ("tm", "tmpl"), split_axis=0, concat_axis=0, tiled=True)
+    blocks = [swap(held, "tm", other) for other in range(1, tm)]
+    mine, *blocks = lax.optimization_barrier((mine, *blocks))
+    others = swap(mine, "tmpl", 1)
+    blocks = [held] + blocks
     bank = pl.pallas_call(
         functools.partial(bank_kernel, tm),
         out_shape=jax.ShapeDtypeStruct((2, count, ROWS, LANES), f32),
@@ -269,12 +276,15 @@
     return pl.pallas_call(
         functools.partial(filter_kernel, energy),
         out_shape=jax.ShapeDtypeStruct((own, count), f32),
-        in_specs=[vmem] * 4,
+        in_specs=[vmem] * 5,
         out_specs=vmem,
-        scratch_shapes=[pltpu.VMEM((segs * FINE, LANES), f32)],
+        scratch_shapes=[
+            pltpu.VMEM((segs * FINE, LANES), f32),
+            pltpu.VMEM((devices, 2, size * ROWS // 2, LANES), f32),
+        ],
         compiler_params=params,
         name="matched_filter",
-    )(record, bank, jnp.asarray(narrow), jnp.asarray(broad))
+    )(mine, others, bank, jnp.asarray(narrow), jnp.asarray(broad))
 
 
 def solution(mesh):

time: 23.5 us -> 22.7 us (0.966)
  waiting for transfers between devices: 6.5 us -> 5.45 us
    all_to_all x1, waiting for transfers between devices: 2.75 us -> 0.01 us  [on_device(): lax.all_to_all(copies, ('tm', 'tmpl'), split_axis=0, concat_axis=0, tiled...]
    ppermute x3 -> x4, waiting for transfers between devices: 3.75 us -> 5.45 us  [swap(): lax.ppermute(array, axis, [(i, i ^ bits) for i in range(lax.axis_size(axi...]
    ppermute x3 -> x4, starting transfers between devices: 3.55 us -> 3.81 us  [swap(): lax.ppermute(array, axis, [(i, i ^ bits) for i in range(lax.axis_size(axi...]
  transfers between devices with their start and end apart: 4 -> 5, of which waited for: 4 -> 4; matrix products, arithmetic and copies ran while one was open for 0% -> 0% of each run, Pallas kernels for 1% -> 1%
where the time goes in v12:
time: 22.7 us; the launch traced here: 22.5 us
  starting transfers between devices  11.1 us (49%)
  waiting for transfers between devices  5.45 us (24%)
  Pallas kernels  5.15 us (23%)
  local copies, waits for them, and re-layouts  0.71 us (3%)
    all_to_all x1, starting transfers between devices, on_device(): lax.all_to_all(copies, ('tm', 'tmpl'), split_axis=0, concat_axis=0, tiled...  7.3 us
    ppermute x4, waiting for transfers between devices, swap(): lax.ppermute(array, axis, [(i, i ^ bits) for i in range(lax.axis_size(axi...  5.45 us
    pallas_call x1, Pallas kernels, on_device(): pl.pallas_call(functools.partial(filter_kernel, energy), out_shape=jax.Sh...  4.21 us
    ppermute x4, starting transfers between devices, swap(): lax.ppermute(array, axis, [(i, i ^ bits) for i in range(lax.axis_size(axi...  3.81 us
    unnamed x10, local copies, waits for them, and re-layouts  0.71 us
    pallas_call x1, Pallas kernels, on_device(): pl.pallas_call(pack_kernel, out_shape=jax.ShapeDtypeStruct((devices // 2,...  0.65 us
  transfers between devices with their start and end apart: 5, of which 4 were waited for; matrix products, arithmetic and copies ran while one was open for 0% of the time, Pallas kernels for 1%

profile of v12, /device:TPU:0, one launch (start us, length us, event | category | flops | bytes accessed | tf_op | source)
XLA Modules:
  0.0 22.5 jit_solution(406556936889640802)
XLA Ops:
  0.0 0.0 copy-start.3
  0.0 0.7 %copy-done.3 = f32[2048]{0:T(1024)S(1)} copy-done((f32[2048]{0:T(1024)S(1)}, f32[2048]{0:T(1024)}, u32[]{:S(2)}) %copy-start.3) | copy-done | bytes 8216
  0.7 0.0 copy-start.2
  0.7 0.0 copy-start.4
  0.7 0.7 %pack.1 = f32[16,16,128]{2,1,0:T(8,128)} custom-call(f32[16,128]{1,0:T(8,128)S(1)} %bitcast.3), custom_call_target="tpu_custom_call" | custom-call | tf_op jit(solution)/shard_map/pack/pallas_call | solution.py:250
  1.4 0.0 copy-start
  1.4 7.3 %all-to-all-start = ((f32[32,8,128]{2,1,0:T(8,128)}), f32[32,8,128]{2,1,0:T(8,128)S(1)}, u32[]{:S(2)}, u32[]{:S(2)}) async-start(f32[32,8,128]{2,1,0:T(8,128)} %bitcast.1), calls=%async_computation | async-start | bytes 262144 | tf_op jit(solution)/shard_map/all_to_all | solution.py:260
  8.7 0.0 copy-done.2
  8.7 1.8 %collective-permute-start = (bf16[2,16,512]{2,1,0:T(8,128)(2,1)S(1)}, bf16[2,16,512]{2,1,0:T(8,128)(2,1)S(1)}, u32[]{:S(2)}, u32[]{:S(2)}) collective-permute-start(bf16[2,16,512]{2,1,0:T(8,128)(2,1)S(1)} %copy-done.2), channel_id=1, source_target_pairs={{0,8},{8,0},{16,24},{24,16},{1,9},{9,1},{17,25},{25,17},{2,10},{10... | collective-permute-start | bytes 98312 | tf_op jit(solution)/shard_map/ppermute | solution.py:237
  10.5 1.5 %collective-permute-start.1 = (bf16[2,16,512]{2,1,0:T(8,128)(2,1)S(1)}, bf16[2,16,512]{2,1,0:T(8,128)(2,1)S(1)}, u32[]{:S(2)}, u32[]{:S(2)}) collective-permute-start(bf16[2,16,512]{2,1,0:T(8,128)(2,1)S(1)} %copy-done.2), channel_id=1, source_target_pairs={{0,16},{8,24},{16,0},{24,8},{1,17},{9,25},{17,1},{25,9},{2,18},{10... | collective-permute-start | bytes 98312 | tf_op jit(solution)/shard_map/ppermute | solution.py:237
  12.0 0.3 %collective-permute-start.2 = (bf16[2,16,512]{2,1,0:T(8,128)(2,1)S(1)}, bf16[2,16,512]{2,1,0:T(8,128)(2,1)S(1)}, u32[]{:S(2)}, u32[]{:S(2)}) collective-permute-start(bf16[2,16,512]{2,1,0:T(8,128)(2,1)S(1)} %copy-done.2), channel_id=1, source_target_pairs={{0,24},{8,16},{16,8},{24,0},{1,25},{9,17},{17,9},{25,1},{2,26},{10... | collective-permute-start | bytes 98312 | tf_op jit(solution)/shard_map/ppermute | solution.py:237
  12.2 0.6 %collective-permute-done.refs_1_ = bf16[2,16,512]{2,1,0:T(8,128)(2,1)S(1)} collective-permute-done((bf16[2,16,512]{2,1,0:T(8,128)(2,1)S(1)}, bf16[2,16,512]{2,1,0:T(8,128)(2,1)S(1)}, u32[]{:S(2)}, u32[]{:S(2)}) %collective-permute-start) | collective-permute-done | bytes 32800 | tf_op jit(solution)/shard_map/ppermute | solution.py:237
  12.8 1.7 %collective-permute-done.1.refs_2_ = bf16[2,16,512]{2,1,0:T(8,128)(2,1)S(1)} collective-permute-done((bf16[2,16,512]{2,1,0:T(8,128)(2,1)S(1)}, bf16[2,16,512]{2,1,0:T(8,128)(2,1)S(1)}, u32[]{:S(2)}, u32[]{:S(2)}) %collective-permute-start.1) | collective-permute-done | bytes 32800 | tf_op jit(solution)/shard_map/ppermute | solution.py:237
  14.5 2.4 %collective-permute-done.2.refs_3_ = bf16[2,16,512]{2,1,0:T(8,128)(2,1)S(1)} collective-permute-done((bf16[2,16,512]{2,1,0:T(8,128)(2,1)S(1)}, bf16[2,16,512]{2,1,0:T(8,128)(2,1)S(1)}, u32[]{:S(2)}, u32[]{:S(2)}) %collective-permute-start.2) | collective-permute-done | bytes 32800 | tf_op jit(solution)/shard_map/ppermute | solution.py:237
  16.9 0.0 all-to-all-done.mine
  16.9 0.3 %collective-permute-start.3 = (f32[32,8,128]{2,1,0:T(8,128)S(1)}, f32[32,8,128]{2,1,0:T(8,128)S(1)}, u32[]{:S(2)}, u32[]{:S(2)}) collective-permute-start(f32[32,8,128]{2,1,0:T(8,128)S(1)} %all-to-all-done.mine), channel_id=1, source_target_pairs={{0,1},{1,0},{2,3},{3,2},{4,5},{5,4},{6,7},{7,6},{8,9},{9,8},{10,11... | collective-permute-start | bytes 393224 | tf_op jit(solution)/shard_map/ppermute | solution.py:237
  17.1 0.0 copy-done.4
  17.2 0.0 copy-start.1
  17.2 0.3 %bank.1 = f32[2,16,16,128]{3,2,1,0:T(8,128)S(1)} custom-call(bf16[2,16,512]{2,1,0:T(8,128)(2,1)S(1)} %copy-done.2, bf16[2,16,512]{2,1,0:T(8,128)(2,1)S(1)} %collective-permute-done.refs_1_, bf16[2,16,512]{2,1,0:T(8,128)(2,1)S(1)} %collective-permute-done.1.refs_2_, bf16[2,16,512]{2,1,0:T(8,128)(2,1)S(1)} %collective-permute-done.2.refs_3_, s32[1,16]{1,0:T(1,128)S(1)} %bitcast.4), custom_call_target="tpu_custom_call" | custom-call | bytes 2500000 | tf_op jit(solution)/shard_map/bank/pallas_call | solution.py:265
  17.5 0.8 %collective-permute-done.3.others = f32[32,8,128]{2,1,0:T(8,128)S(1)} collective-permute-done((f32[32,8,128]{2,1,0:T(8,128)S(1)}, f32[32,8,128]{2,1,0:T(8,128)S(1)}, u32[]{:S(2)}, u32[]{:S(2)}) %collective-permute-start.3) | collective-permute-done | bytes 131104 | tf_op jit(solution)/shard_map/ppermute | solution.py:237
  18.2 0.0 copy-done
  18.2 0.0 copy-done.1
  18.2 4.2 %matched_filter.1 = f32[8,16]{1,0:T(8,128)} custom-call(f32[32,8,128]{2,1,0:T(8,128)S(1)} %all-to-all-done.mine, f32[32,8,128]{2,1,0:T(8,128)S(1)} %collective-permute-done.3.others, f32[2,16,16,128]{3,2,1,0:T(8,128)S(1)} %bank.1, bf16[704,256]{1,0:T(8,128)(2,1)S(1)} %copy-done, f32[160,128]{1,0:T(8,128)S(1)} %copy-done.1), custom_call_target="tpu_custom_call" | custom-call | tf_op jit(solution)/shard_map/matched_filter/pallas_call | solution.py:276
Async XLA Ops:
  0.0 0.7 %copy-start.3 = (f32[2048]{0:T(1024)S(1)}, f32[2048]{0:T(1024)}, u32[]{:S(2)}) copy-start(f32[2048]{0:T(1024)} %param.5) | copy-start | bytes 24580
  0.7 8.0 %copy-start.2 = (bf16[2,16,512]{2,1,0:T(8,128)(2,1)S(1)}, bf16[2,16,512]{2,1,0:T(8,128)(2,1)}, u32[]{:S(2)}) copy-start(bf16[2,16,512]{2,1,0:T(8,128)(2,1)} %refs_0_) | copy-start | bytes 98308
  0.7 16.5 %copy-start.4 = (s32[16]{0:T(128)S(1)}, s32[16]{0:T(128)}, u32[]{:S(2)}) copy-start(s32[16]{0:T(128)} %param.7) | copy-start | bytes 196
  1.4 16.9 %copy-start = (bf16[704,256]{1,0:T(8,128)(2,1)S(1)}, bf16[704,256]{1,0:T(8,128)(2,1)}, u32[]{:S(2)}) copy-start(bf16[704,256]{1,0:T(8,128)(2,1)} %constant.4.clone.narrow) | copy-start | bytes 1081348
  1.4 15.5 %all-to-all-start = ((f32[32,8,128]{2,1,0:T(8,128)}), f32[32,8,128]{2,1,0:T(8,128)S(1)}, u32[]{:S(2)}, u32[]{:S(2)}) async-start(f32[32,8,128]{2,1,0:T(8,128)} %bitcast.1), calls=%async_computation | async-start | bytes 262144 | tf_op jit(solution)/shard_map/all_to_all | solution.py:260
  8.7 4.2 %collective-permute-start = (bf16[2,16,512]{2,1,0:T(8,128)(2,1)S(1)}, bf16[2,16,512]{2,1,0:T(8,128)(2,1)S(1)}, u32[]{:S(2)}, u32[]{:S(2)}) collective-permute-start(bf16[2,16,512]{2,1,0:T(8,128)(2,1)S(1)} %copy-done.2), channel_id=1, source_target_pairs={{0,8},{8,0},{16,24},{24,16},{1,9},{9,1},{17,25},{25,17},{2,10},{10... | collective-permute-start | bytes 98312 | tf_op jit(solution)/shard_map/ppermute | solution.py:237
  10.5 4.0 %collective-permute-start.1 = (bf16[2,16,512]{2,1,0:T(8,128)(2,1)S(1)}, bf16[2,16,512]{2,1,0:T(8,128)(2,1)S(1)}, u32[]{:S(2)}, u32[]{:S(2)}) collective-permute-start(bf16[2,16,512]{2,1,0:T(8,128)(2,1)S(1)} %copy-done.2), channel_id=1, source_target_pairs={{0,16},{8,24},{16,0},{24,8},{1,17},{9,25},{17,1},{25,9},{2,18},{10... | collective-permute-start | bytes 98312 | tf_op jit(solution)/shard_map/ppermute | solution.py:237
  12.0 4.9 %collective-permute-start.2 = (bf16[2,16,512]{2,1,0:T(8,128)(2,1)S(1)}, bf16[2,16,512]{2,1,0:T(8,128)(2,1)S(1)}, u32[]{:S(2)}, u32[]{:S(2)}) collective-permute-start(bf16[2,16,512]{2,1,0:T(8,128)(2,1)S(1)} %copy-done.2), channel_id=1, source_target_pairs={{0,24},{8,16},{16,8},{24,0},{1,25},{9,17},{17,9},{25,1},{2,26},{10... | collective-permute-start | bytes 98312 | tf_op jit(solution)/shard_map/ppermute | solution.py:237
  16.9 1.3 %collective-permute-start.3 = (f32[32,8,128]{2,1,0:T(8,128)S(1)}, f32[32,8,128]{2,1,0:T(8,128)S(1)}, u32[]{:S(2)}, u32[]{:S(2)}) collective-permute-start(f32[32,8,128]{2,1,0:T(8,128)S(1)} %all-to-all-done.mine), channel_id=1, source_target_pairs={{0,1},{1,0},{2,3},{3,2},{4,5},{5,4},{6,7},{7,6},{8,9},{9,8},{10,11... | collective-permute-start | bytes 393224 | tf_op jit(solution)/shard_map/ppermute | solution.py:237
  17.2 1.1 %copy-start.1 = (f32[160,128]{1,0:T(8,128)S(1)}, f32[160,128]{1,0:T(8,128)}, u32[]{:S(2)}) copy-start(f32[160,128]{1,0:T(8,128)} %constant.5.clone.broad) | copy-start | bytes 245764

commit v13 on v12

--- a/solution.py
+++ b/solution.py
@@ -107,10 +107,6 @@
     return result
 
 
-def pack_kernel(strain, copies):
-    copies[...] = jnp.broadcast_to(strain[...][None], copies.shape)
-
-
 def bank_kernel(devices, *refs):
     blocks = refs[:devices]
     cutoff, bank, gathered = refs[devices:]
@@ -166,10 +162,12 @@
         both = jnp.concatenate([here * w_low, after * w_high], axis=1)
         return both.reshape(half, LANES)
 
-    def forward(start, power, last):
+    def first_product(start, last):
         pair = jnp.concatenate([frames(start, False), frames(start + GROUP, last)], axis=1)
         high, low = split(pair)
-        step = dot(first, jnp.concatenate([high, low, high], axis=0))
+        return dot(first, jnp.concatenate([high, low, high], axis=0))
+
+    def second_product(step, start, power):
         for h in range(2):
             re = step[:half, h * LANES:(h + 1) * LANES].reshape(GROUP, FINE, LANES)
             im = step[half:, h * LANES:(h + 1) * LANES].reshape(GROUP, FINE, LANES)
@@ -183,8 +181,17 @@
 
     power = jnp.zeros((FINE, LANES), jnp.float32)
     pairs = segs // (2 * GROUP)
-    power = repeat(pairs - 1, lambda i, p: forward(i * 2 * GROUP, p, False), power)
-    power = forward((pairs - 1) * 2 * GROUP, power, True)
+    stride = 2 * GROUP
+    if pairs <= 4:
+        steps = [first_product(i * stride, i == pairs - 1) for i in range(pairs)]
+        for i, step in enumerate(steps):
+            power = second_product(step, i * stride, power)
+    else:
+        power = lax.fori_loop(
+            0, pairs - 1, lambda i, p: second_product(first_product(i * stride, False), i * stride, p), power
+        )
+        start = (pairs - 1) * stride
+        power = second_product(first_product(start, True), start, power)
     power = power + pltpu.roll(power, LANES // 2, 1)
     density = power / (segs * energy) + FLOOR
     inverse_density = natural((1.0 / jnp.concatenate([density] * 4, axis=0)).T, 0, None)
@@ -204,17 +211,18 @@
                 im_parts.append(natural(flipped, LANES // 2, s))
         white_re, white_im = jnp.stack(re_parts), jnp.stack(im_parts)
 
-        def pair_of(step, result):
+        def section_of(step):
             sides, norms = [], []
-            for side in range(2):
-                m = 2 * step + side
+            for m in (2 * step, 2 * step + 1):
                 h_re, h_im = bank[0, m], bank[1, m]
                 norms.append(jnp.sum((h_re * h_re + h_im * h_im) * inverse_density, keepdims=True))
                 c_re = h_re[None] * white_re + h_im[None] * white_im
                 c_im = h_re[None] * white_im - h_im[None] * white_re
                 both = jnp.concatenate([c_re, c_im], axis=0).reshape(2 * GROUP * ROWS, LANES)
                 sides.append(both.astype(jnp.bfloat16))
-            section = dot(third, jnp.concatenate(sides, axis=1))
+            return dot(third, jnp.concatenate(sides, axis=1)), norms
+
+        def peaks_of(step, section, norms, result):
             for side in range(2):
                 re = section[:half, side * LANES:(side + 1) * LANES].reshape(GROUP, FINE, LANES)
                 im = section[half:, side * LANES:(side + 1) * LANES].reshape(GROUP, FINE, LANES)
@@ -226,7 +234,13 @@
                 result = jnp.where(column == 2 * step + side, value, result)
             return result
 
-        result = repeat(count // 2, pair_of, jnp.zeros((GROUP, LANES), jnp.float32))
+        result = jnp.zeros((GROUP, LANES), jnp.float32)
+        ready = section_of(0)
+        for step in range(count // 2):
+            current = ready
+            if step + 1 < count // 2:
+                ready = section_of(step + 1)
+            result = peaks_of(step, *current, result)
         out[pl.ds(number * GROUP, GROUP)] = result[:, :count]
         return carry
 
@@ -247,14 +261,8 @@
     params = pltpu.CompilerParams(vmem_limit_bytes=40 * 1024 * 1024)
     f32 = jnp.float32
 
-    copies = pl.pallas_call(
-        pack_kernel,
-        out_shape=jax.ShapeDtypeStruct((devices // 2, size * ROWS, LANES), f32),
-        in_specs=[vmem],
-        out_specs=vmem,
-        compiler_params=params,
-        name="pack",
-    )(strain.reshape(size * ROWS, LANES))
+    chunk = strain.reshape(1, size * ROWS, LANES)
+    copies = jnp.broadcast_to(chunk, (devices // 2, size * ROWS, LANES))
     copies, held = lax.optimization_barrier((copies, templates))
     copies = copies.reshape(devices, size * ROWS // 2, LANES)
     mine = lax.all_to_all(copies, ("tm", "tmpl"), split_axis=0, concat_axis=0, tiled=True)

time: 22.7 us -> 22.1 us (0.974)
  Pallas kernels: 5.15 us -> 3.9 us
  local copies, waits for them, and re-layouts: 0.71 us -> 1.37 us
    broadcast_in_dim x0 -> x1, local copies, waits for them, and re-layouts: none -> 1.36 us  [on_device(): copies = jnp.broadcast_to(chunk, (devices // 2, size * ROWS, LANES))]
    unnamed x10 -> x8, local copies, waits for them, and re-layouts: 0.71 us -> 0.01 us
    pallas_call x1 -> x0, Pallas kernels: 0.65 us -> none  [on_device(): pl.pallas_call(pack_kernel, out_shape=jax.ShapeDtypeStruct((devices // 2,...]
    pallas_call x1, Pallas kernels: 4.21 us -> 3.61 us  [on_device(): pl.pallas_call(functools.partial(filter_kernel, energy), out_shape=jax.Sh...]
where the time goes in v13:
time: 22.1 us; the launch traced here: 21.9 us
  starting transfers between devices  11.1 us (50%)
  waiting for transfers between devices  5.45 us (25%)
  Pallas kernels  3.9 us (18%)
  local copies, waits for them, and re-layouts  1.37 us (6%)
    all_to_all x1, starting transfers between devices, on_device(): lax.all_to_all(copies, ('tm', 'tmpl'), split_axis=0, concat_axis=0, tiled...  7.3 us
    ppermute x4, waiting for transfers between devices, swap(): lax.ppermute(array, axis, [(i, i ^ bits) for i in range(lax.axis_size(axi...  5.45 us
    ppermute x4, starting transfers between devices, swap(): lax.ppermute(array, axis, [(i, i ^ bits) for i in range(lax.axis_size(axi...  3.81 us
    pallas_call x1, Pallas kernels, on_device(): pl.pallas_call(functools.partial(filter_kernel, energy), out_shape=jax.Sh...  3.61 us
    broadcast_in_dim x1, local copies, waits for them, and re-layouts, on_device(): copies = jnp.broadcast_to(chunk, (devices // 2, size * ROWS, LANES))  1.36 us
  transfers between devices with their start and end apart: 5, of which 4 were waited for; matrix products, arithmetic and copies ran while one was open for 0% of the time, Pallas kernels for 1%

profile of v13, /device:TPU:0, one launch (start us, length us, event | category | flops | bytes accessed | tf_op | source)
XLA Modules:
  0.0 21.9 jit_solution(17630153460005853484)
XLA Ops:
  0.0 0.0 copy-start.2
  0.0 0.0 copy-start.3
  0.0 1.4 %broadcast_in_dim.8 = f32[16,16,128]{2,1,0:T(8,128)} broadcast(f32[16,128]{1,0:T(8,128)} %bitcast.4), dimensions={1,2} | broadcast | bytes 139264 | tf_op jit(solution)/shard_map/broadcast_in_dim | solution.py:265
  1.4 0.0 copy-start
  1.4 7.3 %all-to-all-start = ((f32[32,8,128]{2,1,0:T(8,128)}), f32[32,8,128]{2,1,0:T(8,128)S(1)}, u32[]{:S(2)}, u32[]{:S(2)}) async-start(f32[32,8,128]{2,1,0:T(8,128)} %bitcast.1), calls=%async_computation | async-start | bytes 262144 | tf_op jit(solution)/shard_map/all_to_all | solution.py:268
  8.7 0.0 copy-done.2
  8.7 1.8 %collective-permute-start = (bf16[2,16,512]{2,1,0:T(8,128)(2,1)S(1)}, bf16[2,16,512]{2,1,0:T(8,128)(2,1)S(1)}, u32[]{:S(2)}, u32[]{:S(2)}) collective-permute-start(bf16[2,16,512]{2,1,0:T(8,128)(2,1)S(1)} %copy-done.2), channel_id=1, source_target_pairs={{0,8},{8,0},{16,24},{24,16},{1,9},{9,1},{17,25},{25,17},{2,10},{10... | collective-permute-start | bytes 98312 | tf_op jit(solution)/shard_map/ppermute | solution.py:251
  10.5 1.5 %collective-permute-start.1 = (bf16[2,16,512]{2,1,0:T(8,128)(2,1)S(1)}, bf16[2,16,512]{2,1,0:T(8,128)(2,1)S(1)}, u32[]{:S(2)}, u32[]{:S(2)}) collective-permute-start(bf16[2,16,512]{2,1,0:T(8,128)(2,1)S(1)} %copy-done.2), channel_id=1, source_target_pairs={{0,16},{8,24},{16,0},{24,8},{1,17},{9,25},{17,1},{25,9},{2,18},{10... | collective-permute-start | bytes 98312 | tf_op jit(solution)/shard_map/ppermute | solution.py:251
  12.0 0.3 %collective-permute-start.2 = (bf16[2,16,512]{2,1,0:T(8,128)(2,1)S(1)}, bf16[2,16,512]{2,1,0:T(8,128)(2,1)S(1)}, u32[]{:S(2)}, u32[]{:S(2)}) collective-permute-start(bf16[2,16,512]{2,1,0:T(8,128)(2,1)S(1)} %copy-done.2), channel_id=1, source_target_pairs={{0,24},{8,16},{16,8},{24,0},{1,25},{9,17},{17,9},{25,1},{2,26},{10... | collective-permute-start | bytes 98312 | tf_op jit(solution)/shard_map/ppermute | solution.py:251
  12.2 0.6 %collective-permute-done.refs_1_ = bf16[2,16,512]{2,1,0:T(8,128)(2,1)S(1)} collective-permute-done((bf16[2,16,512]{2,1,0:T(8,128)(2,1)S(1)}, bf16[2,16,512]{2,1,0:T(8,128)(2,1)S(1)}, u32[]{:S(2)}, u32[]{:S(2)}) %collective-permute-start) | collective-permute-done | bytes 32800 | tf_op jit(solution)/shard_map/ppermute | solution.py:251
  12.8 1.7 %collective-permute-done.1.refs_2_ = bf16[2,16,512]{2,1,0:T(8,128)(2,1)S(1)} collective-permute-done((bf16[2,16,512]{2,1,0:T(8,128)(2,1)S(1)}, bf16[2,16,512]{2,1,0:T(8,128)(2,1)S(1)}, u32[]{:S(2)}, u32[]{:S(2)}) %collective-permute-start.1) | collective-permute-done | bytes 32800 | tf_op jit(solution)/shard_map/ppermute | solution.py:251
  14.5 2.4 %collective-permute-done.2.refs_3_ = bf16[2,16,512]{2,1,0:T(8,128)(2,1)S(1)} collective-permute-done((bf16[2,16,512]{2,1,0:T(8,128)(2,1)S(1)}, bf16[2,16,512]{2,1,0:T(8,128)(2,1)S(1)}, u32[]{:S(2)}, u32[]{:S(2)}) %collective-permute-start.2) | collective-permute-done | bytes 32800 | tf_op jit(solution)/shard_map/ppermute | solution.py:251
  16.9 0.0 all-to-all-done.mine
  16.9 0.3 %collective-permute-start.3 = (f32[32,8,128]{2,1,0:T(8,128)S(1)}, f32[32,8,128]{2,1,0:T(8,128)S(1)}, u32[]{:S(2)}, u32[]{:S(2)}) collective-permute-start(f32[32,8,128]{2,1,0:T(8,128)S(1)} %all-to-all-done.mine), channel_id=1, source_target_pairs={{0,1},{1,0},{2,3},{3,2},{4,5},{5,4},{6,7},{7,6},{8,9},{9,8},{10,11... | collective-permute-start | bytes 393224 | tf_op jit(solution)/shard_map/ppermute | solution.py:251
  17.2 0.0 copy-done.3
  17.2 0.0 copy-start.1
  17.2 0.3 %bank.1 = f32[2,16,16,128]{3,2,1,0:T(8,128)S(1)} custom-call(bf16[2,16,512]{2,1,0:T(8,128)(2,1)S(1)} %copy-done.2, bf16[2,16,512]{2,1,0:T(8,128)(2,1)S(1)} %collective-permute-done.refs_1_, bf16[2,16,512]{2,1,0:T(8,128)(2,1)S(1)} %collective-permute-done.1.refs_2_, bf16[2,16,512]{2,1,0:T(8,128)(2,1)S(1)} %collective-permute-done.2.refs_3_, s32[1,16]{1,0:T(1,128)S(1)} %bitcast.3), custom_call_target="tpu_custom_call" | custom-call | bytes 2500000 | tf_op jit(solution)/shard_map/bank/pallas_call | solution.py:273
  17.5 0.8 %collective-permute-done.3.others = f32[32,8,128]{2,1,0:T(8,128)S(1)} collective-permute-done((f32[32,8,128]{2,1,0:T(8,128)S(1)}, f32[32,8,128]{2,1,0:T(8,128)S(1)}, u32[]{:S(2)}, u32[]{:S(2)}) %collective-permute-start.3) | collective-permute-done | bytes 131104 | tf_op jit(solution)/shard_map/ppermute | solution.py:251
  18.2 0.0 copy-done
  18.3 0.0 copy-done.1
  18.3 3.6 %matched_filter.1 = f32[8,16]{1,0:T(8,128)} custom-call(f32[32,8,128]{2,1,0:T(8,128)S(1)} %all-to-all-done.mine, f32[32,8,128]{2,1,0:T(8,128)S(1)} %collective-permute-done.3.others, f32[2,16,16,128]{3,2,1,0:T(8,128)S(1)} %bank.1, bf16[704,256]{1,0:T(8,128)(2,1)S(1)} %copy-done, f32[160,128]{1,0:T(8,128)S(1)} %copy-done.1), custom_call_target="tpu_custom_call" | custom-call | tf_op jit(solution)/shard_map/matched_filter/pallas_call | solution.py:284
Async XLA Ops:
  0.0 8.7 %copy-start.2 = (bf16[2,16,512]{2,1,0:T(8,128)(2,1)S(1)}, bf16[2,16,512]{2,1,0:T(8,128)(2,1)}, u32[]{:S(2)}) copy-start(bf16[2,16,512]{2,1,0:T(8,128)(2,1)} %refs_0_) | copy-start | bytes 98308
  0.0 17.2 %copy-start.3 = (s32[16]{0:T(128)S(1)}, s32[16]{0:T(128)}, u32[]{:S(2)}) copy-start(s32[16]{0:T(128)} %param.7) | copy-start | bytes 196
  1.4 16.9 %copy-start = (bf16[704,256]{1,0:T(8,128)(2,1)S(1)}, bf16[704,256]{1,0:T(8,128)(2,1)}, u32[]{:S(2)}) copy-start(bf16[704,256]{1,0:T(8,128)(2,1)} %constant.4.clone.narrow) | copy-start | bytes 1081348
  1.4 15.5 %all-to-all-start = ((f32[32,8,128]{2,1,0:T(8,128)}), f32[32,8,128]{2,1,0:T(8,128)S(1)}, u32[]{:S(2)}, u32[]{:S(2)}) async-start(f32[32,8,128]{2,1,0:T(8,128)} %bitcast.1), calls=%async_computation | async-start | bytes 262144 | tf_op jit(solution)/shard_map/all_to_all | solution.py:268
  8.7 4.2 %collective-permute-start = (bf16[2,16,512]{2,1,0:T(8,128)(2,1)S(1)}, bf16[2,16,512]{2,1,0:T(8,128)(2,1)S(1)}, u32[]{:S(2)}, u32[]{:S(2)}) collective-permute-start(bf16[2,16,512]{2,1,0:T(8,128)(2,1)S(1)} %copy-done.2), channel_id=1, source_target_pairs={{0,8},{8,0},{16,24},{24,16},{1,9},{9,1},{17,25},{25,17},{2,10},{10... | collective-permute-start | bytes 98312 | tf_op jit(solution)/shard_map/ppermute | solution.py:251
  10.5 4.0 %collective-permute-start.1 = (bf16[2,16,512]{2,1,0:T(8,128)(2,1)S(1)}, bf16[2,16,512]{2,1,0:T(8,128)(2,1)S(1)}, u32[]{:S(2)}, u32[]{:S(2)}) collective-permute-start(bf16[2,16,512]{2,1,0:T(8,128)(2,1)S(1)} %copy-done.2), channel_id=1, source_target_pairs={{0,16},{8,24},{16,0},{24,8},{1,17},{9,25},{17,1},{25,9},{2,18},{10... | collective-permute-start | bytes 98312 | tf_op jit(solution)/shard_map/ppermute | solution.py:251
  12.0 4.9 %collective-permute-start.2 = (bf16[2,16,512]{2,1,0:T(8,128)(2,1)S(1)}, bf16[2,16,512]{2,1,0:T(8,128)(2,1)S(1)}, u32[]{:S(2)}, u32[]{:S(2)}) collective-permute-start(bf16[2,16,512]{2,1,0:T(8,128)(2,1)S(1)} %copy-done.2), channel_id=1, source_target_pairs={{0,24},{8,16},{16,8},{24,0},{1,25},{9,17},{17,9},{25,1},{2,26},{10... | collective-permute-start | bytes 98312 | tf_op jit(solution)/shard_map/ppermute | solution.py:251
  16.9 1.3 %collective-permute-start.3 = (f32[32,8,128]{2,1,0:T(8,128)S(1)}, f32[32,8,128]{2,1,0:T(8,128)S(1)}, u32[]{:S(2)}, u32[]{:S(2)}) collective-permute-start(f32[32,8,128]{2,1,0:T(8,128)S(1)} %all-to-all-done.mine), channel_id=1, source_target_pairs={{0,1},{1,0},{2,3},{3,2},{4,5},{5,4},{6,7},{7,6},{8,9},{9,8},{10,11... | collective-permute-start | bytes 393224 | tf_op jit(solution)/shard_map/ppermute | solution.py:251
  17.2 1.1 %copy-start.1 = (f32[160,128]{1,0:T(8,128)S(1)}, f32[160,128]{1,0:T(8,128)}, u32[]{:S(2)}) copy-start(f32[160,128]{1,0:T(8,128)} %constant.5.clone.broad) | copy-start | bytes 245764

commit v14 on v13

--- a/solution.py
+++ b/solution.py
@@ -167,16 +167,22 @@
         high, low = split(pair)
         return dot(first, jnp.concatenate([high, low, high], axis=0))
 
-    def second_product(step, start, power):
+    def second_product(step, h):
+        re = step[:half, h * LANES:(h + 1) * LANES].reshape(GROUP, FINE, LANES)
+        im = step[half:, h * LANES:(h + 1) * LANES].reshape(GROUP, FINE, LANES)
+        turned = jnp.concatenate([re * fwd_cos + im * fwd_sin, im * fwd_cos - re * fwd_sin], axis=2)
+        high, low = split(turned.reshape(half, 2 * LANES))
+        return dot(jnp.concatenate([high, low], axis=1), jnp.concatenate([narrow[second]] * 2, axis=0))
+
+    def add_power(both, at, power):
+        value = both[:, :LANES] + both[:, LANES:]
+        spec[pl.ds(at * FINE, half)] = value
+        return power + jnp.sum((value * value).reshape(GROUP, FINE, LANES), axis=0)
+
+    def whole(start, last, power):
+        step = first_product(start, last)
         for h in range(2):
-            re = step[:half, h * LANES:(h + 1) * LANES].reshape(GROUP, FINE, LANES)
-            im = step[half:, h * LANES:(h + 1) * LANES].reshape(GROUP, FINE, LANES)
-            turned = jnp.concatenate([re * fwd_cos + im * fwd_sin, im * fwd_cos - re * fwd_sin], axis=2)
-            high, low = split(turned.reshape(half, 2 * LANES))
-            both = dot(jnp.concatenate([high, low], axis=1), jnp.concatenate([narrow[second]] * 2, axis=0))
-            value = both[:, :LANES] + both[:, LANES:]
-            spec[pl.ds((start + h * GROUP) * FINE, half)] = value
-            power = power + jnp.sum((value * value).reshape(GROUP, FINE, LANES), axis=0)
+            power = add_power(second_product(step, h), start + h * GROUP, power)
         return power
 
     power = jnp.zeros((FINE, LANES), jnp.float32)
@@ -184,14 +190,17 @@
     stride = 2 * GROUP
     if pairs <= 4:
         steps = [first_product(i * stride, i == pairs - 1) for i in range(pairs)]
+        waiting = None
         for i, step in enumerate(steps):
-            power = second_product(step, i * stride, power)
+            for h in range(2):
+                both = second_product(step, h)
+                if waiting is not None:
+                    power = add_power(*waiting, power)
+                waiting = (both, i * stride + h * GROUP)
+        power = add_power(*waiting, power)
     else:
-        power = lax.fori_loop(
-            0, pairs - 1, lambda i, p: second_product(first_product(i * stride, False), i * stride, p), power
-        )
-        start = (pairs - 1) * stride
-        power = second_product(first_product(start, True), start, power)
+        power = lax.fori_loop(0, pairs - 1, lambda i, p: whole(i * stride, False, p), power)
+        power = whole((pairs - 1) * stride, True, power)
     power = power + pltpu.roll(power, LANES // 2, 1)
     density = power / (segs * energy) + FLOOR
     inverse_density = natural((1.0 / jnp.concatenate([density] * 4, axis=0)).T, 0, None)
@@ -222,25 +231,30 @@
                 sides.append(both.astype(jnp.bfloat16))
             return dot(third, jnp.concatenate(sides, axis=1)), norms
 
-        def peaks_of(step, section, norms, result):
-            for side in range(2):
-                re = section[:half, side * LANES:(side + 1) * LANES].reshape(GROUP, FINE, LANES)
-                im = section[half:, side * LANES:(side + 1) * LANES].reshape(GROUP, FINE, LANES)
-                turned = jnp.concatenate([re * inv_cos - im * inv_sin, re * inv_sin + im * inv_cos], axis=2)
-                wave = dot(turned.reshape(half, 2 * LANES).astype(jnp.bfloat16), narrow[fourth])
-                square = wave[:, :LANES] * wave[:, :LANES] + wave[:, LANES:] * wave[:, LANES:]
-                top = jnp.max(jnp.max(square.reshape(GROUP, FINE, LANES), axis=1), axis=1, keepdims=True)
-                value = jnp.sqrt(top) / (jnp.sqrt(norms[side]) * math.sqrt(energy))
-                result = jnp.where(column == 2 * step + side, value, result)
-            return result
+        def wave_of(section, side):
+            re = section[:half, side * LANES:(side + 1) * LANES].reshape(GROUP, FINE, LANES)
+            im = section[half:, side * LANES:(side + 1) * LANES].reshape(GROUP, FINE, LANES)
+            turned = jnp.concatenate([re * inv_cos - im * inv_sin, re * inv_sin + im * inv_cos], axis=2)
+            return dot(turned.reshape(half, 2 * LANES).astype(jnp.bfloat16), narrow[fourth])
+
+        def peak_of(m, wave, norm, result):
+            square = wave[:, :LANES] * wave[:, :LANES] + wave[:, LANES:] * wave[:, LANES:]
+            top = jnp.max(jnp.max(square.reshape(GROUP, FINE, LANES), axis=1), axis=1, keepdims=True)
+            value = jnp.sqrt(top) / (jnp.sqrt(norm) * math.sqrt(energy))
+            return jnp.where(column == m, value, result)
 
         result = jnp.zeros((GROUP, LANES), jnp.float32)
-        ready = section_of(0)
+        ready, waiting = section_of(0), None
         for step in range(count // 2):
-            current = ready
+            section, norms = ready
             if step + 1 < count // 2:
                 ready = section_of(step + 1)
-            result = peaks_of(step, *current, result)
+            for side in range(2):
+                wave = wave_of(section, side)
+                if waiting is not None:
+                    result = peak_of(*waiting, result)
+                waiting = (2 * step + side, wave, norms[side])
+        result = peak_of(*waiting, result)
         out[pl.ds(number * GROUP, GROUP)] = result[:, :count]
         return carry
 

time: 22.1 us -> 22.1 us (level)
  no operation moved by 1% of the time
where the time goes in v14:
time: 22.1 us; the launch traced here: 21.9 us
  starting transfers between devices  11.1 us (50%)
  waiting for transfers between devices  5.45 us (25%)
  Pallas kernels  3.9 us (18%)
  local copies, waits for them, and re-layouts  1.37 us (6%)
    all_to_all x1, starting transfers between devices, on_device(): lax.all_to_all(copies, ('tm', 'tmpl'), split_axis=0, concat_axis=0, tiled...  7.3 us
    ppermute x4, waiting for transfers between devices, swap(): lax.ppermute(array, axis, [(i, i ^ bits) for i in range(lax.axis_size(axi...  5.45 us
    ppermute x4, starting transfers between devices, swap(): lax.ppermute(array, axis, [(i, i ^ bits) for i in range(lax.axis_size(axi...  3.81 us
    pallas_call x1, Pallas kernels, on_device(): pl.pallas_call(functools.partial(filter_kernel, energy), out_shape=jax.Sh...  3.61 us
    broadcast_in_dim x1, local copies, waits for them, and re-layouts, on_device(): copies = jnp.broadcast_to(chunk, (devices // 2, size * ROWS, LANES))  1.36 us
  transfers between devices with their start and end apart: 5, of which 4 were waited for; matrix products, arithmetic and copies ran while one was open for 0% of the time, Pallas kernels for 1%

profile of v14, /device:TPU:0, one launch (start us, length us, event | category | flops | bytes accessed | tf_op | source)
XLA Modules:
  0.0 21.9 jit_solution(10673185498667478802)
XLA Ops:
  0.0 0.0 copy-start.2
  0.0 0.0 copy-start.3
  0.0 1.4 %broadcast_in_dim.8 = f32[16,16,128]{2,1,0:T(8,128)} broadcast(f32[16,128]{1,0:T(8,128)} %bitcast.4), dimensions={1,2} | broadcast | bytes 139264 | tf_op jit(solution)/shard_map/broadcast_in_dim | solution.py:279
  1.4 0.0 copy-start
  1.4 7.3 %all-to-all-start = ((f32[32,8,128]{2,1,0:T(8,128)}), f32[32,8,128]{2,1,0:T(8,128)S(1)}, u32[]{:S(2)}, u32[]{:S(2)}) async-start(f32[32,8,128]{2,1,0:T(8,128)} %bitcast.1), calls=%async_computation | async-start | bytes 262144 | tf_op jit(solution)/shard_map/all_to_all | solution.py:282
  8.7 0.0 copy-done.2
  8.7 1.8 %collective-permute-start = (bf16[2,16,512]{2,1,0:T(8,128)(2,1)S(1)}, bf16[2,16,512]{2,1,0:T(8,128)(2,1)S(1)}, u32[]{:S(2)}, u32[]{:S(2)}) collective-permute-start(bf16[2,16,512]{2,1,0:T(8,128)(2,1)S(1)} %copy-done.2), channel_id=1, source_target_pairs={{0,8},{8,0},{16,24},{24,16},{1,9},{9,1},{17,25},{25,17},{2,10},{10... | collective-permute-start | bytes 98312 | tf_op jit(solution)/shard_map/ppermute | solution.py:265
  10.5 1.5 %collective-permute-start.1 = (bf16[2,16,512]{2,1,0:T(8,128)(2,1)S(1)}, bf16[2,16,512]{2,1,0:T(8,128)(2,1)S(1)}, u32[]{:S(2)}, u32[]{:S(2)}) collective-permute-start(bf16[2,16,512]{2,1,0:T(8,128)(2,1)S(1)} %copy-done.2), channel_id=1, source_target_pairs={{0,16},{8,24},{16,0},{24,8},{1,17},{9,25},{17,1},{25,9},{2,18},{10... | collective-permute-start | bytes 98312 | tf_op jit(solution)/shard_map/ppermute | solution.py:265
  12.0 0.3 %collective-permute-start.2 = (bf16[2,16,512]{2,1,0:T(8,128)(2,1)S(1)}, bf16[2,16,512]{2,1,0:T(8,128)(2,1)S(1)}, u32[]{:S(2)}, u32[]{:S(2)}) collective-permute-start(bf16[2,16,512]{2,1,0:T(8,128)(2,1)S(1)} %copy-done.2), channel_id=1, source_target_pairs={{0,24},{8,16},{16,8},{24,0},{1,25},{9,17},{17,9},{25,1},{2,26},{10... | collective-permute-start | bytes 98312 | tf_op jit(solution)/shard_map/ppermute | solution.py:265
  12.2 0.6 %collective-permute-done.refs_1_ = bf16[2,16,512]{2,1,0:T(8,128)(2,1)S(1)} collective-permute-done((bf16[2,16,512]{2,1,0:T(8,128)(2,1)S(1)}, bf16[2,16,512]{2,1,0:T(8,128)(2,1)S(1)}, u32[]{:S(2)}, u32[]{:S(2)}) %collective-permute-start) | collective-permute-done | bytes 32800 | tf_op jit(solution)/shard_map/ppermute | solution.py:265
  12.8 1.7 %collective-permute-done.1.refs_2_ = bf16[2,16,512]{2,1,0:T(8,128)(2,1)S(1)} collective-permute-done((bf16[2,16,512]{2,1,0:T(8,128)(2,1)S(1)}, bf16[2,16,512]{2,1,0:T(8,128)(2,1)S(1)}, u32[]{:S(2)}, u32[]{:S(2)}) %collective-permute-start.1) | collective-permute-done | bytes 32800 | tf_op jit(solution)/shard_map/ppermute | solution.py:265
  14.5 2.4 %collective-permute-done.2.refs_3_ = bf16[2,16,512]{2,1,0:T(8,128)(2,1)S(1)} collective-permute-done((bf16[2,16,512]{2,1,0:T(8,128)(2,1)S(1)}, bf16[2,16,512]{2,1,0:T(8,128)(2,1)S(1)}, u32[]{:S(2)}, u32[]{:S(2)}) %collective-permute-start.2) | collective-permute-done | bytes 32800 | tf_op jit(solution)/shard_map/ppermute | solution.py:265
  16.9 0.0 all-to-all-done.mine
  16.9 0.3 %collective-permute-start.3 = (f32[32,8,128]{2,1,0:T(8,128)S(1)}, f32[32,8,128]{2,1,0:T(8,128)S(1)}, u32[]{:S(2)}, u32[]{:S(2)}) collective-permute-start(f32[32,8,128]{2,1,0:T(8,128)S(1)} %all-to-all-done.mine), channel_id=1, source_target_pairs={{0,1},{1,0},{2,3},{3,2},{4,5},{5,4},{6,7},{7,6},{8,9},{9,8},{10,11... | collective-permute-start | bytes 393224 | tf_op jit(solution)/shard_map/ppermute | solution.py:265
  17.2 0.0 copy-done.3
  17.2 0.0 copy-start.1
  17.2 0.3 %bank.1 = f32[2,16,16,128]{3,2,1,0:T(8,128)S(1)} custom-call(bf16[2,16,512]{2,1,0:T(8,128)(2,1)S(1)} %copy-done.2, bf16[2,16,512]{2,1,0:T(8,128)(2,1)S(1)} %collective-permute-done.refs_1_, bf16[2,16,512]{2,1,0:T(8,128)(2,1)S(1)} %collective-permute-done.1.refs_2_, bf16[2,16,512]{2,1,0:T(8,128)(2,1)S(1)} %collective-permute-done.2.refs_3_, s32[1,16]{1,0:T(1,128)S(1)} %bitcast.3), custom_call_target="tpu_custom_call" | custom-call | bytes 2500000 | tf_op jit(solution)/shard_map/bank/pallas_call | solution.py:287
  17.5 0.8 %collective-permute-done.3.others = f32[32,8,128]{2,1,0:T(8,128)S(1)} collective-permute-done((f32[32,8,128]{2,1,0:T(8,128)S(1)}, f32[32,8,128]{2,1,0:T(8,128)S(1)}, u32[]{:S(2)}, u32[]{:S(2)}) %collective-permute-start.3) | collective-permute-done | bytes 131104 | tf_op jit(solution)/shard_map/ppermute | solution.py:265
  18.2 0.0 copy-done
  18.3 0.0 copy-done.1
  18.3 3.6 %matched_filter.1 = f32[8,16]{1,0:T(8,128)} custom-call(f32[32,8,128]{2,1,0:T(8,128)S(1)} %all-to-all-done.mine, f32[32,8,128]{2,1,0:T(8,128)S(1)} %collective-permute-done.3.others, f32[2,16,16,128]{3,2,1,0:T(8,128)S(1)} %bank.1, bf16[704,256]{1,0:T(8,128)(2,1)S(1)} %copy-done, f32[160,128]{1,0:T(8,128)S(1)} %copy-done.1), custom_call_target="tpu_custom_call" | custom-call | tf_op jit(solution)/shard_map/matched_filter/pallas_call | solution.py:298
Async XLA Ops:
  0.0 8.7 %copy-start.2 = (bf16[2,16,512]{2,1,0:T(8,128)(2,1)S(1)}, bf16[2,16,512]{2,1,0:T(8,128)(2,1)}, u32[]{:S(2)}) copy-start(bf16[2,16,512]{2,1,0:T(8,128)(2,1)} %refs_0_) | copy-start | bytes 98308
  0.0 17.2 %copy-start.3 = (s32[16]{0:T(128)S(1)}, s32[16]{0:T(128)}, u32[]{:S(2)}) copy-start(s32[16]{0:T(128)} %param.7) | copy-start | bytes 196
  1.4 16.9 %copy-start = (bf16[704,256]{1,0:T(8,128)(2,1)S(1)}, bf16[704,256]{1,0:T(8,128)(2,1)}, u32[]{:S(2)}) copy-start(bf16[704,256]{1,0:T(8,128)(2,1)} %constant.4.clone.narrow) | copy-start | bytes 1081348
  1.4 15.5 %all-to-all-start = ((f32[32,8,128]{2,1,0:T(8,128)}), f32[32,8,128]{2,1,0:T(8,128)S(1)}, u32[]{:S(2)}, u32[]{:S(2)}) async-start(f32[32,8,128]{2,1,0:T(8,128)} %bitcast.1), calls=%async_computation | async-start | bytes 262144 | tf_op jit(solution)/shard_map/all_to_all | solution.py:282
  8.7 4.2 %collective-permute-start = (bf16[2,16,512]{2,1,0:T(8,128)(2,1)S(1)}, bf16[2,16,512]{2,1,0:T(8,128)(2,1)S(1)}, u32[]{:S(2)}, u32[]{:S(2)}) collective-permute-start(bf16[2,16,512]{2,1,0:T(8,128)(2,1)S(1)} %copy-done.2), channel_id=1, source_target_pairs={{0,8},{8,0},{16,24},{24,16},{1,9},{9,1},{17,25},{25,17},{2,10},{10... | collective-permute-start | bytes 98312 | tf_op jit(solution)/shard_map/ppermute | solution.py:265
  10.5 4.0 %collective-permute-start.1 = (bf16[2,16,512]{2,1,0:T(8,128)(2,1)S(1)}, bf16[2,16,512]{2,1,0:T(8,128)(2,1)S(1)}, u32[]{:S(2)}, u32[]{:S(2)}) collective-permute-start(bf16[2,16,512]{2,1,0:T(8,128)(2,1)S(1)} %copy-done.2), channel_id=1, source_target_pairs={{0,16},{8,24},{16,0},{24,8},{1,17},{9,25},{17,1},{25,9},{2,18},{10... | collective-permute-start | bytes 98312 | tf_op jit(solution)/shard_map/ppermute | solution.py:265
  12.0 4.9 %collective-permute-start.2 = (bf16[2,16,512]{2,1,0:T(8,128)(2,1)S(1)}, bf16[2,16,512]{2,1,0:T(8,128)(2,1)S(1)}, u32[]{:S(2)}, u32[]{:S(2)}) collective-permute-start(bf16[2,16,512]{2,1,0:T(8,128)(2,1)S(1)} %copy-done.2), channel_id=1, source_target_pairs={{0,24},{8,16},{16,8},{24,0},{1,25},{9,17},{17,9},{25,1},{2,26},{10... | collective-permute-start | bytes 98312 | tf_op jit(solution)/shard_map/ppermute | solution.py:265
  16.9 1.3 %collective-permute-start.3 = (f32[32,8,128]{2,1,0:T(8,128)S(1)}, f32[32,8,128]{2,1,0:T(8,128)S(1)}, u32[]{:S(2)}, u32[]{:S(2)}) collective-permute-start(f32[32,8,128]{2,1,0:T(8,128)S(1)} %all-to-all-done.mine), channel_id=1, source_target_pairs={{0,1},{1,0},{2,3},{3,2},{4,5},{5,4},{6,7},{7,6},{8,9},{9,8},{10,11... | collective-permute-start | bytes 393224 | tf_op jit(solution)/shard_map/ppermute | solution.py:265
  17.2 1.1 %copy-start.1 = (f32[160,128]{1,0:T(8,128)S(1)}, f32[160,128]{1,0:T(8,128)}, u32[]{:S(2)}) copy-start(f32[160,128]{1,0:T(8,128)} %constant.5.clone.broad) | copy-start | bytes 245764

commit v15 on v14

--- a/solution.py
+++ b/solution.py
@@ -281,7 +281,6 @@
     copies = copies.reshape(devices, size * ROWS // 2, LANES)
     mine = lax.all_to_all(copies, ("tm", "tmpl"), split_axis=0, concat_axis=0, tiled=True)
     blocks = [swap(held, "tm", other) for other in range(1, tm)]
-    mine, *blocks = lax.optimization_barrier((mine, *blocks))
     others = swap(mine, "tmpl", 1)
     blocks = [held] + blocks
     bank = pl.pallas_call(

time: 22.1 us -> 27.1 us (1.23)
  blocking collectives: 0 us -> 15.3 us
  starting transfers between devices: 11.1 us -> 3.8 us
  waiting for transfers between devices: 5.45 us -> 2.55 us
    all_to_all x0 -> x1, blocking collectives: none -> 15.3 us  [on_device(): lax.all_to_all(copies, ('tm', 'tmpl'), split_axis=0, concat_axis=0, tiled...]
    all_to_all x1 -> x0, starting transfers between devices: 7.3 us -> none  [on_device(): lax.all_to_all(copies, ('tm', 'tmpl'), split_axis=0, concat_axis=0, tiled...]
    ppermute x4, waiting for transfers between devices: 5.45 us -> 2.55 us  [swap(): lax.ppermute(array, axis, [(i, i ^ bits) for i in range(lax.axis_size(axi...]
    broadcast_in_dim x1, local copies, waits for them, and re-layouts: 1.36 us -> 0.71 us  [on_device(): copies = jnp.broadcast_to(chunk, (devices // 2, size * ROWS, LANES))]
    unnamed x8, local copies, waits for them, and re-layouts: 0.01 us -> 0.58 us
  transfers between devices with their start and end apart: 5 -> 4, of which waited for: 4 -> 3; matrix products, arithmetic and copies ran while one was open for 0% -> 0% of each run, Pallas kernels for 1% -> 1%
where the time goes in v15:
time: 27.1 us; the launch traced here: 26.9 us
  blocking collectives  15.3 us (56%)
  Pallas kernels  3.9 us (14%)
  starting transfers between devices  3.8 us (14%)
  waiting for transfers between devices  2.55 us (9%)
  local copies, waits for them, and re-layouts  1.29 us (5%)
    all_to_all x1, blocking collectives, on_device(): lax.all_to_all(copies, ('tm', 'tmpl'), split_axis=0, concat_axis=0, tiled...  15.3 us
    ppermute x4, starting transfers between devices, swap(): lax.ppermute(array, axis, [(i, i ^ bits) for i in range(lax.axis_size(axi...  3.8 us
    pallas_call x1, Pallas kernels, on_device(): pl.pallas_call(functools.partial(filter_kernel, energy), out_shape=jax.Sh...  3.6 us
    ppermute x4, waiting for transfers between devices, swap(): lax.ppermute(array, axis, [(i, i ^ bits) for i in range(lax.axis_size(axi...  2.55 us
    broadcast_in_dim x1, local copies, waits for them, and re-layouts, on_device(): copies = jnp.broadcast_to(chunk, (devices // 2, size * ROWS, LANES))  0.71 us
    unnamed x8, local copies, waits for them, and re-layouts  0.58 us
  transfers between devices with their start and end apart: 4, of which 3 were waited for; matrix products, arithmetic and copies ran while one was open for 0% of the time, Pallas kernels for 1%

profile of v15, /device:TPU:0, one launch (start us, length us, event | category | flops | bytes accessed | tf_op | source)
XLA Modules:
  0.0 26.9 jit_solution(17475185031771098588)
XLA Ops:
  0.0 0.0 copy-start.2
  0.0 0.0 copy-start.3
  0.0 0.7 %broadcast_in_dim.8 = f32[16,16,128]{2,1,0:T(8,128)S(1)} broadcast(f32[16,128]{1,0:T(8,128)} %bitcast.5), dimensions={1,2} | broadcast | bytes 139264 | tf_op jit(solution)/shard_map/broadcast_in_dim | solution.py:279
  0.7 0.0 copy-start
  0.7 15.3 %all_to_all.5.mine = f32[32,8,128]{2,1,0:T(8,128)S(1)} all-to-all(f32[32,8,128]{2,1,0:T(8,128)S(1)} %bitcast.4), channel_id=1, replica_groups=mesh['tm'=4,'tmpl'=8] {'tm','tmpl'}, dimensions={0} | all-to-all | bytes 262144 | tf_op jit(solution)/shard_map/all_to_all | solution.py:282
  16.0 0.3 %collective-permute-start = (f32[32,8,128]{2,1,0:T(8,128)S(1)}, f32[32,8,128]{2,1,0:T(8,128)S(1)}, u32[]{:S(2)}, u32[]{:S(2)}) collective-permute-start(f32[32,8,128]{2,1,0:T(8,128)S(1)} %all_to_all.5.mine), channel_id=1, source_target_pairs={{0,1},{1,0},{2,3},{3,2},{4,5},{5,4},{6,7},{7,6},{8,9},{9,8},{10,11... | collective-permute-start | bytes 393224 | tf_op jit(solution)/shard_map/ppermute | solution.py:265
  16.3 0.0 copy-done.2
  16.3 0.5 %collective-permute-start.1 = (bf16[2,16,512]{2,1,0:T(8,128)(2,1)S(1)}, bf16[2,16,512]{2,1,0:T(8,128)(2,1)S(1)}, u32[]{:S(2)}, u32[]{:S(2)}) collective-permute-start(bf16[2,16,512]{2,1,0:T(8,128)(2,1)S(1)} %copy-done.2), channel_id=1, source_target_pairs={{0,8},{8,0},{16,24},{24,16},{1,9},{9,1},{17,25},{25,17},{2,10},{10... | collective-permute-start | bytes 98312 | tf_op jit(solution)/shard_map/ppermute | solution.py:265
  16.8 0.7 %collective-permute-start.2 = (bf16[2,16,512]{2,1,0:T(8,128)(2,1)S(1)}, bf16[2,16,512]{2,1,0:T(8,128)(2,1)S(1)}, u32[]{:S(2)}, u32[]{:S(2)}) collective-permute-start(bf16[2,16,512]{2,1,0:T(8,128)(2,1)S(1)} %copy-done.2), channel_id=1, source_target_pairs={{0,16},{8,24},{16,0},{24,8},{1,17},{9,25},{17,1},{25,9},{2,18},{10... | collective-permute-start | bytes 98312 | tf_op jit(solution)/shard_map/ppermute | solution.py:265
  17.6 2.3 %collective-permute-start.3 = (bf16[2,16,512]{2,1,0:T(8,128)(2,1)S(1)}, bf16[2,16,512]{2,1,0:T(8,128)(2,1)S(1)}, u32[]{:S(2)}, u32[]{:S(2)}) collective-permute-start(bf16[2,16,512]{2,1,0:T(8,128)(2,1)S(1)} %copy-done.2), channel_id=1, source_target_pairs={{0,24},{8,16},{16,8},{24,0},{1,25},{9,17},{17,9},{25,1},{2,26},{10... | collective-permute-start | bytes 98312 | tf_op jit(solution)/shard_map/ppermute | solution.py:265
  19.8 0.4 %collective-permute-done.1.refs_1_ = bf16[2,16,512]{2,1,0:T(8,128)(2,1)S(1)} collective-permute-done((bf16[2,16,512]{2,1,0:T(8,128)(2,1)S(1)}, bf16[2,16,512]{2,1,0:T(8,128)(2,1)S(1)}, u32[]{:S(2)}, u32[]{:S(2)}) %collective-permute-start.1) | collective-permute-done | bytes 32800 | tf_op jit(solution)/shard_map/ppermute | solution.py:265
  20.2 0.5 %collective-permute-done.2.refs_2_ = bf16[2,16,512]{2,1,0:T(8,128)(2,1)S(1)} collective-permute-done((bf16[2,16,512]{2,1,0:T(8,128)(2,1)S(1)}, bf16[2,16,512]{2,1,0:T(8,128)(2,1)S(1)}, u32[]{:S(2)}, u32[]{:S(2)}) %collective-permute-start.2) | collective-permute-done | bytes 32800 | tf_op jit(solution)/shard_map/ppermute | solution.py:265
  20.8 1.6 %collective-permute-done.3.refs_3_ = bf16[2,16,512]{2,1,0:T(8,128)(2,1)S(1)} collective-permute-done((bf16[2,16,512]{2,1,0:T(8,128)(2,1)S(1)}, bf16[2,16,512]{2,1,0:T(8,128)(2,1)S(1)}, u32[]{:S(2)}, u32[]{:S(2)}) %collective-permute-start.3) | collective-permute-done | bytes 32800 | tf_op jit(solution)/shard_map/ppermute | solution.py:265
  22.4 0.0 copy-done.3
  22.4 0.0 copy-start.1
  22.4 0.3 %bank.1 = f32[2,16,16,128]{3,2,1,0:T(8,128)S(1)} custom-call(bf16[2,16,512]{2,1,0:T(8,128)(2,1)S(1)} %copy-done.2, bf16[2,16,512]{2,1,0:T(8,128)(2,1)S(1)} %collective-permute-done.1.refs_1_, bf16[2,16,512]{2,1,0:T(8,128)(2,1)S(1)} %collective-permute-done.2.refs_2_, bf16[2,16,512]{2,1,0:T(8,128)(2,1)S(1)} %collective-permute-done.3.refs_3_, s32[1,16]{1,0:T(1,128)S(1)} %bitcast.3), custom_call_target="tpu_custom_call" | custom-call | bytes 2500000 | tf_op jit(solution)/shard_map/bank/pallas_call | solution.py:286
  22.7 0.0 collective-permute-done.others
  22.7 0.0 copy-done
  22.7 0.6 %copy-done.1 = f32[160,128]{1,0:T(8,128)S(1)} copy-done((f32[160,128]{1,0:T(8,128)S(1)}, f32[160,128]{1,0:T(8,128)}, u32[]{:S(2)}) %copy-start.1) | copy-done | bytes 81944
  23.3 3.6 %matched_filter.1 = f32[8,16]{1,0:T(8,128)} custom-call(f32[32,8,128]{2,1,0:T(8,128)S(1)} %all_to_all.5.mine, f32[32,8,128]{2,1,0:T(8,128)S(1)} %collective-permute-done.others, f32[2,16,16,128]{3,2,1,0:T(8,128)S(1)} %bank.1, bf16[704,256]{1,0:T(8,128)(2,1)S(1)} %copy-done, f32[160,128]{1,0:T(8,128)S(1)} %copy-done.1), custom_call_target="tpu_custom_call" | custom-call | tf_op jit(solution)/shard_map/matched_filter/pallas_call | solution.py:297
Async XLA Ops:
  0.0 16.3 %copy-start.2 = (bf16[2,16,512]{2,1,0:T(8,128)(2,1)S(1)}, bf16[2,16,512]{2,1,0:T(8,128)(2,1)}, u32[]{:S(2)}) copy-start(bf16[2,16,512]{2,1,0:T(8,128)(2,1)} %refs_0_) | copy-start | bytes 98308
  0.0 22.4 %copy-start.3 = (s32[16]{0:T(128)S(1)}, s32[16]{0:T(128)}, u32[]{:S(2)}) copy-start(s32[16]{0:T(128)} %param.7) | copy-start | bytes 196
  0.7 22.0 %copy-start = (bf16[704,256]{1,0:T(8,128)(2,1)S(1)}, bf16[704,256]{1,0:T(8,128)(2,1)}, u32[]{:S(2)}) copy-start(bf16[704,256]{1,0:T(8,128)(2,1)} %constant.4.clone.narrow) | copy-start | bytes 1081348
  16.0 6.7 %collective-permute-start = (f32[32,8,128]{2,1,0:T(8,128)S(1)}, f32[32,8,128]{2,1,0:T(8,128)S(1)}, u32[]{:S(2)}, u32[]{:S(2)}) collective-permute-start(f32[32,8,128]{2,1,0:T(8,128)S(1)} %all_to_all.5.mine), channel_id=1, source_target_pairs={{0,1},{1,0},{2,3},{3,2},{4,5},{5,4},{6,7},{7,6},{8,9},{9,8},{10,11... | collective-permute-start | bytes 393224 | tf_op jit(solution)/shard_map/ppermute | solution.py:265
  16.3 3.9 %collective-permute-start.1 = (bf16[2,16,512]{2,1,0:T(8,128)(2,1)S(1)}, bf16[2,16,512]{2,1,0:T(8,128)(2,1)S(1)}, u32[]{:S(2)}, u32[]{:S(2)}) collective-permute-start(bf16[2,16,512]{2,1,0:T(8,128)(2,1)S(1)} %copy-done.2), channel_id=1, source_target_pairs={{0,8},{8,0},{16,24},{24,16},{1,9},{9,1},{17,25},{25,17},{2,10},{10... | collective-permute-start | bytes 98312 | tf_op jit(solution)/shard_map/ppermute | solution.py:265
  16.8 3.9 %collective-permute-start.2 = (bf16[2,16,512]{2,1,0:T(8,128)(2,1)S(1)}, bf16[2,16,512]{2,1,0:T(8,128)(2,1)S(1)}, u32[]{:S(2)}, u32[]{:S(2)}) collective-permute-start(bf16[2,16,512]{2,1,0:T(8,128)(2,1)S(1)} %copy-done.2), channel_id=1, source_target_pairs={{0,16},{8,24},{16,0},{24,8},{1,17},{9,25},{17,1},{25,9},{2,18},{10... | collective-permute-start | bytes 98312 | tf_op jit(solution)/shard_map/ppermute | solution.py:265
  17.6 4.8 %collective-permute-start.3 = (bf16[2,16,512]{2,1,0:T(8,128)(2,1)S(1)}, bf16[2,16,512]{2,1,0:T(8,128)(2,1)S(1)}, u32[]{:S(2)}, u32[]{:S(2)}) collective-permute-start(bf16[2,16,512]{2,1,0:T(8,128)(2,1)S(1)} %copy-done.2), channel_id=1, source_target_pairs={{0,24},{8,16},{16,8},{24,0},{1,25},{9,17},{17,9},{25,1},{2,26},{10... | collective-permute-start | bytes 98312 | tf_op jit(solution)/shard_map/ppermute | solution.py:265
  22.4 0.9 %copy-start.1 = (f32[160,128]{1,0:T(8,128)S(1)}, f32[160,128]{1,0:T(8,128)}, u32[]{:S(2)}) copy-start(f32[160,128]{1,0:T(8,128)} %constant.5.clone.broad) | copy-start | bytes 245764

commit v16 on v14

--- a/solution.py
+++ b/solution.py
@@ -107,11 +107,11 @@
     return result
 
 
-def bank_kernel(devices, *refs):
-    blocks = refs[:devices]
-    cutoff, bank, gathered = refs[devices:]
+def bank_kernel(*refs):
+    *stacks, cutoff, bank, gathered = refs
     rank = lax.axis_index("tm")
-    _, count, width = blocks[0].shape
+    _, _, count, width = stacks[0].shape
+    blocks = [stack.at[i] for stack in stacks for i in range(stack.shape[0])]
     shape = (count, count)
     same = lax.broadcasted_iota(jnp.int32, shape, 0) == lax.broadcasted_iota(jnp.int32, shape, 1)
     column = jnp.sum(jnp.where(same, cutoff[...], 0), axis=1, keepdims=True)
@@ -277,17 +277,19 @@
 
     chunk = strain.reshape(1, size * ROWS, LANES)
     copies = jnp.broadcast_to(chunk, (devices // 2, size * ROWS, LANES))
-    copies, held = lax.optimization_barrier((copies, templates))
     copies = copies.reshape(devices, size * ROWS // 2, LANES)
     mine = lax.all_to_all(copies, ("tm", "tmpl"), split_axis=0, concat_axis=0, tiled=True)
-    blocks = [swap(held, "tm", other) for other in range(1, tm)]
+    blocks, bits = [templates[None]], 1
+    while bits < tm:
+        known = blocks[0] if bits == 1 else jnp.concatenate(blocks, axis=0)
+        blocks.append(swap(known, "tm", bits))
+        bits *= 2
     mine, *blocks = lax.optimization_barrier((mine, *blocks))
     others = swap(mine, "tmpl", 1)
-    blocks = [held] + blocks
     bank = pl.pallas_call(
-        functools.partial(bank_kernel, tm),
+        bank_kernel,
         out_shape=jax.ShapeDtypeStruct((2, count, ROWS, LANES), f32),
-        in_specs=[vmem] * (tm + 1),
+        in_specs=[vmem] * (len(blocks) + 1),
         out_specs=vmem,
         scratch_shapes=[pltpu.VMEM((ROWS, count, 2 * LANES), jnp.bfloat16)],
         compiler_params=params,

time: 22.1 us -> 22.4 us (1.014)
  waiting for transfers between devices: 5.45 us -> 5.89 us
    ppermute x4 -> x3, waiting for transfers between devices: 5.45 us -> 5.89 us  [swap(): lax.ppermute(array, axis, [(i, i ^ bits) for i in range(lax.axis_size(axi...]
    ppermute x4 -> x3, starting transfers between devices: 3.81 us -> 3.67 us  [swap(): lax.ppermute(array, axis, [(i, i ^ bits) for i in range(lax.axis_size(axi...]
  transfers between devices with their start and end apart: 5 -> 4, of which waited for: 4 -> 3; matrix products, arithmetic and copies ran while one was open for 0% -> 0% of each run, Pallas kernels for 1% -> 1%
where the time goes in v16:
time: 22.4 us; the launch traced here: 22.2 us
  starting transfers between devices  11 us (49%)
  waiting for transfers between devices  5.89 us (26%)
  Pallas kernels  3.9 us (17%)
  local copies, waits for them, and re-layouts  1.38 us (6%)
    all_to_all x1, starting transfers between devices, on_device(): lax.all_to_all(copies, ('tm', 'tmpl'), split_axis=0, concat_axis=0, tiled...  7.3 us
    ppermute x3, waiting for transfers between devices, swap(): lax.ppermute(array, axis, [(i, i ^ bits) for i in range(lax.axis_size(axi...  5.89 us
    ppermute x3, starting transfers between devices, swap(): lax.ppermute(array, axis, [(i, i ^ bits) for i in range(lax.axis_size(axi...  3.67 us
    pallas_call x1, Pallas kernels, on_device(): pl.pallas_call(functools.partial(filter_kernel, energy), out_shape=jax.Sh...  3.6 us
    broadcast_in_dim x1, local copies, waits for them, and re-layouts, on_device(): copies = jnp.broadcast_to(chunk, (devices // 2, size * ROWS, LANES))  1.36 us
  transfers between devices with their start and end apart: 4, of which 3 were waited for; matrix products, arithmetic and copies ran while one was open for 0% of the time, Pallas kernels for 1%

profile of v16, /device:TPU:0, one launch (start us, length us, event | category | flops | bytes accessed | tf_op | source)
XLA Modules:
  0.0 22.2 jit_solution(9678274660035054121)
XLA Ops:
  0.0 0.0 copy-start.1
  0.0 1.4 %broadcast_in_dim.11 = f32[16,16,128]{2,1,0:T(8,128)} broadcast(f32[16,128]{1,0:T(8,128)} %bitcast.8), dimensions={1,2} | broadcast | bytes 139264 | tf_op jit(solution)/shard_map/broadcast_in_dim | solution.py:279
  1.4 0.0 copy-start
  1.4 7.3 %all-to-all-start = ((f32[32,8,128]{2,1,0:T(8,128)}), f32[32,8,128]{2,1,0:T(8,128)S(1)}, u32[]{:S(2)}, u32[]{:S(2)}) async-start(f32[32,8,128]{2,1,0:T(8,128)} %bitcast.1), calls=%async_computation | async-start | bytes 262144 | tf_op jit(solution)/shard_map/all_to_all | solution.py:281
  8.7 0.0 copy-done.1
  8.7 1.8 %collective-permute-start = (bf16[1,2,16,512]{3,2,1,0:T(8,128)(2,1)S(1)}, bf16[1,2,16,512]{3,2,1,0:T(8,128)(2,1)S(1)}, u32[]{:S(2)}, u32[]{:S(2)}) collective-permute-start(bf16[1,2,16,512]{3,2,1,0:T(8,128)(2,1)S(1)} %bitcast.4), channel_id=1, source_target_pairs={{0,8},{8,0},{16,24},{24,16},{1,9},{9,1},{17,25},{25,17},{2,10},{10... | collective-permute-start | bytes 98312 | tf_op jit(solution)/shard_map/ppermute | solution.py:265
  10.5 2.3 %collective-permute-done.refs_1_ = bf16[1,2,16,512]{3,2,1,0:T(8,128)(2,1)S(1)} collective-permute-done((bf16[1,2,16,512]{3,2,1,0:T(8,128)(2,1)S(1)}, bf16[1,2,16,512]{3,2,1,0:T(8,128)(2,1)S(1)}, u32[]{:S(2)}, u32[]{:S(2)}) %collective-permute-start) | collective-permute-done | bytes 32800 | tf_op jit(solution)/shard_map/ppermute | solution.py:265
  12.8 0.0 copy-start.3
  12.9 1.8 %collective-permute-start.1 = (bf16[2,2,16,512]{3,2,1,0:T(8,128)(2,1)S(1)}, bf16[2,2,16,512]{3,2,1,0:T(8,128)(2,1)S(1)}, u32[]{:S(2)}, u32[]{:S(2)}) collective-permute-start(bf16[2,2,16,512]{3,2,1,0:T(8,128)(2,1)S(1)} %pad_maximum_fusion), channel_id=1, source_target_pairs={{0,16},{8,24},{16,0},{24,8},{1,17},{9,25},{17,1},{25,9},{2,18},{10... | collective-permute-start | bytes 196616 | tf_op jit(solution)/shard_map/ppermute | solution.py:265
  14.7 2.5 %collective-permute-done.1.refs_2_ = bf16[2,2,16,512]{3,2,1,0:T(8,128)(2,1)S(1)} collective-permute-done((bf16[2,2,16,512]{3,2,1,0:T(8,128)(2,1)S(1)}, bf16[2,2,16,512]{3,2,1,0:T(8,128)(2,1)S(1)}, u32[]{:S(2)}, u32[]{:S(2)}) %collective-permute-start.1) | collective-permute-done | bytes 65568 | tf_op jit(solution)/shard_map/ppermute | solution.py:265
  17.2 0.0 all-to-all-done.mine
  17.2 0.0 collective-permute-start.2
  17.2 0.0 copy-done.3
  17.2 0.0 copy-start.2
  17.3 0.3 %bank.1 = f32[2,16,16,128]{3,2,1,0:T(8,128)S(1)} custom-call(bf16[1,2,16,512]{3,2,1,0:T(8,128)(2,1)S(1)} %bitcast.6, bf16[1,2,16,512]{3,2,1,0:T(8,128)(2,1)S(1)} %collective-permute-done.refs_1_, bf16[2,2,16,512]{3,2,1,0:T(8,128)(2,1)S(1)} %collective-permute-done.1.refs_2_, s32[1,16]{1,0:T(1,128)S(1)} %bitcast.7), custom_call_target="tpu_custom_call" | custom-call | bytes 2500000 | tf_op jit(solution)/shard_map/bank/pallas_call | solution.py:289
  17.6 1.0 %collective-permute-done.2.others = f32[32,8,128]{2,1,0:T(8,128)S(1)} collective-permute-done((f32[32,8,128]{2,1,0:T(8,128)S(1)}, f32[32,8,128]{2,1,0:T(8,128)S(1)}, u32[]{:S(2)}, u32[]{:S(2)}) %collective-permute-start.2) | collective-permute-done | bytes 131104 | tf_op jit(solution)/shard_map/ppermute | solution.py:265
  18.6 0.0 copy-done
  18.6 0.0 copy-done.2
  18.6 3.6 %matched_filter.1 = f32[8,16]{1,0:T(8,128)} custom-call(f32[32,8,128]{2,1,0:T(8,128)S(1)} %all-to-all-done.mine, f32[32,8,128]{2,1,0:T(8,128)S(1)} %collective-permute-done.2.others, f32[2,16,16,128]{3,2,1,0:T(8,128)S(1)} %bank.1, bf16[704,256]{1,0:T(8,128)(2,1)S(1)} %copy-done, f32[160,128]{1,0:T(8,128)S(1)} %copy-done.2), custom_call_target="tpu_custom_call" | custom-call | tf_op jit(solution)/shard_map/matched_filter/pallas_call | solution.py:300
  (1 shorter events, 0.0 us)
Async XLA Ops:
  0.0 8.7 %copy-start.1 = (bf16[2,16,512]{2,1,0:T(8,128)(2,1)S(1)}, bf16[2,16,512]{2,1,0:T(8,128)(2,1)}, u32[]{:S(2)}) copy-start(bf16[2,16,512]{2,1,0:T(8,128)(2,1)} %param.6) | copy-start | bytes 98308
  1.4 17.2 %copy-start = (bf16[704,256]{1,0:T(8,128)(2,1)S(1)}, bf16[704,256]{1,0:T(8,128)(2,1)}, u32[]{:S(2)}) copy-start(bf16[704,256]{1,0:T(8,128)(2,1)} %constant.4.clone.narrow) | copy-start | bytes 1081348
  1.4 15.9 %all-to-all-start = ((f32[32,8,128]{2,1,0:T(8,128)}), f32[32,8,128]{2,1,0:T(8,128)S(1)}, u32[]{:S(2)}, u32[]{:S(2)}) async-start(f32[32,8,128]{2,1,0:T(8,128)} %bitcast.1), calls=%async_computation | async-start | bytes 262144 | tf_op jit(solution)/shard_map/all_to_all | solution.py:281
  8.7 4.2 %collective-permute-start = (bf16[1,2,16,512]{3,2,1,0:T(8,128)(2,1)S(1)}, bf16[1,2,16,512]{3,2,1,0:T(8,128)(2,1)S(1)}, u32[]{:S(2)}, u32[]{:S(2)}) collective-permute-start(bf16[1,2,16,512]{3,2,1,0:T(8,128)(2,1)S(1)} %bitcast.4), channel_id=1, source_target_pairs={{0,8},{8,0},{16,24},{24,16},{1,9},{9,1},{17,25},{25,17},{2,10},{10... | collective-permute-start | bytes 98312 | tf_op jit(solution)/shard_map/ppermute | solution.py:265
  12.8 4.4 %copy-start.3 = (s32[16]{0:T(128)S(1)}, s32[16]{0:T(128)}, u32[]{:S(2)}) copy-start(s32[16]{0:T(128)} %param.7) | copy-start | bytes 196
  12.9 4.4 %collective-permute-start.1 = (bf16[2,2,16,512]{3,2,1,0:T(8,128)(2,1)S(1)}, bf16[2,2,16,512]{3,2,1,0:T(8,128)(2,1)S(1)}, u32[]{:S(2)}, u32[]{:S(2)}) collective-permute-start(bf16[2,2,16,512]{3,2,1,0:T(8,128)(2,1)S(1)} %pad_maximum_fusion), channel_id=1, source_target_pairs={{0,16},{8,24},{16,0},{24,8},{1,17},{9,25},{17,1},{25,9},{2,18},{10... | collective-permute-start | bytes 196616 | tf_op jit(solution)/shard_map/ppermute | solution.py:265
  17.2 1.3 %collective-permute-start.2 = (f32[32,8,128]{2,1,0:T(8,128)S(1)}, f32[32,8,128]{2,1,0:T(8,128)S(1)}, u32[]{:S(2)}, u32[]{:S(2)}) collective-permute-start(f32[32,8,128]{2,1,0:T(8,128)S(1)} %all-to-all-done.mine), channel_id=1, source_target_pairs={{0,1},{1,0},{2,3},{3,2},{4,5},{5,4},{6,7},{7,6},{8,9},{9,8},{10,11... | collective-permute-start | bytes 393224 | tf_op jit(solution)/shard_map/ppermute | solution.py:265
  17.2 1.3 %copy-start.2 = (f32[160,128]{1,0:T(8,128)S(1)}, f32[160,128]{1,0:T(8,128)}, u32[]{:S(2)}) copy-start(f32[160,128]{1,0:T(8,128)} %constant.5.clone.broad) | copy-start | bytes 245764

commit v17 on v14

--- a/solution.py
+++ b/solution.py
@@ -203,22 +203,25 @@
         power = whole((pairs - 1) * stride, True, power)
     power = power + pltpu.roll(power, LANES // 2, 1)
     density = power / (segs * energy) + FLOOR
-    inverse_density = natural((1.0 / jnp.concatenate([density] * 4, axis=0)).T, 0, None)
+    density = natural(jnp.concatenate([density] * 4, axis=0).T, 0, None)
+    inverse_density = 1.0 / density
 
     place = lax.axis_index("tm") * own
     column = lax.broadcasted_iota(jnp.int32, (GROUP, LANES), 1)
 
     def block(number, carry):
         at = pl.multiple_of((place + number * GROUP) * FINE, half)
-        white = spec[pl.ds(at, half)].reshape(GROUP, FINE, LANES) / density[None]
-        white = white.astype(jnp.bfloat16).astype(jnp.float32).reshape(2, 4 * FINE, LANES)
+        values = spec[pl.ds(at, half)].reshape(2, 4 * FINE, LANES)
         re_parts, im_parts = [], []
         for side in range(2):
-            flipped = white[side].T
+            flipped = values[side].T
             for s in range(4):
                 re_parts.append(natural(flipped, 0, s))
                 im_parts.append(natural(flipped, LANES // 2, s))
-        white_re, white_im = jnp.stack(re_parts), jnp.stack(im_parts)
+        white_re, white_im = (
+            (jnp.stack(parts) / density[None]).astype(jnp.bfloat16).astype(jnp.float32)
+            for parts in (re_parts, im_parts)
+        )
 
         def section_of(step):
             sides, norms = [], []

time: 22.1 us -> 22.1 us (level)
  no operation moved by 1% of the time
where the time goes in v17:
time: 22.1 us; the launch traced here: 21.8 us
  starting transfers between devices  11.1 us (50%)
  waiting for transfers between devices  5.45 us (25%)
  Pallas kernels  3.88 us (18%)
  local copies, waits for them, and re-layouts  1.37 us (6%)
    all_to_all x1, starting transfers between devices, on_device(): lax.all_to_all(copies, ('tm', 'tmpl'), split_axis=0, concat_axis=0, tiled...  7.3 us
    ppermute x4, waiting for transfers between devices, swap(): lax.ppermute(array, axis, [(i, i ^ bits) for i in range(lax.axis_size(axi...  5.45 us
    ppermute x4, starting transfers between devices, swap(): lax.ppermute(array, axis, [(i, i ^ bits) for i in range(lax.axis_size(axi...  3.81 us
    pallas_call x1, Pallas kernels, on_device(): pl.pallas_call(functools.partial(filter_kernel, energy), out_shape=jax.Sh...  3.59 us
    broadcast_in_dim x1, local copies, waits for them, and re-layouts, on_device(): copies = jnp.broadcast_to(chunk, (devices // 2, size * ROWS, LANES))  1.36 us
  transfers between devices with their start and end apart: 5, of which 4 were waited for; matrix products, arithmetic and copies ran while one was open for 0% of the time, Pallas kernels for 1%

profile of v17, /device:TPU:0, one launch (start us, length us, event | category | flops | bytes accessed | tf_op | source)
XLA Modules:
  0.0 21.8 jit_solution(11113437711059599201)
XLA Ops:
  0.0 0.0 copy-start.2
  0.0 0.0 copy-start.3
  0.0 1.4 %broadcast_in_dim.8 = f32[16,16,128]{2,1,0:T(8,128)} broadcast(f32[16,128]{1,0:T(8,128)} %bitcast.4), dimensions={1,2} | broadcast | bytes 139264 | tf_op jit(solution)/shard_map/broadcast_in_dim | solution.py:282
  1.4 0.0 copy-start
  1.4 7.3 %all-to-all-start = ((f32[32,8,128]{2,1,0:T(8,128)}), f32[32,8,128]{2,1,0:T(8,128)S(1)}, u32[]{:S(2)}, u32[]{:S(2)}) async-start(f32[32,8,128]{2,1,0:T(8,128)} %bitcast.1), calls=%async_computation | async-start | bytes 262144 | tf_op jit(solution)/shard_map/all_to_all | solution.py:285
  8.7 0.0 copy-done.2
  8.7 1.8 %collective-permute-start = (bf16[2,16,512]{2,1,0:T(8,128)(2,1)S(1)}, bf16[2,16,512]{2,1,0:T(8,128)(2,1)S(1)}, u32[]{:S(2)}, u32[]{:S(2)}) collective-permute-start(bf16[2,16,512]{2,1,0:T(8,128)(2,1)S(1)} %copy-done.2), channel_id=1, source_target_pairs={{0,8},{8,0},{16,24},{24,16},{1,9},{9,1},{17,25},{25,17},{2,10},{10... | collective-permute-start | bytes 98312 | tf_op jit(solution)/shard_map/ppermute | solution.py:268
  10.5 1.5 %collective-permute-start.1 = (bf16[2,16,512]{2,1,0:T(8,128)(2,1)S(1)}, bf16[2,16,512]{2,1,0:T(8,128)(2,1)S(1)}, u32[]{:S(2)}, u32[]{:S(2)}) collective-permute-start(bf16[2,16,512]{2,1,0:T(8,128)(2,1)S(1)} %copy-done.2), channel_id=1, source_target_pairs={{0,16},{8,24},{16,0},{24,8},{1,17},{9,25},{17,1},{25,9},{2,18},{10... | collective-permute-start | bytes 98312 | tf_op jit(solution)/shard_map/ppermute | solution.py:268
  12.0 0.3 %collective-permute-start.2 = (bf16[2,16,512]{2,1,0:T(8,128)(2,1)S(1)}, bf16[2,16,512]{2,1,0:T(8,128)(2,1)S(1)}, u32[]{:S(2)}, u32[]{:S(2)}) collective-permute-start(bf16[2,16,512]{2,1,0:T(8,128)(2,1)S(1)} %copy-done.2), channel_id=1, source_target_pairs={{0,24},{8,16},{16,8},{24,0},{1,25},{9,17},{17,9},{25,1},{2,26},{10... | collective-permute-start | bytes 98312 | tf_op jit(solution)/shard_map/ppermute | solution.py:268
  12.2 0.6 %collective-permute-done.refs_1_ = bf16[2,16,512]{2,1,0:T(8,128)(2,1)S(1)} collective-permute-done((bf16[2,16,512]{2,1,0:T(8,128)(2,1)S(1)}, bf16[2,16,512]{2,1,0:T(8,128)(2,1)S(1)}, u32[]{:S(2)}, u32[]{:S(2)}) %collective-permute-start) | collective-permute-done | bytes 32800 | tf_op jit(solution)/shard_map/ppermute | solution.py:268
  12.8 1.7 %collective-permute-done.1.refs_2_ = bf16[2,16,512]{2,1,0:T(8,128)(2,1)S(1)} collective-permute-done((bf16[2,16,512]{2,1,0:T(8,128)(2,1)S(1)}, bf16[2,16,512]{2,1,0:T(8,128)(2,1)S(1)}, u32[]{:S(2)}, u32[]{:S(2)}) %collective-permute-start.1) | collective-permute-done | bytes 32800 | tf_op jit(solution)/shard_map/ppermute | solution.py:268
  14.5 2.4 %collective-permute-done.2.refs_3_ = bf16[2,16,512]{2,1,0:T(8,128)(2,1)S(1)} collective-permute-done((bf16[2,16,512]{2,1,0:T(8,128)(2,1)S(1)}, bf16[2,16,512]{2,1,0:T(8,128)(2,1)S(1)}, u32[]{:S(2)}, u32[]{:S(2)}) %collective-permute-start.2) | collective-permute-done | bytes 32800 | tf_op jit(solution)/shard_map/ppermute | solution.py:268
  16.9 0.0 all-to-all-done.mine
  16.9 0.3 %collective-permute-start.3 = (f32[32,8,128]{2,1,0:T(8,128)S(1)}, f32[32,8,128]{2,1,0:T(8,128)S(1)}, u32[]{:S(2)}, u32[]{:S(2)}) collective-permute-start(f32[32,8,128]{2,1,0:T(8,128)S(1)} %all-to-all-done.mine), channel_id=1, source_target_pairs={{0,1},{1,0},{2,3},{3,2},{4,5},{5,4},{6,7},{7,6},{8,9},{9,8},{10,11... | collective-permute-start | bytes 393224 | tf_op jit(solution)/shard_map/ppermute | solution.py:268
  17.2 0.0 copy-done.3
  17.2 0.0 copy-start.1
  17.2 0.3 %bank.1 = f32[2,16,16,128]{3,2,1,0:T(8,128)S(1)} custom-call(bf16[2,16,512]{2,1,0:T(8,128)(2,1)S(1)} %copy-done.2, bf16[2,16,512]{2,1,0:T(8,128)(2,1)S(1)} %collective-permute-done.refs_1_, bf16[2,16,512]{2,1,0:T(8,128)(2,1)S(1)} %collective-permute-done.1.refs_2_, bf16[2,16,512]{2,1,0:T(8,128)(2,1)S(1)} %collective-permute-done.2.refs_3_, s32[1,16]{1,0:T(1,128)S(1)} %bitcast.3), custom_call_target="tpu_custom_call" | custom-call | bytes 2500000 | tf_op jit(solution)/shard_map/bank/pallas_call | solution.py:290
  17.5 0.8 %collective-permute-done.3.others = f32[32,8,128]{2,1,0:T(8,128)S(1)} collective-permute-done((f32[32,8,128]{2,1,0:T(8,128)S(1)}, f32[32,8,128]{2,1,0:T(8,128)S(1)}, u32[]{:S(2)}, u32[]{:S(2)}) %collective-permute-start.3) | collective-permute-done | bytes 131104 | tf_op jit(solution)/shard_map/ppermute | solution.py:268
  18.2 0.0 copy-done
  18.3 0.0 copy-done.1
  18.3 3.6 %matched_filter.1 = f32[8,16]{1,0:T(8,128)} custom-call(f32[32,8,128]{2,1,0:T(8,128)S(1)} %all-to-all-done.mine, f32[32,8,128]{2,1,0:T(8,128)S(1)} %collective-permute-done.3.others, f32[2,16,16,128]{3,2,1,0:T(8,128)S(1)} %bank.1, bf16[704,256]{1,0:T(8,128)(2,1)S(1)} %copy-done, f32[160,128]{1,0:T(8,128)S(1)} %copy-done.1), custom_call_target="tpu_custom_call" | custom-call | tf_op jit(solution)/shard_map/matched_filter/pallas_call | solution.py:301
Async XLA Ops:
  0.0 8.7 %copy-start.2 = (bf16[2,16,512]{2,1,0:T(8,128)(2,1)S(1)}, bf16[2,16,512]{2,1,0:T(8,128)(2,1)}, u32[]{:S(2)}) copy-start(bf16[2,16,512]{2,1,0:T(8,128)(2,1)} %refs_0_) | copy-start | bytes 98308
  0.0 17.2 %copy-start.3 = (s32[16]{0:T(128)S(1)}, s32[16]{0:T(128)}, u32[]{:S(2)}) copy-start(s32[16]{0:T(128)} %param.7) | copy-start | bytes 196
  1.4 16.9 %copy-start = (bf16[704,256]{1,0:T(8,128)(2,1)S(1)}, bf16[704,256]{1,0:T(8,128)(2,1)}, u32[]{:S(2)}) copy-start(bf16[704,256]{1,0:T(8,128)(2,1)} %constant.4.clone.narrow) | copy-start | bytes 1081348
  1.4 15.5 %all-to-all-start = ((f32[32,8,128]{2,1,0:T(8,128)}), f32[32,8,128]{2,1,0:T(8,128)S(1)}, u32[]{:S(2)}, u32[]{:S(2)}) async-start(f32[32,8,128]{2,1,0:T(8,128)} %bitcast.1), calls=%async_computation | async-start | bytes 262144 | tf_op jit(solution)/shard_map/all_to_all | solution.py:285
  8.7 4.2 %collective-permute-start = (bf16[2,16,512]{2,1,0:T(8,128)(2,1)S(1)}, bf16[2,16,512]{2,1,0:T(8,128)(2,1)S(1)}, u32[]{:S(2)}, u32[]{:S(2)}) collective-permute-start(bf16[2,16,512]{2,1,0:T(8,128)(2,1)S(1)} %copy-done.2), channel_id=1, source_target_pairs={{0,8},{8,0},{16,24},{24,16},{1,9},{9,1},{17,25},{25,17},{2,10},{10... | collective-permute-start | bytes 98312 | tf_op jit(solution)/shard_map/ppermute | solution.py:268
  10.5 4.0 %collective-permute-start.1 = (bf16[2,16,512]{2,1,0:T(8,128)(2,1)S(1)}, bf16[2,16,512]{2,1,0:T(8,128)(2,1)S(1)}, u32[]{:S(2)}, u32[]{:S(2)}) collective-permute-start(bf16[2,16,512]{2,1,0:T(8,128)(2,1)S(1)} %copy-done.2), channel_id=1, source_target_pairs={{0,16},{8,24},{16,0},{24,8},{1,17},{9,25},{17,1},{25,9},{2,18},{10... | collective-permute-start | bytes 98312 | tf_op jit(solution)/shard_map/ppermute | solution.py:268
  12.0 4.9 %collective-permute-start.2 = (bf16[2,16,512]{2,1,0:T(8,128)(2,1)S(1)}, bf16[2,16,512]{2,1,0:T(8,128)(2,1)S(1)}, u32[]{:S(2)}, u32[]{:S(2)}) collective-permute-start(bf16[2,16,512]{2,1,0:T(8,128)(2,1)S(1)} %copy-done.2), channel_id=1, source_target_pairs={{0,24},{8,16},{16,8},{24,0},{1,25},{9,17},{17,9},{25,1},{2,26},{10... | collective-permute-start | bytes 98312 | tf_op jit(solution)/shard_map/ppermute | solution.py:268
  16.9 1.3 %collective-permute-start.3 = (f32[32,8,128]{2,1,0:T(8,128)S(1)}, f32[32,8,128]{2,1,0:T(8,128)S(1)}, u32[]{:S(2)}, u32[]{:S(2)}) collective-permute-start(f32[32,8,128]{2,1,0:T(8,128)S(1)} %all-to-all-done.mine), channel_id=1, source_target_pairs={{0,1},{1,0},{2,3},{3,2},{4,5},{5,4},{6,7},{7,6},{8,9},{9,8},{10,11... | collective-permute-start | bytes 393224 | tf_op jit(solution)/shard_map/ppermute | solution.py:268
  17.2 1.1 %copy-start.1 = (f32[160,128]{1,0:T(8,128)S(1)}, f32[160,128]{1,0:T(8,128)}, u32[]{:S(2)}) copy-start(f32[160,128]{1,0:T(8,128)} %constant.5.clone.broad) | copy-start | bytes 245764

commit v18 on v17

--- a/solution.py
+++ b/solution.py
@@ -107,9 +107,16 @@
     return result
 
 
+def spread(part, width):
+    return jnp.concatenate([block_diagonal(part[:FINE], width), block_diagonal(part[FINE:], width)])
+
+
 def bank_kernel(devices, *refs):
     blocks = refs[:devices]
-    cutoff, bank, gathered = refs[devices:]
+    cutoff, narrow, bank, first, third, gathered = refs[devices:]
+    first[0] = spread(narrow[:2 * FINE], FINE)
+    first[1] = spread(narrow[2 * FINE:4 * FINE], FINE)
+    third[...] = spread(narrow[4 * FINE:6 * FINE], ROWS)
     rank = lax.axis_index("tm")
     _, count, width = blocks[0].shape
     shape = (count, count)
@@ -131,7 +138,7 @@
     bank[1] = value[:, LANES:].reshape(count, ROWS, LANES)
 
 
-def filter_kernel(energy, mine, others, bank, narrow, broad, out, spec, halves):
+def filter_kernel(energy, mine, others, bank, tables, third, narrow, broad, out, spec, halves):
     core = lax.rem(lax.axis_index("tmpl"), 2)
     halves[:, core] = mine[...]
     halves[:, 1 - core] = others[...]
@@ -142,14 +149,7 @@
     w_low, w_high = broad[:ROWS][None], broad[ROWS:FINE][None]
     fwd_cos, fwd_sin = broad[FINE:2 * FINE][None], broad[2 * FINE:3 * FINE][None]
     inv_cos, inv_sin = broad[3 * FINE:4 * FINE][None], broad[4 * FINE:5 * FINE][None]
-    high, low = narrow[:2 * FINE], narrow[2 * FINE:4 * FINE]
-    spread = lambda part: jnp.concatenate(
-        [block_diagonal(part[:FINE], part.shape[1] // GROUP), block_diagonal(part[FINE:], part.shape[1] // GROUP)]
-    )
-    first_high = spread(high)
-    first = jnp.concatenate([first_high, first_high, spread(low)], axis=1)
-    third_rows = narrow[4 * FINE:6 * FINE]
-    third = jnp.concatenate([block_diagonal(third_rows[:FINE], ROWS), block_diagonal(third_rows[FINE:], ROWS)])
+    first = jnp.concatenate([tables[0], tables[0], tables[1]], axis=1)
     second = slice(6 * FINE, 6 * FINE + 2 * LANES)
     fourth = slice(6 * FINE + 2 * LANES, 6 * FINE + 4 * LANES)
 
@@ -232,7 +232,7 @@
                 c_im = h_re[None] * white_im - h_im[None] * white_re
                 both = jnp.concatenate([c_re, c_im], axis=0).reshape(2 * GROUP * ROWS, LANES)
                 sides.append(both.astype(jnp.bfloat16))
-            return dot(third, jnp.concatenate(sides, axis=1)), norms
+            return dot(third[...], jnp.concatenate(sides, axis=1)), norms
 
         def wave_of(section, side):
             re = section[:half, side * LANES:(side + 1) * LANES].reshape(GROUP, FINE, LANES)
@@ -287,21 +287,27 @@
     mine, *blocks = lax.optimization_barrier((mine, *blocks))
     others = swap(mine, "tmpl", 1)
     blocks = [held] + blocks
-    bank = pl.pallas_call(
+    narrow, broad, energy = tables()
+    narrow, broad = jnp.asarray(narrow), jnp.asarray(broad)
+    square = (2 * GROUP * FINE, 2 * GROUP * ROWS)
+    bank, first, third = pl.pallas_call(
         functools.partial(bank_kernel, tm),
-        out_shape=jax.ShapeDtypeStruct((2, count, ROWS, LANES), f32),
-        in_specs=[vmem] * (tm + 1),
-        out_specs=vmem,
+        out_shape=(
+            jax.ShapeDtypeStruct((2, count, ROWS, LANES), f32),
+            jax.ShapeDtypeStruct((2,) + square, jnp.bfloat16),
+            jax.ShapeDtypeStruct(square, jnp.bfloat16),
+        ),
+        in_specs=[vmem] * (tm + 2),
+        out_specs=(vmem,) * 3,
         scratch_shapes=[pltpu.VMEM((ROWS, count, 2 * LANES), jnp.bfloat16)],
         compiler_params=params,
         cost_estimate=pl.CostEstimate(flops=0, bytes_accessed=2500000, transcendentals=0),
         name="bank",
-    )(*blocks, cutoff.reshape(1, count))
-    narrow, broad, energy = tables()
+    )(*blocks, cutoff.reshape(1, count), narrow)
     return pl.pallas_call(
         functools.partial(filter_kernel, energy),
         out_shape=jax.ShapeDtypeStruct((own, count), f32),
-        in_specs=[vmem] * 5,
+        in_specs=[vmem] * 7,
         out_specs=vmem,
         scratch_shapes=[
             pltpu.VMEM((segs * FINE, LANES), f32),
@@ -309,7 +315,7 @@
         ],
         compiler_params=params,
         name="matched_filter",
-    )(mine, others, bank, jnp.asarray(narrow), jnp.asarray(broad))
+    )(mine, others, bank, first, third, narrow, broad)
 
 
 def solution(mesh):

time: 22.1 us -> 22.2 us (level)
  no operation moved by 1% of the time
where the time goes in v18:
time: 22.2 us; the launch traced here: 21.9 us
  starting transfers between devices  11.1 us (50%)
  waiting for transfers between devices  5.43 us (24%)
  Pallas kernels  3.94 us (18%)
  local copies, waits for them, and re-layouts  1.41 us (6%)
    all_to_all x1, starting transfers between devices, on_device(): lax.all_to_all(copies, ('tm', 'tmpl'), split_axis=0, concat_axis=0, tiled...  7.3 us
    ppermute x4, waiting for transfers between devices, swap(): lax.ppermute(array, axis, [(i, i ^ bits) for i in range(lax.axis_size(axi...  5.43 us
    ppermute x4, starting transfers between devices, swap(): lax.ppermute(array, axis, [(i, i ^ bits) for i in range(lax.axis_size(axi...  3.81 us
    pallas_call x1, Pallas kernels, on_device(): pl.pallas_call(functools.partial(filter_kernel, energy), out_shape=jax.Sh...  3.64 us
    broadcast_in_dim x1, local copies, waits for them, and re-layouts, on_device(): copies = jnp.broadcast_to(chunk, (devices // 2, size * ROWS, LANES))  1.4 us
  transfers between devices with their start and end apart: 5, of which 4 were waited for; matrix products, arithmetic and copies ran while one was open for 0% of the time, Pallas kernels for 1%

profile of v18, /device:TPU:0, one launch (start us, length us, event | category | flops | bytes accessed | tf_op | source)
XLA Modules:
  0.0 21.9 jit_solution(5802190750936318157)
XLA Ops:
  0.0 0.0 copy-start
  0.0 1.4 %broadcast_in_dim.8 = f32[16,16,128]{2,1,0:T(8,128)} broadcast(f32[16,128]{1,0:T(8,128)} %bitcast.4), dimensions={1,2} | broadcast | bytes 139264 | tf_op jit(solution)/shard_map/broadcast_in_dim | solution.py:282
  1.4 0.0 copy-start.2
  1.4 7.3 %all-to-all-start = ((f32[32,8,128]{2,1,0:T(8,128)}), f32[32,8,128]{2,1,0:T(8,128)S(1)}, u32[]{:S(2)}, u32[]{:S(2)}) async-start(f32[32,8,128]{2,1,0:T(8,128)} %bitcast.1), calls=%async_computation | async-start | bytes 262144 | tf_op jit(solution)/shard_map/all_to_all | solution.py:285
  8.7 0.0 copy-done.2
  8.7 0.0 copy-start.3
  8.7 1.8 %collective-permute-start = (bf16[2,16,512]{2,1,0:T(8,128)(2,1)S(1)}, bf16[2,16,512]{2,1,0:T(8,128)(2,1)S(1)}, u32[]{:S(2)}, u32[]{:S(2)}) collective-permute-start(bf16[2,16,512]{2,1,0:T(8,128)(2,1)S(1)} %copy-done.2), channel_id=1, source_target_pairs={{0,8},{8,0},{16,24},{24,16},{1,9},{9,1},{17,25},{25,17},{2,10},{10... | collective-permute-start | bytes 98312 | tf_op jit(solution)/shard_map/ppermute | solution.py:268
  10.6 1.5 %collective-permute-start.1 = (bf16[2,16,512]{2,1,0:T(8,128)(2,1)S(1)}, bf16[2,16,512]{2,1,0:T(8,128)(2,1)S(1)}, u32[]{:S(2)}, u32[]{:S(2)}) collective-permute-start(bf16[2,16,512]{2,1,0:T(8,128)(2,1)S(1)} %copy-done.2), channel_id=1, source_target_pairs={{0,16},{8,24},{16,0},{24,8},{1,17},{9,25},{17,1},{25,9},{2,18},{10... | collective-permute-start | bytes 98312 | tf_op jit(solution)/shard_map/ppermute | solution.py:268
  12.0 0.3 %collective-permute-start.2 = (bf16[2,16,512]{2,1,0:T(8,128)(2,1)S(1)}, bf16[2,16,512]{2,1,0:T(8,128)(2,1)S(1)}, u32[]{:S(2)}, u32[]{:S(2)}) collective-permute-start(bf16[2,16,512]{2,1,0:T(8,128)(2,1)S(1)} %copy-done.2), channel_id=1, source_target_pairs={{0,24},{8,16},{16,8},{24,0},{1,25},{9,17},{17,9},{25,1},{2,26},{10... | collective-permute-start | bytes 98312 | tf_op jit(solution)/shard_map/ppermute | solution.py:268
  12.3 0.6 %collective-permute-done.refs_1_ = bf16[2,16,512]{2,1,0:T(8,128)(2,1)S(1)} collective-permute-done((bf16[2,16,512]{2,1,0:T(8,128)(2,1)S(1)}, bf16[2,16,512]{2,1,0:T(8,128)(2,1)S(1)}, u32[]{:S(2)}, u32[]{:S(2)}) %collective-permute-start) | collective-permute-done | bytes 32800 | tf_op jit(solution)/shard_map/ppermute | solution.py:268
  12.9 1.6 %collective-permute-done.1.refs_2_ = bf16[2,16,512]{2,1,0:T(8,128)(2,1)S(1)} collective-permute-done((bf16[2,16,512]{2,1,0:T(8,128)(2,1)S(1)}, bf16[2,16,512]{2,1,0:T(8,128)(2,1)S(1)}, u32[]{:S(2)}, u32[]{:S(2)}) %collective-permute-start.1) | collective-permute-done | bytes 32800 | tf_op jit(solution)/shard_map/ppermute | solution.py:268
  14.5 2.4 %collective-permute-done.2.refs_3_ = bf16[2,16,512]{2,1,0:T(8,128)(2,1)S(1)} collective-permute-done((bf16[2,16,512]{2,1,0:T(8,128)(2,1)S(1)}, bf16[2,16,512]{2,1,0:T(8,128)(2,1)S(1)}, u32[]{:S(2)}, u32[]{:S(2)}) %collective-permute-start.2) | collective-permute-done | bytes 32800 | tf_op jit(solution)/shard_map/ppermute | solution.py:268
  16.9 0.0 all-to-all-done.mine
  16.9 0.3 %collective-permute-start.3 = (f32[32,8,128]{2,1,0:T(8,128)S(1)}, f32[32,8,128]{2,1,0:T(8,128)S(1)}, u32[]{:S(2)}, u32[]{:S(2)}) collective-permute-start(f32[32,8,128]{2,1,0:T(8,128)S(1)} %all-to-all-done.mine), channel_id=1, source_target_pairs={{0,1},{1,0},{2,3},{3,2},{4,5},{5,4},{6,7},{7,6},{8,9},{9,8},{10,11... | collective-permute-start | bytes 393224 | tf_op jit(solution)/shard_map/ppermute | solution.py:268
  17.2 0.0 copy-done
  17.2 0.0 copy-done.3
  17.2 0.0 copy-start.1
  17.2 0.3 %bank.1 = (f32[2,16,16,128]{3,2,1,0:T(8,128)S(1)}, bf16[2,512,256]{2,1,0:T(8,128)(2,1)S(1)}, bf16[512,256]{1,0:T(8,128)(2,1)S(1)}) custom-call(bf16[2,16,512]{2,1,0:T(8,128)(2,1)S(1)} %copy-done.2, bf16[2,16,512]{2,1,0:T(8,128)(2,1)S(1)} %collective-permute-done.refs_1_, bf16[2,16,512]{2,1,0:T(8,128)(2,1)S(1)} %collective-permute-done.1.refs_2_, ...), custom_call_target="tpu_custom_call" | custom-call | bytes 2500000 | tf_op jit(solution)/shard_map/bank/pallas_call | solution.py:293
  17.5 0.8 %collective-permute-done.3.others = f32[32,8,128]{2,1,0:T(8,128)S(1)} collective-permute-done((f32[32,8,128]{2,1,0:T(8,128)S(1)}, f32[32,8,128]{2,1,0:T(8,128)S(1)}, u32[]{:S(2)}, u32[]{:S(2)}) %collective-permute-start.3) | collective-permute-done | bytes 131104 | tf_op jit(solution)/shard_map/ppermute | solution.py:268
  18.3 0.0 copy-done.1
  18.3 3.6 %matched_filter.1 = f32[8,16]{1,0:T(8,128)} custom-call(f32[32,8,128]{2,1,0:T(8,128)S(1)} %all-to-all-done.mine, f32[32,8,128]{2,1,0:T(8,128)S(1)} %collective-permute-done.3.others, f32[2,16,16,128]{3,2,1,0:T(8,128)S(1)} %get-tuple-element.20.bank, bf16[2,512,256]{2,1,0:T(8,128)(2,1)S(1)} %get-tuple-element.21.tables, ...), custom_call_target="tpu_custom_call" | custom-call | tf_op jit(solution)/shard_map/matched_filter/pallas_call | solution.py:307
Async XLA Ops:
  0.0 17.2 %copy-start = (bf16[704,256]{1,0:T(8,128)(2,1)S(1)}, bf16[704,256]{1,0:T(8,128)(2,1)}, u32[]{:S(2)}) copy-start(bf16[704,256]{1,0:T(8,128)(2,1)} %constant.4.clone.refs_5_.narrow) | copy-start | bytes 1081348
  1.4 7.3 %copy-start.2 = (bf16[2,16,512]{2,1,0:T(8,128)(2,1)S(1)}, bf16[2,16,512]{2,1,0:T(8,128)(2,1)}, u32[]{:S(2)}) copy-start(bf16[2,16,512]{2,1,0:T(8,128)(2,1)} %refs_0_) | copy-start | bytes 98308
  1.4 15.5 %all-to-all-start = ((f32[32,8,128]{2,1,0:T(8,128)}), f32[32,8,128]{2,1,0:T(8,128)S(1)}, u32[]{:S(2)}, u32[]{:S(2)}) async-start(f32[32,8,128]{2,1,0:T(8,128)} %bitcast.1), calls=%async_computation | async-start | bytes 262144 | tf_op jit(solution)/shard_map/all_to_all | solution.py:285
  8.7 8.5 %copy-start.3 = (s32[16]{0:T(128)S(1)}, s32[16]{0:T(128)}, u32[]{:S(2)}) copy-start(s32[16]{0:T(128)} %param.7) | copy-start | bytes 196
  8.7 4.2 %collective-permute-start = (bf16[2,16,512]{2,1,0:T(8,128)(2,1)S(1)}, bf16[2,16,512]{2,1,0:T(8,128)(2,1)S(1)}, u32[]{:S(2)}, u32[]{:S(2)}) collective-permute-start(bf16[2,16,512]{2,1,0:T(8,128)(2,1)S(1)} %copy-done.2), channel_id=1, source_target_pairs={{0,8},{8,0},{16,24},{24,16},{1,9},{9,1},{17,25},{25,17},{2,10},{10... | collective-permute-start | bytes 98312 | tf_op jit(solution)/shard_map/ppermute | solution.py:268
  10.6 4.0 %collective-permute-start.1 = (bf16[2,16,512]{2,1,0:T(8,128)(2,1)S(1)}, bf16[2,16,512]{2,1,0:T(8,128)(2,1)S(1)}, u32[]{:S(2)}, u32[]{:S(2)}) collective-permute-start(bf16[2,16,512]{2,1,0:T(8,128)(2,1)S(1)} %copy-done.2), channel_id=1, source_target_pairs={{0,16},{8,24},{16,0},{24,8},{1,17},{9,25},{17,1},{25,9},{2,18},{10... | collective-permute-start | bytes 98312 | tf_op jit(solution)/shard_map/ppermute | solution.py:268
  12.0 4.9 %collective-permute-start.2 = (bf16[2,16,512]{2,1,0:T(8,128)(2,1)S(1)}, bf16[2,16,512]{2,1,0:T(8,128)(2,1)S(1)}, u32[]{:S(2)}, u32[]{:S(2)}) collective-permute-start(bf16[2,16,512]{2,1,0:T(8,128)(2,1)S(1)} %copy-done.2), channel_id=1, source_target_pairs={{0,24},{8,16},{16,8},{24,0},{1,25},{9,17},{17,9},{25,1},{2,26},{10... | collective-permute-start | bytes 98312 | tf_op jit(solution)/shard_map/ppermute | solution.py:268
  16.9 1.3 %collective-permute-start.3 = (f32[32,8,128]{2,1,0:T(8,128)S(1)}, f32[32,8,128]{2,1,0:T(8,128)S(1)}, u32[]{:S(2)}, u32[]{:S(2)}) collective-permute-start(f32[32,8,128]{2,1,0:T(8,128)S(1)} %all-to-all-done.mine), channel_id=1, source_target_pairs={{0,1},{1,0},{2,3},{3,2},{4,5},{5,4},{6,7},{7,6},{8,9},{9,8},{10,11... | collective-permute-start | bytes 393224 | tf_op jit(solution)/shard_map/ppermute | solution.py:268
  17.2 1.1 %copy-start.1 = (f32[160,128]{1,0:T(8,128)S(1)}, f32[160,128]{1,0:T(8,128)}, u32[]{:S(2)}) copy-start(f32[160,128]{1,0:T(8,128)} %constant.5.clone.broad) | copy-start | bytes 245764

commit v19 on v17

--- a/solution.py
+++ b/solution.py
@@ -223,7 +223,7 @@
             for parts in (re_parts, im_parts)
         )
 
-        def section_of(step):
+        def products_of(step):
             sides, norms = [], []
             for m in (2 * step, 2 * step + 1):
                 h_re, h_im = bank[0, m], bank[1, m]
@@ -232,7 +232,7 @@
                 c_im = h_re[None] * white_im - h_im[None] * white_re
                 both = jnp.concatenate([c_re, c_im], axis=0).reshape(2 * GROUP * ROWS, LANES)
                 sides.append(both.astype(jnp.bfloat16))
-            return dot(third, jnp.concatenate(sides, axis=1)), norms
+            return jnp.concatenate(sides, axis=1), norms
 
         def wave_of(section, side):
             re = section[:half, side * LANES:(side + 1) * LANES].reshape(GROUP, FINE, LANES)
@@ -247,11 +247,15 @@
             return jnp.where(column == m, value, result)
 
         result = jnp.zeros((GROUP, LANES), jnp.float32)
-        ready, waiting = section_of(0), None
-        for step in range(count // 2):
-            section, norms = ready
-            if step + 1 < count // 2:
-                ready = section_of(step + 1)
+        steps = count // 2
+        made = [products_of(step) for step in range(min(2, steps))]
+        ready, waiting = dot(third, made[0][0]), None
+        for step in range(steps):
+            section, norms = ready, made[step][1]
+            if step + 2 < steps:
+                made.append(products_of(step + 2))
+            if step + 1 < steps:
+                ready = dot(third, made[step + 1][0])
             for side in range(2):
                 wave = wave_of(section, side)
                 if waiting is not None:

time: 22.1 us -> 22.1 us (level)
  no operation moved by 1% of the time
where the time goes in v19:
time: 22.1 us; the launch traced here: 21.8 us
  starting transfers between devices  11.1 us (50%)
  waiting for transfers between devices  5.45 us (25%)
  Pallas kernels  3.88 us (18%)
  local copies, waits for them, and re-layouts  1.37 us (6%)
    all_to_all x1, starting transfers between devices, on_device(): lax.all_to_all(copies, ('tm', 'tmpl'), split_axis=0, concat_axis=0, tiled...  7.3 us
    ppermute x4, waiting for transfers between devices, swap(): lax.ppermute(array, axis, [(i, i ^ bits) for i in range(lax.axis_size(axi...  5.45 us
    ppermute x4, starting transfers between devices, swap(): lax.ppermute(array, axis, [(i, i ^ bits) for i in range(lax.axis_size(axi...  3.81 us
    pallas_call x1, Pallas kernels, on_device(): pl.pallas_call(functools.partial(filter_kernel, energy), out_shape=jax.Sh...  3.59 us
    broadcast_in_dim x1, local copies, waits for them, and re-layouts, on_device(): copies = jnp.broadcast_to(chunk, (devices // 2, size * ROWS, LANES))  1.36 us
  transfers between devices with their start and end apart: 5, of which 4 were waited for; matrix products, arithmetic and copies ran while one was open for 0% of the time, Pallas kernels for 1%

profile of v19, /device:TPU:0, one launch (start us, length us, event | category | flops | bytes accessed | tf_op | source)
XLA Modules:
  0.0 21.8 jit_solution(11113437711059599201)
XLA Ops:
  0.0 0.0 copy-start.2
  0.0 0.0 copy-start.3
  0.0 1.4 %broadcast_in_dim.8 = f32[16,16,128]{2,1,0:T(8,128)} broadcast(f32[16,128]{1,0:T(8,128)} %bitcast.4), dimensions={1,2} | broadcast | bytes 139264 | tf_op jit(solution)/shard_map/broadcast_in_dim | solution.py:286
  1.4 0.0 copy-start
  1.4 7.3 %all-to-all-start = ((f32[32,8,128]{2,1,0:T(8,128)}), f32[32,8,128]{2,1,0:T(8,128)S(1)}, u32[]{:S(2)}, u32[]{:S(2)}) async-start(f32[32,8,128]{2,1,0:T(8,128)} %bitcast.1), calls=%async_computation | async-start | bytes 262144 | tf_op jit(solution)/shard_map/all_to_all | solution.py:289
  8.7 0.0 copy-done.2
  8.7 1.8 %collective-permute-start = (bf16[2,16,512]{2,1,0:T(8,128)(2,1)S(1)}, bf16[2,16,512]{2,1,0:T(8,128)(2,1)S(1)}, u32[]{:S(2)}, u32[]{:S(2)}) collective-permute-start(bf16[2,16,512]{2,1,0:T(8,128)(2,1)S(1)} %copy-done.2), channel_id=1, source_target_pairs={{0,8},{8,0},{16,24},{24,16},{1,9},{9,1},{17,25},{25,17},{2,10},{10... | collective-permute-start | bytes 98312 | tf_op jit(solution)/shard_map/ppermute | solution.py:272
  10.5 1.5 %collective-permute-start.1 = (bf16[2,16,512]{2,1,0:T(8,128)(2,1)S(1)}, bf16[2,16,512]{2,1,0:T(8,128)(2,1)S(1)}, u32[]{:S(2)}, u32[]{:S(2)}) collective-permute-start(bf16[2,16,512]{2,1,0:T(8,128)(2,1)S(1)} %copy-done.2), channel_id=1, source_target_pairs={{0,16},{8,24},{16,0},{24,8},{1,17},{9,25},{17,1},{25,9},{2,18},{10... | collective-permute-start | bytes 98312 | tf_op jit(solution)/shard_map/ppermute | solution.py:272
  12.0 0.3 %collective-permute-start.2 = (bf16[2,16,512]{2,1,0:T(8,128)(2,1)S(1)}, bf16[2,16,512]{2,1,0:T(8,128)(2,1)S(1)}, u32[]{:S(2)}, u32[]{:S(2)}) collective-permute-start(bf16[2,16,512]{2,1,0:T(8,128)(2,1)S(1)} %copy-done.2), channel_id=1, source_target_pairs={{0,24},{8,16},{16,8},{24,0},{1,25},{9,17},{17,9},{25,1},{2,26},{10... | collective-permute-start | bytes 98312 | tf_op jit(solution)/shard_map/ppermute | solution.py:272
  12.2 0.6 %collective-permute-done.refs_1_ = bf16[2,16,512]{2,1,0:T(8,128)(2,1)S(1)} collective-permute-done((bf16[2,16,512]{2,1,0:T(8,128)(2,1)S(1)}, bf16[2,16,512]{2,1,0:T(8,128)(2,1)S(1)}, u32[]{:S(2)}, u32[]{:S(2)}) %collective-permute-start) | collective-permute-done | bytes 32800 | tf_op jit(solution)/shard_map/ppermute | solution.py:272
  12.8 1.7 %collective-permute-done.1.refs_2_ = bf16[2,16,512]{2,1,0:T(8,128)(2,1)S(1)} collective-permute-done((bf16[2,16,512]{2,1,0:T(8,128)(2,1)S(1)}, bf16[2,16,512]{2,1,0:T(8,128)(2,1)S(1)}, u32[]{:S(2)}, u32[]{:S(2)}) %collective-permute-start.1) | collective-permute-done | bytes 32800 | tf_op jit(solution)/shard_map/ppermute | solution.py:272
  14.5 2.4 %collective-permute-done.2.refs_3_ = bf16[2,16,512]{2,1,0:T(8,128)(2,1)S(1)} collective-permute-done((bf16[2,16,512]{2,1,0:T(8,128)(2,1)S(1)}, bf16[2,16,512]{2,1,0:T(8,128)(2,1)S(1)}, u32[]{:S(2)}, u32[]{:S(2)}) %collective-permute-start.2) | collective-permute-done | bytes 32800 | tf_op jit(solution)/shard_map/ppermute | solution.py:272
  16.9 0.0 all-to-all-done.mine
  16.9 0.3 %collective-permute-start.3 = (f32[32,8,128]{2,1,0:T(8,128)S(1)}, f32[32,8,128]{2,1,0:T(8,128)S(1)}, u32[]{:S(2)}, u32[]{:S(2)}) collective-permute-start(f32[32,8,128]{2,1,0:T(8,128)S(1)} %all-to-all-done.mine), channel_id=1, source_target_pairs={{0,1},{1,0},{2,3},{3,2},{4,5},{5,4},{6,7},{7,6},{8,9},{9,8},{10,11... | collective-permute-start | bytes 393224 | tf_op jit(solution)/shard_map/ppermute | solution.py:272
  17.2 0.0 copy-done.3
  17.2 0.0 copy-start.1
  17.2 0.3 %bank.1 = f32[2,16,16,128]{3,2,1,0:T(8,128)S(1)} custom-call(bf16[2,16,512]{2,1,0:T(8,128)(2,1)S(1)} %copy-done.2, bf16[2,16,512]{2,1,0:T(8,128)(2,1)S(1)} %collective-permute-done.refs_1_, bf16[2,16,512]{2,1,0:T(8,128)(2,1)S(1)} %collective-permute-done.1.refs_2_, bf16[2,16,512]{2,1,0:T(8,128)(2,1)S(1)} %collective-permute-done.2.refs_3_, s32[1,16]{1,0:T(1,128)S(1)} %bitcast.3), custom_call_target="tpu_custom_call" | custom-call | bytes 2500000 | tf_op jit(solution)/shard_map/bank/pallas_call | solution.py:294
  17.5 0.8 %collective-permute-done.3.others = f32[32,8,128]{2,1,0:T(8,128)S(1)} collective-permute-done((f32[32,8,128]{2,1,0:T(8,128)S(1)}, f32[32,8,128]{2,1,0:T(8,128)S(1)}, u32[]{:S(2)}, u32[]{:S(2)}) %collective-permute-start.3) | collective-permute-done | bytes 131104 | tf_op jit(solution)/shard_map/ppermute | solution.py:272
  18.2 0.0 copy-done
  18.3 0.0 copy-done.1
  18.3 3.6 %matched_filter.1 = f32[8,16]{1,0:T(8,128)} custom-call(f32[32,8,128]{2,1,0:T(8,128)S(1)} %all-to-all-done.mine, f32[32,8,128]{2,1,0:T(8,128)S(1)} %collective-permute-done.3.others, f32[2,16,16,128]{3,2,1,0:T(8,128)S(1)} %bank.1, bf16[704,256]{1,0:T(8,128)(2,1)S(1)} %copy-done, f32[160,128]{1,0:T(8,128)S(1)} %copy-done.1), custom_call_target="tpu_custom_call" | custom-call | tf_op jit(solution)/shard_map/matched_filter/pallas_call | solution.py:305
Async XLA Ops:
  0.0 8.7 %copy-start.2 = (bf16[2,16,512]{2,1,0:T(8,128)(2,1)S(1)}, bf16[2,16,512]{2,1,0:T(8,128)(2,1)}, u32[]{:S(2)}) copy-start(bf16[2,16,512]{2,1,0:T(8,128)(2,1)} %refs_0_) | copy-start | bytes 98308
  0.0 17.2 %copy-start.3 = (s32[16]{0:T(128)S(1)}, s32[16]{0:T(128)}, u32[]{:S(2)}) copy-start(s32[16]{0:T(128)} %param.7) | copy-start | bytes 196
  1.4 16.9 %copy-start = (bf16[704,256]{1,0:T(8,128)(2,1)S(1)}, bf16[704,256]{1,0:T(8,128)(2,1)}, u32[]{:S(2)}) copy-start(bf16[704,256]{1,0:T(8,128)(2,1)} %constant.4.clone.narrow) | copy-start | bytes 1081348
  1.4 15.5 %all-to-all-start = ((f32[32,8,128]{2,1,0:T(8,128)}), f32[32,8,128]{2,1,0:T(8,128)S(1)}, u32[]{:S(2)}, u32[]{:S(2)}) async-start(f32[32,8,128]{2,1,0:T(8,128)} %bitcast.1), calls=%async_computation | async-start | bytes 262144 | tf_op jit(solution)/shard_map/all_to_all | solution.py:289
  8.7 4.2 %collective-permute-start = (bf16[2,16,512]{2,1,0:T(8,128)(2,1)S(1)}, bf16[2,16,512]{2,1,0:T(8,128)(2,1)S(1)}, u32[]{:S(2)}, u32[]{:S(2)}) collective-permute-start(bf16[2,16,512]{2,1,0:T(8,128)(2,1)S(1)} %copy-done.2), channel_id=1, source_target_pairs={{0,8},{8,0},{16,24},{24,16},{1,9},{9,1},{17,25},{25,17},{2,10},{10... | collective-permute-start | bytes 98312 | tf_op jit(solution)/shard_map/ppermute | solution.py:272
  10.5 4.0 %collective-permute-start.1 = (bf16[2,16,512]{2,1,0:T(8,128)(2,1)S(1)}, bf16[2,16,512]{2,1,0:T(8,128)(2,1)S(1)}, u32[]{:S(2)}, u32[]{:S(2)}) collective-permute-start(bf16[2,16,512]{2,1,0:T(8,128)(2,1)S(1)} %copy-done.2), channel_id=1, source_target_pairs={{0,16},{8,24},{16,0},{24,8},{1,17},{9,25},{17,1},{25,9},{2,18},{10... | collective-permute-start | bytes 98312 | tf_op jit(solution)/shard_map/ppermute | solution.py:272
  12.0 4.9 %collective-permute-start.2 = (bf16[2,16,512]{2,1,0:T(8,128)(2,1)S(1)}, bf16[2,16,512]{2,1,0:T(8,128)(2,1)S(1)}, u32[]{:S(2)}, u32[]{:S(2)}) collective-permute-start(bf16[2,16,512]{2,1,0:T(8,128)(2,1)S(1)} %copy-done.2), channel_id=1, source_target_pairs={{0,24},{8,16},{16,8},{24,0},{1,25},{9,17},{17,9},{25,1},{2,26},{10... | collective-permute-start | bytes 98312 | tf_op jit(solution)/shard_map/ppermute | solution.py:272
  16.9 1.3 %collective-permute-start.3 = (f32[32,8,128]{2,1,0:T(8,128)S(1)}, f32[32,8,128]{2,1,0:T(8,128)S(1)}, u32[]{:S(2)}, u32[]{:S(2)}) collective-permute-start(f32[32,8,128]{2,1,0:T(8,128)S(1)} %all-to-all-done.mine), channel_id=1, source_target_pairs={{0,1},{1,0},{2,3},{3,2},{4,5},{5,4},{6,7},{7,6},{8,9},{9,8},{10,11... | collective-permute-start | bytes 393224 | tf_op jit(solution)/shard_map/ppermute | solution.py:272
  17.2 1.1 %copy-start.1 = (f32[160,128]{1,0:T(8,128)S(1)}, f32[160,128]{1,0:T(8,128)}, u32[]{:S(2)}) copy-start(f32[160,128]{1,0:T(8,128)} %constant.5.clone.broad) | copy-start | bytes 245764

commit v20 on v17

--- a/solution.py
+++ b/solution.py
@@ -234,11 +234,14 @@
                 sides.append(both.astype(jnp.bfloat16))
             return dot(third, jnp.concatenate(sides, axis=1)), norms
 
-        def wave_of(section, side):
-            re = section[:half, side * LANES:(side + 1) * LANES].reshape(GROUP, FINE, LANES)
-            im = section[half:, side * LANES:(side + 1) * LANES].reshape(GROUP, FINE, LANES)
-            turned = jnp.concatenate([re * inv_cos - im * inv_sin, re * inv_sin + im * inv_cos], axis=2)
-            return dot(turned.reshape(half, 2 * LANES).astype(jnp.bfloat16), narrow[fourth])
+        def waves_of(section):
+            sides = []
+            for side in range(2):
+                re = section[:half, side * LANES:(side + 1) * LANES].reshape(GROUP, FINE, LANES)
+                im = section[half:, side * LANES:(side + 1) * LANES].reshape(GROUP, FINE, LANES)
+                turned = jnp.concatenate([re * inv_cos - im * inv_sin, re * inv_sin + im * inv_cos], axis=2)
+                sides.append(turned.reshape(half, 2 * LANES).astype(jnp.bfloat16))
+            return dot(jnp.concatenate(sides, axis=0), narrow[fourth])
 
         def peak_of(m, wave, norm, result):
             square = wave[:, :LANES] * wave[:, :LANES] + wave[:, LANES:] * wave[:, LANES:]
@@ -252,12 +255,13 @@
             section, norms = ready
             if step + 1 < count // 2:
                 ready = section_of(step + 1)
-            for side in range(2):
-                wave = wave_of(section, side)
-                if waiting is not None:
-                    result = peak_of(*waiting, result)
-                waiting = (2 * step + side, wave, norms[side])
-        result = peak_of(*waiting, result)
+            waves = waves_of(section)
+            if waiting is not None:
+                for ready_peak in waiting:
+                    result = peak_of(*ready_peak, result)
+            waiting = [(2 * step + i, waves[i * half:(i + 1) * half], norms[i]) for i in range(2)]
+        for ready_peak in waiting:
+            result = peak_of(*ready_peak, result)
         out[pl.ds(number * GROUP, GROUP)] = result[:, :count]
         return carry
 

time: 22.1 us -> 22 us (level)
  no operation moved by 1% of the time
where the time goes in v20:
time: 22 us; the launch traced here: 21.8 us
  starting transfers between devices  11.1 us (50%)
  waiting for transfers between devices  5.45 us (25%)
  Pallas kernels  3.79 us (17%)
  local copies, waits for them, and re-layouts  1.37 us (6%)
    all_to_all x1, starting transfers between devices, on_device(): lax.all_to_all(copies, ('tm', 'tmpl'), split_axis=0, concat_axis=0, tiled...  7.3 us
    ppermute x4, waiting for transfers between devices, swap(): lax.ppermute(array, axis, [(i, i ^ bits) for i in range(lax.axis_size(axi...  5.45 us
    ppermute x4, starting transfers between devices, swap(): lax.ppermute(array, axis, [(i, i ^ bits) for i in range(lax.axis_size(axi...  3.81 us
    pallas_call x1, Pallas kernels, on_device(): pl.pallas_call(functools.partial(filter_kernel, energy), out_shape=jax.Sh...  3.5 us
    broadcast_in_dim x1, local copies, waits for them, and re-layouts, on_device(): copies = jnp.broadcast_to(chunk, (devices // 2, size * ROWS, LANES))  1.36 us
  transfers between devices with their start and end apart: 5, of which 4 were waited for; matrix products, arithmetic and copies ran while one was open for 0% of the time, Pallas kernels for 1%

profile of v20, /device:TPU:0, one launch (start us, length us, event | category | flops | bytes accessed | tf_op | source)
XLA Modules:
  0.0 21.8 jit_solution(14719676881043563656)
XLA Ops:
  0.0 0.0 copy-start.2
  0.0 0.0 copy-start.3
  0.0 1.4 %broadcast_in_dim.8 = f32[16,16,128]{2,1,0:T(8,128)} broadcast(f32[16,128]{1,0:T(8,128)} %bitcast.4), dimensions={1,2} | broadcast | bytes 139264 | tf_op jit(solution)/shard_map/broadcast_in_dim | solution.py:286
  1.4 0.0 copy-start
  1.4 7.3 %all-to-all-start = ((f32[32,8,128]{2,1,0:T(8,128)}), f32[32,8,128]{2,1,0:T(8,128)S(1)}, u32[]{:S(2)}, u32[]{:S(2)}) async-start(f32[32,8,128]{2,1,0:T(8,128)} %bitcast.1), calls=%async_computation | async-start | bytes 262144 | tf_op jit(solution)/shard_map/all_to_all | solution.py:289
  8.7 0.0 copy-done.2
  8.7 1.8 %collective-permute-start = (bf16[2,16,512]{2,1,0:T(8,128)(2,1)S(1)}, bf16[2,16,512]{2,1,0:T(8,128)(2,1)S(1)}, u32[]{:S(2)}, u32[]{:S(2)}) collective-permute-start(bf16[2,16,512]{2,1,0:T(8,128)(2,1)S(1)} %copy-done.2), channel_id=1, source_target_pairs={{0,8},{8,0},{16,24},{24,16},{1,9},{9,1},{17,25},{25,17},{2,10},{10... | collective-permute-start | bytes 98312 | tf_op jit(solution)/shard_map/ppermute | solution.py:272
  10.5 1.5 %collective-permute-start.1 = (bf16[2,16,512]{2,1,0:T(8,128)(2,1)S(1)}, bf16[2,16,512]{2,1,0:T(8,128)(2,1)S(1)}, u32[]{:S(2)}, u32[]{:S(2)}) collective-permute-start(bf16[2,16,512]{2,1,0:T(8,128)(2,1)S(1)} %copy-done.2), channel_id=1, source_target_pairs={{0,16},{8,24},{16,0},{24,8},{1,17},{9,25},{17,1},{25,9},{2,18},{10... | collective-permute-start | bytes 98312 | tf_op jit(solution)/shard_map/ppermute | solution.py:272
  12.0 0.3 %collective-permute-start.2 = (bf16[2,16,512]{2,1,0:T(8,128)(2,1)S(1)}, bf16[2,16,512]{2,1,0:T(8,128)(2,1)S(1)}, u32[]{:S(2)}, u32[]{:S(2)}) collective-permute-start(bf16[2,16,512]{2,1,0:T(8,128)(2,1)S(1)} %copy-done.2), channel_id=1, source_target_pairs={{0,24},{8,16},{16,8},{24,0},{1,25},{9,17},{17,9},{25,1},{2,26},{10... | collective-permute-start | bytes 98312 | tf_op jit(solution)/shard_map/ppermute | solution.py:272
  12.2 0.6 %collective-permute-done.refs_1_ = bf16[2,16,512]{2,1,0:T(8,128)(2,1)S(1)} collective-permute-done((bf16[2,16,512]{2,1,0:T(8,128)(2,1)S(1)}, bf16[2,16,512]{2,1,0:T(8,128)(2,1)S(1)}, u32[]{:S(2)}, u32[]{:S(2)}) %collective-permute-start) | collective-permute-done | bytes 32800 | tf_op jit(solution)/shard_map/ppermute | solution.py:272
  12.8 1.7 %collective-permute-done.1.refs_2_ = bf16[2,16,512]{2,1,0:T(8,128)(2,1)S(1)} collective-permute-done((bf16[2,16,512]{2,1,0:T(8,128)(2,1)S(1)}, bf16[2,16,512]{2,1,0:T(8,128)(2,1)S(1)}, u32[]{:S(2)}, u32[]{:S(2)}) %collective-permute-start.1) | collective-permute-done | bytes 32800 | tf_op jit(solution)/shard_map/ppermute | solution.py:272
  14.5 2.4 %collective-permute-done.2.refs_3_ = bf16[2,16,512]{2,1,0:T(8,128)(2,1)S(1)} collective-permute-done((bf16[2,16,512]{2,1,0:T(8,128)(2,1)S(1)}, bf16[2,16,512]{2,1,0:T(8,128)(2,1)S(1)}, u32[]{:S(2)}, u32[]{:S(2)}) %collective-permute-start.2) | collective-permute-done | bytes 32800 | tf_op jit(solution)/shard_map/ppermute | solution.py:272
  16.9 0.0 all-to-all-done.mine
  16.9 0.3 %collective-permute-start.3 = (f32[32,8,128]{2,1,0:T(8,128)S(1)}, f32[32,8,128]{2,1,0:T(8,128)S(1)}, u32[]{:S(2)}, u32[]{:S(2)}) collective-permute-start(f32[32,8,128]{2,1,0:T(8,128)S(1)} %all-to-all-done.mine), channel_id=1, source_target_pairs={{0,1},{1,0},{2,3},{3,2},{4,5},{5,4},{6,7},{7,6},{8,9},{9,8},{10,11... | collective-permute-start | bytes 393224 | tf_op jit(solution)/shard_map/ppermute | solution.py:272
  17.2 0.0 copy-done.3
  17.2 0.0 copy-start.1
  17.2 0.3 %bank.1 = f32[2,16,16,128]{3,2,1,0:T(8,128)S(1)} custom-call(bf16[2,16,512]{2,1,0:T(8,128)(2,1)S(1)} %copy-done.2, bf16[2,16,512]{2,1,0:T(8,128)(2,1)S(1)} %collective-permute-done.refs_1_, bf16[2,16,512]{2,1,0:T(8,128)(2,1)S(1)} %collective-permute-done.1.refs_2_, bf16[2,16,512]{2,1,0:T(8,128)(2,1)S(1)} %collective-permute-done.2.refs_3_, s32[1,16]{1,0:T(1,128)S(1)} %bitcast.3), custom_call_target="tpu_custom_call" | custom-call | bytes 2500000 | tf_op jit(solution)/shard_map/bank/pallas_call | solution.py:294
  17.5 0.8 %collective-permute-done.3.others = f32[32,8,128]{2,1,0:T(8,128)S(1)} collective-permute-done((f32[32,8,128]{2,1,0:T(8,128)S(1)}, f32[32,8,128]{2,1,0:T(8,128)S(1)}, u32[]{:S(2)}, u32[]{:S(2)}) %collective-permute-start.3) | collective-permute-done | bytes 131104 | tf_op jit(solution)/shard_map/ppermute | solution.py:272
  18.2 0.0 copy-done
  18.3 0.0 copy-done.1
  18.3 3.5 %matched_filter.1 = f32[8,16]{1,0:T(8,128)} custom-call(f32[32,8,128]{2,1,0:T(8,128)S(1)} %all-to-all-done.mine, f32[32,8,128]{2,1,0:T(8,128)S(1)} %collective-permute-done.3.others, f32[2,16,16,128]{3,2,1,0:T(8,128)S(1)} %bank.1, bf16[704,256]{1,0:T(8,128)(2,1)S(1)} %copy-done, f32[160,128]{1,0:T(8,128)S(1)} %copy-done.1), custom_call_target="tpu_custom_call" | custom-call | tf_op jit(solution)/shard_map/matched_filter/pallas_call | solution.py:305
Async XLA Ops:
  0.0 8.7 %copy-start.2 = (bf16[2,16,512]{2,1,0:T(8,128)(2,1)S(1)}, bf16[2,16,512]{2,1,0:T(8,128)(2,1)}, u32[]{:S(2)}) copy-start(bf16[2,16,512]{2,1,0:T(8,128)(2,1)} %refs_0_) | copy-start | bytes 98308
  0.0 17.2 %copy-start.3 = (s32[16]{0:T(128)S(1)}, s32[16]{0:T(128)}, u32[]{:S(2)}) copy-start(s32[16]{0:T(128)} %param.7) | copy-start | bytes 196
  1.4 16.9 %copy-start = (bf16[704,256]{1,0:T(8,128)(2,1)S(1)}, bf16[704,256]{1,0:T(8,128)(2,1)}, u32[]{:S(2)}) copy-start(bf16[704,256]{1,0:T(8,128)(2,1)} %constant.4.clone.narrow) | copy-start | bytes 1081348
  1.4 15.5 %all-to-all-start = ((f32[32,8,128]{2,1,0:T(8,128)}), f32[32,8,128]{2,1,0:T(8,128)S(1)}, u32[]{:S(2)}, u32[]{:S(2)}) async-start(f32[32,8,128]{2,1,0:T(8,128)} %bitcast.1), calls=%async_computation | async-start | bytes 262144 | tf_op jit(solution)/shard_map/all_to_all | solution.py:289
  8.7 4.2 %collective-permute-start = (bf16[2,16,512]{2,1,0:T(8,128)(2,1)S(1)}, bf16[2,16,512]{2,1,0:T(8,128)(2,1)S(1)}, u32[]{:S(2)}, u32[]{:S(2)}) collective-permute-start(bf16[2,16,512]{2,1,0:T(8,128)(2,1)S(1)} %copy-done.2), channel_id=1, source_target_pairs={{0,8},{8,0},{16,24},{24,16},{1,9},{9,1},{17,25},{25,17},{2,10},{10... | collective-permute-start | bytes 98312 | tf_op jit(solution)/shard_map/ppermute | solution.py:272
  10.5 4.0 %collective-permute-start.1 = (bf16[2,16,512]{2,1,0:T(8,128)(2,1)S(1)}, bf16[2,16,512]{2,1,0:T(8,128)(2,1)S(1)}, u32[]{:S(2)}, u32[]{:S(2)}) collective-permute-start(bf16[2,16,512]{2,1,0:T(8,128)(2,1)S(1)} %copy-done.2), channel_id=1, source_target_pairs={{0,16},{8,24},{16,0},{24,8},{1,17},{9,25},{17,1},{25,9},{2,18},{10... | collective-permute-start | bytes 98312 | tf_op jit(solution)/shard_map/ppermute | solution.py:272
  12.0 4.9 %collective-permute-start.2 = (bf16[2,16,512]{2,1,0:T(8,128)(2,1)S(1)}, bf16[2,16,512]{2,1,0:T(8,128)(2,1)S(1)}, u32[]{:S(2)}, u32[]{:S(2)}) collective-permute-start(bf16[2,16,512]{2,1,0:T(8,128)(2,1)S(1)} %copy-done.2), channel_id=1, source_target_pairs={{0,24},{8,16},{16,8},{24,0},{1,25},{9,17},{17,9},{25,1},{2,26},{10... | collective-permute-start | bytes 98312 | tf_op jit(solution)/shard_map/ppermute | solution.py:272
  16.9 1.3 %collective-permute-start.3 = (f32[32,8,128]{2,1,0:T(8,128)S(1)}, f32[32,8,128]{2,1,0:T(8,128)S(1)}, u32[]{:S(2)}, u32[]{:S(2)}) collective-permute-start(f32[32,8,128]{2,1,0:T(8,128)S(1)} %all-to-all-done.mine), channel_id=1, source_target_pairs={{0,1},{1,0},{2,3},{3,2},{4,5},{5,4},{6,7},{7,6},{8,9},{9,8},{10,11... | collective-permute-start | bytes 393224 | tf_op jit(solution)/shard_map/ppermute | solution.py:272
  17.2 1.1 %copy-start.1 = (f32[160,128]{1,0:T(8,128)S(1)}, f32[160,128]{1,0:T(8,128)}, u32[]{:S(2)}) copy-start(f32[160,128]{1,0:T(8,128)} %constant.5.clone.broad) | copy-start | bytes 245764

commit v21 on v20

--- a/solution.py
+++ b/solution.py
@@ -167,23 +167,23 @@
         high, low = split(pair)
         return dot(first, jnp.concatenate([high, low, high], axis=0))
 
-    def second_product(step, h):
-        re = step[:half, h * LANES:(h + 1) * LANES].reshape(GROUP, FINE, LANES)
-        im = step[half:, h * LANES:(h + 1) * LANES].reshape(GROUP, FINE, LANES)
-        turned = jnp.concatenate([re * fwd_cos + im * fwd_sin, im * fwd_cos - re * fwd_sin], axis=2)
-        high, low = split(turned.reshape(half, 2 * LANES))
-        return dot(jnp.concatenate([high, low], axis=1), jnp.concatenate([narrow[second]] * 2, axis=0))
+    def second_product(step):
+        sides = []
+        for h in range(2):
+            re = step[:half, h * LANES:(h + 1) * LANES].reshape(GROUP, FINE, LANES)
+            im = step[half:, h * LANES:(h + 1) * LANES].reshape(GROUP, FINE, LANES)
+            turned = jnp.concatenate([re * fwd_cos + im * fwd_sin, im * fwd_cos - re * fwd_sin], axis=2)
+            high, low = split(turned.reshape(half, 2 * LANES))
+            sides.append(jnp.concatenate([high, low], axis=1))
+        return dot(jnp.concatenate(sides, axis=0), jnp.concatenate([narrow[second]] * 2, axis=0))
 
     def add_power(both, at, power):
         value = both[:, :LANES] + both[:, LANES:]
-        spec[pl.ds(at * FINE, half)] = value
-        return power + jnp.sum((value * value).reshape(GROUP, FINE, LANES), axis=0)
+        spec[pl.ds(at * FINE, 2 * half)] = value
+        return power + jnp.sum((value * value).reshape(2 * GROUP, FINE, LANES), axis=0)
 
     def whole(start, last, power):
-        step = first_product(start, last)
-        for h in range(2):
-            power = add_power(second_product(step, h), start + h * GROUP, power)
-        return power
+        return add_power(second_product(first_product(start, last)), start, power)
 
     power = jnp.zeros((FINE, LANES), jnp.float32)
     pairs = segs // (2 * GROUP)
@@ -192,11 +192,10 @@
         steps = [first_product(i * stride, i == pairs - 1) for i in range(pairs)]
         waiting = None
         for i, step in enumerate(steps):
-            for h in range(2):
-                both = second_product(step, h)
-                if waiting is not None:
-                    power = add_power(*waiting, power)
-                waiting = (both, i * stride + h * GROUP)
+            both = second_product(step)
+            if waiting is not None:
+                power = add_power(*waiting, power)
+            waiting = (both, i * stride)
         power = add_power(*waiting, power)
     else:
         power = lax.fori_loop(0, pairs - 1, lambda i, p: whole(i * stride, False, p), power)

time: 22 us -> 22 us (level)
  no operation moved by 1% of the time
where the time goes in v21:
time: 22 us; the launch traced here: 21.7 us
  starting transfers between devices  11.1 us (50%)
  waiting for transfers between devices  5.45 us (25%)
  Pallas kernels  3.77 us (17%)
  local copies, waits for them, and re-layouts  1.37 us (6%)
    all_to_all x1, starting transfers between devices, on_device(): lax.all_to_all(copies, ('tm', 'tmpl'), split_axis=0, concat_axis=0, tiled...  7.3 us
    ppermute x4, waiting for transfers between devices, swap(): lax.ppermute(array, axis, [(i, i ^ bits) for i in range(lax.axis_size(axi...  5.45 us
    ppermute x4, starting transfers between devices, swap(): lax.ppermute(array, axis, [(i, i ^ bits) for i in range(lax.axis_size(axi...  3.81 us
    pallas_call x1, Pallas kernels, on_device(): pl.pallas_call(functools.partial(filter_kernel, energy), out_shape=jax.Sh...  3.48 us
    broadcast_in_dim x1, local copies, waits for them, and re-layouts, on_device(): copies = jnp.broadcast_to(chunk, (devices // 2, size * ROWS, LANES))  1.36 us
  transfers between devices with their start and end apart: 5, of which 4 were waited for; matrix products, arithmetic and copies ran while one was open for 0% of the time, Pallas kernels for 1%

profile of v21, /device:TPU:0, one launch (start us, length us, event | category | flops | bytes accessed | tf_op | source)
XLA Modules:
  0.0 21.7 jit_solution(11741282704408274027)
XLA Ops:
  0.0 0.0 copy-start.2
  0.0 0.0 copy-start.3
  0.0 1.4 %broadcast_in_dim.8 = f32[16,16,128]{2,1,0:T(8,128)} broadcast(f32[16,128]{1,0:T(8,128)} %bitcast.4), dimensions={1,2} | broadcast | bytes 139264 | tf_op jit(solution)/shard_map/broadcast_in_dim | solution.py:285
  1.4 0.0 copy-start
  1.4 7.3 %all-to-all-start = ((f32[32,8,128]{2,1,0:T(8,128)}), f32[32,8,128]{2,1,0:T(8,128)S(1)}, u32[]{:S(2)}, u32[]{:S(2)}) async-start(f32[32,8,128]{2,1,0:T(8,128)} %bitcast.1), calls=%async_computation | async-start | bytes 262144 | tf_op jit(solution)/shard_map/all_to_all | solution.py:288
  8.7 0.0 copy-done.2
  8.7 1.8 %collective-permute-start = (bf16[2,16,512]{2,1,0:T(8,128)(2,1)S(1)}, bf16[2,16,512]{2,1,0:T(8,128)(2,1)S(1)}, u32[]{:S(2)}, u32[]{:S(2)}) collective-permute-start(bf16[2,16,512]{2,1,0:T(8,128)(2,1)S(1)} %copy-done.2), channel_id=1, source_target_pairs={{0,8},{8,0},{16,24},{24,16},{1,9},{9,1},{17,25},{25,17},{2,10},{10... | collective-permute-start | bytes 98312 | tf_op jit(solution)/shard_map/ppermute | solution.py:271
  10.5 1.5 %collective-permute-start.1 = (bf16[2,16,512]{2,1,0:T(8,128)(2,1)S(1)}, bf16[2,16,512]{2,1,0:T(8,128)(2,1)S(1)}, u32[]{:S(2)}, u32[]{:S(2)}) collective-permute-start(bf16[2,16,512]{2,1,0:T(8,128)(2,1)S(1)} %copy-done.2), channel_id=1, source_target_pairs={{0,16},{8,24},{16,0},{24,8},{1,17},{9,25},{17,1},{25,9},{2,18},{10... | collective-permute-start | bytes 98312 | tf_op jit(solution)/shard_map/ppermute | solution.py:271
  12.0 0.3 %collective-permute-start.2 = (bf16[2,16,512]{2,1,0:T(8,128)(2,1)S(1)}, bf16[2,16,512]{2,1,0:T(8,128)(2,1)S(1)}, u32[]{:S(2)}, u32[]{:S(2)}) collective-permute-start(bf16[2,16,512]{2,1,0:T(8,128)(2,1)S(1)} %copy-done.2), channel_id=1, source_target_pairs={{0,24},{8,16},{16,8},{24,0},{1,25},{9,17},{17,9},{25,1},{2,26},{10... | collective-permute-start | bytes 98312 | tf_op jit(solution)/shard_map/ppermute | solution.py:271
  12.2 0.6 %collective-permute-done.refs_1_ = bf16[2,16,512]{2,1,0:T(8,128)(2,1)S(1)} collective-permute-done((bf16[2,16,512]{2,1,0:T(8,128)(2,1)S(1)}, bf16[2,16,512]{2,1,0:T(8,128)(2,1)S(1)}, u32[]{:S(2)}, u32[]{:S(2)}) %collective-permute-start) | collective-permute-done | bytes 32800 | tf_op jit(solution)/shard_map/ppermute | solution.py:271
  12.8 1.7 %collective-permute-done.1.refs_2_ = bf16[2,16,512]{2,1,0:T(8,128)(2,1)S(1)} collective-permute-done((bf16[2,16,512]{2,1,0:T(8,128)(2,1)S(1)}, bf16[2,16,512]{2,1,0:T(8,128)(2,1)S(1)}, u32[]{:S(2)}, u32[]{:S(2)}) %collective-permute-start.1) | collective-permute-done | bytes 32800 | tf_op jit(solution)/shard_map/ppermute | solution.py:271
  14.5 2.4 %collective-permute-done.2.refs_3_ = bf16[2,16,512]{2,1,0:T(8,128)(2,1)S(1)} collective-permute-done((bf16[2,16,512]{2,1,0:T(8,128)(2,1)S(1)}, bf16[2,16,512]{2,1,0:T(8,128)(2,1)S(1)}, u32[]{:S(2)}, u32[]{:S(2)}) %collective-permute-start.2) | collective-permute-done | bytes 32800 | tf_op jit(solution)/shard_map/ppermute | solution.py:271
  16.9 0.0 all-to-all-done.mine
  16.9 0.3 %collective-permute-start.3 = (f32[32,8,128]{2,1,0:T(8,128)S(1)}, f32[32,8,128]{2,1,0:T(8,128)S(1)}, u32[]{:S(2)}, u32[]{:S(2)}) collective-permute-start(f32[32,8,128]{2,1,0:T(8,128)S(1)} %all-to-all-done.mine), channel_id=1, source_target_pairs={{0,1},{1,0},{2,3},{3,2},{4,5},{5,4},{6,7},{7,6},{8,9},{9,8},{10,11... | collective-permute-start | bytes 393224 | tf_op jit(solution)/shard_map/ppermute | solution.py:271
  17.2 0.0 copy-done.3
  17.2 0.0 copy-start.1
  17.2 0.3 %bank.1 = f32[2,16,16,128]{3,2,1,0:T(8,128)S(1)} custom-call(bf16[2,16,512]{2,1,0:T(8,128)(2,1)S(1)} %copy-done.2, bf16[2,16,512]{2,1,0:T(8,128)(2,1)S(1)} %collective-permute-done.refs_1_, bf16[2,16,512]{2,1,0:T(8,128)(2,1)S(1)} %collective-permute-done.1.refs_2_, bf16[2,16,512]{2,1,0:T(8,128)(2,1)S(1)} %collective-permute-done.2.refs_3_, s32[1,16]{1,0:T(1,128)S(1)} %bitcast.3), custom_call_target="tpu_custom_call" | custom-call | bytes 2500000 | tf_op jit(solution)/shard_map/bank/pallas_call | solution.py:293
  17.5 0.8 %collective-permute-done.3.others = f32[32,8,128]{2,1,0:T(8,128)S(1)} collective-permute-done((f32[32,8,128]{2,1,0:T(8,128)S(1)}, f32[32,8,128]{2,1,0:T(8,128)S(1)}, u32[]{:S(2)}, u32[]{:S(2)}) %collective-permute-start.3) | collective-permute-done | bytes 131104 | tf_op jit(solution)/shard_map/ppermute | solution.py:271
  18.2 0.0 copy-done
  18.3 0.0 copy-done.1
  18.3 3.5 %matched_filter.1 = f32[8,16]{1,0:T(8,128)} custom-call(f32[32,8,128]{2,1,0:T(8,128)S(1)} %all-to-all-done.mine, f32[32,8,128]{2,1,0:T(8,128)S(1)} %collective-permute-done.3.others, f32[2,16,16,128]{3,2,1,0:T(8,128)S(1)} %bank.1, bf16[704,256]{1,0:T(8,128)(2,1)S(1)} %copy-done, f32[160,128]{1,0:T(8,128)S(1)} %copy-done.1), custom_call_target="tpu_custom_call" | custom-call | tf_op jit(solution)/shard_map/matched_filter/pallas_call | solution.py:304
Async XLA Ops:
  0.0 8.7 %copy-start.2 = (bf16[2,16,512]{2,1,0:T(8,128)(2,1)S(1)}, bf16[2,16,512]{2,1,0:T(8,128)(2,1)}, u32[]{:S(2)}) copy-start(bf16[2,16,512]{2,1,0:T(8,128)(2,1)} %refs_0_) | copy-start | bytes 98308
  0.0 17.2 %copy-start.3 = (s32[16]{0:T(128)S(1)}, s32[16]{0:T(128)}, u32[]{:S(2)}) copy-start(s32[16]{0:T(128)} %param.7) | copy-start | bytes 196
  1.4 16.9 %copy-start = (bf16[704,256]{1,0:T(8,128)(2,1)S(1)}, bf16[704,256]{1,0:T(8,128)(2,1)}, u32[]{:S(2)}) copy-start(bf16[704,256]{1,0:T(8,128)(2,1)} %constant.4.clone.narrow) | copy-start | bytes 1081348
  1.4 15.5 %all-to-all-start = ((f32[32,8,128]{2,1,0:T(8,128)}), f32[32,8,128]{2,1,0:T(8,128)S(1)}, u32[]{:S(2)}, u32[]{:S(2)}) async-start(f32[32,8,128]{2,1,0:T(8,128)} %bitcast.1), calls=%async_computation | async-start | bytes 262144 | tf_op jit(solution)/shard_map/all_to_all | solution.py:288
  8.7 4.2 %collective-permute-start = (bf16[2,16,512]{2,1,0:T(8,128)(2,1)S(1)}, bf16[2,16,512]{2,1,0:T(8,128)(2,1)S(1)}, u32[]{:S(2)}, u32[]{:S(2)}) collective-permute-start(bf16[2,16,512]{2,1,0:T(8,128)(2,1)S(1)} %copy-done.2), channel_id=1, source_target_pairs={{0,8},{8,0},{16,24},{24,16},{1,9},{9,1},{17,25},{25,17},{2,10},{10... | collective-permute-start | bytes 98312 | tf_op jit(solution)/shard_map/ppermute | solution.py:271
  10.5 4.0 %collective-permute-start.1 = (bf16[2,16,512]{2,1,0:T(8,128)(2,1)S(1)}, bf16[2,16,512]{2,1,0:T(8,128)(2,1)S(1)}, u32[]{:S(2)}, u32[]{:S(2)}) collective-permute-start(bf16[2,16,512]{2,1,0:T(8,128)(2,1)S(1)} %copy-done.2), channel_id=1, source_target_pairs={{0,16},{8,24},{16,0},{24,8},{1,17},{9,25},{17,1},{25,9},{2,18},{10... | collective-permute-start | bytes 98312 | tf_op jit(solution)/shard_map/ppermute | solution.py:271
  12.0 4.9 %collective-permute-start.2 = (bf16[2,16,512]{2,1,0:T(8,128)(2,1)S(1)}, bf16[2,16,512]{2,1,0:T(8,128)(2,1)S(1)}, u32[]{:S(2)}, u32[]{:S(2)}) collective-permute-start(bf16[2,16,512]{2,1,0:T(8,128)(2,1)S(1)} %copy-done.2), channel_id=1, source_target_pairs={{0,24},{8,16},{16,8},{24,0},{1,25},{9,17},{17,9},{25,1},{2,26},{10... | collective-permute-start | bytes 98312 | tf_op jit(solution)/shard_map/ppermute | solution.py:271
  16.9 1.3 %collective-permute-start.3 = (f32[32,8,128]{2,1,0:T(8,128)S(1)}, f32[32,8,128]{2,1,0:T(8,128)S(1)}, u32[]{:S(2)}, u32[]{:S(2)}) collective-permute-start(f32[32,8,128]{2,1,0:T(8,128)S(1)} %all-to-all-done.mine), channel_id=1, source_target_pairs={{0,1},{1,0},{2,3},{3,2},{4,5},{5,4},{6,7},{7,6},{8,9},{9,8},{10,11... | collective-permute-start | bytes 393224 | tf_op jit(solution)/shard_map/ppermute | solution.py:271
  17.2 1.1 %copy-start.1 = (f32[160,128]{1,0:T(8,128)S(1)}, f32[160,128]{1,0:T(8,128)}, u32[]{:S(2)}) copy-start(f32[160,128]{1,0:T(8,128)} %constant.5.clone.broad) | copy-start | bytes 245764

commit v22 on v21

--- a/solution.py
+++ b/solution.py
@@ -223,15 +223,14 @@
         )
 
         def section_of(step):
-            sides, norms = [], []
+            sides = []
             for m in (2 * step, 2 * step + 1):
                 h_re, h_im = bank[0, m], bank[1, m]
-                norms.append(jnp.sum((h_re * h_re + h_im * h_im) * inverse_density, keepdims=True))
                 c_re = h_re[None] * white_re + h_im[None] * white_im
                 c_im = h_re[None] * white_im - h_im[None] * white_re
                 both = jnp.concatenate([c_re, c_im], axis=0).reshape(2 * GROUP * ROWS, LANES)
                 sides.append(both.astype(jnp.bfloat16))
-            return dot(third, jnp.concatenate(sides, axis=1)), norms
+            return dot(third, jnp.concatenate(sides, axis=1))
 
         def waves_of(section):
             sides = []
@@ -242,25 +241,29 @@
                 sides.append(turned.reshape(half, 2 * LANES).astype(jnp.bfloat16))
             return dot(jnp.concatenate(sides, axis=0), narrow[fourth])
 
-        def peak_of(m, wave, norm, result):
+        def peak_of(m, wave, result):
             square = wave[:, :LANES] * wave[:, :LANES] + wave[:, LANES:] * wave[:, LANES:]
             top = jnp.max(jnp.max(square.reshape(GROUP, FINE, LANES), axis=1), axis=1, keepdims=True)
-            value = jnp.sqrt(top) / (jnp.sqrt(norm) * math.sqrt(energy))
-            return jnp.where(column == m, value, result)
+            return jnp.where(column == m, top, result)
 
         result = jnp.zeros((GROUP, LANES), jnp.float32)
         ready, waiting = section_of(0), None
         for step in range(count // 2):
-            section, norms = ready
+            section = ready
             if step + 1 < count // 2:
                 ready = section_of(step + 1)
             waves = waves_of(section)
             if waiting is not None:
                 for ready_peak in waiting:
                     result = peak_of(*ready_peak, result)
-            waiting = [(2 * step + i, waves[i * half:(i + 1) * half], norms[i]) for i in range(2)]
+            waiting = [(2 * step + i, waves[i * half:(i + 1) * half]) for i in range(2)]
         for ready_peak in waiting:
             result = peak_of(*ready_peak, result)
+        weight = jnp.sum((bank[0] * bank[0] + bank[1] * bank[1]) * inverse_density[None], axis=1)
+        norm = jnp.sum(weight, axis=1, keepdims=True)
+        spot = lax.broadcasted_iota(jnp.int32, (count, LANES), 0) == lax.broadcasted_iota(jnp.int32, (count, LANES), 1)
+        norm = jnp.sum(jnp.where(spot, norm, 0.0), axis=0, keepdims=True)
+        result = jnp.sqrt(result) / (jnp.sqrt(norm) * math.sqrt(energy))
         out[pl.ds(number * GROUP, GROUP)] = result[:, :count]
         return carry
 

time: 22 us -> 22 us (level)
  no operation moved by 1% of the time
where the time goes in v22:
time: 22 us; the launch traced here: 21.7 us
  starting transfers between devices  11.1 us (50%)
  waiting for transfers between devices  5.45 us (25%)
  Pallas kernels  3.77 us (17%)
  local copies, waits for them, and re-layouts  1.37 us (6%)
    all_to_all x1, starting transfers between devices, on_device(): lax.all_to_all(copies, ('tm', 'tmpl'), split_axis=0, concat_axis=0, tiled...  7.3 us
    ppermute x4, waiting for transfers between devices, swap(): lax.ppermute(array, axis, [(i, i ^ bits) for i in range(lax.axis_size(axi...  5.45 us
    ppermute x4, starting transfers between devices, swap(): lax.ppermute(array, axis, [(i, i ^ bits) for i in range(lax.axis_size(axi...  3.81 us
    pallas_call x1, Pallas kernels, on_device(): pl.pallas_call(functools.partial(filter_kernel, energy), out_shape=jax.Sh...  3.48 us
    broadcast_in_dim x1, local copies, waits for them, and re-layouts, on_device(): copies = jnp.broadcast_to(chunk, (devices // 2, size * ROWS, LANES))  1.36 us
  transfers between devices with their start and end apart: 5, of which 4 were waited for; matrix products, arithmetic and copies ran while one was open for 0% of the time, Pallas kernels for 1%

profile of v22, /device:TPU:0, one launch (start us, length us, event | category | flops | bytes accessed | tf_op | source)
XLA Modules:
  0.0 21.7 jit_solution(1492284907414226823)
XLA Ops:
  0.0 0.0 copy-start.2
  0.0 0.0 copy-start.3
  0.0 1.4 %broadcast_in_dim.8 = f32[16,16,128]{2,1,0:T(8,128)} broadcast(f32[16,128]{1,0:T(8,128)} %bitcast.4), dimensions={1,2} | broadcast | bytes 139264 | tf_op jit(solution)/shard_map/broadcast_in_dim | solution.py:288
  1.4 0.0 copy-start
  1.4 7.3 %all-to-all-start = ((f32[32,8,128]{2,1,0:T(8,128)}), f32[32,8,128]{2,1,0:T(8,128)S(1)}, u32[]{:S(2)}, u32[]{:S(2)}) async-start(f32[32,8,128]{2,1,0:T(8,128)} %bitcast.1), calls=%async_computation | async-start | bytes 262144 | tf_op jit(solution)/shard_map/all_to_all | solution.py:291
  8.7 0.0 copy-done.2
  8.7 1.8 %collective-permute-start = (bf16[2,16,512]{2,1,0:T(8,128)(2,1)S(1)}, bf16[2,16,512]{2,1,0:T(8,128)(2,1)S(1)}, u32[]{:S(2)}, u32[]{:S(2)}) collective-permute-start(bf16[2,16,512]{2,1,0:T(8,128)(2,1)S(1)} %copy-done.2), channel_id=1, source_target_pairs={{0,8},{8,0},{16,24},{24,16},{1,9},{9,1},{17,25},{25,17},{2,10},{10... | collective-permute-start | bytes 98312 | tf_op jit(solution)/shard_map/ppermute | solution.py:274
  10.5 1.5 %collective-permute-start.1 = (bf16[2,16,512]{2,1,0:T(8,128)(2,1)S(1)}, bf16[2,16,512]{2,1,0:T(8,128)(2,1)S(1)}, u32[]{:S(2)}, u32[]{:S(2)}) collective-permute-start(bf16[2,16,512]{2,1,0:T(8,128)(2,1)S(1)} %copy-done.2), channel_id=1, source_target_pairs={{0,16},{8,24},{16,0},{24,8},{1,17},{9,25},{17,1},{25,9},{2,18},{10... | collective-permute-start | bytes 98312 | tf_op jit(solution)/shard_map/ppermute | solution.py:274
  12.0 0.3 %collective-permute-start.2 = (bf16[2,16,512]{2,1,0:T(8,128)(2,1)S(1)}, bf16[2,16,512]{2,1,0:T(8,128)(2,1)S(1)}, u32[]{:S(2)}, u32[]{:S(2)}) collective-permute-start(bf16[2,16,512]{2,1,0:T(8,128)(2,1)S(1)} %copy-done.2), channel_id=1, source_target_pairs={{0,24},{8,16},{16,8},{24,0},{1,25},{9,17},{17,9},{25,1},{2,26},{10... | collective-permute-start | bytes 98312 | tf_op jit(solution)/shard_map/ppermute | solution.py:274
  12.2 0.6 %collective-permute-done.refs_1_ = bf16[2,16,512]{2,1,0:T(8,128)(2,1)S(1)} collective-permute-done((bf16[2,16,512]{2,1,0:T(8,128)(2,1)S(1)}, bf16[2,16,512]{2,1,0:T(8,128)(2,1)S(1)}, u32[]{:S(2)}, u32[]{:S(2)}) %collective-permute-start) | collective-permute-done | bytes 32800 | tf_op jit(solution)/shard_map/ppermute | solution.py:274
  12.8 1.7 %collective-permute-done.1.refs_2_ = bf16[2,16,512]{2,1,0:T(8,128)(2,1)S(1)} collective-permute-done((bf16[2,16,512]{2,1,0:T(8,128)(2,1)S(1)}, bf16[2,16,512]{2,1,0:T(8,128)(2,1)S(1)}, u32[]{:S(2)}, u32[]{:S(2)}) %collective-permute-start.1) | collective-permute-done | bytes 32800 | tf_op jit(solution)/shard_map/ppermute | solution.py:274
  14.5 2.4 %collective-permute-done.2.refs_3_ = bf16[2,16,512]{2,1,0:T(8,128)(2,1)S(1)} collective-permute-done((bf16[2,16,512]{2,1,0:T(8,128)(2,1)S(1)}, bf16[2,16,512]{2,1,0:T(8,128)(2,1)S(1)}, u32[]{:S(2)}, u32[]{:S(2)}) %collective-permute-start.2) | collective-permute-done | bytes 32800 | tf_op jit(solution)/shard_map/ppermute | solution.py:274
  16.9 0.0 all-to-all-done.mine
  16.9 0.3 %collective-permute-start.3 = (f32[32,8,128]{2,1,0:T(8,128)S(1)}, f32[32,8,128]{2,1,0:T(8,128)S(1)}, u32[]{:S(2)}, u32[]{:S(2)}) collective-permute-start(f32[32,8,128]{2,1,0:T(8,128)S(1)} %all-to-all-done.mine), channel_id=1, source_target_pairs={{0,1},{1,0},{2,3},{3,2},{4,5},{5,4},{6,7},{7,6},{8,9},{9,8},{10,11... | collective-permute-start | bytes 393224 | tf_op jit(solution)/shard_map/ppermute | solution.py:274
  17.2 0.0 copy-done.3
  17.2 0.0 copy-start.1
  17.2 0.3 %bank.1 = f32[2,16,16,128]{3,2,1,0:T(8,128)S(1)} custom-call(bf16[2,16,512]{2,1,0:T(8,128)(2,1)S(1)} %copy-done.2, bf16[2,16,512]{2,1,0:T(8,128)(2,1)S(1)} %collective-permute-done.refs_1_, bf16[2,16,512]{2,1,0:T(8,128)(2,1)S(1)} %collective-permute-done.1.refs_2_, bf16[2,16,512]{2,1,0:T(8,128)(2,1)S(1)} %collective-permute-done.2.refs_3_, s32[1,16]{1,0:T(1,128)S(1)} %bitcast.3), custom_call_target="tpu_custom_call" | custom-call | bytes 2500000 | tf_op jit(solution)/shard_map/bank/pallas_call | solution.py:296
  17.5 0.8 %collective-permute-done.3.others = f32[32,8,128]{2,1,0:T(8,128)S(1)} collective-permute-done((f32[32,8,128]{2,1,0:T(8,128)S(1)}, f32[32,8,128]{2,1,0:T(8,128)S(1)}, u32[]{:S(2)}, u32[]{:S(2)}) %collective-permute-start.3) | collective-permute-done | bytes 131104 | tf_op jit(solution)/shard_map/ppermute | solution.py:274
  18.2 0.0 copy-done
  18.3 0.0 copy-done.1
  18.3 3.5 %matched_filter.1 = f32[8,16]{1,0:T(8,128)} custom-call(f32[32,8,128]{2,1,0:T(8,128)S(1)} %all-to-all-done.mine, f32[32,8,128]{2,1,0:T(8,128)S(1)} %collective-permute-done.3.others, f32[2,16,16,128]{3,2,1,0:T(8,128)S(1)} %bank.1, bf16[704,256]{1,0:T(8,128)(2,1)S(1)} %copy-done, f32[160,128]{1,0:T(8,128)S(1)} %copy-done.1), custom_call_target="tpu_custom_call" | custom-call | tf_op jit(solution)/shard_map/matched_filter/pallas_call | solution.py:307
Async XLA Ops:
  0.0 8.7 %copy-start.2 = (bf16[2,16,512]{2,1,0:T(8,128)(2,1)S(1)}, bf16[2,16,512]{2,1,0:T(8,128)(2,1)}, u32[]{:S(2)}) copy-start(bf16[2,16,512]{2,1,0:T(8,128)(2,1)} %refs_0_) | copy-start | bytes 98308
  0.0 17.2 %copy-start.3 = (s32[16]{0:T(128)S(1)}, s32[16]{0:T(128)}, u32[]{:S(2)}) copy-start(s32[16]{0:T(128)} %param.7) | copy-start | bytes 196
  1.4 16.9 %copy-start = (bf16[704,256]{1,0:T(8,128)(2,1)S(1)}, bf16[704,256]{1,0:T(8,128)(2,1)}, u32[]{:S(2)}) copy-start(bf16[704,256]{1,0:T(8,128)(2,1)} %constant.4.clone.narrow) | copy-start | bytes 1081348
  1.4 15.5 %all-to-all-start = ((f32[32,8,128]{2,1,0:T(8,128)}), f32[32,8,128]{2,1,0:T(8,128)S(1)}, u32[]{:S(2)}, u32[]{:S(2)}) async-start(f32[32,8,128]{2,1,0:T(8,128)} %bitcast.1), calls=%async_computation | async-start | bytes 262144 | tf_op jit(solution)/shard_map/all_to_all | solution.py:291
  8.7 4.2 %collective-permute-start = (bf16[2,16,512]{2,1,0:T(8,128)(2,1)S(1)}, bf16[2,16,512]{2,1,0:T(8,128)(2,1)S(1)}, u32[]{:S(2)}, u32[]{:S(2)}) collective-permute-start(bf16[2,16,512]{2,1,0:T(8,128)(2,1)S(1)} %copy-done.2), channel_id=1, source_target_pairs={{0,8},{8,0},{16,24},{24,16},{1,9},{9,1},{17,25},{25,17},{2,10},{10... | collective-permute-start | bytes 98312 | tf_op jit(solution)/shard_map/ppermute | solution.py:274
  10.5 4.0 %collective-permute-start.1 = (bf16[2,16,512]{2,1,0:T(8,128)(2,1)S(1)}, bf16[2,16,512]{2,1,0:T(8,128)(2,1)S(1)}, u32[]{:S(2)}, u32[]{:S(2)}) collective-permute-start(bf16[2,16,512]{2,1,0:T(8,128)(2,1)S(1)} %copy-done.2), channel_id=1, source_target_pairs={{0,16},{8,24},{16,0},{24,8},{1,17},{9,25},{17,1},{25,9},{2,18},{10... | collective-permute-start | bytes 98312 | tf_op jit(solution)/shard_map/ppermute | solution.py:274
  12.0 4.9 %collective-permute-start.2 = (bf16[2,16,512]{2,1,0:T(8,128)(2,1)S(1)}, bf16[2,16,512]{2,1,0:T(8,128)(2,1)S(1)}, u32[]{:S(2)}, u32[]{:S(2)}) collective-permute-start(bf16[2,16,512]{2,1,0:T(8,128)(2,1)S(1)} %copy-done.2), channel_id=1, source_target_pairs={{0,24},{8,16},{16,8},{24,0},{1,25},{9,17},{17,9},{25,1},{2,26},{10... | collective-permute-start | bytes 98312 | tf_op jit(solution)/shard_map/ppermute | solution.py:274
  16.9 1.3 %collective-permute-start.3 = (f32[32,8,128]{2,1,0:T(8,128)S(1)}, f32[32,8,128]{2,1,0:T(8,128)S(1)}, u32[]{:S(2)}, u32[]{:S(2)}) collective-permute-start(f32[32,8,128]{2,1,0:T(8,128)S(1)} %all-to-all-done.mine), channel_id=1, source_target_pairs={{0,1},{1,0},{2,3},{3,2},{4,5},{5,4},{6,7},{7,6},{8,9},{9,8},{10,11... | collective-permute-start | bytes 393224 | tf_op jit(solution)/shard_map/ppermute | solution.py:274
  17.2 1.1 %copy-start.1 = (f32[160,128]{1,0:T(8,128)S(1)}, f32[160,128]{1,0:T(8,128)}, u32[]{:S(2)}) copy-start(f32[160,128]{1,0:T(8,128)} %constant.5.clone.broad) | copy-start | bytes 245764
